TPU v7x, 512 devices: a whole 4x4x16 slice. The times are simulated.
512 devices in a mesh: segment: 8 (over x, core), row: 64 (over y, z).
Axes of the slice: x: 4, y: 4, z: 16, core: 2. Of those that a mesh axis runs over, the one named last changes fastest.
Arguments:
- layer_input: bfloat16 [8, 240, 65536], P('segment', None, 'row'), may hold values from 0.0099487305 to 4
- weight_blocks: bfloat16 [8, 512, 16, 128, 128], P('segment', 'row'), may hold values from -0.125 to 0.125
- neuron_bias: float32 [8, 65536], P('segment', 'row'), may hold values from -0.5 to 0.5
- block_slots: int32 [8, 512, 16], P('segment', 'row'), may hold values from 0 to 127, as said below
- send_lists: int32 [8, 64, 64, 2], P('segment', 'row'), may hold values from -1 to 511, as said below
Outputs:
- next_state: bfloat16 [8, 240, 65536], P('segment', None, 'row')
Inputs may be any that keep to these rules, and one draw needn't show every extreme that they name: `send_lists`: each entry is -1 or a block of the sending device s, from s * 8 to (s + 1) * 8 - 1; the entries of one sender and receiver are distinct. For each layer and receiving device exactly 64 entries are not -1, and some sender fills all 2 of its slots. `block_slots`: every slot named is a non-empty entry of that device's incoming list; the 16 slots of one block are distinct, and every non-empty slot of a device's list is named by some block of that device.
All inputs are finite; a program needn't handle non-finite values.
Results may differ from a plain program's by a relative error of at most 0.001.
Values may be sent and summed in bfloat16 or wider, within the bound.
No kernel may reach another device: no remote copies, remote signals or barrier semaphores. Data moves between devices by JAX's collectives and lax.ppermute only.
A program may use at most 192 MiB of HBM per device.

v0:
```python
import jax
import jax.numpy as jnp
from jax import lax
from jax.sharding import PartitionSpec as P

CLAMP_TOP = 3.0


def shifted_2(value, axis, steps):
    count = lax.axis_size(axis)
    pairs = [(source, (source + steps) % count) for source in range(count)]
    return lax.ppermute(value, axis, pairs)


def apply_layer(samples_in, weight_blocks, neuron_bias, block_slots, send_lists):
    sample_count = samples_in.shape[0]
    per_device = weight_blocks.shape[0]
    block_width = weight_blocks.shape[-1]
    slot_index = block_slots.reshape(-1)
    position = lax.axis_index("row")
    blocks = samples_in.reshape(sample_count, per_device, block_width)
    sent_blocks = send_lists.reshape(-1)
    occupied = sent_blocks >= 0
    local_ids = jnp.clip(sent_blocks - position * per_device, 0, per_device - 1)
    outgoing = jnp.take(blocks, local_ids, axis=1)
    outgoing = jnp.where(occupied[None, :, None], outgoing, jnp.zeros((), jnp.bfloat16))
    incoming = lax.all_to_all(outgoing, "row", split_axis=1, concat_axis=1, tiled=True)
    picked = jnp.take(incoming, slot_index, axis=1)
    picked = picked.reshape(sample_count, per_device, -1, block_width)
    mixed = jnp.einsum("mjkb,jkbc->mjc", picked, weight_blocks, preferred_element_type=jnp.float32)
    result = mixed.reshape(sample_count, per_device * block_width) + neuron_bias
    return jnp.clip(result, 0.0, CLAMP_TOP).astype(jnp.bfloat16)


def body(layer_input, weight_blocks, neuron_bias, block_slots, send_lists):
    samples_all = layer_input[0]
    weights_here = weight_blocks[0]
    bias_here = neuron_bias[0]
    slots_here = block_slots[0]
    lists_here = send_lists[0]
    layer_out = apply_layer(samples_all, weights_here, bias_here, slots_here, lists_here)
    shifted = shifted_2(layer_out, "segment", 1)
    return shifted[None]


def solution(mesh):
    placed = (
        P("segment", None, "row"),
        P("segment", "row", None, None, None),
        P("segment", "row"),
        P("segment", "row", None),
        P("segment", "row", None, None),
    )
    return jax.shard_map(
        body, mesh=mesh, in_specs=placed, out_specs=P("segment", None, "row"), check_vma=False
    )
```

profile of v0, /device:TPU:1, one launch (start us, length us, event | category | flops | bytes accessed | tf_op | source)
XLA Modules:
  0.0 407.4 jit_solution(13141801650619304970)
XLA Ops:
  0.0 0.7 subtract_clamp_fusion
  0.7 0.1 copy.15
  0.8 0.1 min.26
  0.9 0.1 min.24
  1.1 0.7 broadcast_compare_fusion
  1.8 1.1 copy.21
  2.9 0.1 copy.17
  3.0 0.1 copy.14
  3.1 0.1 ge.32
  3.2 6.5 %gather_fusion = bf16[128,240,128]{2,1,0:T(8,128)(2,1)} fusion(bf16[240,8,128]{2,0,1:T(8,128)(2,1)S(1)} %copy.17, s32[1024]{0:T(1024)S(1)} %pad_clamp_fusion.1), kind=kCustom, calls=%fused_computation | custom fusion | bytes 15729152 | tf_op jit(solution)/shard_map/jit(_take)/gather | solution.py:25
  9.7 7.4 %select_bitcast_fusion = bf16[240,128,128]{2,0,1:T(8,128)(2,1)} fusion(bf16[128,240,128]{2,1,0:T(8,128)(2,1)} %gather_fusion, pred[128]{0:T(512)(128)(4,1)S(1)} %ge.32, pred[128]{0:T(512)(128)(4,1)S(1)} %compare_and_fusion.1), kind=kLoop, calls=%fused_computation.2 | loop fusion | flops 7864320 | bytes 15728896 | tf_op jit(solution)/shard_map/jit(_where)/select_n | solution.py:26
  17.1 0.0 copy-start
  17.1 19.6 %all-to-all-start = ((bf16[240,128,128]{2,0,1:T(8,128)(2,1)}), bf16[240,128,128]{2,0,1:T(8,128)(2,1)}, u32[]{:S(2)}, u32[]{:S(2)}) async-start(bf16[240,128,128]{2,0,1:T(8,128)(2,1)} %select_bitcast_fusion), calls=%async_computation | async-start | bytes 15728640 | tf_op jit(solution)/shard_map/all_to_all | solution.py:27
  36.7 0.0 copy-done
  36.8 0.1 reshape_squeeze.11
  36.9 342.3 %all-to-all-done = bf16[240,128,128]{2,0,1:T(8,128)(2,1)} async-done(((bf16[240,128,128]{2,0,1:T(8,128)(2,1)}), bf16[240,128,128]{2,0,1:T(8,128)(2,1)}, u32[]{:S(2)}, u32[]{:S(2)}) %all-to-all-start) | async-done | bytes 7864352 | tf_op jit(solution)/shard_map/all_to_all | solution.py:27
  379.2 9.4 %gather_fusion.1 = bf16[128,240,128]{2,1,0:T(8,128)(2,1)} fusion(bf16[240,128,128]{2,0,1:T(8,128)(2,1)} %all-to-all-done, s32[1024]{0:T(1024)S(1)} %pad_clamp_fusion), kind=kCustom, calls=%fused_computation.1 | custom fusion | bytes 15729152 | tf_op jit(solution)/shard_map/jit(_take)/gather | solution.py:28
  388.6 0.0 copy-start.1
  388.6 6.7 %fusion.5 = f32[8,30,8,128]{3,2,1,0:T(8,128)S(1)} fusion(bf16[1,8,16,128,128]{4,3,2,1,0:T(8,128)(2,1)} %param.6, bf16[240,8,16,128]{3,0,2,1:T(8,128)(2,1)} %bitcast.41, pred[8,16]{1,0:T(8,128)(4,1)S(1)} %compare_and_fusion), kind=kOutput, calls=%fused_computation.8 | convolution fusion | flops 1010565120 | bytes 13041792 | tf_op jit(solution)/shard_map/mjkb,jkbc->mjc/dot_general | solution.py:30
  395.3 0.0 copy-done.1
  395.3 0.1 fusion.11
  395.4 5.4 %collective-permute-start = (bf16[240,1024]{1,0:T(8,128)(2,1)S(1)}, bf16[240,1024]{1,0:T(8,128)(2,1)S(1)}, u32[]{:S(2)}, u32[]{:S(2)}) collective-permute-start(bf16[240,1024]{1,0:T(8,128)(2,1)S(1)} %fusion.11), channel_id=1, source_target_pairs={{0,64},{64,128},{128,192},{192,256},{256,320},{320,384},{384,448},... | collective-permute-start | bytes 1474568 | tf_op jit(solution)/shard_map/ppermute | solution.py:12
  400.8 5.8 %collective-permute-done = bf16[240,1024]{1,0:T(8,128)(2,1)S(1)} collective-permute-done((bf16[240,1024]{1,0:T(8,128)(2,1)S(1)}, bf16[240,1024]{1,0:T(8,128)(2,1)S(1)}, u32[]{:S(2)}, u32[]{:S(2)}) %collective-permute-start) | collective-permute-done | bytes 491552 | tf_op jit(solution)/shard_map/ppermute | solution.py:12
  406.6 0.8 copy.24
  (6 shorter events, 0.0 us)
Async XLA Ops:
  17.1 19.6 %copy-start = (s32[1,8,16]{2,1,0:T(8,128)S(1)}, s32[1,8,16]{2,1,0:T(8,128)}, u32[]{:S(2)}) copy-start(s32[1,8,16]{2,1,0:T(8,128)} %param.8) | copy-start | bytes 1540
  17.1 362.1 %all-to-all-start = ((bf16[240,128,128]{2,0,1:T(8,128)(2,1)}), bf16[240,128,128]{2,0,1:T(8,128)(2,1)}, u32[]{:S(2)}, u32[]{:S(2)}) async-start(bf16[240,128,128]{2,0,1:T(8,128)(2,1)} %select_bitcast_fusion), calls=%async_computation | async-start | bytes 15728640 | tf_op jit(solution)/shard_map/all_to_all | solution.py:27
  388.6 6.7 %copy-start.1 = (f32[1,1024]{1,0:T(1,128)S(1)}, f32[1,1024]{1,0:T(1,128)}, u32[]{:S(2)}) copy-start(f32[1,1024]{1,0:T(1,128)} %param.7) | copy-start | bytes 12292
  395.4 11.2 %collective-permute-start = (bf16[240,1024]{1,0:T(8,128)(2,1)S(1)}, bf16[240,1024]{1,0:T(8,128)(2,1)S(1)}, u32[]{:S(2)}, u32[]{:S(2)}) collective-permute-start(bf16[240,1024]{1,0:T(8,128)(2,1)S(1)} %fusion.11), channel_id=1, source_target_pairs={{0,64},{64,128},{128,192},{192,256},{256,320},{320,384},{384,448},... | collective-permute-start | bytes 1474568 | tf_op jit(solution)/shard_map/ppermute | solution.py:12
where the time goes:
time: 409 us; the launch traced here: 407 us
  waiting for transfers between devices  348 us (85%)
  starting transfers between devices  25 us (6%)
  local copies, waits for them, and re-layouts  18.6 us (5%)
  other arithmetic  8.89 us (2%)
  matrix products  6.7 us (2%)
    all_to_all x1, waiting for transfers between devices, apply_layer(): lax.all_to_all(outgoing, 'row', split_axis=1, concat_axis=1, tiled=True)  342 us
    all_to_all x1, starting transfers between devices, apply_layer(): lax.all_to_all(outgoing, 'row', split_axis=1, concat_axis=1, tiled=True)  19.6 us
    gather x1, local copies, waits for them, and re-layouts, apply_layer(): picked = jnp.take(incoming, slot_index, axis=1)  9.44 us
  transfers between devices with their start and end apart: 2, of which 2 were waited for; matrix products, arithmetic and copies ran while one was open for 0% of the time, Pallas kernels for 0%

commit v1 on v0

v1 whole, which is shorter than its diff:
```python
import jax
import jax.numpy as jnp
from jax import lax
from jax.experimental import pallas as pl
from jax.experimental.pallas import tpu as pltpu
from jax.sharding import Mesh, PartitionSpec as P

CLAMP_TOP = 3.0
LINES = 4
STEPS = 16
CAP = 2
BLOCK = 128


def pick_kernel(ids_ref, line_ref, out_ref, sem):
    slots = STEPS * CAP

    def start(i, carry):
        z = i // (LINES * CAP)
        y = (i // CAP) % LINES
        c = i % CAP
        block = ids_ref[i] & 7
        columns = pl.ds(pl.multiple_of(block * BLOCK, BLOCK), BLOCK)
        pltpu.make_async_copy(
            line_ref.at[z, :, columns], out_ref.at[y * slots + z * CAP + c], sem
        ).start()
        return carry

    lax.fori_loop(0, STEPS * LINES * CAP, start, 0)
    pltpu.make_async_copy(out_ref, out_ref, sem).wait()


def pick(ids, line):
    rows = line.shape[1]
    count = LINES * STEPS * CAP
    return pl.pallas_call(
        pick_kernel,
        grid_spec=pltpu.PrefetchScalarGridSpec(
            num_scalar_prefetch=1,
            grid=(1,),
            in_specs=[pl.BlockSpec(memory_space=pl.ANY)],
            out_specs=pl.BlockSpec(memory_space=pl.ANY),
            scratch_shapes=[pltpu.SemaphoreType.DMA],
        ),
        out_shape=jax.ShapeDtypeStruct((count, rows, BLOCK), jnp.bfloat16),
        cost_estimate=pl.CostEstimate(
            flops=0, bytes_accessed=2 * count * rows * BLOCK * 2, transcendentals=0
        ),
        name="pick",
    )(ids, line)


def mix_kernel(slots_ref, blocks_ref, weight_ref, bias_ref, out_ref, held, sems):
    j = pl.program_id(0)
    per_device = pl.num_programs(0)
    taps = weight_ref.shape[1]

    def fetch(which, into):
        for k in range(taps):
            pltpu.make_async_copy(
                blocks_ref.at[slots_ref[which * taps + k]],
                held.at[into, :, k * BLOCK : (k + 1) * BLOCK],
                sems.at[into],
            ).start()

    @pl.when(j == 0)
    def _():
        fetch(0, 0)

    @pl.when(j + 1 < per_device)
    def _():
        fetch(j + 1, (j + 1) % 2)

    now = j % 2
    pltpu.make_async_copy(held.at[now], held.at[now], sems.at[now]).wait()
    weights = weight_ref[0].reshape(taps * BLOCK, BLOCK)
    mixed = jnp.dot(held[now], weights, preferred_element_type=jnp.float32)
    result = mixed + bias_ref[0]
    out_ref[...] = jnp.clip(result, 0.0, CLAMP_TOP).astype(jnp.bfloat16)


def mix(slots, blocks, weights, bias):
    per_device, taps = weights.shape[:2]
    rows = blocks.shape[1]
    return pl.pallas_call(
        mix_kernel,
        grid_spec=pltpu.PrefetchScalarGridSpec(
            num_scalar_prefetch=1,
            grid=(per_device,),
            in_specs=[
                pl.BlockSpec(memory_space=pl.ANY),
                pl.BlockSpec((1, taps, BLOCK, BLOCK), lambda j, s: (j, 0, 0, 0)),
                pl.BlockSpec((1, 1, BLOCK), lambda j, s: (j, 0, 0)),
            ],
            out_specs=pl.BlockSpec((rows, BLOCK), lambda j, s: (0, j)),
            scratch_shapes=[
                pltpu.VMEM((2, rows, taps * BLOCK), jnp.bfloat16),
                pltpu.SemaphoreType.DMA((2,)),
            ],
        ),
        out_shape=jax.ShapeDtypeStruct((rows, per_device * BLOCK), jnp.bfloat16),
        compiler_params=pltpu.CompilerParams(vmem_limit_bytes=16 * 2**20),
        cost_estimate=pl.CostEstimate(
            flops=2 * rows * per_device * taps * BLOCK * BLOCK,
            bytes_accessed=per_device * taps * (rows + BLOCK) * BLOCK * 2,
            transcendentals=0,
        ),
        name="mix",
    )(slots, blocks, weights, bias.reshape(per_device, 1, BLOCK))


def body(layer_input, weight_blocks, neuron_bias, block_slots, send_lists):
    samples = layer_input[0]
    lists = send_lists.reshape(LINES, STEPS, CAP).transpose(1, 0, 2)
    ids = lax.all_to_all(lists, "z", 0, 0, tiled=True).reshape(-1)
    line = lax.all_gather(samples, "z")
    outgoing = pick(ids, line)
    incoming = lax.all_to_all(outgoing, "y", 0, 0, tiled=True)
    out = mix(block_slots.reshape(-1), incoming, weight_blocks[0], neuron_bias[0])
    count = lax.axis_size("segment")
    shifted = lax.ppermute(out, "segment", [(i, (i + 1) % count) for i in range(count)])
    return shifted[None]


def solution(mesh):
    segments, row = mesh.devices.shape
    split = Mesh(
        mesh.devices.reshape(segments, row // STEPS, STEPS), ("segment", "y", "z")
    )
    row = ("y", "z")
    placed = (
        P("segment", None, row),
        P("segment", row, None, None, None),
        P("segment", row),
        P("segment", row, None),
        P("segment", row, None, None),
    )
    return jax.shard_map(
        body,
        mesh=split,
        in_specs=placed,
        out_specs=P("segment", None, row),
        check_vma=False,
    )
```

time: 409 us -> 475 us (1.16)
  Pallas kernels: 0 us -> 248 us
  waiting for transfers between devices: 348 us -> 174 us
  blocking collectives: 0 us -> 26.9 us
  starting transfers between devices: 25 us -> 8.27 us
  local copies, waits for them, and re-layouts: 18.6 us -> 4.78 us
  between operations: 0.08 us -> 13.4 us
  other arithmetic: 8.89 us -> 0 us
  matrix products: 6.7 us -> 0 us
    all_to_all x1, waiting for transfers between devices: 342 us -> 87.5 us  [body(): incoming = lax.all_to_all(outgoing, 'y', 0, 0, tiled=True)]
    pallas_call x0 -> x2, Pallas kernels: none -> 248 us  [the longest x1 240 us: pick(): pl.pallas_call(pick_kernel, grid_spec=pltpu.PrefetchScalarGridSpec(num_sc...]
    all_gather x0 -> x1, waiting for transfers between devices: none -> 79.6 us  [body(): line = lax.all_gather(samples, 'z')]
    all_to_all x0 -> x1, blocking collectives: none -> 26.9 us  [body(): ids = lax.all_to_all(lists, 'z', 0, 0, tiled=True).reshape(-1)]
    gather x2 -> x0, local copies, waits for them, and re-layouts: 15.9 us -> none  [the longest x1 9.44 us: apply_layer(): picked = jnp.take(incoming, slot_index, axis=1)]
    all_to_all x1, starting transfers between devices: 19.6 us -> 5.61 us  [body(): incoming = lax.all_to_all(outgoing, 'y', 0, 0, tiled=True)]
    select_n x3 -> x0, other arithmetic: 7.4 us -> none  [the longest x1 7.39 us: apply_layer(): jnp.where(occupied[None, :, None], outgoing, jnp.zeros((), jnp.bfloat16))]
    dot_general x1 -> x0, matrix products: 6.7 us -> none  [apply_layer(): jnp.einsum('mjkb,jkbc->mjc', picked, weight_blocks, preferred_element_typ...]
  transfers between devices with their start and end apart: 2 -> 3, of which waited for: 2 -> 3; matrix products, arithmetic and copies ran while one was open for 0% -> 0% of each run, Pallas kernels for 0% -> 0%
where the time goes in v1:
time: 475 us
  Pallas kernels  248 us (52%)
  waiting for transfers between devices  174 us (37%)
  blocking collectives  26.9 us (6%)
  between operations  13.4 us (3%)
  starting transfers between devices  8.27 us (2%)
  local copies, waits for them, and re-layouts  4.78 us (1%)
    pallas_call x1, Pallas kernels, pick(): pl.pallas_call(pick_kernel, grid_spec=pltpu.PrefetchScalarGridSpec(num_sc...  240 us
    all_to_all x1, waiting for transfers between devices, body(): incoming = lax.all_to_all(outgoing, 'y', 0, 0, tiled=True)  87.5 us
    all_gather x1, waiting for transfers between devices, body(): line = lax.all_gather(samples, 'z')  79.6 us
    all_to_all x1, blocking collectives, body(): ids = lax.all_to_all(lists, 'z', 0, 0, tiled=True).reshape(-1)  26.9 us
  transfers between devices with their start and end apart: 3, of which 3 were waited for; matrix products, arithmetic and copies ran while one was open for 0% of the time, Pallas kernels for 0%

profile of v1, /device:TPU:1, one launch (start us, length us, event | category | flops | bytes accessed | tf_op | source)
XLA Modules:
  0.0 474.7 jit_solution(16146052296978159456)
XLA Ops:
  6.5 0.0 all-gather.2.cloned.1.call-start
  6.5 0.7 all-gather.2.cloned.1.call-update
  7.3 0.8 reshape.10
  8.0 0.1 copy.8
  8.1 26.9 %all_to_all.10 = s32[16,4,2]{1,2,0:T(2,128)S(1)} all-to-all(s32[16,4,2]{1,2,0:T(2,128)S(1)} %copy.8), channel_id=1, replica_groups=mesh['segment'=8,'y'=4,'z'=16] {'z'}, dimensions={0} | all-to-all | bytes 1024 | tf_op jit(solution)/shard_map/all_to_all | solution.py:115
  35.0 0.2 copy.9
  35.2 0.7 reshape.11.ids_ref
  35.9 79.6 %all-gather.2.cloned.1.call-done.line_ref = bf16[16,240,1024]{2,1,0:T(8,128)(2,1)} async-done(((bf16[1,240,1024]{2,1,0:T(8,128)(2,1)}), bf16[16,240,1024]{2,1,0:T(8,128)(2,1)}) %all-gather.2.cloned.1.call-update) | async-done | bytes 7864336 | tf_op jit(solution)/shard_map/all_gather | solution.py:116
  115.5 240.1 %pick.1 = bf16[128,240,128]{2,1,0:T(8,128)(2,1)} custom-call(s32[128]{0:T(128)} %reshape.11.ids_ref, bf16[16,240,1024]{2,1,0:T(8,128)(2,1)} %all-gather.2.cloned.1.call-done.line_ref), custom_call_target="tpu_custom_call" | custom-call | bytes 15728640 | tf_op jit(solution)/shard_map/pick/pallas_call | solution.py:36
  355.5 0.0 copy-start.2
  355.5 0.0 copy-start.1
  355.6 5.6 %all-to-all-start.1 = ((bf16[128,240,128]{2,1,0:T(8,128)(2,1)}), bf16[128,240,128]{2,1,0:T(8,128)(2,1)}, u32[]{:S(2)}, u32[]{:S(2)}) async-start(bf16[128,240,128]{2,1,0:T(8,128)(2,1)} %pick.1), calls=%async_computation.1 | async-start | bytes 15728640 | tf_op jit(solution)/shard_map/all_to_all | solution.py:118
  361.2 0.0 copy-done.2
  361.2 0.1 reshape.9.slots_ref
  361.3 87.5 %all-to-all-done.1.blocks_ref = bf16[128,240,128]{2,1,0:T(8,128)(2,1)} async-done(((bf16[128,240,128]{2,1,0:T(8,128)(2,1)}), bf16[128,240,128]{2,1,0:T(8,128)(2,1)}, u32[]{:S(2)}, u32[]{:S(2)}) %all-to-all-start.1) | async-done | bytes 7864352 | tf_op jit(solution)/shard_map/all_to_all | solution.py:118
  448.8 0.0 copy-done.1
  448.8 0.0 copy-start
  448.8 2.2 copy-done
  451.0 7.7 %mix.1 = bf16[240,1024]{1,0:T(8,128)(2,1)S(1)} custom-call(s32[128]{0:T(128)S(1)} %reshape.9.slots_ref, bf16[128,240,128]{2,1,0:T(8,128)(2,1)} %all-to-all-done.1.blocks_ref, bf16[8,16,128,128]{3,2,1,0:T(8,128)(2,1)S(1)} %bitcast.6, f32[8,1,128]{2,1,0:T(1,128)S(1)} %bitcast.7), custom_call_target="tpu_custom_call" | custom-call | flops 1006632960 | bytes 12058624 | tf_op jit(solution)/shard_map/mix/pallas_call | solution.py:85
  458.7 2.7 collective-permute-start
  461.3 5.8 %collective-permute-done = bf16[240,1024]{1,0:T(8,128)(2,1)S(1)} collective-permute-done((bf16[240,1024]{1,0:T(8,128)(2,1)S(1)}, bf16[240,1024]{1,0:T(8,128)(2,1)S(1)}, u32[]{:S(2)}, u32[]{:S(2)}) %collective-permute-start) | collective-permute-done | bytes 491552 | tf_op jit(solution)/shard_map/ppermute | solution.py:121
  467.1 0.8 copy.11
Async XLA Ops:
  6.5 108.9 %all-gather.2.cloned.1.call-start = ((), (), s32[]{:S(2)}) async-start(), calls=%async_computation.2 | async-start | bytes 8355840 | tf_op jit(solution)/shard_map/all_gather | solution.py:116
  355.5 5.6 %copy-start.2 = (s32[1,8,16]{2,1,0:T(8,128)S(1)}, s32[1,8,16]{2,1,0:T(8,128)}, u32[]{:S(2)}) copy-start(s32[1,8,16]{2,1,0:T(8,128)} %param.8) | copy-start | bytes 1540
  355.5 93.2 %copy-start.1 = (f32[1,1024]{1,0:T(1,128)S(1)}, f32[1,1024]{1,0:T(1,128)}, u32[]{:S(2)}) copy-start(f32[1,1024]{1,0:T(1,128)} %param.7) | copy-start | bytes 12292
  355.6 93.2 %all-to-all-start.1 = ((bf16[128,240,128]{2,1,0:T(8,128)(2,1)}), bf16[128,240,128]{2,1,0:T(8,128)(2,1)}, u32[]{:S(2)}, u32[]{:S(2)}) async-start(bf16[128,240,128]{2,1,0:T(8,128)(2,1)} %pick.1), calls=%async_computation.1 | async-start | bytes 15728640 | tf_op jit(solution)/shard_map/all_to_all | solution.py:118
  448.8 2.2 copy-start
  458.7 8.4 %collective-permute-start = (bf16[240,1024]{1,0:T(8,128)(2,1)S(1)}, bf16[240,1024]{1,0:T(8,128)(2,1)S(1)}, u32[]{:S(2)}, u32[]{:S(2)}) collective-permute-start(bf16[240,1024]{1,0:T(8,128)(2,1)S(1)} %mix.1), channel_id=1, source_target_pairs={{0,64},{64,128},{128,192},{192,256},{256,320},{320,384},{384,448},... | collective-permute-start | bytes 1474568 | tf_op jit(solution)/shard_map/ppermute | solution.py:121
Sparse Core Ops, SparseCore 0:
  9.4 105.9 all-gather.1

commit v2 on v1

--- a/solution.py
+++ b/solution.py
@@ -13,38 +13,37 @@
 
 
 def pick_kernel(ids_ref, line_ref, out_ref, sem):
-    slots = STEPS * CAP
+    y = pl.program_id(0)
 
     def start(i, carry):
-        z = i // (LINES * CAP)
-        y = (i // CAP) % LINES
-        c = i % CAP
-        block = ids_ref[i] & 7
+        z = i // CAP
+        block = ids_ref[(z * LINES + y) * CAP + i % CAP] & 7
         columns = pl.ds(pl.multiple_of(block * BLOCK, BLOCK), BLOCK)
-        pltpu.make_async_copy(
-            line_ref.at[z, :, columns], out_ref.at[y * slots + z * CAP + c], sem
-        ).start()
+        pltpu.make_async_copy(line_ref.at[z, :, columns], out_ref.at[i], sem).start()
         return carry
 
-    lax.fori_loop(0, STEPS * LINES * CAP, start, 0)
+    lax.fori_loop(0, STEPS * CAP, start, 0)
     pltpu.make_async_copy(out_ref, out_ref, sem).wait()
 
 
 def pick(ids, line):
     rows = line.shape[1]
-    count = LINES * STEPS * CAP
+    count = STEPS * CAP
     return pl.pallas_call(
         pick_kernel,
         grid_spec=pltpu.PrefetchScalarGridSpec(
             num_scalar_prefetch=1,
-            grid=(1,),
+            grid=(LINES,),
             in_specs=[pl.BlockSpec(memory_space=pl.ANY)],
-            out_specs=pl.BlockSpec(memory_space=pl.ANY),
+            out_specs=pl.BlockSpec((count, rows, BLOCK), lambda y, ids: (y, 0, 0)),
             scratch_shapes=[pltpu.SemaphoreType.DMA],
         ),
-        out_shape=jax.ShapeDtypeStruct((count, rows, BLOCK), jnp.bfloat16),
+        out_shape=jax.ShapeDtypeStruct((LINES * count, rows, BLOCK), jnp.bfloat16),
+        compiler_params=pltpu.CompilerParams(vmem_limit_bytes=16 * 2**20),
         cost_estimate=pl.CostEstimate(
-            flops=0, bytes_accessed=2 * count * rows * BLOCK * 2, transcendentals=0
+            flops=0,
+            bytes_accessed=2 * LINES * count * rows * BLOCK * 2,
+            transcendentals=0,
         ),
         name="pick",
     )(ids, line)

time: 475 us -> 247 us (0.52)
  Pallas kernels: 248 us -> 12.9 us
  local copies, waits for them, and re-layouts: 4.78 us -> 10.6 us
    pallas_call x1, Pallas kernels: 240 us -> 5.24 us  [pick(): pl.pallas_call(pick_kernel, grid_spec=pltpu.PrefetchScalarGridSpec(num_sc...]
    unnamed x7 -> x11, local copies, waits for them, and re-layouts: 2.98 us -> 9.36 us
  transfers between devices with their start and end apart: 3 -> 3, of which waited for: 3 -> 3; matrix products, arithmetic and copies ran while one was open for 0% -> 1% of each run, Pallas kernels for 0% -> 0%
where the time goes in v2:
time: 247 us; the launch traced here: 246 us
  waiting for transfers between devices  174 us (70%)
  blocking collectives  26.9 us (11%)
  between operations  13.4 us (5%)
  Pallas kernels  12.9 us (5%)
  local copies, waits for them, and re-layouts  10.6 us (4%)
  starting transfers between devices  8.32 us (3%)
    all_to_all x1, waiting for transfers between devices, body(): incoming = lax.all_to_all(outgoing, 'y', 0, 0, tiled=True)  87.5 us
    all_gather x1, waiting for transfers between devices, body(): line = lax.all_gather(samples, 'z')  80.1 us
    all_to_all x1, blocking collectives, body(): ids = lax.all_to_all(lists, 'z', 0, 0, tiled=True).reshape(-1)  26.9 us
    unnamed x11, local copies, waits for them, and re-layouts  9.36 us
    pallas_call x1, Pallas kernels, mix(): pl.pallas_call(mix_kernel, grid_spec=pltpu.PrefetchScalarGridSpec(num_sca...  7.71 us
    ppermute x1, waiting for transfers between devices, body(): lax.ppermute(out, 'segment', [(i, (i + 1) % count) for i in range(count)])  5.77 us
    all_to_all x1, starting transfers between devices, body(): incoming = lax.all_to_all(outgoing, 'y', 0, 0, tiled=True)  5.68 us
    pallas_call x1, Pallas kernels, pick(): pl.pallas_call(pick_kernel, grid_spec=pltpu.PrefetchScalarGridSpec(num_sc...  5.24 us
  transfers between devices with their start and end apart: 3, of which 3 were waited for; matrix products, arithmetic and copies ran while one was open for 1% of the time, Pallas kernels for 0%

profile of v2, /device:TPU:1, one launch (start us, length us, event | category | flops | bytes accessed | tf_op | source)
XLA Modules:
  0.0 246.3 jit_solution(14068596563924218839)
XLA Ops:
  6.5 0.0 all-gather.2.cloned.1.call-start
  6.5 0.7 all-gather.2.cloned.1.call-update
  7.3 0.8 reshape.10
  8.0 0.1 copy.8
  8.1 26.9 %all_to_all.10 = s32[16,4,2]{1,2,0:T(2,128)S(1)} all-to-all(s32[16,4,2]{1,2,0:T(2,128)S(1)} %copy.8), channel_id=1, replica_groups=mesh['segment'=8,'y'=4,'z'=16] {'z'}, dimensions={0} | all-to-all | bytes 1024 | tf_op jit(solution)/shard_map/all_to_all | solution.py:114
  35.0 0.2 copy.9
  35.2 0.1 reshape.11.ids_ref
  35.4 80.1 %all-gather.2.cloned.1.call-done.line_ref = bf16[16,240,1024]{2,1,0:T(8,128)(2,1)} async-done(((bf16[1,240,1024]{2,1,0:T(8,128)(2,1)}), bf16[16,240,1024]{2,1,0:T(8,128)(2,1)}) %all-gather.2.cloned.1.call-update) | async-done | bytes 7864336 | tf_op jit(solution)/shard_map/all_gather | solution.py:115
  115.5 0.0 copy-start.1
  115.5 3.2 %copy-done.1 = bf16[16,240,1024]{2,1,0:T(8,128)(2,1)S(1)} copy-done((bf16[16,240,1024]{2,1,0:T(8,128)(2,1)S(1)}, bf16[16,240,1024]{2,1,0:T(8,128)(2,1)}, u32[]{:S(2)}) %copy-start.1) | copy-done | bytes 7864344
  118.7 5.2 %pick.1 = bf16[128,240,128]{2,1,0:T(8,128)(2,1)S(1)} custom-call(s32[128]{0:T(128)S(1)} %reshape.11.ids_ref, bf16[16,240,1024]{2,1,0:T(8,128)(2,1)S(1)} %copy-done.1), custom_call_target="tpu_custom_call" | custom-call | bytes 15728640 | tf_op jit(solution)/shard_map/pick/pallas_call | solution.py:32
  123.9 0.0 copy-start
  124.0 3.2 %copy-done = bf16[128,240,128]{2,1,0:T(8,128)(2,1)} copy-done((bf16[128,240,128]{2,1,0:T(8,128)(2,1)}, bf16[128,240,128]{2,1,0:T(8,128)(2,1)S(1)}, u32[]{:S(2)}) %copy-start) | copy-done | bytes 7864344
  127.1 0.0 copy-start.4
  127.1 0.0 copy-start.3
  127.1 5.7 %all-to-all-start.1 = ((bf16[128,240,128]{2,1,0:T(8,128)(2,1)}), bf16[128,240,128]{2,1,0:T(8,128)(2,1)}, u32[]{:S(2)}, u32[]{:S(2)}) async-start(bf16[128,240,128]{2,1,0:T(8,128)(2,1)} %copy-done), calls=%async_computation.1 | async-start | bytes 15728640 | tf_op jit(solution)/shard_map/all_to_all | solution.py:117
  132.8 0.0 copy-done.4
  132.8 0.1 reshape.9.slots_ref
  132.9 87.5 %all-to-all-done.1.blocks_ref = bf16[128,240,128]{2,1,0:T(8,128)(2,1)} async-done(((bf16[128,240,128]{2,1,0:T(8,128)(2,1)}), bf16[128,240,128]{2,1,0:T(8,128)(2,1)}, u32[]{:S(2)}, u32[]{:S(2)}) %all-to-all-start.1) | async-done | bytes 7864352 | tf_op jit(solution)/shard_map/all_to_all | solution.py:117
  220.4 0.0 copy-done.3
  220.4 0.0 copy-start.2
  220.4 2.2 copy-done.2
  222.6 7.7 %mix.1 = bf16[240,1024]{1,0:T(8,128)(2,1)S(1)} custom-call(s32[128]{0:T(128)S(1)} %reshape.9.slots_ref, bf16[128,240,128]{2,1,0:T(8,128)(2,1)} %all-to-all-done.1.blocks_ref, bf16[8,16,128,128]{3,2,1,0:T(8,128)(2,1)S(1)} %bitcast.6, f32[8,1,128]{2,1,0:T(1,128)S(1)} %bitcast.7), custom_call_target="tpu_custom_call" | custom-call | flops 1006632960 | bytes 12058624 | tf_op jit(solution)/shard_map/mix/pallas_call | solution.py:84
  230.3 2.6 %collective-permute-start = (bf16[240,1024]{1,0:T(8,128)(2,1)S(1)}, bf16[240,1024]{1,0:T(8,128)(2,1)S(1)}, u32[]{:S(2)}, u32[]{:S(2)}) collective-permute-start(bf16[240,1024]{1,0:T(8,128)(2,1)S(1)} %mix.1), channel_id=1, source_target_pairs={{0,64},{64,128},{128,192},{192,256},{256,320},{320,384},{384,448},... | collective-permute-start | bytes 1474568 | tf_op jit(solution)/shard_map/ppermute | solution.py:120
  232.9 5.8 %collective-permute-done = bf16[240,1024]{1,0:T(8,128)(2,1)S(1)} collective-permute-done((bf16[240,1024]{1,0:T(8,128)(2,1)S(1)}, bf16[240,1024]{1,0:T(8,128)(2,1)S(1)}, u32[]{:S(2)}, u32[]{:S(2)}) %collective-permute-start) | collective-permute-done | bytes 491552 | tf_op jit(solution)/shard_map/ppermute | solution.py:120
  238.7 0.8 copy.11
Async XLA Ops:
  6.5 108.9 %all-gather.2.cloned.1.call-start = ((), (), s32[]{:S(2)}) async-start(), calls=%async_computation.2 | async-start | bytes 8355840 | tf_op jit(solution)/shard_map/all_gather | solution.py:115
  115.5 3.2 %copy-start.1 = (bf16[16,240,1024]{2,1,0:T(8,128)(2,1)S(1)}, bf16[16,240,1024]{2,1,0:T(8,128)(2,1)}, u32[]{:S(2)}) copy-start(bf16[16,240,1024]{2,1,0:T(8,128)(2,1)} %all-gather.2.cloned.1.call-done.line_ref) | copy-start | bytes 23592964
  123.9 3.2 %copy-start = (bf16[128,240,128]{2,1,0:T(8,128)(2,1)}, bf16[128,240,128]{2,1,0:T(8,128)(2,1)S(1)}, u32[]{:S(2)}) copy-start(bf16[128,240,128]{2,1,0:T(8,128)(2,1)S(1)} %pick.1) | copy-start | bytes 23592964
  127.1 5.7 %copy-start.4 = (s32[1,8,16]{2,1,0:T(8,128)S(1)}, s32[1,8,16]{2,1,0:T(8,128)}, u32[]{:S(2)}) copy-start(s32[1,8,16]{2,1,0:T(8,128)} %param.8) | copy-start | bytes 1540
  127.1 93.3 %copy-start.3 = (f32[1,1024]{1,0:T(1,128)S(1)}, f32[1,1024]{1,0:T(1,128)}, u32[]{:S(2)}) copy-start(f32[1,1024]{1,0:T(1,128)} %param.7) | copy-start | bytes 12292
  127.1 93.3 %all-to-all-start.1 = ((bf16[128,240,128]{2,1,0:T(8,128)(2,1)}), bf16[128,240,128]{2,1,0:T(8,128)(2,1)}, u32[]{:S(2)}, u32[]{:S(2)}) async-start(bf16[128,240,128]{2,1,0:T(8,128)(2,1)} %copy-done), calls=%async_computation.1 | async-start | bytes 15728640 | tf_op jit(solution)/shard_map/all_to_all | solution.py:117
  220.4 2.2 copy-start.2
  230.3 8.4 %collective-permute-start = (bf16[240,1024]{1,0:T(8,128)(2,1)S(1)}, bf16[240,1024]{1,0:T(8,128)(2,1)S(1)}, u32[]{:S(2)}, u32[]{:S(2)}) collective-permute-start(bf16[240,1024]{1,0:T(8,128)(2,1)S(1)} %mix.1), channel_id=1, source_target_pairs={{0,64},{64,128},{128,192},{192,256},{256,320},{320,384},{384,448},... | collective-permute-start | bytes 1474568 | tf_op jit(solution)/shard_map/ppermute | solution.py:120
Sparse Core Ops, SparseCore 0:
  9.4 105.9 all-gather.1

commit v3 on v1

v3 whole, which is shorter than its diff:
```python
import jax
import jax.numpy as jnp
from jax import lax
from jax.experimental import pallas as pl
from jax.experimental.pallas import tpu as pltpu
from jax.sharding import Mesh, PartitionSpec as P

CLAMP_TOP = 3.0
LINES = 4
STEPS = 16
CAP = 2
BLOCK = 128
KERNEL_VMEM = 24 * 2**20
RING = 160
LATE = 7
PARTS = (
    (0, -1, 1, -2, 2),
    (-3, 3, -4, 4),
    (-5, 5, -6, 6),
    (-7, 7, 8),
)


def copy_blocks(ids_ref, senders, out_ref, held, in_sems, out_sem):
    for y in range(LINES):
        for i, (z, pieces) in enumerate(senders):
            for c in range(CAP):
                block = ids_ref[(z * LINES + y) * CAP + c] & 7
                columns = pl.ds(pl.multiple_of(block * BLOCK, BLOCK), BLOCK)
                for ref, first in pieces:
                    rows = pl.ds(first, ref.shape[0])
                    pltpu.make_async_copy(
                        ref.at[:, columns], held.at[y, i * CAP + c, rows], in_sems.at[y]
                    ).start()
    for y in range(LINES):
        pltpu.make_async_copy(held.at[y], held.at[y], in_sems.at[y]).wait()
        pltpu.make_async_copy(held.at[y], out_ref.at[y], out_sem).start()
    pltpu.make_async_copy(held, held, out_sem).wait()


def pick_call(kernel, scalars, operands, count, rows, name):
    shape = (LINES, count, rows, BLOCK)
    size = LINES * count * rows * BLOCK * 2
    return pl.pallas_call(
        kernel,
        grid_spec=pltpu.PrefetchScalarGridSpec(
            num_scalar_prefetch=len(scalars),
            grid=(1,),
            in_specs=[pl.BlockSpec(memory_space=pltpu.HBM)] * len(operands),
            out_specs=pl.BlockSpec(memory_space=pltpu.HBM),
            scratch_shapes=[
                pltpu.VMEM(shape, jnp.bfloat16),
                pltpu.SemaphoreType.DMA((LINES,)),
                pltpu.SemaphoreType.DMA,
            ],
        ),
        out_shape=jax.ShapeDtypeStruct(shape, jnp.bfloat16),
        compiler_params=pltpu.CompilerParams(vmem_limit_bytes=KERNEL_VMEM),
        cost_estimate=pl.CostEstimate(
            flops=0, bytes_accessed=2 * size, transcendentals=0
        ),
        name=name,
    )(*scalars, *operands)


def pick_part(ids, here, part, pieces, rows):
    flat = [array for ps in pieces for array, _ in ps]

    def kernel(ids_ref, here_ref, *refs):
        sources, (out_ref, held, in_sems, out_sem) = refs[:-4], refs[-4:]
        senders, at = [], 0
        for offset, ps in zip(part, pieces):
            z = (here_ref[0] + (offset + STEPS)) & (STEPS - 1)
            senders.append((z, [(sources[at + n], f) for n, (_, f) in enumerate(ps)]))
            at += len(ps)
        copy_blocks(ids_ref, senders, out_ref, held, in_sems, out_sem)

    return pick_call(kernel, (ids, here), flat, len(part) * CAP, rows, "pick_part")


def pick_line(ids, line):
    def kernel(ids_ref, line_ref, out_ref, held, in_sems, out_sem):
        senders = [(z, [(line_ref.at[z], 0)]) for z in range(STEPS)]
        copy_blocks(ids_ref, senders, out_ref, held, in_sems, out_sem)

    return pick_call(kernel, (ids,), (line,), STEPS * CAP, line.shape[1], "pick_line")


def mix(codes, arrays, weights, bias):
    per_device, taps = weights.shape[:2]
    rows = arrays[0].shape[1]

    def kernel(codes_ref, *refs):
        blocks_refs = refs[: len(arrays)]
        weight_ref, bias_ref, out_ref, held, sems = refs[len(arrays) :]
        j = pl.program_id(0)

        def fetch(which, into):
            for k in range(taps):
                code = codes_ref[which * taps + k]
                for a, ref in enumerate(blocks_refs):

                    def go(ref=ref, k=k, code=code):
                        pltpu.make_async_copy(
                            ref.at[code & 255],
                            held.at[into, :, k * BLOCK : (k + 1) * BLOCK],
                            sems.at[into],
                        ).start()

                    if len(blocks_refs) == 1:
                        go()
                    else:
                        pl.when((code >> 8) == a)(go)

        @pl.when(j == 0)
        def _():
            fetch(0, 0)

        @pl.when(j + 1 < per_device)
        def _():
            fetch(j + 1, (j + 1) % 2)

        now = j % 2
        pltpu.make_async_copy(held.at[now], held.at[now], sems.at[now]).wait()
        stacked = weight_ref[0].reshape(taps * BLOCK, BLOCK)
        mixed = jnp.dot(held[now], stacked, preferred_element_type=jnp.float32)
        result = mixed + bias_ref[0]
        out_ref[...] = jnp.clip(result, 0.0, CLAMP_TOP).astype(jnp.bfloat16)

    return pl.pallas_call(
        kernel,
        grid_spec=pltpu.PrefetchScalarGridSpec(
            num_scalar_prefetch=1,
            grid=(per_device,),
            in_specs=[pl.BlockSpec(memory_space=pltpu.HBM)] * len(arrays)
            + [
                pl.BlockSpec((1, taps, BLOCK, BLOCK), lambda j, s: (j, 0, 0, 0)),
                pl.BlockSpec((1, 1, BLOCK), lambda j, s: (j, 0, 0)),
            ],
            out_specs=pl.BlockSpec((rows, BLOCK), lambda j, s: (0, j)),
            scratch_shapes=[
                pltpu.VMEM((2, rows, taps * BLOCK), jnp.bfloat16),
                pltpu.SemaphoreType.DMA((2,)),
            ],
        ),
        out_shape=jax.ShapeDtypeStruct((rows, per_device * BLOCK), jnp.bfloat16),
        compiler_params=pltpu.CompilerParams(vmem_limit_bytes=KERNEL_VMEM),
        cost_estimate=pl.CostEstimate(
            flops=2 * rows * per_device * taps * BLOCK * BLOCK,
            bytes_accessed=per_device * taps * (rows + BLOCK) * BLOCK * 2,
            transcendentals=0,
        ),
        name="mix",
    )(codes, *arrays, weights, bias.reshape(per_device, 1, BLOCK))


def shifted(value, axis, by):
    count = lax.axis_size(axis)
    return lax.ppermute(value, axis, [(i, (i + by) % count) for i in range(count)])


def over_lines(outgoing):
    incoming = lax.all_to_all(outgoing, "y", 0, 0, tiled=True)
    return incoming.reshape((-1,) + incoming.shape[2:])


def part_codes(slots, here):
    line, z, c = slots >> 5, (slots >> 1) & (STEPS - 1), slots & 1
    offset = (z - here) & (STEPS - 1)
    codes = jnp.zeros_like(slots)
    for p, part in enumerate(PARTS):
        for i, o in enumerate(part):
            code = p * 256 + line * (len(part) * CAP) + i * CAP + c
            codes = jnp.where(offset == o % STEPS, code, codes)
    return codes


def body(layer_input, weight_blocks, neuron_bias, block_slots, send_lists):
    samples, weights, bias = layer_input[0], weight_blocks[0], neuron_bias[0]
    slots = block_slots.reshape(-1)
    here = lax.axis_index("z").astype(jnp.int32)
    rest = samples[RING:]
    ring = samples[:RING]

    line = lax.all_gather(rest, "z")
    lists = send_lists.reshape(LINES, STEPS, CAP).transpose(1, 0, 2)
    ids = lax.all_to_all(lists, "z", 0, 0, tiled=True).reshape(-1)

    held = {0: [(ring, 0)]}
    up = down = ring
    for step in range(1, STEPS // 2):
        if step == 2:
            ids, up, down = lax.optimization_barrier((ids, up, down))
        if step == LATE:
            line, up, down = lax.optimization_barrier((line, up, down))
        up, down = shifted(up, "z", 1), shifted(down, "z", -1)
        held[-step], held[step] = [(up, 0)], [(down, 0)]
    half = RING // 2
    held[STEPS // 2] = [
        (shifted(up[:half], "z", 1), 0),
        (shifted(down[half:], "z", -1), half),
    ]

    arrived = []
    for part in PARTS:
        pieces = [held[o] for o in part]
        picked = pick_part(ids, here.reshape(1), part, pieces, RING)
        arrived.append(over_lines(picked))
    arrived_rest = over_lines(pick_line(ids, line))

    out_rest = shifted(mix(slots, [arrived_rest], weights, bias), "segment", 1)
    codes = part_codes(slots, here)
    out_ring = shifted(mix(codes, arrived, weights, bias), "segment", 1)
    return jnp.concatenate([out_ring, out_rest], axis=0)[None]


def solution(mesh):
    segments, row = mesh.devices.shape
    split = Mesh(
        mesh.devices.reshape(segments, row // STEPS, STEPS), ("segment", "y", "z")
    )
    row = ("y", "z")
    placed = (
        P("segment", None, row),
        P("segment", row, None, None, None),
        P("segment", row),
        P("segment", row, None),
        P("segment", row, None, None),
    )
    return jax.shard_map(
        body,
        mesh=split,
        in_specs=placed,
        out_specs=P("segment", None, row),
        check_vma=False,
    )
```

time: 475 us -> 223 us (0.47)
  Pallas kernels: 248 us -> 21.8 us
  waiting for transfers between devices: 174 us -> 42 us
  starting transfers between devices: 8.27 us -> 102 us
  local copies, waits for them, and re-layouts: 4.78 us -> 21.4 us
  blocking collectives: 26.9 us -> 19.5 us
    pallas_call x2 -> x7, Pallas kernels: 248 us -> 21.8 us  [the longest x2 11.3 us: mix(): pl.pallas_call(kernel, grid_spec=pltpu.PrefetchScalarGridSpec(num_scalar_...]
    all_to_all x1 -> x5, waiting for transfers between devices: 87.5 us -> 3.25 us  [over_lines(): incoming = lax.all_to_all(outgoing, 'y', 0, 0, tiled=True)]
    all_gather x1, waiting for transfers between devices: 79.6 us -> 0.01 us  [body(): line = lax.all_gather(rest, 'z')]
    ppermute x1 -> x18, starting transfers between devices: 2.65 us -> 81.4 us  [shifted(): lax.ppermute(value, axis, [(i, (i + by) % count) for i in range(count)])]
    ppermute x1 -> x18, waiting for transfers between devices: 5.77 us -> 38.7 us  [shifted(): lax.ppermute(value, axis, [(i, (i + by) % count) for i in range(count)])]
    all_to_all x1 -> x5, starting transfers between devices: 5.61 us -> 20.8 us  [over_lines(): incoming = lax.all_to_all(outgoing, 'y', 0, 0, tiled=True)]
    unnamed x7 -> x36, local copies, waits for them, and re-layouts: 2.98 us -> 17.5 us
    all_to_all x1, blocking collectives: 26.9 us -> 19.5 us  [body(): ids = lax.all_to_all(lists, 'z', 0, 0, tiled=True).reshape(-1)]
  transfers between devices with their start and end apart: 3 -> 24, of which waited for: 3 -> 14; matrix products, arithmetic and copies ran while one was open for 0% -> 1% of each run, Pallas kernels for 0% -> 10%
where the time goes in v3:
time: 223 us; the launch traced here: 222 us
  starting transfers between devices  102 us (46%)
  waiting for transfers between devices  42 us (19%)
  Pallas kernels  21.8 us (10%)
  local copies, waits for them, and re-layouts  21.4 us (10%)
  blocking collectives  19.5 us (9%)
  between operations  13.7 us (6%)
    ppermute x18, starting transfers between devices, shifted(): lax.ppermute(value, axis, [(i, (i + by) % count) for i in range(count)])  81.4 us
    ppermute x18, waiting for transfers between devices, shifted(): lax.ppermute(value, axis, [(i, (i + by) % count) for i in range(count)])  38.7 us
    all_to_all x5, starting transfers between devices, over_lines(): incoming = lax.all_to_all(outgoing, 'y', 0, 0, tiled=True)  20.8 us
    all_to_all x1, blocking collectives, body(): ids = lax.all_to_all(lists, 'z', 0, 0, tiled=True).reshape(-1)  19.5 us
    unnamed x36, local copies, waits for them, and re-layouts  17.5 us
    pallas_call x2, Pallas kernels, mix(): pl.pallas_call(kernel, grid_spec=pltpu.PrefetchScalarGridSpec(num_scalar_...  11.3 us
    pallas_call x5, Pallas kernels, pick_call(): pl.pallas_call(kernel, grid_spec=pltpu.PrefetchScalarGridSpec(num_scalar_...  10.5 us
  transfers between devices with their start and end apart: 24, of which 14 were waited for; matrix products, arithmetic and copies ran while one was open for 1% of the time, Pallas kernels for 10%

profile of v3, /device:TPU:1, one launch (start us, length us, event | category | flops | bytes accessed | tf_op | source)
XLA Modules:
  0.0 221.6 jit_solution(1068855711094832940)
XLA Ops:
  9.2 4.4 %collective-permute-start = (bf16[160,1024]{1,0:T(8,128)(2,1)S(1)}, bf16[160,1024]{1,0:T(8,128)(2,1)S(1)}, u32[]{:S(2)}, u32[]{:S(2)}) collective-permute-start(bf16[160,1024]{1,0:T(8,128)(2,1)S(1)} %slice_bitcast_fusion.refs_0_), channel_id=1, source_target_pairs={{0,1},{1,2},{2,3},{3,4},{4,5},{5,6},{6,7},{7,8},{8,9},{9,10},{10,1... | collective-permute-start | bytes 983048 | tf_op jit(solution)/shard_map/ppermute | solution.py:159
  13.5 9.5 %collective-permute-start.1 = (bf16[160,1024]{1,0:T(8,128)(2,1)S(1)}, bf16[160,1024]{1,0:T(8,128)(2,1)S(1)}, u32[]{:S(2)}, u32[]{:S(2)}) collective-permute-start(bf16[160,1024]{1,0:T(8,128)(2,1)S(1)} %slice_bitcast_fusion.refs_0_), channel_id=1, source_target_pairs={{0,15},{1,0},{2,1},{3,2},{4,3},{5,4},{6,5},{7,6},{8,7},{9,8},{10,9... | collective-permute-start | bytes 983048 | tf_op jit(solution)/shard_map/ppermute | solution.py:159
  23.9 19.5 %all_to_all.30 = s32[16,4,2]{1,2,0:T(2,128)S(1)} all-to-all(s32[16,4,2]{1,2,0:T(2,128)S(1)} %copy.8), channel_id=1, replica_groups=mesh['segment'=8,'y'=4,'z'=16] {'z'}, dimensions={0} | all-to-all | bytes 1024 | tf_op jit(solution)/shard_map/all_to_all | solution.py:187
  46.0 4.3 %collective-permute-start.3 = (bf16[160,1024]{1,0:T(8,128)(2,1)S(1)}, bf16[160,1024]{1,0:T(8,128)(2,1)S(1)}, u32[]{:S(2)}, u32[]{:S(2)}) collective-permute-start(bf16[160,1024]{1,0:T(8,128)(2,1)S(1)} %collective-permute-done.1.refs_2_), channel_id=1, source_target_pairs={{0,15},{1,0},{2,1},{3,2},{4,3},{5,4},{6,5},{7,6},{8,7},{9,8},{10,9... | collective-permute-start | bytes 983048 | tf_op jit(solution)/shard_map/ppermute | solution.py:159
  50.3 8.1 %collective-permute-done.2.refs_3_ = bf16[160,1024]{1,0:T(8,128)(2,1)S(1)} collective-permute-done((bf16[160,1024]{1,0:T(8,128)(2,1)S(1)}, bf16[160,1024]{1,0:T(8,128)(2,1)S(1)}, u32[]{:S(2)}, u32[]{:S(2)}) %collective-permute-start.2) | collective-permute-done | bytes 327712 | tf_op jit(solution)/shard_map/ppermute | solution.py:159
  58.4 2.5 %pick_part.4 = bf16[4,10,160,128]{3,2,1,0:T(8,128)(2,1)} custom-call(s32[128]{0:T(128)S(1)} %reshape.35.ids_ref, s32[1]{0:T(128)} %bitcast.2.here_ref, bf16[160,1024]{1,0:T(8,128)(2,1)S(1)} %slice_bitcast_fusion.refs_0_, bf16[160,1024]{1,0:T(8,128)(2,1)S(1)} %collective-permute-done.refs_1_, bf16[160,1024]{1,0:T(8,128)(2,1)S(1)} %collective-permute-done.1.refs_2_, ...), custom_call_target="tpu_custom_call" | custom-call | bytes 3276800 | tf_op jit(solution)/shard_map/pick_part/pallas_call | solution.py:44
  60.9 4.6 %all-to-all-start.1 = ((bf16[4,10,160,128]{3,2,1,0:T(8,128)(2,1)}), bf16[4,10,160,128]{3,2,1,0:T(8,128)(2,1)S(1)}, u32[]{:S(2)}, u32[]{:S(2)}) async-start(bf16[4,10,160,128]{3,2,1,0:T(8,128)(2,1)} %pick_part.4), calls=%async_computation.1 | async-start | bytes 3276800 | tf_op jit(solution)/shard_map/all_to_all | solution.py:163
  65.5 2.7 %collective-permute-start.4 = (bf16[160,1024]{1,0:T(8,128)(2,1)S(1)}, bf16[160,1024]{1,0:T(8,128)(2,1)S(1)}, u32[]{:S(2)}, u32[]{:S(2)}) collective-permute-start(bf16[160,1024]{1,0:T(8,128)(2,1)S(1)} %collective-permute-done.2.refs_3_), channel_id=1, source_target_pairs={{0,1},{1,2},{2,3},{3,4},{4,5},{5,6},{6,7},{7,8},{8,9},{9,10},{10,1... | collective-permute-start | bytes 983048 | tf_op jit(solution)/shard_map/ppermute | solution.py:159
  68.2 4.3 %collective-permute-start.5 = (bf16[160,1024]{1,0:T(8,128)(2,1)S(1)}, bf16[160,1024]{1,0:T(8,128)(2,1)S(1)}, u32[]{:S(2)}, u32[]{:S(2)}) collective-permute-start(bf16[160,1024]{1,0:T(8,128)(2,1)S(1)} %collective-permute-done.3.refs_4_), channel_id=1, source_target_pairs={{0,15},{1,0},{2,1},{3,2},{4,3},{5,4},{6,5},{7,6},{8,7},{9,8},{10,9... | collective-permute-start | bytes 983048 | tf_op jit(solution)/shard_map/ppermute | solution.py:159
  72.5 8.6 %collective-permute-done.4.refs_0_ = bf16[160,1024]{1,0:T(8,128)(2,1)S(1)} collective-permute-done((bf16[160,1024]{1,0:T(8,128)(2,1)S(1)}, bf16[160,1024]{1,0:T(8,128)(2,1)S(1)}, u32[]{:S(2)}, u32[]{:S(2)}) %collective-permute-start.4) | collective-permute-done | bytes 327712 | tf_op jit(solution)/shard_map/ppermute | solution.py:159
  83.0 4.6 %collective-permute-start.7 = (bf16[160,1024]{1,0:T(8,128)(2,1)S(1)}, bf16[160,1024]{1,0:T(8,128)(2,1)S(1)}, u32[]{:S(2)}, u32[]{:S(2)}) collective-permute-start(bf16[160,1024]{1,0:T(8,128)(2,1)S(1)} %collective-permute-done.5.refs_1_), channel_id=1, source_target_pairs={{0,15},{1,0},{2,1},{3,2},{4,3},{5,4},{6,5},{7,6},{8,7},{9,8},{10,9... | collective-permute-start | bytes 983048 | tf_op jit(solution)/shard_map/ppermute | solution.py:159
  87.6 3.9 %collective-permute-done.6.refs_2_ = bf16[160,1024]{1,0:T(8,128)(2,1)S(1)} collective-permute-done((bf16[160,1024]{1,0:T(8,128)(2,1)S(1)}, bf16[160,1024]{1,0:T(8,128)(2,1)S(1)}, u32[]{:S(2)}, u32[]{:S(2)}) %collective-permute-start.6) | collective-permute-done | bytes 327712 | tf_op jit(solution)/shard_map/ppermute | solution.py:159
  95.8 3.9 %all-to-all-start.2 = ((bf16[4,8,160,128]{3,2,1,0:T(8,128)(2,1)}), bf16[4,8,160,128]{3,2,1,0:T(8,128)(2,1)S(1)}, u32[]{:S(2)}, u32[]{:S(2)}) async-start(bf16[4,8,160,128]{3,2,1,0:T(8,128)(2,1)} %copy-done.10), calls=%async_computation.2 | async-start | bytes 2621440 | tf_op jit(solution)/shard_map/all_to_all | solution.py:163
  99.7 2.7 %collective-permute-start.8 = (bf16[160,1024]{1,0:T(8,128)(2,1)S(1)}, bf16[160,1024]{1,0:T(8,128)(2,1)S(1)}, u32[]{:S(2)}, u32[]{:S(2)}) collective-permute-start(bf16[160,1024]{1,0:T(8,128)(2,1)S(1)} %collective-permute-done.6.refs_2_), channel_id=1, source_target_pairs={{0,1},{1,2},{2,3},{3,4},{4,5},{5,6},{6,7},{7,8},{8,9},{9,10},{10,1... | collective-permute-start | bytes 983048 | tf_op jit(solution)/shard_map/ppermute | solution.py:159
  102.4 4.1 %collective-permute-start.9 = (bf16[160,1024]{1,0:T(8,128)(2,1)}, bf16[160,1024]{1,0:T(8,128)(2,1)S(1)}, u32[]{:S(2)}, u32[]{:S(2)}) collective-permute-start(bf16[160,1024]{1,0:T(8,128)(2,1)} %copy-done.15), channel_id=1, source_target_pairs={{0,15},{1,0},{2,1},{3,2},{4,3},{5,4},{6,5},{7,6},{8,7},{9,8},{10,9... | collective-permute-start | bytes 983048 | tf_op jit(solution)/shard_map/ppermute | solution.py:159
  106.5 2.5 %collective-permute-done.8.refs_0_ = bf16[160,1024]{1,0:T(8,128)(2,1)S(1)} collective-permute-done((bf16[160,1024]{1,0:T(8,128)(2,1)S(1)}, bf16[160,1024]{1,0:T(8,128)(2,1)S(1)}, u32[]{:S(2)}, u32[]{:S(2)}) %collective-permute-start.8) | collective-permute-done | bytes 327712 | tf_op jit(solution)/shard_map/ppermute | solution.py:159
  111.9 4.1 %collective-permute-start.11 = (bf16[160,1024]{1,0:T(8,128)(2,1)S(1)}, bf16[160,1024]{1,0:T(8,128)(2,1)S(1)}, u32[]{:S(2)}, u32[]{:S(2)}) collective-permute-start(bf16[160,1024]{1,0:T(8,128)(2,1)S(1)} %collective-permute-done.9.refs_1_), channel_id=1, source_target_pairs={{0,15},{1,0},{2,1},{3,2},{4,3},{5,4},{6,5},{7,6},{8,7},{9,8},{10,9... | collective-permute-start | bytes 983048 | tf_op jit(solution)/shard_map/ppermute | solution.py:159
  116.0 2.6 %collective-permute-done.10.refs_2_ = bf16[160,1024]{1,0:T(8,128)(2,1)S(1)} collective-permute-done((bf16[160,1024]{1,0:T(8,128)(2,1)S(1)}, bf16[160,1024]{1,0:T(8,128)(2,1)S(1)}, u32[]{:S(2)}, u32[]{:S(2)}) %collective-permute-start.10) | collective-permute-done | bytes 327712 | tf_op jit(solution)/shard_map/ppermute | solution.py:159
  123.9 4.5 %all-to-all-start.3 = ((bf16[4,8,160,128]{3,2,1,0:T(8,128)(2,1)}), bf16[4,8,160,128]{3,2,1,0:T(8,128)(2,1)S(1)}, u32[]{:S(2)}, u32[]{:S(2)}) async-start(bf16[4,8,160,128]{3,2,1,0:T(8,128)(2,1)} %copy-done.9), calls=%async_computation.3 | async-start | bytes 2621440 | tf_op jit(solution)/shard_map/all_to_all | solution.py:163
  128.4 3.4 %collective-permute-start.12 = (bf16[160,1024]{1,0:T(8,128)(2,1)}, bf16[160,1024]{1,0:T(8,128)(2,1)S(1)}, u32[]{:S(2)}, u32[]{:S(2)}) collective-permute-start(bf16[160,1024]{1,0:T(8,128)(2,1)} %copy-done.14), channel_id=1, source_target_pairs={{0,1},{1,2},{2,3},{3,4},{4,5},{5,6},{6,7},{7,8},{8,9},{9,10},{10,1... | collective-permute-start | bytes 983048 | tf_op jit(solution)/shard_map/ppermute | solution.py:159
  131.8 3.5 %collective-permute-start.13 = (bf16[160,1024]{1,0:T(8,128)(2,1)S(1)}, bf16[160,1024]{1,0:T(8,128)(2,1)S(1)}, u32[]{:S(2)}, u32[]{:S(2)}) collective-permute-start(bf16[160,1024]{1,0:T(8,128)(2,1)S(1)} %collective-permute-done.11.refs_3_), channel_id=1, source_target_pairs={{0,15},{1,0},{2,1},{3,2},{4,3},{5,4},{6,5},{7,6},{8,7},{9,8},{10,9... | collective-permute-start | bytes 983048 | tf_op jit(solution)/shard_map/ppermute | solution.py:159
  135.4 2.7 %collective-permute-done.12.refs_0_ = bf16[160,1024]{1,0:T(8,128)(2,1)S(1)} collective-permute-done((bf16[160,1024]{1,0:T(8,128)(2,1)}, bf16[160,1024]{1,0:T(8,128)(2,1)S(1)}, u32[]{:S(2)}, u32[]{:S(2)}) %collective-permute-start.12) | collective-permute-done | bytes 327712 | tf_op jit(solution)/shard_map/ppermute | solution.py:159
  140.3 4.4 %collective-permute-start.15 = (bf16[80,1024]{1,0:T(8,128)(2,1)S(1)}, bf16[80,1024]{1,0:T(8,128)(2,1)S(1)}, u32[]{:S(2)}, u32[]{:S(2)}) collective-permute-start(bf16[80,1024]{1,0:T(8,128)(2,1)S(1)} %slice.22), channel_id=1, source_target_pairs={{0,15},{1,0},{2,1},{3,2},{4,3},{5,4},{6,5},{7,6},{8,7},{9,8},{10,9... | collective-permute-start | bytes 491528 | tf_op jit(solution)/shard_map/ppermute | solution.py:159
  144.7 2.8 %collective-permute-done.14.refs_2_ = bf16[80,1024]{1,0:T(8,128)(2,1)S(1)} collective-permute-done((bf16[80,1024]{1,0:T(8,128)(2,1)S(1)}, bf16[80,1024]{1,0:T(8,128)(2,1)S(1)}, u32[]{:S(2)}, u32[]{:S(2)}) %collective-permute-start.14) | collective-permute-done | bytes 163872 | tf_op jit(solution)/shard_map/ppermute | solution.py:159
  150.7 4.1 %all-to-all-start.4 = ((bf16[4,6,160,128]{3,2,1,0:T(8,128)(2,1)}), bf16[4,6,160,128]{3,2,1,0:T(8,128)(2,1)S(1)}, u32[]{:S(2)}, u32[]{:S(2)}) async-start(bf16[4,6,160,128]{3,2,1,0:T(8,128)(2,1)} %pick_part.7), calls=%async_computation.4 | async-start | bytes 1966080 | tf_op jit(solution)/shard_map/all_to_all | solution.py:163
  156.6 2.9 %pick_line.1 = bf16[4,32,80,128]{3,2,1,0:T(8,128)(2,1)S(1)} custom-call(s32[128]{0:T(128)S(1)} %reshape.35.ids_ref, bf16[16,80,1024]{2,1,0:T(8,128)(2,1)S(1)} %copy-done.13), custom_call_target="tpu_custom_call" | custom-call | bytes 5242880 | tf_op jit(solution)/shard_map/pick_line/pallas_call | solution.py:44
  161.0 3.2 %all-to-all-done.4 = bf16[4,6,160,128]{3,2,1,0:T(8,128)(2,1)S(1)} async-done(((bf16[4,6,160,128]{3,2,1,0:T(8,128)(2,1)}), bf16[4,6,160,128]{3,2,1,0:T(8,128)(2,1)S(1)}, u32[]{:S(2)}, u32[]{:S(2)}) %all-to-all-start.4) | async-done | bytes 983072 | tf_op jit(solution)/shard_map/all_to_all | solution.py:163
  165.3 3.7 %all-to-all-start.5 = ((bf16[4,32,80,128]{3,2,1,0:T(8,128)(2,1)}), bf16[4,32,80,128]{3,2,1,0:T(8,128)(2,1)S(1)}, u32[]{:S(2)}, u32[]{:S(2)}) async-start(bf16[4,32,80,128]{3,2,1,0:T(8,128)(2,1)} %copy-done.2), calls=%async_computation.5 | async-start | bytes 5242880 | tf_op jit(solution)/shard_map/all_to_all | solution.py:163
  176.5 7.4 %mix.2 = bf16[160,1024]{1,0:T(8,128)(2,1)S(1)} custom-call(s32[128]{0:T(128)S(1)} %compare_select_fusion.15.codes_ref, bf16[40,160,128]{2,1,0:T(8,128)(2,1)S(1)} %bitcast.18, bf16[32,160,128]{2,1,0:T(8,128)(2,1)S(1)} %bitcast.19, bf16[32,160,128]{2,1,0:T(8,128)(2,1)S(1)} %bitcast.20, bf16[24,160,128]{2,1,0:T(8,128)(2,1)S(1)} %bitcast.21, ...), custom_call_target="tpu_custom_call" | custom-call | flops 671088640 | bytes 9437184 | tf_op jit(solution)/shard_map/mix/pallas_call | solution.py:130
  183.9 15.5 %collective-permute-start.16 = (bf16[160,1024]{1,0:T(8,128)(2,1)S(1)}, bf16[160,1024]{1,0:T(8,128)(2,1)S(1)}, u32[]{:S(2)}, u32[]{:S(2)}) collective-permute-start(bf16[160,1024]{1,0:T(8,128)(2,1)S(1)} %mix.2), channel_id=1, source_target_pairs={{0,64},{64,128},{128,192},{192,256},{256,320},{320,384},{384,448},... | collective-permute-start | bytes 983048 | tf_op jit(solution)/shard_map/ppermute | solution.py:159
  201.6 3.9 %mix.3 = bf16[80,1024]{1,0:T(8,128)(2,1)S(1)} custom-call(s32[128]{0:T(128)S(1)} %reshape.33.codes_ref, bf16[128,80,128]{2,1,0:T(8,128)(2,1)S(1)} %bitcast.17, bf16[8,16,128,128]{3,2,1,0:T(8,128)(2,1)S(1)} %bitcast.16, f32[8,1,128]{2,1,0:T(1,128)S(1)} %bitcast.23), custom_call_target="tpu_custom_call" | custom-call | flops 335544320 | bytes 6815744 | tf_op jit(solution)/shard_map/mix/pallas_call | solution.py:130
  205.5 6.2 %collective-permute-start.17 = (bf16[80,1024]{1,0:T(8,128)(2,1)S(1)}, bf16[80,1024]{1,0:T(8,128)(2,1)S(1)}, u32[]{:S(2)}, u32[]{:S(2)}) collective-permute-start(bf16[80,1024]{1,0:T(8,128)(2,1)S(1)} %mix.3), channel_id=1, source_target_pairs={{0,64},{64,128},{128,192},{192,256},{256,320},{320,384},{384,448},... | collective-permute-start | bytes 491528 | tf_op jit(solution)/shard_map/ppermute | solution.py:159
  (72 shorter events, 43.0 us)
Async XLA Ops:
  6.5 121.9 %all-gather.2.cloned.1.call-start = ((), (), s32[]{:S(2)}) async-start(), calls=%async_computation.6 | async-start | bytes 2785280 | tf_op jit(solution)/shard_map/all_gather | solution.py:185
  9.2 34.6 %collective-permute-start = (bf16[160,1024]{1,0:T(8,128)(2,1)S(1)}, bf16[160,1024]{1,0:T(8,128)(2,1)S(1)}, u32[]{:S(2)}, u32[]{:S(2)}) collective-permute-start(bf16[160,1024]{1,0:T(8,128)(2,1)S(1)} %slice_bitcast_fusion.refs_0_), channel_id=1, source_target_pairs={{0,1},{1,2},{2,3},{3,4},{4,5},{5,6},{6,7},{7,8},{8,9},{9,10},{10,1... | collective-permute-start | bytes 983048 | tf_op jit(solution)/shard_map/ppermute | solution.py:159
  13.5 30.3 %collective-permute-start.1 = (bf16[160,1024]{1,0:T(8,128)(2,1)S(1)}, bf16[160,1024]{1,0:T(8,128)(2,1)S(1)}, u32[]{:S(2)}, u32[]{:S(2)}) collective-permute-start(bf16[160,1024]{1,0:T(8,128)(2,1)S(1)} %slice_bitcast_fusion.refs_0_), channel_id=1, source_target_pairs={{0,15},{1,0},{2,1},{3,2},{4,3},{5,4},{6,5},{7,6},{8,7},{9,8},{10,9... | collective-permute-start | bytes 983048 | tf_op jit(solution)/shard_map/ppermute | solution.py:159
  43.8 14.6 %collective-permute-start.2 = (bf16[160,1024]{1,0:T(8,128)(2,1)S(1)}, bf16[160,1024]{1,0:T(8,128)(2,1)S(1)}, u32[]{:S(2)}, u32[]{:S(2)}) collective-permute-start(bf16[160,1024]{1,0:T(8,128)(2,1)S(1)} %collective-permute-done.refs_1_), channel_id=1, source_target_pairs={{0,1},{1,2},{2,3},{3,4},{4,5},{5,6},{6,7},{7,8},{8,9},{9,10},{10,1... | collective-permute-start | bytes 983048 | tf_op jit(solution)/shard_map/ppermute | solution.py:159
  46.0 12.4 %collective-permute-start.3 = (bf16[160,1024]{1,0:T(8,128)(2,1)S(1)}, bf16[160,1024]{1,0:T(8,128)(2,1)S(1)}, u32[]{:S(2)}, u32[]{:S(2)}) collective-permute-start(bf16[160,1024]{1,0:T(8,128)(2,1)S(1)} %collective-permute-done.1.refs_2_), channel_id=1, source_target_pairs={{0,15},{1,0},{2,1},{3,2},{4,3},{5,4},{6,5},{7,6},{8,7},{9,8},{10,9... | collective-permute-start | bytes 983048 | tf_op jit(solution)/shard_map/ppermute | solution.py:159
  60.9 34.9 %all-to-all-start.1 = ((bf16[4,10,160,128]{3,2,1,0:T(8,128)(2,1)}), bf16[4,10,160,128]{3,2,1,0:T(8,128)(2,1)S(1)}, u32[]{:S(2)}, u32[]{:S(2)}) async-start(bf16[4,10,160,128]{3,2,1,0:T(8,128)(2,1)} %pick_part.4), calls=%async_computation.1 | async-start | bytes 3276800 | tf_op jit(solution)/shard_map/all_to_all | solution.py:163
  65.5 15.5 %collective-permute-start.4 = (bf16[160,1024]{1,0:T(8,128)(2,1)S(1)}, bf16[160,1024]{1,0:T(8,128)(2,1)S(1)}, u32[]{:S(2)}, u32[]{:S(2)}) collective-permute-start(bf16[160,1024]{1,0:T(8,128)(2,1)S(1)} %collective-permute-done.2.refs_3_), channel_id=1, source_target_pairs={{0,1},{1,2},{2,3},{3,4},{4,5},{5,6},{6,7},{7,8},{8,9},{9,10},{10,1... | collective-permute-start | bytes 983048 | tf_op jit(solution)/shard_map/ppermute | solution.py:159
  68.2 14.8 %collective-permute-start.5 = (bf16[160,1024]{1,0:T(8,128)(2,1)S(1)}, bf16[160,1024]{1,0:T(8,128)(2,1)S(1)}, u32[]{:S(2)}, u32[]{:S(2)}) collective-permute-start(bf16[160,1024]{1,0:T(8,128)(2,1)S(1)} %collective-permute-done.3.refs_4_), channel_id=1, source_target_pairs={{0,15},{1,0},{2,1},{3,2},{4,3},{5,4},{6,5},{7,6},{8,7},{9,8},{10,9... | collective-permute-start | bytes 983048 | tf_op jit(solution)/shard_map/ppermute | solution.py:159
  81.1 10.4 %collective-permute-start.6 = (bf16[160,1024]{1,0:T(8,128)(2,1)S(1)}, bf16[160,1024]{1,0:T(8,128)(2,1)S(1)}, u32[]{:S(2)}, u32[]{:S(2)}) collective-permute-start(bf16[160,1024]{1,0:T(8,128)(2,1)S(1)} %collective-permute-done.4.refs_0_), channel_id=1, source_target_pairs={{0,1},{1,2},{2,3},{3,4},{4,5},{5,6},{6,7},{7,8},{8,9},{9,10},{10,1... | collective-permute-start | bytes 983048 | tf_op jit(solution)/shard_map/ppermute | solution.py:159
  83.0 9.5 %collective-permute-start.7 = (bf16[160,1024]{1,0:T(8,128)(2,1)S(1)}, bf16[160,1024]{1,0:T(8,128)(2,1)S(1)}, u32[]{:S(2)}, u32[]{:S(2)}) collective-permute-start(bf16[160,1024]{1,0:T(8,128)(2,1)S(1)} %collective-permute-done.5.refs_1_), channel_id=1, source_target_pairs={{0,15},{1,0},{2,1},{3,2},{4,3},{5,4},{6,5},{7,6},{8,7},{9,8},{10,9... | collective-permute-start | bytes 983048 | tf_op jit(solution)/shard_map/ppermute | solution.py:159
  95.8 26.3 %copy-start.3 = (bf16[4,10,160,128]{3,2,1,0:T(8,128)(2,1)}, bf16[4,10,160,128]{3,2,1,0:T(8,128)(2,1)S(1)}, u32[]{:S(2)}) copy-start(bf16[4,10,160,128]{3,2,1,0:T(8,128)(2,1)S(1)} %all-to-all-done.1) | copy-start | bytes 4915204
  95.8 28.1 %all-to-all-start.2 = ((bf16[4,8,160,128]{3,2,1,0:T(8,128)(2,1)}), bf16[4,8,160,128]{3,2,1,0:T(8,128)(2,1)S(1)}, u32[]{:S(2)}, u32[]{:S(2)}) async-start(bf16[4,8,160,128]{3,2,1,0:T(8,128)(2,1)} %copy-done.10), calls=%async_computation.2 | async-start | bytes 2621440 | tf_op jit(solution)/shard_map/all_to_all | solution.py:163
  99.7 9.3 %collective-permute-start.8 = (bf16[160,1024]{1,0:T(8,128)(2,1)S(1)}, bf16[160,1024]{1,0:T(8,128)(2,1)S(1)}, u32[]{:S(2)}, u32[]{:S(2)}) collective-permute-start(bf16[160,1024]{1,0:T(8,128)(2,1)S(1)} %collective-permute-done.6.refs_2_), channel_id=1, source_target_pairs={{0,1},{1,2},{2,3},{3,4},{4,5},{5,6},{6,7},{7,8},{8,9},{9,10},{10,1... | collective-permute-start | bytes 983048 | tf_op jit(solution)/shard_map/ppermute | solution.py:159
  102.4 9.5 %collective-permute-start.9 = (bf16[160,1024]{1,0:T(8,128)(2,1)}, bf16[160,1024]{1,0:T(8,128)(2,1)S(1)}, u32[]{:S(2)}, u32[]{:S(2)}) collective-permute-start(bf16[160,1024]{1,0:T(8,128)(2,1)} %copy-done.15), channel_id=1, source_target_pairs={{0,15},{1,0},{2,1},{3,2},{4,3},{5,4},{6,5},{7,6},{8,7},{9,8},{10,9... | collective-permute-start | bytes 983048 | tf_op jit(solution)/shard_map/ppermute | solution.py:159
  109.0 9.6 %collective-permute-start.10 = (bf16[160,1024]{1,0:T(8,128)(2,1)S(1)}, bf16[160,1024]{1,0:T(8,128)(2,1)S(1)}, u32[]{:S(2)}, u32[]{:S(2)}) collective-permute-start(bf16[160,1024]{1,0:T(8,128)(2,1)S(1)} %collective-permute-done.8.refs_0_), channel_id=1, source_target_pairs={{0,1},{1,2},{2,3},{3,4},{4,5},{5,6},{6,7},{7,8},{8,9},{9,10},{10,1... | collective-permute-start | bytes 983048 | tf_op jit(solution)/shard_map/ppermute | solution.py:159
  111.9 8.6 %collective-permute-start.11 = (bf16[160,1024]{1,0:T(8,128)(2,1)S(1)}, bf16[160,1024]{1,0:T(8,128)(2,1)S(1)}, u32[]{:S(2)}, u32[]{:S(2)}) collective-permute-start(bf16[160,1024]{1,0:T(8,128)(2,1)S(1)} %collective-permute-done.9.refs_1_), channel_id=1, source_target_pairs={{0,15},{1,0},{2,1},{3,2},{4,3},{5,4},{6,5},{7,6},{8,7},{9,8},{10,9... | collective-permute-start | bytes 983048 | tf_op jit(solution)/shard_map/ppermute | solution.py:159
  123.9 16.4 %copy-start.5 = (bf16[4,8,160,128]{3,2,1,0:T(8,128)(2,1)}, bf16[4,8,160,128]{3,2,1,0:T(8,128)(2,1)S(1)}, u32[]{:S(2)}) copy-start(bf16[4,8,160,128]{3,2,1,0:T(8,128)(2,1)S(1)} %all-to-all-done.2) | copy-start | bytes 3932164
  123.9 26.8 %all-to-all-start.3 = ((bf16[4,8,160,128]{3,2,1,0:T(8,128)(2,1)}), bf16[4,8,160,128]{3,2,1,0:T(8,128)(2,1)S(1)}, u32[]{:S(2)}, u32[]{:S(2)}) async-start(bf16[4,8,160,128]{3,2,1,0:T(8,128)(2,1)} %copy-done.9), calls=%async_computation.3 | async-start | bytes 2621440 | tf_op jit(solution)/shard_map/all_to_all | solution.py:163
  128.4 9.7 %collective-permute-start.12 = (bf16[160,1024]{1,0:T(8,128)(2,1)}, bf16[160,1024]{1,0:T(8,128)(2,1)S(1)}, u32[]{:S(2)}, u32[]{:S(2)}) collective-permute-start(bf16[160,1024]{1,0:T(8,128)(2,1)} %copy-done.14), channel_id=1, source_target_pairs={{0,1},{1,2},{2,3},{3,4},{4,5},{5,6},{6,7},{7,8},{8,9},{9,10},{10,1... | collective-permute-start | bytes 983048 | tf_op jit(solution)/shard_map/ppermute | solution.py:159
  131.8 8.4 %collective-permute-start.13 = (bf16[160,1024]{1,0:T(8,128)(2,1)S(1)}, bf16[160,1024]{1,0:T(8,128)(2,1)S(1)}, u32[]{:S(2)}, u32[]{:S(2)}) collective-permute-start(bf16[160,1024]{1,0:T(8,128)(2,1)S(1)} %collective-permute-done.11.refs_3_), channel_id=1, source_target_pairs={{0,15},{1,0},{2,1},{3,2},{4,3},{5,4},{6,5},{7,6},{8,7},{9,8},{10,9... | collective-permute-start | bytes 983048 | tf_op jit(solution)/shard_map/ppermute | solution.py:159
  138.1 9.3 %collective-permute-start.14 = (bf16[80,1024]{1,0:T(8,128)(2,1)S(1)}, bf16[80,1024]{1,0:T(8,128)(2,1)S(1)}, u32[]{:S(2)}, u32[]{:S(2)}) collective-permute-start(bf16[80,1024]{1,0:T(8,128)(2,1)S(1)} %slice.21), channel_id=1, source_target_pairs={{0,1},{1,2},{2,3},{3,4},{4,5},{5,6},{6,7},{7,8},{8,9},{9,10},{10,1... | collective-permute-start | bytes 491528 | tf_op jit(solution)/shard_map/ppermute | solution.py:159
  140.3 8.4 %collective-permute-start.15 = (bf16[80,1024]{1,0:T(8,128)(2,1)S(1)}, bf16[80,1024]{1,0:T(8,128)(2,1)S(1)}, u32[]{:S(2)}, u32[]{:S(2)}) collective-permute-start(bf16[80,1024]{1,0:T(8,128)(2,1)S(1)} %slice.22), channel_id=1, source_target_pairs={{0,15},{1,0},{2,1},{3,2},{4,3},{5,4},{6,5},{7,6},{8,7},{9,8},{10,9... | collective-permute-start | bytes 491528 | tf_op jit(solution)/shard_map/ppermute | solution.py:159
  150.7 8.8 %copy-start.7 = (bf16[4,8,160,128]{3,2,1,0:T(8,128)(2,1)}, bf16[4,8,160,128]{3,2,1,0:T(8,128)(2,1)S(1)}, u32[]{:S(2)}) copy-start(bf16[4,8,160,128]{3,2,1,0:T(8,128)(2,1)S(1)} %all-to-all-done.3) | copy-start | bytes 3932164
  150.7 13.5 %all-to-all-start.4 = ((bf16[4,6,160,128]{3,2,1,0:T(8,128)(2,1)}), bf16[4,6,160,128]{3,2,1,0:T(8,128)(2,1)S(1)}, u32[]{:S(2)}, u32[]{:S(2)}) async-start(bf16[4,6,160,128]{3,2,1,0:T(8,128)(2,1)} %pick_part.7), calls=%async_computation.4 | async-start | bytes 1966080 | tf_op jit(solution)/shard_map/all_to_all | solution.py:163
  154.9 1.7 copy-start.13
  161.0 7.9 %copy-start.17 = (s32[1,8,16]{2,1,0:T(8,128)S(1)}, s32[1,8,16]{2,1,0:T(8,128)}, u32[]{:S(2)}) copy-start(s32[1,8,16]{2,1,0:T(8,128)} %param.8) | copy-start | bytes 1540
  161.0 8.0 %copy-start.16 = (f32[1,1024]{1,0:T(1,128)S(1)}, f32[1,1024]{1,0:T(1,128)}, u32[]{:S(2)}) copy-start(f32[1,1024]{1,0:T(1,128)} %param.7) | copy-start | bytes 12292
  165.3 34.1 %all-to-all-start.5 = ((bf16[4,32,80,128]{3,2,1,0:T(8,128)(2,1)}), bf16[4,32,80,128]{3,2,1,0:T(8,128)(2,1)S(1)}, u32[]{:S(2)}, u32[]{:S(2)}) async-start(bf16[4,32,80,128]{3,2,1,0:T(8,128)(2,1)} %copy-done.2), calls=%async_computation.5 | async-start | bytes 5242880 | tf_op jit(solution)/shard_map/all_to_all | solution.py:163
  169.1 2.2 copy-start
  183.9 27.8 %collective-permute-start.16 = (bf16[160,1024]{1,0:T(8,128)(2,1)S(1)}, bf16[160,1024]{1,0:T(8,128)(2,1)S(1)}, u32[]{:S(2)}, u32[]{:S(2)}) collective-permute-start(bf16[160,1024]{1,0:T(8,128)(2,1)S(1)} %mix.2), channel_id=1, source_target_pairs={{0,64},{64,128},{128,192},{192,256},{256,320},{320,384},{384,448},... | collective-permute-start | bytes 983048 | tf_op jit(solution)/shard_map/ppermute | solution.py:159
  199.4 2.2 copy-start.1
  205.5 8.4 %collective-permute-start.17 = (bf16[80,1024]{1,0:T(8,128)(2,1)S(1)}, bf16[80,1024]{1,0:T(8,128)(2,1)S(1)}, u32[]{:S(2)}, u32[]{:S(2)}) collective-permute-start(bf16[80,1024]{1,0:T(8,128)(2,1)S(1)} %mix.3), channel_id=1, source_target_pairs={{0,64},{64,128},{128,192},{192,256},{256,320},{320,384},{384,448},... | collective-permute-start | bytes 491528 | tf_op jit(solution)/shard_map/ppermute | solution.py:159
  (10 other events, 11.4 us)
Sparse Core Ops, SparseCore 0:
  9.4 75.5 all-gather.1

commit v4 on v3

--- a/solution.py
+++ b/solution.py
@@ -10,14 +10,19 @@
 STEPS = 16
 CAP = 2
 BLOCK = 128
-KERNEL_VMEM = 24 * 2**20
+PICK_VMEM = 24 * 2**20
+MIX_VMEM = 58 * 2**20
+PICK_WEIGHT = 12 * 10**9
+IDS_STEP = 2
+MIX_WEIGHT = 40
+TIE = 4
+LATE = 7
 RING = 160
-LATE = 7
 PARTS = (
-    (0, -1, 1, -2, 2),
-    (-3, 3, -4, 4),
-    (-5, 5, -6, 6),
-    (-7, 7, 8),
+    (0, -1, 1),
+    (-2, 2, -3, 3),
+    (-4, 4, -5, 5),
+    (-6, 6, -7, 7, 8),
 )
 
 
@@ -55,9 +60,9 @@
             ],
         ),
         out_shape=jax.ShapeDtypeStruct(shape, jnp.bfloat16),
-        compiler_params=pltpu.CompilerParams(vmem_limit_bytes=KERNEL_VMEM),
+        compiler_params=pltpu.CompilerParams(vmem_limit_bytes=PICK_VMEM),
         cost_estimate=pl.CostEstimate(
-            flops=0, bytes_accessed=2 * size, transcendentals=0
+            flops=PICK_WEIGHT, bytes_accessed=2 * size, transcendentals=0
         ),
         name=name,
     )(*scalars, *operands)
@@ -86,7 +91,7 @@
     return pick_call(kernel, (ids,), (line,), STEPS * CAP, line.shape[1], "pick_line")
 
 
-def mix(codes, arrays, weights, bias):
+def mix(codes, arrays, weights, bias, weight=1):
     per_device, taps = weights.shape[:2]
     rows = arrays[0].shape[1]
 
@@ -96,21 +101,21 @@
         j = pl.program_id(0)
 
         def fetch(which, into):
+            def choose(code, k, first, last):
+                if last - first == 1:
+                    pltpu.make_async_copy(
+                        blocks_refs[first].at[code & 255],
+                        held.at[into, :, k * BLOCK : (k + 1) * BLOCK],
+                        sems.at[into],
+                    ).start()
+                    return
+                middle = (first + last) // 2
+                low = (code >> 8) < middle
+                pl.when(low)(lambda: choose(code, k, first, middle))
+                pl.when(jnp.logical_not(low))(lambda: choose(code, k, middle, last))
+
             for k in range(taps):
-                code = codes_ref[which * taps + k]
-                for a, ref in enumerate(blocks_refs):
-
-                    def go(ref=ref, k=k, code=code):
-                        pltpu.make_async_copy(
-                            ref.at[code & 255],
-                            held.at[into, :, k * BLOCK : (k + 1) * BLOCK],
-                            sems.at[into],
-                        ).start()
-
-                    if len(blocks_refs) == 1:
-                        go()
-                    else:
-                        pl.when((code >> 8) == a)(go)
+                choose(codes_ref[which * taps + k], k, 0, len(blocks_refs))
 
         @pl.when(j == 0)
         def _():
@@ -144,9 +149,9 @@
             ],
         ),
         out_shape=jax.ShapeDtypeStruct((rows, per_device * BLOCK), jnp.bfloat16),
-        compiler_params=pltpu.CompilerParams(vmem_limit_bytes=KERNEL_VMEM),
+        compiler_params=pltpu.CompilerParams(vmem_limit_bytes=MIX_VMEM),
         cost_estimate=pl.CostEstimate(
-            flops=2 * rows * per_device * taps * BLOCK * BLOCK,
+            flops=weight * 2 * rows * per_device * taps * BLOCK * BLOCK,
             bytes_accessed=per_device * taps * (rows + BLOCK) * BLOCK * 2,
             transcendentals=0,
         ),
@@ -184,31 +189,53 @@
 
     line = lax.all_gather(rest, "z")
     lists = send_lists.reshape(LINES, STEPS, CAP).transpose(1, 0, 2)
-    ids = lax.all_to_all(lists, "z", 0, 0, tiled=True).reshape(-1)
 
     held = {0: [(ring, 0)]}
     up = down = ring
-    for step in range(1, STEPS // 2):
-        if step == 2:
+    picked, arrived = [], []
+
+    def pick_next():
+        part = PARTS[len(picked)]
+        pieces = [held[o] for o in part]
+        picked.append(pick_part(ids, here.reshape(1), part, pieces, RING))
+
+    def send_next():
+        arrived.append(over_lines(picked[len(arrived)]))
+
+    ids = lax.all_to_all(lists, "z", 0, 0, tiled=True).reshape(-1)
+    last = STEPS // 2
+    half = RING // 32 * 16
+    waiting = []
+    for step in range(1, last + 1):
+        if step == IDS_STEP:
             ids, up, down = lax.optimization_barrier((ids, up, down))
         if step == LATE:
             line, up, down = lax.optimization_barrier((line, up, down))
-        up, down = shifted(up, "z", 1), shifted(down, "z", -1)
-        held[-step], held[step] = [(up, 0)], [(down, 0)]
-    half = RING // 2
-    held[STEPS // 2] = [
-        (shifted(up[:half], "z", 1), 0),
-        (shifted(down[half:], "z", -1), half),
-    ]
-
-    arrived = []
-    for part in PARTS:
-        pieces = [held[o] for o in part]
-        picked = pick_part(ids, here.reshape(1), part, pieces, RING)
-        arrived.append(over_lines(picked))
-    arrived_rest = over_lines(pick_line(ids, line))
-
-    out_rest = shifted(mix(slots, [arrived_rest], weights, bias), "segment", 1)
+            picked_rest = pick_line(ids, line)
+            arrived_rest = over_lines(picked_rest)
+        for ready, index in waiting:
+            if step == ready + 2:
+                picked[index], up, down = lax.optimization_barrier(
+                    (picked[index], up, down)
+                )
+                send_next()
+            if step == ready + TIE:
+                arrived[index], up, down = lax.optimization_barrier(
+                    (arrived[index], up, down)
+                )
+        if step < last:
+            up, down = shifted(up, "z", 1), shifted(down, "z", -1)
+            held[-step], held[step] = [(up, 0)], [(down, 0)]
+        else:
+            up, down = shifted(up[:half], "z", 1), shifted(down[half:], "z", -1)
+            arrived_rest, up, down = lax.optimization_barrier((arrived_rest, up, down))
+            held[step] = [(up, 0), (down, half)]
+        if all(o in held for o in PARTS[len(picked)]):
+            waiting.append((step, len(picked)))
+            pick_next()
+    send_next()
+
+    out_rest = shifted(mix(slots, [arrived_rest], weights, bias, MIX_WEIGHT), "segment", 1)
     codes = part_codes(slots, here)
     out_ring = shifted(mix(codes, arrived, weights, bias), "segment", 1)
     return jnp.concatenate([out_ring, out_rest], axis=0)[None]

time: 223 us -> 228 us (1.022)
  waiting for transfers between devices: 42 us -> 71.4 us
  blocking collectives: 19.5 us -> 0 us
  local copies, waits for them, and re-layouts: 21.4 us -> 8.5 us
  Pallas kernels: 21.8 us -> 30.6 us
  starting transfers between devices: 102 us -> 99.6 us
    all_to_all x5, waiting for transfers between devices: 3.25 us -> 34.2 us  [over_lines(): incoming = lax.all_to_all(outgoing, 'y', 0, 0, tiled=True)]
    all_to_all x1 -> x0, blocking collectives: 19.5 us -> none  [body(): ids = lax.all_to_all(lists, 'z', 0, 0, tiled=True).reshape(-1)]
    unnamed x36 -> x14, local copies, waits for them, and re-layouts: 17.5 us -> 4.01 us
    ppermute x18, waiting for transfers between devices: 38.7 us -> 25.8 us  [shifted(): lax.ppermute(value, axis, [(i, (i + by) % count) for i in range(count)])]
    all_to_all x0 -> x1, waiting for transfers between devices: none -> 11.4 us  [body(): ids = lax.all_to_all(lists, 'z', 0, 0, tiled=True).reshape(-1)]
    ppermute x18, starting transfers between devices: 81.4 us -> 71.4 us  [shifted(): lax.ppermute(value, axis, [(i, (i + by) % count) for i in range(count)])]
    all_to_all x0 -> x1, starting transfers between devices: none -> 8.36 us  [body(): ids = lax.all_to_all(lists, 'z', 0, 0, tiled=True).reshape(-1)]
    pallas_call x2, Pallas kernels: 11.3 us -> 18.1 us  [mix(): pl.pallas_call(kernel, grid_spec=pltpu.PrefetchScalarGridSpec(num_scalar_...]
  transfers between devices with their start and end apart: 24 -> 25, of which waited for: 14 -> 14; matrix products, arithmetic and copies ran while one was open for 1% -> 2% of each run, Pallas kernels for 10% -> 9%
where the time goes in v4:
time: 228 us; the launch traced here: 225 us
  starting transfers between devices  99.6 us (44%)
  waiting for transfers between devices  71.4 us (31%)
  Pallas kernels  30.6 us (13%)
  between operations  13.7 us (6%)
  local copies, waits for them, and re-layouts  8.5 us (4%)
    ppermute x18, starting transfers between devices, shifted(): lax.ppermute(value, axis, [(i, (i + by) % count) for i in range(count)])  71.4 us
    all_to_all x5, waiting for transfers between devices, over_lines(): incoming = lax.all_to_all(outgoing, 'y', 0, 0, tiled=True)  34.2 us
    ppermute x18, waiting for transfers between devices, shifted(): lax.ppermute(value, axis, [(i, (i + by) % count) for i in range(count)])  25.8 us
    all_to_all x5, starting transfers between devices, over_lines(): incoming = lax.all_to_all(outgoing, 'y', 0, 0, tiled=True)  19.8 us
    pallas_call x2, Pallas kernels, mix(): pl.pallas_call(kernel, grid_spec=pltpu.PrefetchScalarGridSpec(num_scalar_...  18.1 us
    pallas_call x5, Pallas kernels, pick_call(): pl.pallas_call(kernel, grid_spec=pltpu.PrefetchScalarGridSpec(num_scalar_...  12.5 us
    all_to_all x1, waiting for transfers between devices, body(): ids = lax.all_to_all(lists, 'z', 0, 0, tiled=True).reshape(-1)  11.4 us
    all_to_all x1, starting transfers between devices, body(): ids = lax.all_to_all(lists, 'z', 0, 0, tiled=True).reshape(-1)  8.36 us
  transfers between devices with their start and end apart: 25, of which 14 were waited for; matrix products, arithmetic and copies ran while one was open for 2% of the time, Pallas kernels for 9%

profile of v4, /device:TPU:1, one launch (start us, length us, event | category | flops | bytes accessed | tf_op | source)
XLA Modules:
  0.0 225.3 jit_solution(17480300557018644084)
XLA Ops:
  9.2 4.4 %collective-permute-start = (bf16[160,1024]{1,0:T(8,128)(2,1)S(1)}, bf16[160,1024]{1,0:T(8,128)(2,1)S(1)}, u32[]{:S(2)}, u32[]{:S(2)}) collective-permute-start(bf16[160,1024]{1,0:T(8,128)(2,1)S(1)} %slice_bitcast_fusion.refs_0_), channel_id=1, source_target_pairs={{0,1},{1,2},{2,3},{3,4},{4,5},{5,6},{6,7},{7,8},{8,9},{9,10},{10,1... | collective-permute-start | bytes 983048 | tf_op jit(solution)/shard_map/ppermute | solution.py:164
  13.5 9.5 %collective-permute-start.1 = (bf16[160,1024]{1,0:T(8,128)(2,1)S(1)}, bf16[160,1024]{1,0:T(8,128)(2,1)S(1)}, u32[]{:S(2)}, u32[]{:S(2)}) collective-permute-start(bf16[160,1024]{1,0:T(8,128)(2,1)S(1)} %slice_bitcast_fusion.refs_0_), channel_id=1, source_target_pairs={{0,15},{1,0},{2,1},{3,2},{4,3},{5,4},{6,5},{7,6},{8,7},{9,8},{10,9... | collective-permute-start | bytes 983048 | tf_op jit(solution)/shard_map/ppermute | solution.py:164
  24.5 8.4 %all-to-all-start = ((s32[16,4,2]{1,2,0:T(2,128)}), s32[16,4,2]{1,2,0:T(2,128)S(1)}, u32[]{:S(2)}, u32[]{:S(2)}) async-start(s32[16,4,2]{1,2,0:T(2,128)} %copy.8), calls=%async_computation | async-start | bytes 32768 | tf_op jit(solution)/shard_map/all_to_all | solution.py:205
  32.9 11.4 %all-to-all-done = s32[16,4,2]{1,2,0:T(2,128)S(1)} async-done(((s32[16,4,2]{1,2,0:T(2,128)}), s32[16,4,2]{1,2,0:T(2,128)S(1)}, u32[]{:S(2)}, u32[]{:S(2)}) %all-to-all-start) | async-done | bytes 544 | tf_op jit(solution)/shard_map/all_to_all | solution.py:205
  46.8 4.3 %collective-permute-start.3 = (bf16[160,1024]{1,0:T(8,128)(2,1)S(1)}, bf16[160,1024]{1,0:T(8,128)(2,1)S(1)}, u32[]{:S(2)}, u32[]{:S(2)}) collective-permute-start(bf16[160,1024]{1,0:T(8,128)(2,1)S(1)} %collective-permute-done.1.refs_2_), channel_id=1, source_target_pairs={{0,15},{1,0},{2,1},{3,2},{4,3},{5,4},{6,5},{7,6},{8,7},{9,8},{10,9... | collective-permute-start | bytes 983048 | tf_op jit(solution)/shard_map/ppermute | solution.py:164
  53.2 6.4 %collective-permute-done.2.refs_0_ = bf16[160,1024]{1,0:T(8,128)(2,1)S(1)} collective-permute-done((bf16[160,1024]{1,0:T(8,128)(2,1)S(1)}, bf16[160,1024]{1,0:T(8,128)(2,1)S(1)}, u32[]{:S(2)}, u32[]{:S(2)}) %collective-permute-start.2) | collective-permute-done | bytes 327712 | tf_op jit(solution)/shard_map/ppermute | solution.py:164
  61.5 4.6 %collective-permute-start.6 = (bf16[160,1024]{1,0:T(8,128)(2,1)S(1)}, bf16[160,1024]{1,0:T(8,128)(2,1)S(1)}, u32[]{:S(2)}, u32[]{:S(2)}) collective-permute-start(bf16[160,1024]{1,0:T(8,128)(2,1)S(1)} %collective-permute-done.3.refs_1_), channel_id=1, source_target_pairs={{0,15},{1,0},{2,1},{3,2},{4,3},{5,4},{6,5},{7,6},{8,7},{9,8},{10,9... | collective-permute-start | bytes 983048 | tf_op jit(solution)/shard_map/ppermute | solution.py:164
  66.1 4.6 %all-to-all-start.1 = ((bf16[4,6,160,128]{3,2,1,0:T(8,128)(2,1)}), bf16[4,6,160,128]{3,2,1,0:T(8,128)(2,1)S(1)}, u32[]{:S(2)}, u32[]{:S(2)}) async-start(bf16[4,6,160,128]{3,2,1,0:T(8,128)(2,1)} %pick_part.4), calls=%async_computation.1 | async-start | bytes 1966080 | tf_op jit(solution)/shard_map/all_to_all | solution.py:168
  70.7 3.5 %collective-permute-done.4.refs_2_ = bf16[160,1024]{1,0:T(8,128)(2,1)S(1)} collective-permute-done((bf16[160,1024]{1,0:T(8,128)(2,1)S(1)}, bf16[160,1024]{1,0:T(8,128)(2,1)S(1)}, u32[]{:S(2)}, u32[]{:S(2)}) %collective-permute-start.4) | collective-permute-done | bytes 327712 | tf_op jit(solution)/shard_map/ppermute | solution.py:164
  76.2 4.6 %collective-permute-start.7 = (bf16[160,1024]{1,0:T(8,128)(2,1)S(1)}, bf16[160,1024]{1,0:T(8,128)(2,1)S(1)}, u32[]{:S(2)}, u32[]{:S(2)}) collective-permute-start(bf16[160,1024]{1,0:T(8,128)(2,1)S(1)} %collective-permute-done.6.refs_3_), channel_id=1, source_target_pairs={{0,15},{1,0},{2,1},{3,2},{4,3},{5,4},{6,5},{7,6},{8,7},{9,8},{10,9... | collective-permute-start | bytes 983048 | tf_op jit(solution)/shard_map/ppermute | solution.py:164
  83.0 4.4 %collective-permute-done.5.refs_0_ = bf16[160,1024]{1,0:T(8,128)(2,1)S(1)} collective-permute-done((bf16[160,1024]{1,0:T(8,128)(2,1)S(1)}, bf16[160,1024]{1,0:T(8,128)(2,1)S(1)}, u32[]{:S(2)}, u32[]{:S(2)}) %collective-permute-start.5) | collective-permute-done | bytes 327712 | tf_op jit(solution)/shard_map/ppermute | solution.py:164
  90.9 4.2 %collective-permute-start.10 = (bf16[160,1024]{1,0:T(8,128)(2,1)S(1)}, bf16[160,1024]{1,0:T(8,128)(2,1)S(1)}, u32[]{:S(2)}, u32[]{:S(2)}) collective-permute-start(bf16[160,1024]{1,0:T(8,128)(2,1)S(1)} %collective-permute-done.7.refs_1_), channel_id=1, source_target_pairs={{0,15},{1,0},{2,1},{3,2},{4,3},{5,4},{6,5},{7,6},{8,7},{9,8},{10,9... | collective-permute-start | bytes 983048 | tf_op jit(solution)/shard_map/ppermute | solution.py:164
  95.1 2.5 %collective-permute-done.8.refs_2_ = bf16[160,1024]{1,0:T(8,128)(2,1)S(1)} collective-permute-done((bf16[160,1024]{1,0:T(8,128)(2,1)S(1)}, bf16[160,1024]{1,0:T(8,128)(2,1)S(1)}, u32[]{:S(2)}, u32[]{:S(2)}) %collective-permute-start.8) | collective-permute-done | bytes 327712 | tf_op jit(solution)/shard_map/ppermute | solution.py:164
  97.7 3.0 %collective-permute-start.9 = (bf16[160,1024]{1,0:T(8,128)(2,1)S(1)}, bf16[160,1024]{1,0:T(8,128)(2,1)S(1)}, u32[]{:S(2)}, u32[]{:S(2)}) collective-permute-start(bf16[160,1024]{1,0:T(8,128)(2,1)S(1)} %collective-permute-done.8.refs_2_), channel_id=1, source_target_pairs={{0,1},{1,2},{2,3},{3,4},{4,5},{5,6},{6,7},{7,8},{8,9},{9,10},{10,1... | collective-permute-start | bytes 983048 | tf_op jit(solution)/shard_map/ppermute | solution.py:164
  101.5 2.7 %collective-permute-start.11 = (bf16[160,1024]{1,0:T(8,128)(2,1)S(1)}, bf16[160,1024]{1,0:T(8,128)(2,1)S(1)}, u32[]{:S(2)}, u32[]{:S(2)}) collective-permute-start(bf16[160,1024]{1,0:T(8,128)(2,1)S(1)} %collective-permute-done.10.refs_3_), channel_id=1, source_target_pairs={{0,15},{1,0},{2,1},{3,2},{4,3},{5,4},{6,5},{7,6},{8,7},{9,8},{10,9... | collective-permute-start | bytes 983048 | tf_op jit(solution)/shard_map/ppermute | solution.py:164
  104.2 3.6 %all-to-all-start.2 = ((bf16[4,8,160,128]{3,2,1,0:T(8,128)(2,1)}), bf16[4,8,160,128]{3,2,1,0:T(8,128)(2,1)S(1)}, u32[]{:S(2)}, u32[]{:S(2)}) async-start(bf16[4,8,160,128]{3,2,1,0:T(8,128)(2,1)} %pick_part.5), calls=%async_computation.2 | async-start | bytes 2621440 | tf_op jit(solution)/shard_map/all_to_all | solution.py:168
  111.3 3.6 %pick_line.1 = bf16[4,32,80,128]{3,2,1,0:T(8,128)(2,1)} custom-call(s32[128]{0:T(128)S(1)} %reshape.35.ids_ref, bf16[16,80,1024]{2,1,0:T(8,128)(2,1)S(1)} %copy-done), custom_call_target="tpu_custom_call" | custom-call | flops 12000000000 | bytes 5242880 | tf_op jit(solution)/shard_map/pick_line/pallas_call | solution.py:49
  114.9 3.9 %all-to-all-done.2 = bf16[4,8,160,128]{3,2,1,0:T(8,128)(2,1)S(1)} async-done(((bf16[4,8,160,128]{3,2,1,0:T(8,128)(2,1)}), bf16[4,8,160,128]{3,2,1,0:T(8,128)(2,1)S(1)}, u32[]{:S(2)}, u32[]{:S(2)}) %all-to-all-start.2) | async-done | bytes 1310752 | tf_op jit(solution)/shard_map/all_to_all | solution.py:168
  119.9 4.6 %all-to-all-start.4 = ((bf16[4,32,80,128]{3,2,1,0:T(8,128)(2,1)}), bf16[4,32,80,128]{3,2,1,0:T(8,128)(2,1)}, u32[]{:S(2)}, u32[]{:S(2)}) async-start(bf16[4,32,80,128]{3,2,1,0:T(8,128)(2,1)} %pick_line.1), calls=%async_computation.4 | async-start | bytes 5242880 | tf_op jit(solution)/shard_map/all_to_all | solution.py:168
  126.7 3.4 %collective-permute-start.12 = (bf16[160,1024]{1,0:T(8,128)(2,1)S(1)}, bf16[160,1024]{1,0:T(8,128)(2,1)S(1)}, u32[]{:S(2)}, u32[]{:S(2)}) collective-permute-start(bf16[160,1024]{1,0:T(8,128)(2,1)S(1)} %collective-permute-done.9.refs_0_), channel_id=1, source_target_pairs={{0,1},{1,2},{2,3},{3,4},{4,5},{5,6},{6,7},{7,8},{8,9},{9,10},{10,1... | collective-permute-start | bytes 983048 | tf_op jit(solution)/shard_map/ppermute | solution.py:164
  130.2 3.1 %collective-permute-start.13 = (bf16[160,1024]{1,0:T(8,128)(2,1)S(1)}, bf16[160,1024]{1,0:T(8,128)(2,1)S(1)}, u32[]{:S(2)}, u32[]{:S(2)}) collective-permute-start(bf16[160,1024]{1,0:T(8,128)(2,1)S(1)} %collective-permute-done.11.refs_1_), channel_id=1, source_target_pairs={{0,15},{1,0},{2,1},{3,2},{4,3},{5,4},{6,5},{7,6},{8,7},{9,8},{10,9... | collective-permute-start | bytes 983048 | tf_op jit(solution)/shard_map/ppermute | solution.py:164
  135.8 2.6 %collective-permute-start.14 = (bf16[80,1024]{1,0:T(8,128)(2,1)S(1)}, bf16[80,1024]{1,0:T(8,128)(2,1)S(1)}, u32[]{:S(2)}, u32[]{:S(2)}) collective-permute-start(bf16[80,1024]{1,0:T(8,128)(2,1)S(1)} %slice.21), channel_id=1, source_target_pairs={{0,1},{1,2},{2,3},{3,4},{4,5},{5,6},{6,7},{7,8},{8,9},{9,10},{10,1... | collective-permute-start | bytes 491528 | tf_op jit(solution)/shard_map/ppermute | solution.py:164
  138.4 4.2 %collective-permute-start.15 = (bf16[80,1024]{1,0:T(8,128)(2,1)S(1)}, bf16[80,1024]{1,0:T(8,128)(2,1)S(1)}, u32[]{:S(2)}, u32[]{:S(2)}) collective-permute-start(bf16[80,1024]{1,0:T(8,128)(2,1)S(1)} %slice.22), channel_id=1, source_target_pairs={{0,15},{1,0},{2,1},{3,2},{4,3},{5,4},{6,5},{7,6},{8,7},{9,8},{10,9... | collective-permute-start | bytes 491528 | tf_op jit(solution)/shard_map/ppermute | solution.py:164
  142.7 4.4 %all-to-all-done.4 = bf16[4,32,80,128]{3,2,1,0:T(8,128)(2,1)} async-done(((bf16[4,32,80,128]{3,2,1,0:T(8,128)(2,1)}), bf16[4,32,80,128]{3,2,1,0:T(8,128)(2,1)}, u32[]{:S(2)}, u32[]{:S(2)}) %all-to-all-start.4) | async-done | bytes 2621472 | tf_op jit(solution)/shard_map/all_to_all | solution.py:168
  147.1 3.5 %all-to-all-start.3 = ((bf16[4,8,160,128]{3,2,1,0:T(8,128)(2,1)}), bf16[4,8,160,128]{3,2,1,0:T(8,128)(2,1)S(1)}, u32[]{:S(2)}, u32[]{:S(2)}) async-start(bf16[4,8,160,128]{3,2,1,0:T(8,128)(2,1)} %pick_part.6), calls=%async_computation.3 | async-start | bytes 2621440 | tf_op jit(solution)/shard_map/all_to_all | solution.py:168
  153.1 10.6 %all-to-all-done.3 = bf16[4,8,160,128]{3,2,1,0:T(8,128)(2,1)S(1)} async-done(((bf16[4,8,160,128]{3,2,1,0:T(8,128)(2,1)}), bf16[4,8,160,128]{3,2,1,0:T(8,128)(2,1)S(1)}, u32[]{:S(2)}, u32[]{:S(2)}) %all-to-all-start.3) | async-done | bytes 1310752 | tf_op jit(solution)/shard_map/all_to_all | solution.py:168
  163.7 3.6 %all-to-all-start.5 = ((bf16[4,10,160,128]{3,2,1,0:T(8,128)(2,1)}), bf16[4,10,160,128]{3,2,1,0:T(8,128)(2,1)S(1)}, u32[]{:S(2)}, u32[]{:S(2)}) async-start(bf16[4,10,160,128]{3,2,1,0:T(8,128)(2,1)} %pick_part.7), calls=%async_computation.5 | async-start | bytes 3276800 | tf_op jit(solution)/shard_map/all_to_all | solution.py:168
  168.0 15.3 %all-to-all-done.5 = bf16[4,10,160,128]{3,2,1,0:T(8,128)(2,1)S(1)} async-done(((bf16[4,10,160,128]{3,2,1,0:T(8,128)(2,1)}), bf16[4,10,160,128]{3,2,1,0:T(8,128)(2,1)S(1)}, u32[]{:S(2)}, u32[]{:S(2)}) %all-to-all-start.5) | async-done | bytes 1638432 | tf_op jit(solution)/shard_map/all_to_all | solution.py:168
  184.4 9.3 %mix.2 = bf16[160,1024]{1,0:T(8,128)(2,1)} custom-call(s32[128]{0:T(128)} %compare_select_fusion.15.codes_ref, bf16[24,160,128]{2,1,0:T(8,128)(2,1)} %bitcast.20, bf16[32,160,128]{2,1,0:T(8,128)(2,1)} %bitcast.16, bf16[32,160,128]{2,1,0:T(8,128)(2,1)} %bitcast.17, bf16[40,160,128]{2,1,0:T(8,128)(2,1)} %bitcast.15, bf16[8,16,128,128]{3,2,1,0:T(8,128)(2,1)} %bitcast.18, ...), custom_call_target="tpu_custom_call" | custom-call | flops 671088640 | bytes 9437184 | tf_op jit(solution)/shard_map/mix/pallas_call | solution.py:135
  193.8 12.5 %collective-permute-start.16 = (bf16[160,1024]{1,0:T(8,128)(2,1)}, bf16[160,1024]{1,0:T(8,128)(2,1)S(1)}, u32[]{:S(2)}, u32[]{:S(2)}) collective-permute-start(bf16[160,1024]{1,0:T(8,128)(2,1)} %mix.2), channel_id=1, source_target_pairs={{0,64},{64,128},{128,192},{192,256},{256,320},{320,384},{384,448},... | collective-permute-start | bytes 983048 | tf_op jit(solution)/shard_map/ppermute | solution.py:164
  206.3 8.7 %mix.3 = bf16[80,1024]{1,0:T(8,128)(2,1)} custom-call(s32[128]{0:T(128)} %copy-done.6, bf16[128,80,128]{2,1,0:T(8,128)(2,1)} %bitcast.6.refs_0_, bf16[8,16,128,128]{3,2,1,0:T(8,128)(2,1)} %bitcast.19, f32[8,1,128]{2,1,0:T(1,128)} %bitcast.23), custom_call_target="tpu_custom_call" | custom-call | flops 13421772800 | bytes 6815744 | tf_op jit(solution)/shard_map/mix/pallas_call | solution.py:135
  215.1 2.6 %collective-permute-done.17 = bf16[80,1024]{1,0:T(8,128)(2,1)S(1)} collective-permute-done((bf16[80,1024]{1,0:T(8,128)(2,1)}, bf16[80,1024]{1,0:T(8,128)(2,1)S(1)}, u32[]{:S(2)}, u32[]{:S(2)}) %collective-permute-start.17) | collective-permute-done | bytes 163872 | tf_op jit(solution)/shard_map/ppermute | solution.py:164
  (51 shorter events, 33.4 us)
Async XLA Ops:
  6.5 103.0 %all-gather.2.cloned.1.call-start = ((), (), s32[]{:S(2)}) async-start(), calls=%async_computation.6 | async-start | bytes 2785280 | tf_op jit(solution)/shard_map/all_gather | solution.py:190
  9.2 35.5 %collective-permute-start = (bf16[160,1024]{1,0:T(8,128)(2,1)S(1)}, bf16[160,1024]{1,0:T(8,128)(2,1)S(1)}, u32[]{:S(2)}, u32[]{:S(2)}) collective-permute-start(bf16[160,1024]{1,0:T(8,128)(2,1)S(1)} %slice_bitcast_fusion.refs_0_), channel_id=1, source_target_pairs={{0,1},{1,2},{2,3},{3,4},{4,5},{5,6},{6,7},{7,8},{8,9},{9,10},{10,1... | collective-permute-start | bytes 983048 | tf_op jit(solution)/shard_map/ppermute | solution.py:164
  13.5 31.1 %collective-permute-start.1 = (bf16[160,1024]{1,0:T(8,128)(2,1)S(1)}, bf16[160,1024]{1,0:T(8,128)(2,1)S(1)}, u32[]{:S(2)}, u32[]{:S(2)}) collective-permute-start(bf16[160,1024]{1,0:T(8,128)(2,1)S(1)} %slice_bitcast_fusion.refs_0_), channel_id=1, source_target_pairs={{0,15},{1,0},{2,1},{3,2},{4,3},{5,4},{6,5},{7,6},{8,7},{9,8},{10,9... | collective-permute-start | bytes 983048 | tf_op jit(solution)/shard_map/ppermute | solution.py:164
  24.5 19.8 %all-to-all-start = ((s32[16,4,2]{1,2,0:T(2,128)}), s32[16,4,2]{1,2,0:T(2,128)S(1)}, u32[]{:S(2)}, u32[]{:S(2)}) async-start(s32[16,4,2]{1,2,0:T(2,128)} %copy.8), calls=%async_computation | async-start | bytes 32768 | tf_op jit(solution)/shard_map/all_to_all | solution.py:205
  44.7 14.9 %collective-permute-start.2 = (bf16[160,1024]{1,0:T(8,128)(2,1)S(1)}, bf16[160,1024]{1,0:T(8,128)(2,1)S(1)}, u32[]{:S(2)}, u32[]{:S(2)}) collective-permute-start(bf16[160,1024]{1,0:T(8,128)(2,1)S(1)} %collective-permute-done.refs_1_), channel_id=1, source_target_pairs={{0,1},{1,2},{2,3},{3,4},{4,5},{5,6},{6,7},{7,8},{8,9},{9,10},{10,1... | collective-permute-start | bytes 983048 | tf_op jit(solution)/shard_map/ppermute | solution.py:164
  46.8 12.7 %collective-permute-start.3 = (bf16[160,1024]{1,0:T(8,128)(2,1)S(1)}, bf16[160,1024]{1,0:T(8,128)(2,1)S(1)}, u32[]{:S(2)}, u32[]{:S(2)}) collective-permute-start(bf16[160,1024]{1,0:T(8,128)(2,1)S(1)} %collective-permute-done.1.refs_2_), channel_id=1, source_target_pairs={{0,15},{1,0},{2,1},{3,2},{4,3},{5,4},{6,5},{7,6},{8,7},{9,8},{10,9... | collective-permute-start | bytes 983048 | tf_op jit(solution)/shard_map/ppermute | solution.py:164
  59.6 14.7 %collective-permute-start.4 = (bf16[160,1024]{1,0:T(8,128)(2,1)S(1)}, bf16[160,1024]{1,0:T(8,128)(2,1)S(1)}, u32[]{:S(2)}, u32[]{:S(2)}) collective-permute-start(bf16[160,1024]{1,0:T(8,128)(2,1)S(1)} %collective-permute-done.2.refs_0_), channel_id=1, source_target_pairs={{0,1},{1,2},{2,3},{3,4},{4,5},{5,6},{6,7},{7,8},{8,9},{9,10},{10,1... | collective-permute-start | bytes 983048 | tf_op jit(solution)/shard_map/ppermute | solution.py:164
  61.5 14.7 %collective-permute-start.6 = (bf16[160,1024]{1,0:T(8,128)(2,1)S(1)}, bf16[160,1024]{1,0:T(8,128)(2,1)S(1)}, u32[]{:S(2)}, u32[]{:S(2)}) collective-permute-start(bf16[160,1024]{1,0:T(8,128)(2,1)S(1)} %collective-permute-done.3.refs_1_), channel_id=1, source_target_pairs={{0,15},{1,0},{2,1},{3,2},{4,3},{5,4},{6,5},{7,6},{8,7},{9,8},{10,9... | collective-permute-start | bytes 983048 | tf_op jit(solution)/shard_map/ppermute | solution.py:164
  66.1 22.6 %all-to-all-start.1 = ((bf16[4,6,160,128]{3,2,1,0:T(8,128)(2,1)}), bf16[4,6,160,128]{3,2,1,0:T(8,128)(2,1)S(1)}, u32[]{:S(2)}, u32[]{:S(2)}) async-start(bf16[4,6,160,128]{3,2,1,0:T(8,128)(2,1)} %pick_part.4), calls=%async_computation.1 | async-start | bytes 1966080 | tf_op jit(solution)/shard_map/all_to_all | solution.py:168
  74.2 13.2 %collective-permute-start.5 = (bf16[160,1024]{1,0:T(8,128)(2,1)S(1)}, bf16[160,1024]{1,0:T(8,128)(2,1)S(1)}, u32[]{:S(2)}, u32[]{:S(2)}) collective-permute-start(bf16[160,1024]{1,0:T(8,128)(2,1)S(1)} %collective-permute-done.4.refs_2_), channel_id=1, source_target_pairs={{0,1},{1,2},{2,3},{3,4},{4,5},{5,6},{6,7},{7,8},{8,9},{9,10},{10,1... | collective-permute-start | bytes 983048 | tf_op jit(solution)/shard_map/ppermute | solution.py:164
  76.2 12.5 %collective-permute-start.7 = (bf16[160,1024]{1,0:T(8,128)(2,1)S(1)}, bf16[160,1024]{1,0:T(8,128)(2,1)S(1)}, u32[]{:S(2)}, u32[]{:S(2)}) collective-permute-start(bf16[160,1024]{1,0:T(8,128)(2,1)S(1)} %collective-permute-done.6.refs_3_), channel_id=1, source_target_pairs={{0,15},{1,0},{2,1},{3,2},{4,3},{5,4},{6,5},{7,6},{8,7},{9,8},{10,9... | collective-permute-start | bytes 983048 | tf_op jit(solution)/shard_map/ppermute | solution.py:164
  88.6 15.5 %copy-start.4 = (bf16[4,6,160,128]{3,2,1,0:T(8,128)(2,1)}, bf16[4,6,160,128]{3,2,1,0:T(8,128)(2,1)S(1)}, u32[]{:S(2)}) copy-start(bf16[4,6,160,128]{3,2,1,0:T(8,128)(2,1)S(1)} %all-to-all-done.1) | copy-start | bytes 2949124
  88.6 9.0 %collective-permute-start.8 = (bf16[160,1024]{1,0:T(8,128)(2,1)S(1)}, bf16[160,1024]{1,0:T(8,128)(2,1)S(1)}, u32[]{:S(2)}, u32[]{:S(2)}) collective-permute-start(bf16[160,1024]{1,0:T(8,128)(2,1)S(1)} %collective-permute-done.5.refs_0_), channel_id=1, source_target_pairs={{0,1},{1,2},{2,3},{3,4},{4,5},{5,6},{6,7},{7,8},{8,9},{9,10},{10,1... | collective-permute-start | bytes 983048 | tf_op jit(solution)/shard_map/ppermute | solution.py:164
  90.9 10.6 %collective-permute-start.10 = (bf16[160,1024]{1,0:T(8,128)(2,1)S(1)}, bf16[160,1024]{1,0:T(8,128)(2,1)S(1)}, u32[]{:S(2)}, u32[]{:S(2)}) collective-permute-start(bf16[160,1024]{1,0:T(8,128)(2,1)S(1)} %collective-permute-done.7.refs_1_), channel_id=1, source_target_pairs={{0,15},{1,0},{2,1},{3,2},{4,3},{5,4},{6,5},{7,6},{8,7},{9,8},{10,9... | collective-permute-start | bytes 983048 | tf_op jit(solution)/shard_map/ppermute | solution.py:164
  97.7 10.1 %collective-permute-start.9 = (bf16[160,1024]{1,0:T(8,128)(2,1)S(1)}, bf16[160,1024]{1,0:T(8,128)(2,1)S(1)}, u32[]{:S(2)}, u32[]{:S(2)}) collective-permute-start(bf16[160,1024]{1,0:T(8,128)(2,1)S(1)} %collective-permute-done.8.refs_2_), channel_id=1, source_target_pairs={{0,1},{1,2},{2,3},{3,4},{4,5},{5,6},{6,7},{7,8},{8,9},{9,10},{10,1... | collective-permute-start | bytes 983048 | tf_op jit(solution)/shard_map/ppermute | solution.py:164
  101.5 8.1 %collective-permute-start.11 = (bf16[160,1024]{1,0:T(8,128)(2,1)S(1)}, bf16[160,1024]{1,0:T(8,128)(2,1)S(1)}, u32[]{:S(2)}, u32[]{:S(2)}) collective-permute-start(bf16[160,1024]{1,0:T(8,128)(2,1)S(1)} %collective-permute-done.10.refs_3_), channel_id=1, source_target_pairs={{0,15},{1,0},{2,1},{3,2},{4,3},{5,4},{6,5},{7,6},{8,7},{9,8},{10,9... | collective-permute-start | bytes 983048 | tf_op jit(solution)/shard_map/ppermute | solution.py:164
  104.2 14.7 %all-to-all-start.2 = ((bf16[4,8,160,128]{3,2,1,0:T(8,128)(2,1)}), bf16[4,8,160,128]{3,2,1,0:T(8,128)(2,1)S(1)}, u32[]{:S(2)}, u32[]{:S(2)}) async-start(bf16[4,8,160,128]{3,2,1,0:T(8,128)(2,1)} %pick_part.5), calls=%async_computation.2 | async-start | bytes 2621440 | tf_op jit(solution)/shard_map/all_to_all | solution.py:168
  109.6 1.7 copy-start
  118.9 1.1 copy-start.2
  119.9 27.1 %all-to-all-start.4 = ((bf16[4,32,80,128]{3,2,1,0:T(8,128)(2,1)}), bf16[4,32,80,128]{3,2,1,0:T(8,128)(2,1)}, u32[]{:S(2)}, u32[]{:S(2)}) async-start(bf16[4,32,80,128]{3,2,1,0:T(8,128)(2,1)} %pick_line.1), calls=%async_computation.4 | async-start | bytes 5242880 | tf_op jit(solution)/shard_map/all_to_all | solution.py:168
  126.7 9.0 %collective-permute-start.12 = (bf16[160,1024]{1,0:T(8,128)(2,1)S(1)}, bf16[160,1024]{1,0:T(8,128)(2,1)S(1)}, u32[]{:S(2)}, u32[]{:S(2)}) collective-permute-start(bf16[160,1024]{1,0:T(8,128)(2,1)S(1)} %collective-permute-done.9.refs_0_), channel_id=1, source_target_pairs={{0,1},{1,2},{2,3},{3,4},{4,5},{5,6},{6,7},{7,8},{8,9},{9,10},{10,1... | collective-permute-start | bytes 983048 | tf_op jit(solution)/shard_map/ppermute | solution.py:164
  130.2 8.2 %collective-permute-start.13 = (bf16[160,1024]{1,0:T(8,128)(2,1)S(1)}, bf16[160,1024]{1,0:T(8,128)(2,1)S(1)}, u32[]{:S(2)}, u32[]{:S(2)}) collective-permute-start(bf16[160,1024]{1,0:T(8,128)(2,1)S(1)} %collective-permute-done.11.refs_1_), channel_id=1, source_target_pairs={{0,15},{1,0},{2,1},{3,2},{4,3},{5,4},{6,5},{7,6},{8,7},{9,8},{10,9... | collective-permute-start | bytes 983048 | tf_op jit(solution)/shard_map/ppermute | solution.py:164
  135.8 14.8 %collective-permute-start.14 = (bf16[80,1024]{1,0:T(8,128)(2,1)S(1)}, bf16[80,1024]{1,0:T(8,128)(2,1)S(1)}, u32[]{:S(2)}, u32[]{:S(2)}) collective-permute-start(bf16[80,1024]{1,0:T(8,128)(2,1)S(1)} %slice.21), channel_id=1, source_target_pairs={{0,1},{1,2},{2,3},{3,4},{4,5},{5,6},{6,7},{7,8},{8,9},{9,10},{10,1... | collective-permute-start | bytes 491528 | tf_op jit(solution)/shard_map/ppermute | solution.py:164
  138.4 12.2 %collective-permute-start.15 = (bf16[80,1024]{1,0:T(8,128)(2,1)S(1)}, bf16[80,1024]{1,0:T(8,128)(2,1)S(1)}, u32[]{:S(2)}, u32[]{:S(2)}) collective-permute-start(bf16[80,1024]{1,0:T(8,128)(2,1)S(1)} %slice.22), channel_id=1, source_target_pairs={{0,15},{1,0},{2,1},{3,2},{4,3},{5,4},{6,5},{7,6},{8,7},{9,8},{10,9... | collective-permute-start | bytes 491528 | tf_op jit(solution)/shard_map/ppermute | solution.py:164
  147.1 16.6 %all-to-all-start.3 = ((bf16[4,8,160,128]{3,2,1,0:T(8,128)(2,1)}), bf16[4,8,160,128]{3,2,1,0:T(8,128)(2,1)S(1)}, u32[]{:S(2)}, u32[]{:S(2)}) async-start(bf16[4,8,160,128]{3,2,1,0:T(8,128)(2,1)} %pick_part.6), calls=%async_computation.3 | async-start | bytes 2621440 | tf_op jit(solution)/shard_map/all_to_all | solution.py:168
  153.1 14.2 %copy-start.5 = (s32[1,8,16]{2,1,0:T(8,128)S(1)}, s32[1,8,16]{2,1,0:T(8,128)}, u32[]{:S(2)}) copy-start(s32[1,8,16]{2,1,0:T(8,128)} %param.8) | copy-start | bytes 1540
  163.7 3.7 %copy-start.3 = (bf16[4,8,160,128]{3,2,1,0:T(8,128)(2,1)}, bf16[4,8,160,128]{3,2,1,0:T(8,128)(2,1)S(1)}, u32[]{:S(2)}) copy-start(bf16[4,8,160,128]{3,2,1,0:T(8,128)(2,1)S(1)} %all-to-all-done.3) | copy-start | bytes 3932164
  163.7 19.6 %all-to-all-start.5 = ((bf16[4,10,160,128]{3,2,1,0:T(8,128)(2,1)}), bf16[4,10,160,128]{3,2,1,0:T(8,128)(2,1)S(1)}, u32[]{:S(2)}, u32[]{:S(2)}) async-start(bf16[4,10,160,128]{3,2,1,0:T(8,128)(2,1)} %pick_part.7), calls=%async_computation.5 | async-start | bytes 3276800 | tf_op jit(solution)/shard_map/all_to_all | solution.py:168
  167.4 26.4 %copy-start.6 = (s32[128]{0:T(128)}, s32[128]{0:T(128)S(1)}, u32[]{:S(2)}) copy-start(s32[128]{0:T(128)S(1)} %reshape.33.codes_ref) | copy-start | bytes 1540
  183.3 1.2 copy-start.1
  193.8 23.9 %collective-permute-start.16 = (bf16[160,1024]{1,0:T(8,128)(2,1)}, bf16[160,1024]{1,0:T(8,128)(2,1)S(1)}, u32[]{:S(2)}, u32[]{:S(2)}) collective-permute-start(bf16[160,1024]{1,0:T(8,128)(2,1)} %mix.2), channel_id=1, source_target_pairs={{0,64},{64,128},{128,192},{192,256},{256,320},{320,384},{384,448},... | collective-permute-start | bytes 983048 | tf_op jit(solution)/shard_map/ppermute | solution.py:164
  215.1 2.6 %collective-permute-start.17 = (bf16[80,1024]{1,0:T(8,128)(2,1)}, bf16[80,1024]{1,0:T(8,128)(2,1)S(1)}, u32[]{:S(2)}, u32[]{:S(2)}) collective-permute-start(bf16[80,1024]{1,0:T(8,128)(2,1)} %mix.3), channel_id=1, source_target_pairs={{0,64},{64,128},{128,192},{192,256},{256,320},{320,384},{384,448},... | collective-permute-start | bytes 491528 | tf_op jit(solution)/shard_map/ppermute | solution.py:164
Sparse Core Ops, SparseCore 0:
  9.4 76.4 all-gather.1

commit v5 on v4

--- a/solution.py
+++ b/solution.py
@@ -14,15 +14,13 @@
 MIX_VMEM = 58 * 2**20
 PICK_WEIGHT = 12 * 10**9
 IDS_STEP = 2
-MIX_WEIGHT = 40
-TIE = 4
-LATE = 7
-RING = 160
+HAVE = (5,7,8, 9, 9)
 PARTS = (
     (0, -1, 1),
     (-2, 2, -3, 3),
     (-4, 4, -5, 5),
-    (-6, 6, -7, 7, 8),
+    (-6, 6),
+    (-7, 7, 8),
 )
 
 
@@ -83,15 +81,7 @@
     return pick_call(kernel, (ids, here), flat, len(part) * CAP, rows, "pick_part")
 
 
-def pick_line(ids, line):
-    def kernel(ids_ref, line_ref, out_ref, held, in_sems, out_sem):
-        senders = [(z, [(line_ref.at[z], 0)]) for z in range(STEPS)]
-        copy_blocks(ids_ref, senders, out_ref, held, in_sems, out_sem)
-
-    return pick_call(kernel, (ids,), (line,), STEPS * CAP, line.shape[1], "pick_line")
-
-
-def mix(codes, arrays, weights, bias, weight=1):
+def mix(codes, arrays, weights, bias):
     per_device, taps = weights.shape[:2]
     rows = arrays[0].shape[1]
 
@@ -151,7 +141,7 @@
         out_shape=jax.ShapeDtypeStruct((rows, per_device * BLOCK), jnp.bfloat16),
         compiler_params=pltpu.CompilerParams(vmem_limit_bytes=MIX_VMEM),
         cost_estimate=pl.CostEstimate(
-            flops=weight * 2 * rows * per_device * taps * BLOCK * BLOCK,
+            flops=2 * rows * per_device * taps * BLOCK * BLOCK,
             bytes_accessed=per_device * taps * (rows + BLOCK) * BLOCK * 2,
             transcendentals=0,
         ),
@@ -184,42 +174,34 @@
     samples, weights, bias = layer_input[0], weight_blocks[0], neuron_bias[0]
     slots = block_slots.reshape(-1)
     here = lax.axis_index("z").astype(jnp.int32)
-    rest = samples[RING:]
-    ring = samples[:RING]
-
-    line = lax.all_gather(rest, "z")
     lists = send_lists.reshape(LINES, STEPS, CAP).transpose(1, 0, 2)
 
-    held = {0: [(ring, 0)]}
-    up = down = ring
+    held = {0: [(samples, 0)]}
+    up = down = samples
     picked, arrived = [], []
 
     def pick_next():
         part = PARTS[len(picked)]
         pieces = [held[o] for o in part]
-        picked.append(pick_part(ids, here.reshape(1), part, pieces, RING))
+        picked.append(pick_part(ids, here.reshape(1), part, pieces, samples.shape[0]))
 
     def send_next():
         arrived.append(over_lines(picked[len(arrived)]))
 
     ids = lax.all_to_all(lists, "z", 0, 0, tiled=True).reshape(-1)
     last = STEPS // 2
-    half = RING // 32 * 16
+    half = samples.shape[0] // 32 * 16
     waiting = []
     for step in range(1, last + 1):
         if step == IDS_STEP:
             ids, up, down = lax.optimization_barrier((ids, up, down))
-        if step == LATE:
-            line, up, down = lax.optimization_barrier((line, up, down))
-            picked_rest = pick_line(ids, line)
-            arrived_rest = over_lines(picked_rest)
         for ready, index in waiting:
             if step == ready + 2:
                 picked[index], up, down = lax.optimization_barrier(
                     (picked[index], up, down)
                 )
                 send_next()
-            if step == ready + TIE:
+            if step == HAVE[index]:
                 arrived[index], up, down = lax.optimization_barrier(
                     (arrived[index], up, down)
                 )
@@ -228,17 +210,14 @@
             held[-step], held[step] = [(up, 0)], [(down, 0)]
         else:
             up, down = shifted(up[:half], "z", 1), shifted(down[half:], "z", -1)
-            arrived_rest, up, down = lax.optimization_barrier((arrived_rest, up, down))
             held[step] = [(up, 0), (down, half)]
         if all(o in held for o in PARTS[len(picked)]):
             waiting.append((step, len(picked)))
             pick_next()
     send_next()
 
-    out_rest = shifted(mix(slots, [arrived_rest], weights, bias, MIX_WEIGHT), "segment", 1)
-    codes = part_codes(slots, here)
-    out_ring = shifted(mix(codes, arrived, weights, bias), "segment", 1)
-    return jnp.concatenate([out_ring, out_rest], axis=0)[None]
+    out = mix(part_codes(slots, here), arrived, weights, bias)
+    return shifted(out, "segment", 1)[None]
 
 
 def solution(mesh):

time: 228 us -> 195 us (0.86)
  between operations: 13.7 us -> 0.35 us
  Pallas kernels: 30.6 us -> 22 us
  waiting for transfers between devices: 71.4 us -> 64.3 us
    pallas_call x2 -> x1, Pallas kernels: 18.1 us -> 10.2 us  [mix(): pl.pallas_call(kernel, grid_spec=pltpu.PrefetchScalarGridSpec(num_scalar_...]
    all_to_all x5, waiting for transfers between devices: 34.2 us -> 28.9 us  [over_lines(): incoming = lax.all_to_all(outgoing, 'y', 0, 0, tiled=True)]
    slice x2 -> x0, local copies, waits for them, and re-layouts: 2.59 us -> none  [the longest x1 1.59 us: body(): rest = samples[RING:]]
    ppermute x18 -> x17, waiting for transfers between devices: 25.8 us -> 24.1 us  [shifted(): lax.ppermute(value, axis, [(i, (i + by) % count) for i in range(count)])]
    ppermute x18 -> x17, starting transfers between devices: 71.4 us -> 71.6 us  [shifted(): lax.ppermute(value, axis, [(i, (i + by) % count) for i in range(count)])]
  transfers between devices with their start and end apart: 25 -> 23, of which waited for: 14 -> 17; matrix products, arithmetic and copies ran while one was open for 2% -> 2% of each run, Pallas kernels for 9% -> 6%
where the time goes in v5:
time: 195 us; the launch traced here: 193 us
  starting transfers between devices  99 us (51%)
  waiting for transfers between devices  64.3 us (33%)
  Pallas kernels  22 us (11%)
  local copies, waits for them, and re-layouts  7.19 us (4%)
    ppermute x17, starting transfers between devices, shifted(): lax.ppermute(value, axis, [(i, (i + by) % count) for i in range(count)])  71.6 us
    all_to_all x5, waiting for transfers between devices, over_lines(): incoming = lax.all_to_all(outgoing, 'y', 0, 0, tiled=True)  28.9 us
    ppermute x17, waiting for transfers between devices, shifted(): lax.ppermute(value, axis, [(i, (i + by) % count) for i in range(count)])  24.1 us
    all_to_all x5, starting transfers between devices, over_lines(): incoming = lax.all_to_all(outgoing, 'y', 0, 0, tiled=True)  20.3 us
    pallas_call x5, Pallas kernels, pick_call(): pl.pallas_call(kernel, grid_spec=pltpu.PrefetchScalarGridSpec(num_scalar_...  11.7 us
    all_to_all x1, waiting for transfers between devices, body(): ids = lax.all_to_all(lists, 'z', 0, 0, tiled=True).reshape(-1)  11.4 us
    pallas_call x1, Pallas kernels, mix(): pl.pallas_call(kernel, grid_spec=pltpu.PrefetchScalarGridSpec(num_scalar_...  10.2 us
    all_to_all x1, starting transfers between devices, body(): ids = lax.all_to_all(lists, 'z', 0, 0, tiled=True).reshape(-1)  7.15 us
  transfers between devices with their start and end apart: 23, of which 17 were waited for; matrix products, arithmetic and copies ran while one was open for 2% of the time, Pallas kernels for 6%

profile of v5, /device:TPU:1, one launch (start us, length us, event | category | flops | bytes accessed | tf_op | source)
XLA Modules:
  0.0 193.4 jit_solution(14281756495754806851)
XLA Ops:
  0.0 11.9 %collective-permute-start.1 = (bf16[240,1024]{1,0:T(8,128)(2,1)}, bf16[240,1024]{1,0:T(8,128)(2,1)S(1)}, u32[]{:S(2)}, u32[]{:S(2)}) collective-permute-start(bf16[240,1024]{1,0:T(8,128)(2,1)} %bitcast.13), channel_id=1, source_target_pairs={{0,15},{1,0},{2,1},{3,2},{4,3},{5,4},{6,5},{7,6},{8,7},{9,8},{10,9... | collective-permute-start | bytes 1474568 | tf_op jit(solution)/shard_map/ppermute | solution.py:154
  15.3 7.2 %all-to-all-start = ((s32[16,4,2]{1,2,0:T(2,128)}), s32[16,4,2]{1,2,0:T(2,128)S(1)}, u32[]{:S(2)}, u32[]{:S(2)}) async-start(s32[16,4,2]{1,2,0:T(2,128)} %copy.8), calls=%async_computation | async-start | bytes 32768 | tf_op jit(solution)/shard_map/all_to_all | solution.py:191
  22.5 11.4 %all-to-all-done = s32[16,4,2]{1,2,0:T(2,128)S(1)} async-done(((s32[16,4,2]{1,2,0:T(2,128)}), s32[16,4,2]{1,2,0:T(2,128)S(1)}, u32[]{:S(2)}, u32[]{:S(2)}) %all-to-all-start) | async-done | bytes 544 | tf_op jit(solution)/shard_map/all_to_all | solution.py:191
  34.3 2.3 %collective-permute-start.2 = (bf16[240,1024]{1,0:T(8,128)(2,1)S(1)}, bf16[240,1024]{1,0:T(8,128)(2,1)S(1)}, u32[]{:S(2)}, u32[]{:S(2)}) collective-permute-start(bf16[240,1024]{1,0:T(8,128)(2,1)S(1)} %collective-permute-done.refs_1_), channel_id=1, source_target_pairs={{0,1},{1,2},{2,3},{3,4},{4,5},{5,6},{6,7},{7,8},{8,9},{9,10},{10,1... | collective-permute-start | bytes 1474568 | tf_op jit(solution)/shard_map/ppermute | solution.py:154
  36.6 4.2 %collective-permute-start.3 = (bf16[240,1024]{1,0:T(8,128)(2,1)S(1)}, bf16[240,1024]{1,0:T(8,128)(2,1)S(1)}, u32[]{:S(2)}, u32[]{:S(2)}) collective-permute-start(bf16[240,1024]{1,0:T(8,128)(2,1)S(1)} %collective-permute-done.1.refs_2_), channel_id=1, source_target_pairs={{0,15},{1,0},{2,1},{3,2},{4,3},{5,4},{6,5},{7,6},{8,7},{9,8},{10,9... | collective-permute-start | bytes 1474568 | tf_op jit(solution)/shard_map/ppermute | solution.py:154
  41.8 2.3 %pick_part.5 = bf16[4,6,240,128]{3,2,1,0:T(8,128)(2,1)} custom-call(s32[128]{0:T(128)S(1)} %reshape.68.ids_ref, s32[1]{0:T(128)} %bitcast.1.here_ref, bf16[240,1024]{1,0:T(8,128)(2,1)S(1)} %bitcast.15, bf16[240,1024]{1,0:T(8,128)(2,1)S(1)} %collective-permute-done.refs_1_, bf16[240,1024]{1,0:T(8,128)(2,1)S(1)} %collective-permute-done.1.refs_2_), custom_call_target="tpu_custom_call" | custom-call | flops 12000000000 | bytes 2949120 | tf_op jit(solution)/shard_map/pick_part/pallas_call | solution.py:47
  44.1 3.3 %collective-permute-done.2.refs_0_ = bf16[240,1024]{1,0:T(8,128)(2,1)S(1)} collective-permute-done((bf16[240,1024]{1,0:T(8,128)(2,1)S(1)}, bf16[240,1024]{1,0:T(8,128)(2,1)S(1)}, u32[]{:S(2)}, u32[]{:S(2)}) %collective-permute-start.2) | collective-permute-done | bytes 491552 | tf_op jit(solution)/shard_map/ppermute | solution.py:154
  50.3 5.3 %collective-permute-start.6 = (bf16[240,1024]{1,0:T(8,128)(2,1)S(1)}, bf16[240,1024]{1,0:T(8,128)(2,1)S(1)}, u32[]{:S(2)}, u32[]{:S(2)}) collective-permute-start(bf16[240,1024]{1,0:T(8,128)(2,1)S(1)} %collective-permute-done.3.refs_1_), channel_id=1, source_target_pairs={{0,15},{1,0},{2,1},{3,2},{4,3},{5,4},{6,5},{7,6},{8,7},{9,8},{10,9... | collective-permute-start | bytes 1474568 | tf_op jit(solution)/shard_map/ppermute | solution.py:154
  55.6 4.3 %all-to-all-start.1 = ((bf16[4,6,240,128]{3,2,1,0:T(8,128)(2,1)}), bf16[4,6,240,128]{3,2,1,0:T(8,128)(2,1)}, u32[]{:S(2)}, u32[]{:S(2)}) async-start(bf16[4,6,240,128]{3,2,1,0:T(8,128)(2,1)} %pick_part.5), calls=%async_computation.1 | async-start | bytes 2949120 | tf_op jit(solution)/shard_map/all_to_all | solution.py:158
  63.2 4.6 %collective-permute-start.7 = (bf16[240,1024]{1,0:T(8,128)(2,1)S(1)}, bf16[240,1024]{1,0:T(8,128)(2,1)S(1)}, u32[]{:S(2)}, u32[]{:S(2)}) collective-permute-start(bf16[240,1024]{1,0:T(8,128)(2,1)S(1)} %collective-permute-done.6.refs_3_), channel_id=1, source_target_pairs={{0,15},{1,0},{2,1},{3,2},{4,3},{5,4},{6,5},{7,6},{8,7},{9,8},{10,9... | collective-permute-start | bytes 1474568 | tf_op jit(solution)/shard_map/ppermute | solution.py:154
  67.8 2.6 %pick_part.6 = bf16[4,8,240,128]{3,2,1,0:T(8,128)(2,1)} custom-call(s32[128]{0:T(128)S(1)} %reshape.68.ids_ref, s32[1]{0:T(128)} %bitcast.1.here_ref, bf16[240,1024]{1,0:T(8,128)(2,1)S(1)} %collective-permute-done.2.refs_0_, bf16[240,1024]{1,0:T(8,128)(2,1)S(1)} %collective-permute-done.3.refs_1_, bf16[240,1024]{1,0:T(8,128)(2,1)S(1)} %collective-permute-done.4.refs_2_, ...), custom_call_target="tpu_custom_call" | custom-call | flops 12000000000 | bytes 3932160 | tf_op jit(solution)/shard_map/pick_part/pallas_call | solution.py:47
  70.4 2.3 %collective-permute-done.5.refs_0_ = bf16[240,1024]{1,0:T(8,128)(2,1)S(1)} collective-permute-done((bf16[240,1024]{1,0:T(8,128)(2,1)S(1)}, bf16[240,1024]{1,0:T(8,128)(2,1)S(1)}, u32[]{:S(2)}, u32[]{:S(2)}) %collective-permute-start.5) | collective-permute-done | bytes 491552 | tf_op jit(solution)/shard_map/ppermute | solution.py:154
  76.9 4.6 %collective-permute-start.10 = (bf16[240,1024]{1,0:T(8,128)(2,1)S(1)}, bf16[240,1024]{1,0:T(8,128)(2,1)S(1)}, u32[]{:S(2)}, u32[]{:S(2)}) collective-permute-start(bf16[240,1024]{1,0:T(8,128)(2,1)S(1)} %collective-permute-done.7.refs_1_), channel_id=1, source_target_pairs={{0,15},{1,0},{2,1},{3,2},{4,3},{5,4},{6,5},{7,6},{8,7},{9,8},{10,9... | collective-permute-start | bytes 1474568 | tf_op jit(solution)/shard_map/ppermute | solution.py:154
  81.5 4.4 %all-to-all-start.2 = ((bf16[4,8,240,128]{3,2,1,0:T(8,128)(2,1)}), bf16[4,8,240,128]{3,2,1,0:T(8,128)(2,1)}, u32[]{:S(2)}, u32[]{:S(2)}) async-start(bf16[4,8,240,128]{3,2,1,0:T(8,128)(2,1)} %pick_part.6), calls=%async_computation.2 | async-start | bytes 3932160 | tf_op jit(solution)/shard_map/all_to_all | solution.py:158
  87.9 4.6 %collective-permute-start.11 = (bf16[240,1024]{1,0:T(8,128)(2,1)S(1)}, bf16[240,1024]{1,0:T(8,128)(2,1)S(1)}, u32[]{:S(2)}, u32[]{:S(2)}) collective-permute-start(bf16[240,1024]{1,0:T(8,128)(2,1)S(1)} %collective-permute-done.10.refs_3_), channel_id=1, source_target_pairs={{0,15},{1,0},{2,1},{3,2},{4,3},{5,4},{6,5},{7,6},{8,7},{9,8},{10,9... | collective-permute-start | bytes 1474568 | tf_op jit(solution)/shard_map/ppermute | solution.py:154
  92.5 2.6 %pick_part.7 = bf16[4,8,240,128]{3,2,1,0:T(8,128)(2,1)} custom-call(s32[128]{0:T(128)S(1)} %reshape.68.ids_ref, s32[1]{0:T(128)} %bitcast.1.here_ref, bf16[240,1024]{1,0:T(8,128)(2,1)S(1)} %collective-permute-done.5.refs_0_, bf16[240,1024]{1,0:T(8,128)(2,1)S(1)} %collective-permute-done.7.refs_1_, bf16[240,1024]{1,0:T(8,128)(2,1)S(1)} %collective-permute-done.8.refs_2_, ...), custom_call_target="tpu_custom_call" | custom-call | flops 12000000000 | bytes 3932160 | tf_op jit(solution)/shard_map/pick_part/pallas_call | solution.py:47
  95.1 2.4 %collective-permute-done.9.refs_0_ = bf16[240,1024]{1,0:T(8,128)(2,1)S(1)} collective-permute-done((bf16[240,1024]{1,0:T(8,128)(2,1)S(1)}, bf16[240,1024]{1,0:T(8,128)(2,1)S(1)}, u32[]{:S(2)}, u32[]{:S(2)}) %collective-permute-start.9) | collective-permute-done | bytes 491552 | tf_op jit(solution)/shard_map/ppermute | solution.py:154
  98.8 5.7 %all-to-all-done.2 = bf16[4,8,240,128]{3,2,1,0:T(8,128)(2,1)} async-done(((bf16[4,8,240,128]{3,2,1,0:T(8,128)(2,1)}), bf16[4,8,240,128]{3,2,1,0:T(8,128)(2,1)}, u32[]{:S(2)}, u32[]{:S(2)}) %all-to-all-start.2) | async-done | bytes 1966112 | tf_op jit(solution)/shard_map/all_to_all | solution.py:158
  104.6 4.4 %all-to-all-start.3 = ((bf16[4,8,240,128]{3,2,1,0:T(8,128)(2,1)}), bf16[4,8,240,128]{3,2,1,0:T(8,128)(2,1)}, u32[]{:S(2)}, u32[]{:S(2)}) async-start(bf16[4,8,240,128]{3,2,1,0:T(8,128)(2,1)} %pick_part.7), calls=%async_computation.3 | async-start | bytes 3932160 | tf_op jit(solution)/shard_map/all_to_all | solution.py:158
  110.9 4.6 %collective-permute-start.13 = (bf16[240,1024]{1,0:T(8,128)(2,1)S(1)}, bf16[240,1024]{1,0:T(8,128)(2,1)S(1)}, u32[]{:S(2)}, u32[]{:S(2)}) collective-permute-start(bf16[240,1024]{1,0:T(8,128)(2,1)S(1)} %collective-permute-done.11.refs_1_), channel_id=1, source_target_pairs={{0,15},{1,0},{2,1},{3,2},{4,3},{5,4},{6,5},{7,6},{8,7},{9,8},{10,9... | collective-permute-start | bytes 1474568 | tf_op jit(solution)/shard_map/ppermute | solution.py:154
  117.5 2.3 %collective-permute-done.12.refs_0_ = bf16[240,1024]{1,0:T(8,128)(2,1)S(1)} collective-permute-done((bf16[240,1024]{1,0:T(8,128)(2,1)S(1)}, bf16[240,1024]{1,0:T(8,128)(2,1)S(1)}, u32[]{:S(2)}, u32[]{:S(2)}) %collective-permute-start.12) | collective-permute-done | bytes 491552 | tf_op jit(solution)/shard_map/ppermute | solution.py:154
  121.3 5.1 %all-to-all-done.3 = bf16[4,8,240,128]{3,2,1,0:T(8,128)(2,1)} async-done(((bf16[4,8,240,128]{3,2,1,0:T(8,128)(2,1)}), bf16[4,8,240,128]{3,2,1,0:T(8,128)(2,1)}, u32[]{:S(2)}, u32[]{:S(2)}) %all-to-all-start.3) | async-done | bytes 1966112 | tf_op jit(solution)/shard_map/all_to_all | solution.py:158
  126.4 2.6 %collective-permute-start.15 = (bf16[128,1024]{1,0:T(8,128)(2,1)S(1)}, bf16[128,1024]{1,0:T(8,128)(2,1)S(1)}, u32[]{:S(2)}, u32[]{:S(2)}) collective-permute-start(bf16[128,1024]{1,0:T(8,128)(2,1)S(1)} %slice.7), channel_id=1, source_target_pairs={{0,15},{1,0},{2,1},{3,2},{4,3},{5,4},{6,5},{7,6},{8,7},{9,8},{10,9... | collective-permute-start | bytes 786440 | tf_op jit(solution)/shard_map/ppermute | solution.py:154
  129.0 2.7 %collective-permute-start.14 = (bf16[112,1024]{1,0:T(8,128)(2,1)S(1)}, bf16[112,1024]{1,0:T(8,128)(2,1)S(1)}, u32[]{:S(2)}, u32[]{:S(2)}) collective-permute-start(bf16[112,1024]{1,0:T(8,128)(2,1)S(1)} %slice.6), channel_id=1, source_target_pairs={{0,1},{1,2},{2,3},{3,4},{4,5},{5,6},{6,7},{7,8},{8,9},{9,10},{10,1... | collective-permute-start | bytes 688136 | tf_op jit(solution)/shard_map/ppermute | solution.py:154
  131.7 3.5 %all-to-all-start.4 = ((bf16[4,4,240,128]{3,2,1,0:T(8,128)(2,1)}), bf16[4,4,240,128]{3,2,1,0:T(8,128)(2,1)S(1)}, u32[]{:S(2)}, u32[]{:S(2)}) async-start(bf16[4,4,240,128]{3,2,1,0:T(8,128)(2,1)} %pick_part.8), calls=%async_computation.4 | async-start | bytes 1966080 | tf_op jit(solution)/shard_map/all_to_all | solution.py:158
  137.0 2.3 %pick_part.9 = bf16[4,6,240,128]{3,2,1,0:T(8,128)(2,1)} custom-call(s32[128]{0:T(128)S(1)} %reshape.68.ids_ref, s32[1]{0:T(128)} %bitcast.1.here_ref, bf16[240,1024]{1,0:T(8,128)(2,1)S(1)} %collective-permute-done.12.refs_0_, bf16[240,1024]{1,0:T(8,128)(2,1)S(1)} %collective-permute-done.13.refs_1_, bf16[112,1024]{1,0:T(8,128)(2,1)S(1)} %collective-permute-done.14.refs_2_, ...), custom_call_target="tpu_custom_call" | custom-call | flops 12000000000 | bytes 2949120 | tf_op jit(solution)/shard_map/pick_part/pallas_call | solution.py:47
  139.3 5.3 %all-to-all-done.4 = bf16[4,4,240,128]{3,2,1,0:T(8,128)(2,1)S(1)} async-done(((bf16[4,4,240,128]{3,2,1,0:T(8,128)(2,1)}), bf16[4,4,240,128]{3,2,1,0:T(8,128)(2,1)S(1)}, u32[]{:S(2)}, u32[]{:S(2)}) %all-to-all-start.4) | async-done | bytes 983072 | tf_op jit(solution)/shard_map/all_to_all | solution.py:158
  144.6 3.6 %all-to-all-start.5 = ((bf16[4,6,240,128]{3,2,1,0:T(8,128)(2,1)}), bf16[4,6,240,128]{3,2,1,0:T(8,128)(2,1)S(1)}, u32[]{:S(2)}, u32[]{:S(2)}) async-start(bf16[4,6,240,128]{3,2,1,0:T(8,128)(2,1)} %pick_part.9), calls=%async_computation.5 | async-start | bytes 2949120 | tf_op jit(solution)/shard_map/all_to_all | solution.py:158
  151.2 11.2 %all-to-all-done.5 = bf16[4,6,240,128]{3,2,1,0:T(8,128)(2,1)S(1)} async-done(((bf16[4,6,240,128]{3,2,1,0:T(8,128)(2,1)}), bf16[4,6,240,128]{3,2,1,0:T(8,128)(2,1)S(1)}, u32[]{:S(2)}, u32[]{:S(2)}) %all-to-all-start.5) | async-done | bytes 1474592 | tf_op jit(solution)/shard_map/all_to_all | solution.py:158
  163.6 10.2 %mix.1 = bf16[240,1024]{1,0:T(8,128)(2,1)} custom-call(s32[128]{0:T(128)} %select_select_fusion.codes_ref, bf16[24,240,128]{2,1,0:T(8,128)(2,1)} %bitcast.3.refs_0_, bf16[32,240,128]{2,1,0:T(8,128)(2,1)} %bitcast.4.refs_1_, bf16[32,240,128]{2,1,0:T(8,128)(2,1)} %bitcast.5.refs_2_, bf16[16,240,128]{2,1,0:T(8,128)(2,1)} %bitcast.18, ...), custom_call_target="tpu_custom_call" | custom-call | flops 1006632960 | bytes 12058624 | tf_op jit(solution)/shard_map/mix/pallas_call | solution.py:125
  173.8 12.8 %collective-permute-start.16 = (bf16[240,1024]{1,0:T(8,128)(2,1)}, bf16[240,1024]{1,0:T(8,128)(2,1)S(1)}, u32[]{:S(2)}, u32[]{:S(2)}) collective-permute-start(bf16[240,1024]{1,0:T(8,128)(2,1)} %mix.1), channel_id=1, source_target_pairs={{0,64},{64,128},{128,192},{192,256},{256,320},{320,384},{384,448},... | collective-permute-start | bytes 1474568 | tf_op jit(solution)/shard_map/ppermute | solution.py:154
  186.6 6.1 %collective-permute-done.16 = bf16[240,1024]{1,0:T(8,128)(2,1)S(1)} collective-permute-done((bf16[240,1024]{1,0:T(8,128)(2,1)}, bf16[240,1024]{1,0:T(8,128)(2,1)S(1)}, u32[]{:S(2)}, u32[]{:S(2)}) %collective-permute-start.16) | collective-permute-done | bytes 491552 | tf_op jit(solution)/shard_map/ppermute | solution.py:154
  (66 shorter events, 30.5 us)
Async XLA Ops:
  0.0 34.2 %collective-permute-start.1 = (bf16[240,1024]{1,0:T(8,128)(2,1)}, bf16[240,1024]{1,0:T(8,128)(2,1)S(1)}, u32[]{:S(2)}, u32[]{:S(2)}) collective-permute-start(bf16[240,1024]{1,0:T(8,128)(2,1)} %bitcast.13), channel_id=1, source_target_pairs={{0,15},{1,0},{2,1},{3,2},{4,3},{5,4},{6,5},{7,6},{8,7},{9,8},{10,9... | collective-permute-start | bytes 1474568 | tf_op jit(solution)/shard_map/ppermute | solution.py:154
  12.0 22.3 %collective-permute-start = (bf16[240,1024]{1,0:T(8,128)(2,1)}, bf16[240,1024]{1,0:T(8,128)(2,1)S(1)}, u32[]{:S(2)}, u32[]{:S(2)}) collective-permute-start(bf16[240,1024]{1,0:T(8,128)(2,1)} %bitcast.14), channel_id=1, source_target_pairs={{0,1},{1,2},{2,3},{3,4},{4,5},{5,6},{6,7},{7,8},{8,9},{9,10},{10,1... | collective-permute-start | bytes 1474568 | tf_op jit(solution)/shard_map/ppermute | solution.py:154
  15.3 18.6 %all-to-all-start = ((s32[16,4,2]{1,2,0:T(2,128)}), s32[16,4,2]{1,2,0:T(2,128)S(1)}, u32[]{:S(2)}, u32[]{:S(2)}) async-start(s32[16,4,2]{1,2,0:T(2,128)} %copy.8), calls=%async_computation | async-start | bytes 32768 | tf_op jit(solution)/shard_map/all_to_all | solution.py:191
  34.3 13.2 %collective-permute-start.2 = (bf16[240,1024]{1,0:T(8,128)(2,1)S(1)}, bf16[240,1024]{1,0:T(8,128)(2,1)S(1)}, u32[]{:S(2)}, u32[]{:S(2)}) collective-permute-start(bf16[240,1024]{1,0:T(8,128)(2,1)S(1)} %collective-permute-done.refs_1_), channel_id=1, source_target_pairs={{0,1},{1,2},{2,3},{3,4},{4,5},{5,6},{6,7},{7,8},{8,9},{9,10},{10,1... | collective-permute-start | bytes 1474568 | tf_op jit(solution)/shard_map/ppermute | solution.py:154
  36.6 11.8 %collective-permute-start.3 = (bf16[240,1024]{1,0:T(8,128)(2,1)S(1)}, bf16[240,1024]{1,0:T(8,128)(2,1)S(1)}, u32[]{:S(2)}, u32[]{:S(2)}) collective-permute-start(bf16[240,1024]{1,0:T(8,128)(2,1)S(1)} %collective-permute-done.1.refs_2_), channel_id=1, source_target_pairs={{0,15},{1,0},{2,1},{3,2},{4,3},{5,4},{6,5},{7,6},{8,7},{9,8},{10,9... | collective-permute-start | bytes 1474568 | tf_op jit(solution)/shard_map/ppermute | solution.py:154
  40.8 1.0 copy-start
  48.3 13.0 %collective-permute-start.4 = (bf16[240,1024]{1,0:T(8,128)(2,1)S(1)}, bf16[240,1024]{1,0:T(8,128)(2,1)S(1)}, u32[]{:S(2)}, u32[]{:S(2)}) collective-permute-start(bf16[240,1024]{1,0:T(8,128)(2,1)S(1)} %collective-permute-done.2.refs_0_), channel_id=1, source_target_pairs={{0,1},{1,2},{2,3},{3,4},{4,5},{5,6},{6,7},{7,8},{8,9},{9,10},{10,1... | collective-permute-start | bytes 1474568 | tf_op jit(solution)/shard_map/ppermute | solution.py:154
  50.3 13.0 %collective-permute-start.6 = (bf16[240,1024]{1,0:T(8,128)(2,1)S(1)}, bf16[240,1024]{1,0:T(8,128)(2,1)S(1)}, u32[]{:S(2)}, u32[]{:S(2)}) collective-permute-start(bf16[240,1024]{1,0:T(8,128)(2,1)S(1)} %collective-permute-done.3.refs_1_), channel_id=1, source_target_pairs={{0,15},{1,0},{2,1},{3,2},{4,3},{5,4},{6,5},{7,6},{8,7},{9,8},{10,9... | collective-permute-start | bytes 1474568 | tf_op jit(solution)/shard_map/ppermute | solution.py:154
  55.6 19.5 %all-to-all-start.1 = ((bf16[4,6,240,128]{3,2,1,0:T(8,128)(2,1)}), bf16[4,6,240,128]{3,2,1,0:T(8,128)(2,1)}, u32[]{:S(2)}, u32[]{:S(2)}) async-start(bf16[4,6,240,128]{3,2,1,0:T(8,128)(2,1)} %pick_part.5), calls=%async_computation.1 | async-start | bytes 2949120 | tf_op jit(solution)/shard_map/all_to_all | solution.py:158
  61.3 11.4 %collective-permute-start.5 = (bf16[240,1024]{1,0:T(8,128)(2,1)S(1)}, bf16[240,1024]{1,0:T(8,128)(2,1)S(1)}, u32[]{:S(2)}, u32[]{:S(2)}) collective-permute-start(bf16[240,1024]{1,0:T(8,128)(2,1)S(1)} %collective-permute-done.4.refs_2_), channel_id=1, source_target_pairs={{0,1},{1,2},{2,3},{3,4},{4,5},{5,6},{6,7},{7,8},{8,9},{9,10},{10,1... | collective-permute-start | bytes 1474568 | tf_op jit(solution)/shard_map/ppermute | solution.py:154
  63.2 10.3 %collective-permute-start.7 = (bf16[240,1024]{1,0:T(8,128)(2,1)S(1)}, bf16[240,1024]{1,0:T(8,128)(2,1)S(1)}, u32[]{:S(2)}, u32[]{:S(2)}) collective-permute-start(bf16[240,1024]{1,0:T(8,128)(2,1)S(1)} %collective-permute-done.6.refs_3_), channel_id=1, source_target_pairs={{0,15},{1,0},{2,1},{3,2},{4,3},{5,4},{6,5},{7,6},{8,7},{9,8},{10,9... | collective-permute-start | bytes 1474568 | tf_op jit(solution)/shard_map/ppermute | solution.py:154
  75.0 10.9 %collective-permute-start.8 = (bf16[240,1024]{1,0:T(8,128)(2,1)S(1)}, bf16[240,1024]{1,0:T(8,128)(2,1)S(1)}, u32[]{:S(2)}, u32[]{:S(2)}) collective-permute-start(bf16[240,1024]{1,0:T(8,128)(2,1)S(1)} %collective-permute-done.5.refs_0_), channel_id=1, source_target_pairs={{0,1},{1,2},{2,3},{3,4},{4,5},{5,6},{6,7},{7,8},{8,9},{9,10},{10,1... | collective-permute-start | bytes 1474568 | tf_op jit(solution)/shard_map/ppermute | solution.py:154
  76.9 11.0 %collective-permute-start.10 = (bf16[240,1024]{1,0:T(8,128)(2,1)S(1)}, bf16[240,1024]{1,0:T(8,128)(2,1)S(1)}, u32[]{:S(2)}, u32[]{:S(2)}) collective-permute-start(bf16[240,1024]{1,0:T(8,128)(2,1)S(1)} %collective-permute-done.7.refs_1_), channel_id=1, source_target_pairs={{0,15},{1,0},{2,1},{3,2},{4,3},{5,4},{6,5},{7,6},{8,7},{9,8},{10,9... | collective-permute-start | bytes 1474568 | tf_op jit(solution)/shard_map/ppermute | solution.py:154
  81.5 23.0 %all-to-all-start.2 = ((bf16[4,8,240,128]{3,2,1,0:T(8,128)(2,1)}), bf16[4,8,240,128]{3,2,1,0:T(8,128)(2,1)}, u32[]{:S(2)}, u32[]{:S(2)}) async-start(bf16[4,8,240,128]{3,2,1,0:T(8,128)(2,1)} %pick_part.6), calls=%async_computation.2 | async-start | bytes 3932160 | tf_op jit(solution)/shard_map/all_to_all | solution.py:158
  86.0 11.5 %collective-permute-start.9 = (bf16[240,1024]{1,0:T(8,128)(2,1)S(1)}, bf16[240,1024]{1,0:T(8,128)(2,1)S(1)}, u32[]{:S(2)}, u32[]{:S(2)}) collective-permute-start(bf16[240,1024]{1,0:T(8,128)(2,1)S(1)} %collective-permute-done.8.refs_2_), channel_id=1, source_target_pairs={{0,1},{1,2},{2,3},{3,4},{4,5},{5,6},{6,7},{7,8},{8,9},{9,10},{10,1... | collective-permute-start | bytes 1474568 | tf_op jit(solution)/shard_map/ppermute | solution.py:154
  87.9 10.9 %collective-permute-start.11 = (bf16[240,1024]{1,0:T(8,128)(2,1)S(1)}, bf16[240,1024]{1,0:T(8,128)(2,1)S(1)}, u32[]{:S(2)}, u32[]{:S(2)}) collective-permute-start(bf16[240,1024]{1,0:T(8,128)(2,1)S(1)} %collective-permute-done.10.refs_3_), channel_id=1, source_target_pairs={{0,15},{1,0},{2,1},{3,2},{4,3},{5,4},{6,5},{7,6},{8,7},{9,8},{10,9... | collective-permute-start | bytes 1474568 | tf_op jit(solution)/shard_map/ppermute | solution.py:154
  104.6 21.8 %all-to-all-start.3 = ((bf16[4,8,240,128]{3,2,1,0:T(8,128)(2,1)}), bf16[4,8,240,128]{3,2,1,0:T(8,128)(2,1)}, u32[]{:S(2)}, u32[]{:S(2)}) async-start(bf16[4,8,240,128]{3,2,1,0:T(8,128)(2,1)} %pick_part.7), calls=%async_computation.3 | async-start | bytes 3932160 | tf_op jit(solution)/shard_map/all_to_all | solution.py:158
  109.0 10.8 %collective-permute-start.12 = (bf16[240,1024]{1,0:T(8,128)(2,1)S(1)}, bf16[240,1024]{1,0:T(8,128)(2,1)S(1)}, u32[]{:S(2)}, u32[]{:S(2)}) collective-permute-start(bf16[240,1024]{1,0:T(8,128)(2,1)S(1)} %collective-permute-done.9.refs_0_), channel_id=1, source_target_pairs={{0,1},{1,2},{2,3},{3,4},{4,5},{5,6},{6,7},{7,8},{8,9},{9,10},{10,1... | collective-permute-start | bytes 1474568 | tf_op jit(solution)/shard_map/ppermute | solution.py:154
  110.9 10.3 %collective-permute-start.13 = (bf16[240,1024]{1,0:T(8,128)(2,1)S(1)}, bf16[240,1024]{1,0:T(8,128)(2,1)S(1)}, u32[]{:S(2)}, u32[]{:S(2)}) collective-permute-start(bf16[240,1024]{1,0:T(8,128)(2,1)S(1)} %collective-permute-done.11.refs_1_), channel_id=1, source_target_pairs={{0,15},{1,0},{2,1},{3,2},{4,3},{5,4},{6,5},{7,6},{8,7},{9,8},{10,9... | collective-permute-start | bytes 1474568 | tf_op jit(solution)/shard_map/ppermute | solution.py:154
  126.4 10.6 %collective-permute-start.15 = (bf16[128,1024]{1,0:T(8,128)(2,1)S(1)}, bf16[128,1024]{1,0:T(8,128)(2,1)S(1)}, u32[]{:S(2)}, u32[]{:S(2)}) collective-permute-start(bf16[128,1024]{1,0:T(8,128)(2,1)S(1)} %slice.7), channel_id=1, source_target_pairs={{0,15},{1,0},{2,1},{3,2},{4,3},{5,4},{6,5},{7,6},{8,7},{9,8},{10,9... | collective-permute-start | bytes 786440 | tf_op jit(solution)/shard_map/ppermute | solution.py:154
  129.0 8.0 %collective-permute-start.14 = (bf16[112,1024]{1,0:T(8,128)(2,1)S(1)}, bf16[112,1024]{1,0:T(8,128)(2,1)S(1)}, u32[]{:S(2)}, u32[]{:S(2)}) collective-permute-start(bf16[112,1024]{1,0:T(8,128)(2,1)S(1)} %slice.6), channel_id=1, source_target_pairs={{0,1},{1,2},{2,3},{3,4},{4,5},{5,6},{6,7},{7,8},{8,9},{9,10},{10,1... | collective-permute-start | bytes 688136 | tf_op jit(solution)/shard_map/ppermute | solution.py:154
  131.7 12.9 %all-to-all-start.4 = ((bf16[4,4,240,128]{3,2,1,0:T(8,128)(2,1)}), bf16[4,4,240,128]{3,2,1,0:T(8,128)(2,1)S(1)}, u32[]{:S(2)}, u32[]{:S(2)}) async-start(bf16[4,4,240,128]{3,2,1,0:T(8,128)(2,1)} %pick_part.8), calls=%async_computation.4 | async-start | bytes 1966080 | tf_op jit(solution)/shard_map/all_to_all | solution.py:158
  139.3 8.9 %copy-start.3 = (s32[1,8,16]{2,1,0:T(8,128)S(1)}, s32[1,8,16]{2,1,0:T(8,128)}, u32[]{:S(2)}) copy-start(s32[1,8,16]{2,1,0:T(8,128)} %param.8) | copy-start | bytes 1540
  144.6 17.8 %copy-start.2 = (bf16[4,4,240,128]{3,2,1,0:T(8,128)(2,1)}, bf16[4,4,240,128]{3,2,1,0:T(8,128)(2,1)S(1)}, u32[]{:S(2)}) copy-start(bf16[4,4,240,128]{3,2,1,0:T(8,128)(2,1)S(1)} %all-to-all-done.4) | copy-start | bytes 2949124
  144.6 17.8 %all-to-all-start.5 = ((bf16[4,6,240,128]{3,2,1,0:T(8,128)(2,1)}), bf16[4,6,240,128]{3,2,1,0:T(8,128)(2,1)S(1)}, u32[]{:S(2)}, u32[]{:S(2)}) async-start(bf16[4,6,240,128]{3,2,1,0:T(8,128)(2,1)} %pick_part.9), calls=%async_computation.5 | async-start | bytes 2949120 | tf_op jit(solution)/shard_map/all_to_all | solution.py:158
  162.4 1.1 copy-start.1
  173.8 18.8 %collective-permute-start.16 = (bf16[240,1024]{1,0:T(8,128)(2,1)}, bf16[240,1024]{1,0:T(8,128)(2,1)S(1)}, u32[]{:S(2)}, u32[]{:S(2)}) collective-permute-start(bf16[240,1024]{1,0:T(8,128)(2,1)} %mix.1), channel_id=1, source_target_pairs={{0,64},{64,128},{128,192},{192,256},{256,320},{320,384},{384,448},... | collective-permute-start | bytes 1474568 | tf_op jit(solution)/shard_map/ppermute | solution.py:154

commit v6 on v5

--- a/solution.py
+++ b/solution.py
@@ -8,19 +8,20 @@
 CLAMP_TOP = 3.0
 LINES = 4
 STEPS = 16
+GROUP = 4
+Z = ("far", "near")
 CAP = 2
 BLOCK = 128
 PICK_VMEM = 24 * 2**20
 MIX_VMEM = 58 * 2**20
 PICK_WEIGHT = 12 * 10**9
-IDS_STEP = 2
-HAVE = (5,7,8, 9, 9)
+AFTER = (2,)
+HAVE = (5, 8, 9, 9)
 PARTS = (
     (0, -1, 1),
     (-2, 2, -3, 3),
     (-4, 4, -5, 5),
-    (-6, 6),
-    (-7, 7, 8),
+    (-6, 6, -7, 7, 8),
 )
 
 
@@ -173,8 +174,8 @@
 def body(layer_input, weight_blocks, neuron_bias, block_slots, send_lists):
     samples, weights, bias = layer_input[0], weight_blocks[0], neuron_bias[0]
     slots = block_slots.reshape(-1)
-    here = lax.axis_index("z").astype(jnp.int32)
-    lists = send_lists.reshape(LINES, STEPS, CAP).transpose(1, 0, 2)
+    here = lax.axis_index(Z).astype(jnp.int32)
+    lists = send_lists.reshape(LINES, GROUP, GROUP, CAP).transpose(2, 1, 0, 3)
 
     held = {0: [(samples, 0)]}
     up = down = samples
@@ -188,32 +189,39 @@
     def send_next():
         arrived.append(over_lines(picked[len(arrived)]))
 
-    ids = lax.all_to_all(lists, "z", 0, 0, tiled=True).reshape(-1)
+    near = lax.all_to_all(lists, "near", 0, 0, tiled=True)
     last = STEPS // 2
     half = samples.shape[0] // 32 * 16
-    waiting = []
+    ready = []
     for step in range(1, last + 1):
-        if step == IDS_STEP:
-            ids, up, down = lax.optimization_barrier((ids, up, down))
-        for ready, index in waiting:
-            if step == ready + 2:
+        if step == 2:
+            near, up, down = lax.optimization_barrier((near, up, down))
+            far = near.transpose(1, 0, 2, 3)
+            ids = lax.all_to_all(far, "far", 0, 0, tiled=True).reshape(-1)
+        for index, done in enumerate(ready):
+            if step == done + 2:
+                pick_next()
                 picked[index], up, down = lax.optimization_barrier(
                     (picked[index], up, down)
                 )
+                if index in AFTER:
+                    picked[index], arrived[-1] = lax.optimization_barrier(
+                        (picked[index], arrived[-1])
+                    )
                 send_next()
             if step == HAVE[index]:
                 arrived[index], up, down = lax.optimization_barrier(
                     (arrived[index], up, down)
                 )
         if step < last:
-            up, down = shifted(up, "z", 1), shifted(down, "z", -1)
+            up, down = shifted(up, Z, 1), shifted(down, Z, -1)
             held[-step], held[step] = [(up, 0)], [(down, 0)]
         else:
-            up, down = shifted(up[:half], "z", 1), shifted(down[half:], "z", -1)
+            up, down = shifted(up[:half], Z, 1), shifted(down[half:], Z, -1)
             held[step] = [(up, 0), (down, half)]
-        if all(o in held for o in PARTS[len(picked)]):
-            waiting.append((step, len(picked)))
-            pick_next()
+        if all(o in held for o in PARTS[len(ready)]):
+            ready.append(step)
+    pick_next()
     send_next()
 
     out = mix(part_codes(slots, here), arrived, weights, bias)
@@ -223,9 +231,9 @@
 def solution(mesh):
     segments, row = mesh.devices.shape
     split = Mesh(
-        mesh.devices.reshape(segments, row // STEPS, STEPS), ("segment", "y", "z")
+        mesh.devices.reshape(segments, row // STEPS, GROUP, GROUP), ("segment", "y", *Z)
     )
-    row = ("y", "z")
+    row = ("y", *Z)
     placed = (
         P("segment", None, row),
         P("segment", row, None, None, None),

time: 195 us -> 185 us (0.949)
  waiting for transfers between devices: 64.3 us -> 47.3 us
  blocking collectives: 0 us -> 9.43 us
    all_to_all x5 -> x4, waiting for transfers between devices: 28.9 us -> 14.3 us  [over_lines(): incoming = lax.all_to_all(outgoing, 'y', 0, 0, tiled=True)]
    all_to_all x0 -> x1, blocking collectives: none -> 9.43 us  [body(): near = lax.all_to_all(lists, 'near', 0, 0, tiled=True)]
    all_to_all x1, waiting for transfers between devices: 11.4 us -> 3.6 us  [body(): ids = lax.all_to_all(far, 'far', 0, 0, tiled=True).reshape(-1)]
    ppermute x17, waiting for transfers between devices: 24.1 us -> 29.4 us  [shifted(): lax.ppermute(value, axis, [(i, (i + by) % count) for i in range(count)])]
    ppermute x17, starting transfers between devices: 71.6 us -> 74.9 us  [shifted(): lax.ppermute(value, axis, [(i, (i + by) % count) for i in range(count)])]
    all_to_all x5 -> x4, starting transfers between devices: 20.3 us -> 17.2 us  [over_lines(): incoming = lax.all_to_all(outgoing, 'y', 0, 0, tiled=True)]
    pallas_call x5 -> x4, Pallas kernels: 11.7 us -> 10.5 us  [pick_call(): pl.pallas_call(kernel, grid_spec=pltpu.PrefetchScalarGridSpec(num_scalar_...]
  transfers between devices with their start and end apart: 23 -> 22, of which waited for: 17 -> 17; matrix products, arithmetic and copies ran while one was open for 2% -> 2% of each run, Pallas kernels for 6% -> 6%
where the time goes in v6:
time: 185 us; the launch traced here: 184 us
  starting transfers between devices  97.9 us (53%)
  waiting for transfers between devices  47.3 us (26%)
  Pallas kernels  20.7 us (11%)
  blocking collectives  9.43 us (5%)
  local copies, waits for them, and re-layouts  7.92 us (4%)
    ppermute x17, starting transfers between devices, shifted(): lax.ppermute(value, axis, [(i, (i + by) % count) for i in range(count)])  74.9 us
    ppermute x17, waiting for transfers between devices, shifted(): lax.ppermute(value, axis, [(i, (i + by) % count) for i in range(count)])  29.4 us
    all_to_all x4, starting transfers between devices, over_lines(): incoming = lax.all_to_all(outgoing, 'y', 0, 0, tiled=True)  17.2 us
    all_to_all x4, waiting for transfers between devices, over_lines(): incoming = lax.all_to_all(outgoing, 'y', 0, 0, tiled=True)  14.3 us
    pallas_call x4, Pallas kernels, pick_call(): pl.pallas_call(kernel, grid_spec=pltpu.PrefetchScalarGridSpec(num_scalar_...  10.5 us
    pallas_call x1, Pallas kernels, mix(): pl.pallas_call(kernel, grid_spec=pltpu.PrefetchScalarGridSpec(num_scalar_...  10.2 us
    all_to_all x1, blocking collectives, body(): near = lax.all_to_all(lists, 'near', 0, 0, tiled=True)  9.43 us
    all_to_all x1, starting transfers between devices, body(): ids = lax.all_to_all(far, 'far', 0, 0, tiled=True).reshape(-1)  5.81 us
  transfers between devices with their start and end apart: 22, of which 17 were waited for; matrix products, arithmetic and copies ran while one was open for 2% of the time, Pallas kernels for 6%

profile of v6, /device:TPU:1, one launch (start us, length us, event | category | flops | bytes accessed | tf_op | source)
XLA Modules:
  0.0 184.2 jit_solution(17177489099623497906)
XLA Ops:
  0.0 11.9 %collective-permute-start.1 = (bf16[240,1024]{1,0:T(8,128)(2,1)}, bf16[240,1024]{1,0:T(8,128)(2,1)S(1)}, u32[]{:S(2)}, u32[]{:S(2)}) collective-permute-start(bf16[240,1024]{1,0:T(8,128)(2,1)} %bitcast.13), channel_id=1, source_target_pairs={{0,15},{1,0},{2,1},{3,2},{4,3},{5,4},{6,5},{7,6},{8,7},{9,8},{10,9... | collective-permute-start | bytes 1474568 | tf_op jit(solution)/shard_map/ppermute | solution.py:155
  14.8 9.4 %all_to_all.30 = s32[4,4,4,2]{1,2,3,0:T(4,128)S(1)} all-to-all(s32[4,4,4,2]{1,2,3,0:T(4,128)S(1)} %copy.8), channel_id=1, replica_groups=mesh['segment'=8,'y'=4,'far'=4,'near'=4] {'near'}, dimensions={0} | all-to-all | bytes 1024 | tf_op jit(solution)/shard_map/all_to_all | solution.py:192
  24.2 2.8 %collective-permute-done.refs_1_ = bf16[240,1024]{1,0:T(8,128)(2,1)S(1)} collective-permute-done((bf16[240,1024]{1,0:T(8,128)(2,1)}, bf16[240,1024]{1,0:T(8,128)(2,1)S(1)}, u32[]{:S(2)}, u32[]{:S(2)}) %collective-permute-start) | collective-permute-done | bytes 491552 | tf_op jit(solution)/shard_map/ppermute | solution.py:155
  27.8 5.8 %all-to-all-start.1 = ((s32[4,4,4,2]{1,2,3,0:T(4,128)}), s32[4,4,4,2]{1,2,3,0:T(4,128)S(1)}, u32[]{:S(2)}, u32[]{:S(2)}) async-start(s32[4,4,4,2]{1,2,3,0:T(4,128)} %copy.9), calls=%async_computation.1 | async-start | bytes 32768 | tf_op jit(solution)/shard_map/all_to_all | solution.py:200
  33.6 2.0 %collective-permute-start.2 = (bf16[240,1024]{1,0:T(8,128)(2,1)S(1)}, bf16[240,1024]{1,0:T(8,128)(2,1)S(1)}, u32[]{:S(2)}, u32[]{:S(2)}) collective-permute-start(bf16[240,1024]{1,0:T(8,128)(2,1)S(1)} %collective-permute-done.refs_1_), channel_id=1, source_target_pairs={{0,1},{1,2},{2,3},{3,4},{4,5},{5,6},{6,7},{7,8},{8,9},{9,10},{10,1... | collective-permute-start | bytes 1474568 | tf_op jit(solution)/shard_map/ppermute | solution.py:155
  35.6 5.9 %collective-permute-start.3 = (bf16[240,1024]{1,0:T(8,128)(2,1)S(1)}, bf16[240,1024]{1,0:T(8,128)(2,1)S(1)}, u32[]{:S(2)}, u32[]{:S(2)}) collective-permute-start(bf16[240,1024]{1,0:T(8,128)(2,1)S(1)} %collective-permute-done.1.refs_2_), channel_id=1, source_target_pairs={{0,15},{1,0},{2,1},{3,2},{4,3},{5,4},{6,5},{7,6},{8,7},{9,8},{10,9... | collective-permute-start | bytes 1474568 | tf_op jit(solution)/shard_map/ppermute | solution.py:155
  41.5 3.6 %all-to-all-done.1 = s32[4,4,4,2]{1,2,3,0:T(4,128)S(1)} async-done(((s32[4,4,4,2]{1,2,3,0:T(4,128)}), s32[4,4,4,2]{1,2,3,0:T(4,128)S(1)}, u32[]{:S(2)}, u32[]{:S(2)}) %all-to-all-start.1) | async-done | bytes 544 | tf_op jit(solution)/shard_map/all_to_all | solution.py:200
  46.5 2.3 %pick_part.4 = bf16[4,6,240,128]{3,2,1,0:T(8,128)(2,1)} custom-call(s32[128]{0:T(128)S(1)} %reshape.70.ids_ref, s32[1]{0:T(128)} %bitcast.3.here_ref, bf16[240,1024]{1,0:T(8,128)(2,1)S(1)} %bitcast.15, bf16[240,1024]{1,0:T(8,128)(2,1)S(1)} %collective-permute-done.refs_1_, bf16[240,1024]{1,0:T(8,128)(2,1)S(1)} %collective-permute-done.1.refs_2_), custom_call_target="tpu_custom_call" | custom-call | flops 12000000000 | bytes 2949120 | tf_op jit(solution)/shard_map/pick_part/pallas_call | solution.py:48
  51.3 5.3 %collective-permute-start.6 = (bf16[240,1024]{1,0:T(8,128)(2,1)S(1)}, bf16[240,1024]{1,0:T(8,128)(2,1)S(1)}, u32[]{:S(2)}, u32[]{:S(2)}) collective-permute-start(bf16[240,1024]{1,0:T(8,128)(2,1)S(1)} %collective-permute-done.3.refs_1_), channel_id=1, source_target_pairs={{0,15},{1,0},{2,1},{3,2},{4,3},{5,4},{6,5},{7,6},{8,7},{9,8},{10,9... | collective-permute-start | bytes 1474568 | tf_op jit(solution)/shard_map/ppermute | solution.py:155
  56.6 4.4 %all-to-all-start.2 = ((bf16[4,6,240,128]{3,2,1,0:T(8,128)(2,1)}), bf16[4,6,240,128]{3,2,1,0:T(8,128)(2,1)}, u32[]{:S(2)}, u32[]{:S(2)}) async-start(bf16[4,6,240,128]{3,2,1,0:T(8,128)(2,1)} %pick_part.4), calls=%async_computation.2 | async-start | bytes 2949120 | tf_op jit(solution)/shard_map/all_to_all | solution.py:159
  64.9 4.2 %collective-permute-start.7 = (bf16[240,1024]{1,0:T(8,128)(2,1)S(1)}, bf16[240,1024]{1,0:T(8,128)(2,1)S(1)}, u32[]{:S(2)}, u32[]{:S(2)}) collective-permute-start(bf16[240,1024]{1,0:T(8,128)(2,1)S(1)} %collective-permute-done.6.refs_3_), channel_id=1, source_target_pairs={{0,15},{1,0},{2,1},{3,2},{4,3},{5,4},{6,5},{7,6},{8,7},{9,8},{10,9... | collective-permute-start | bytes 1474568 | tf_op jit(solution)/shard_map/ppermute | solution.py:155
  69.1 2.6 %pick_part.5 = bf16[4,8,240,128]{3,2,1,0:T(8,128)(2,1)} custom-call(s32[128]{0:T(128)S(1)} %reshape.70.ids_ref, s32[1]{0:T(128)} %bitcast.3.here_ref, bf16[240,1024]{1,0:T(8,128)(2,1)S(1)} %collective-permute-done.2.refs_0_, bf16[240,1024]{1,0:T(8,128)(2,1)S(1)} %collective-permute-done.3.refs_1_, bf16[240,1024]{1,0:T(8,128)(2,1)S(1)} %collective-permute-done.4.refs_2_, ...), custom_call_target="tpu_custom_call" | custom-call | flops 12000000000 | bytes 3932160 | tf_op jit(solution)/shard_map/pick_part/pallas_call | solution.py:48
  71.7 2.5 %collective-permute-done.5.refs_0_ = bf16[240,1024]{1,0:T(8,128)(2,1)S(1)} collective-permute-done((bf16[240,1024]{1,0:T(8,128)(2,1)S(1)}, bf16[240,1024]{1,0:T(8,128)(2,1)S(1)}, u32[]{:S(2)}, u32[]{:S(2)}) %collective-permute-start.5) | collective-permute-done | bytes 491552 | tf_op jit(solution)/shard_map/ppermute | solution.py:155
  74.2 2.0 %collective-permute-done.7.refs_1_ = bf16[240,1024]{1,0:T(8,128)(2,1)S(1)} collective-permute-done((bf16[240,1024]{1,0:T(8,128)(2,1)S(1)}, bf16[240,1024]{1,0:T(8,128)(2,1)S(1)}, u32[]{:S(2)}, u32[]{:S(2)}) %collective-permute-start.7) | collective-permute-done | bytes 491552 | tf_op jit(solution)/shard_map/ppermute | solution.py:155
  76.4 2.9 %collective-permute-start.8 = (bf16[240,1024]{1,0:T(8,128)(2,1)S(1)}, bf16[240,1024]{1,0:T(8,128)(2,1)S(1)}, u32[]{:S(2)}, u32[]{:S(2)}) collective-permute-start(bf16[240,1024]{1,0:T(8,128)(2,1)S(1)} %collective-permute-done.5.refs_0_), channel_id=1, source_target_pairs={{0,1},{1,2},{2,3},{3,4},{4,5},{5,6},{6,7},{7,8},{8,9},{9,10},{10,1... | collective-permute-start | bytes 1474568 | tf_op jit(solution)/shard_map/ppermute | solution.py:155
  79.4 3.6 %collective-permute-start.9 = (bf16[240,1024]{1,0:T(8,128)(2,1)S(1)}, bf16[240,1024]{1,0:T(8,128)(2,1)S(1)}, u32[]{:S(2)}, u32[]{:S(2)}) collective-permute-start(bf16[240,1024]{1,0:T(8,128)(2,1)S(1)} %collective-permute-done.7.refs_1_), channel_id=1, source_target_pairs={{0,15},{1,0},{2,1},{3,2},{4,3},{5,4},{6,5},{7,6},{8,7},{9,8},{10,9... | collective-permute-start | bytes 1474568 | tf_op jit(solution)/shard_map/ppermute | solution.py:155
  82.9 4.4 %all-to-all-start.3 = ((bf16[4,8,240,128]{3,2,1,0:T(8,128)(2,1)}), bf16[4,8,240,128]{3,2,1,0:T(8,128)(2,1)}, u32[]{:S(2)}, u32[]{:S(2)}) async-start(bf16[4,8,240,128]{3,2,1,0:T(8,128)(2,1)} %pick_part.5), calls=%async_computation.3 | async-start | bytes 3932160 | tf_op jit(solution)/shard_map/all_to_all | solution.py:159
  89.5 4.4 %collective-permute-start.11 = (bf16[240,1024]{1,0:T(8,128)(2,1)S(1)}, bf16[240,1024]{1,0:T(8,128)(2,1)S(1)}, u32[]{:S(2)}, u32[]{:S(2)}) collective-permute-start(bf16[240,1024]{1,0:T(8,128)(2,1)S(1)} %collective-permute-done.9.refs_3_), channel_id=1, source_target_pairs={{0,15},{1,0},{2,1},{3,2},{4,3},{5,4},{6,5},{7,6},{8,7},{9,8},{10,9... | collective-permute-start | bytes 1474568 | tf_op jit(solution)/shard_map/ppermute | solution.py:155
  93.9 2.7 %pick_part.6 = bf16[4,8,240,128]{3,2,1,0:T(8,128)(2,1)} custom-call(s32[128]{0:T(128)S(1)} %reshape.70.ids_ref, s32[1]{0:T(128)} %bitcast.3.here_ref, bf16[240,1024]{1,0:T(8,128)(2,1)S(1)} %collective-permute-done.5.refs_0_, bf16[240,1024]{1,0:T(8,128)(2,1)S(1)} %collective-permute-done.7.refs_1_, bf16[240,1024]{1,0:T(8,128)(2,1)S(1)} %collective-permute-done.8.refs_2_, ...), custom_call_target="tpu_custom_call" | custom-call | flops 12000000000 | bytes 3932160 | tf_op jit(solution)/shard_map/pick_part/pallas_call | solution.py:48
  100.4 4.3 %collective-permute-start.12 = (bf16[240,1024]{1,0:T(8,128)(2,1)S(1)}, bf16[240,1024]{1,0:T(8,128)(2,1)S(1)}, u32[]{:S(2)}, u32[]{:S(2)}) collective-permute-start(bf16[240,1024]{1,0:T(8,128)(2,1)S(1)} %collective-permute-done.10.refs_0_), channel_id=1, source_target_pairs={{0,1},{1,2},{2,3},{3,4},{4,5},{5,6},{6,7},{7,8},{8,9},{9,10},{10,1... | collective-permute-start | bytes 1474568 | tf_op jit(solution)/shard_map/ppermute | solution.py:155
  104.7 2.5 %collective-permute-start.13 = (bf16[240,1024]{1,0:T(8,128)(2,1)S(1)}, bf16[240,1024]{1,0:T(8,128)(2,1)S(1)}, u32[]{:S(2)}, u32[]{:S(2)}) collective-permute-start(bf16[240,1024]{1,0:T(8,128)(2,1)S(1)} %collective-permute-done.11.refs_1_), channel_id=1, source_target_pairs={{0,15},{1,0},{2,1},{3,2},{4,3},{5,4},{6,5},{7,6},{8,7},{9,8},{10,9... | collective-permute-start | bytes 1474568 | tf_op jit(solution)/shard_map/ppermute | solution.py:155
  107.3 4.4 %all-to-all-start.4 = ((bf16[4,8,240,128]{3,2,1,0:T(8,128)(2,1)}), bf16[4,8,240,128]{3,2,1,0:T(8,128)(2,1)}, u32[]{:S(2)}, u32[]{:S(2)}) async-start(bf16[4,8,240,128]{3,2,1,0:T(8,128)(2,1)} %pick_part.6), calls=%async_computation.4 | async-start | bytes 3932160 | tf_op jit(solution)/shard_map/all_to_all | solution.py:159
  112.0 2.9 %collective-permute-done.13.refs_3_ = bf16[240,1024]{1,0:T(8,128)(2,1)S(1)} collective-permute-done((bf16[240,1024]{1,0:T(8,128)(2,1)S(1)}, bf16[240,1024]{1,0:T(8,128)(2,1)S(1)}, u32[]{:S(2)}, u32[]{:S(2)}) %collective-permute-start.13) | collective-permute-done | bytes 491552 | tf_op jit(solution)/shard_map/ppermute | solution.py:155
  114.9 3.2 %collective-permute-start.15 = (bf16[128,1024]{1,0:T(8,128)(2,1)S(1)}, bf16[128,1024]{1,0:T(8,128)(2,1)S(1)}, u32[]{:S(2)}, u32[]{:S(2)}) collective-permute-start(bf16[128,1024]{1,0:T(8,128)(2,1)S(1)} %slice.7), channel_id=1, source_target_pairs={{0,15},{1,0},{2,1},{3,2},{4,3},{5,4},{6,5},{7,6},{8,7},{9,8},{10,9... | collective-permute-start | bytes 786440 | tf_op jit(solution)/shard_map/ppermute | solution.py:155
  118.1 2.1 %collective-permute-start.14 = (bf16[112,1024]{1,0:T(8,128)(2,1)S(1)}, bf16[112,1024]{1,0:T(8,128)(2,1)S(1)}, u32[]{:S(2)}, u32[]{:S(2)}) collective-permute-start(bf16[112,1024]{1,0:T(8,128)(2,1)S(1)} %slice.6), channel_id=1, source_target_pairs={{0,1},{1,2},{2,3},{3,4},{4,5},{5,6},{6,7},{7,8},{8,9},{9,10},{10,1... | collective-permute-start | bytes 688136 | tf_op jit(solution)/shard_map/ppermute | solution.py:155
  120.2 6.3 %collective-permute-done.14.refs_4_ = bf16[112,1024]{1,0:T(8,128)(2,1)S(1)} collective-permute-done((bf16[112,1024]{1,0:T(8,128)(2,1)S(1)}, bf16[112,1024]{1,0:T(8,128)(2,1)S(1)}, u32[]{:S(2)}, u32[]{:S(2)}) %collective-permute-start.14) | collective-permute-done | bytes 229408 | tf_op jit(solution)/shard_map/ppermute | solution.py:155
  126.5 2.9 %pick_part.7 = bf16[4,10,240,128]{3,2,1,0:T(8,128)(2,1)} custom-call(s32[128]{0:T(128)S(1)} %reshape.70.ids_ref, s32[1]{0:T(128)} %bitcast.3.here_ref, bf16[240,1024]{1,0:T(8,128)(2,1)S(1)} %collective-permute-done.10.refs_0_, bf16[240,1024]{1,0:T(8,128)(2,1)S(1)} %collective-permute-done.11.refs_1_, bf16[240,1024]{1,0:T(8,128)(2,1)S(1)} %collective-permute-done.12.refs_2_, ...), custom_call_target="tpu_custom_call" | custom-call | flops 12000000000 | bytes 4915200 | tf_op jit(solution)/shard_map/pick_part/pallas_call | solution.py:48
  129.5 3.9 %all-to-all-start.5 = ((bf16[4,10,240,128]{3,2,1,0:T(8,128)(2,1)}), bf16[4,10,240,128]{3,2,1,0:T(8,128)(2,1)S(1)}, u32[]{:S(2)}, u32[]{:S(2)}) async-start(bf16[4,10,240,128]{3,2,1,0:T(8,128)(2,1)} %pick_part.7), calls=%async_computation.5 | async-start | bytes 4915200 | tf_op jit(solution)/shard_map/all_to_all | solution.py:159
  136.7 14.2 %all-to-all-done.5 = bf16[4,10,240,128]{3,2,1,0:T(8,128)(2,1)S(1)} async-done(((bf16[4,10,240,128]{3,2,1,0:T(8,128)(2,1)}), bf16[4,10,240,128]{3,2,1,0:T(8,128)(2,1)S(1)}, u32[]{:S(2)}, u32[]{:S(2)}) %all-to-all-start.5) | async-done | bytes 2457632 | tf_op jit(solution)/shard_map/all_to_all | solution.py:159
  152.3 10.2 %mix.1 = bf16[240,1024]{1,0:T(8,128)(2,1)} custom-call(s32[128]{0:T(128)} %select_select_fusion.codes_ref, bf16[24,240,128]{2,1,0:T(8,128)(2,1)} %bitcast.4.refs_0_, bf16[32,240,128]{2,1,0:T(8,128)(2,1)} %bitcast.5.refs_1_, bf16[32,240,128]{2,1,0:T(8,128)(2,1)} %bitcast.6.refs_2_, bf16[40,240,128]{2,1,0:T(8,128)(2,1)} %bitcast.16, ...), custom_call_target="tpu_custom_call" | custom-call | flops 1006632960 | bytes 12058624 | tf_op jit(solution)/shard_map/mix/pallas_call | solution.py:126
  162.6 14.8 %collective-permute-start.16 = (bf16[240,1024]{1,0:T(8,128)(2,1)}, bf16[240,1024]{1,0:T(8,128)(2,1)S(1)}, u32[]{:S(2)}, u32[]{:S(2)}) collective-permute-start(bf16[240,1024]{1,0:T(8,128)(2,1)} %mix.1), channel_id=1, source_target_pairs={{0,64},{64,128},{128,192},{192,256},{256,320},{320,384},{384,448},... | collective-permute-start | bytes 1474568 | tf_op jit(solution)/shard_map/ppermute | solution.py:155
  177.3 6.1 %collective-permute-done.16 = bf16[240,1024]{1,0:T(8,128)(2,1)S(1)} collective-permute-done((bf16[240,1024]{1,0:T(8,128)(2,1)}, bf16[240,1024]{1,0:T(8,128)(2,1)S(1)}, u32[]{:S(2)}, u32[]{:S(2)}) %collective-permute-start.16) | collective-permute-done | bytes 491552 | tf_op jit(solution)/shard_map/ppermute | solution.py:155
  (66 shorter events, 23.3 us)
Async XLA Ops:
  0.0 24.2 %collective-permute-start.1 = (bf16[240,1024]{1,0:T(8,128)(2,1)}, bf16[240,1024]{1,0:T(8,128)(2,1)S(1)}, u32[]{:S(2)}, u32[]{:S(2)}) collective-permute-start(bf16[240,1024]{1,0:T(8,128)(2,1)} %bitcast.13), channel_id=1, source_target_pairs={{0,15},{1,0},{2,1},{3,2},{4,3},{5,4},{6,5},{7,6},{8,7},{9,8},{10,9... | collective-permute-start | bytes 1474568 | tf_op jit(solution)/shard_map/ppermute | solution.py:155
  12.0 15.1 %collective-permute-start = (bf16[240,1024]{1,0:T(8,128)(2,1)}, bf16[240,1024]{1,0:T(8,128)(2,1)S(1)}, u32[]{:S(2)}, u32[]{:S(2)}) collective-permute-start(bf16[240,1024]{1,0:T(8,128)(2,1)} %bitcast.14), channel_id=1, source_target_pairs={{0,1},{1,2},{2,3},{3,4},{4,5},{5,6},{6,7},{7,8},{8,9},{9,10},{10,1... | collective-permute-start | bytes 1474568 | tf_op jit(solution)/shard_map/ppermute | solution.py:155
  27.8 17.4 %all-to-all-start.1 = ((s32[4,4,4,2]{1,2,3,0:T(4,128)}), s32[4,4,4,2]{1,2,3,0:T(4,128)S(1)}, u32[]{:S(2)}, u32[]{:S(2)}) async-start(s32[4,4,4,2]{1,2,3,0:T(4,128)} %copy.9), calls=%async_computation.1 | async-start | bytes 32768 | tf_op jit(solution)/shard_map/all_to_all | solution.py:200
  33.6 15.5 %collective-permute-start.2 = (bf16[240,1024]{1,0:T(8,128)(2,1)S(1)}, bf16[240,1024]{1,0:T(8,128)(2,1)S(1)}, u32[]{:S(2)}, u32[]{:S(2)}) collective-permute-start(bf16[240,1024]{1,0:T(8,128)(2,1)S(1)} %collective-permute-done.refs_1_), channel_id=1, source_target_pairs={{0,1},{1,2},{2,3},{3,4},{4,5},{5,6},{6,7},{7,8},{8,9},{9,10},{10,1... | collective-permute-start | bytes 1474568 | tf_op jit(solution)/shard_map/ppermute | solution.py:155
  35.6 13.8 %collective-permute-start.3 = (bf16[240,1024]{1,0:T(8,128)(2,1)S(1)}, bf16[240,1024]{1,0:T(8,128)(2,1)S(1)}, u32[]{:S(2)}, u32[]{:S(2)}) collective-permute-start(bf16[240,1024]{1,0:T(8,128)(2,1)S(1)} %collective-permute-done.1.refs_2_), channel_id=1, source_target_pairs={{0,15},{1,0},{2,1},{3,2},{4,3},{5,4},{6,5},{7,6},{8,7},{9,8},{10,9... | collective-permute-start | bytes 1474568 | tf_op jit(solution)/shard_map/ppermute | solution.py:155
  45.5 1.0 copy-start
  49.4 13.2 %collective-permute-start.4 = (bf16[240,1024]{1,0:T(8,128)(2,1)S(1)}, bf16[240,1024]{1,0:T(8,128)(2,1)S(1)}, u32[]{:S(2)}, u32[]{:S(2)}) collective-permute-start(bf16[240,1024]{1,0:T(8,128)(2,1)S(1)} %collective-permute-done.2.refs_0_), channel_id=1, source_target_pairs={{0,1},{1,2},{2,3},{3,4},{4,5},{5,6},{6,7},{7,8},{8,9},{9,10},{10,1... | collective-permute-start | bytes 1474568 | tf_op jit(solution)/shard_map/ppermute | solution.py:155
  51.3 13.6 %collective-permute-start.6 = (bf16[240,1024]{1,0:T(8,128)(2,1)S(1)}, bf16[240,1024]{1,0:T(8,128)(2,1)S(1)}, u32[]{:S(2)}, u32[]{:S(2)}) collective-permute-start(bf16[240,1024]{1,0:T(8,128)(2,1)S(1)} %collective-permute-done.3.refs_1_), channel_id=1, source_target_pairs={{0,15},{1,0},{2,1},{3,2},{4,3},{5,4},{6,5},{7,6},{8,7},{9,8},{10,9... | collective-permute-start | bytes 1474568 | tf_op jit(solution)/shard_map/ppermute | solution.py:155
  56.6 19.8 %all-to-all-start.2 = ((bf16[4,6,240,128]{3,2,1,0:T(8,128)(2,1)}), bf16[4,6,240,128]{3,2,1,0:T(8,128)(2,1)}, u32[]{:S(2)}, u32[]{:S(2)}) async-start(bf16[4,6,240,128]{3,2,1,0:T(8,128)(2,1)} %pick_part.4), calls=%async_computation.2 | async-start | bytes 2949120 | tf_op jit(solution)/shard_map/all_to_all | solution.py:159
  62.6 11.6 %collective-permute-start.5 = (bf16[240,1024]{1,0:T(8,128)(2,1)S(1)}, bf16[240,1024]{1,0:T(8,128)(2,1)S(1)}, u32[]{:S(2)}, u32[]{:S(2)}) collective-permute-start(bf16[240,1024]{1,0:T(8,128)(2,1)S(1)} %collective-permute-done.4.refs_2_), channel_id=1, source_target_pairs={{0,1},{1,2},{2,3},{3,4},{4,5},{5,6},{6,7},{7,8},{8,9},{9,10},{10,1... | collective-permute-start | bytes 1474568 | tf_op jit(solution)/shard_map/ppermute | solution.py:155
  64.9 11.4 %collective-permute-start.7 = (bf16[240,1024]{1,0:T(8,128)(2,1)S(1)}, bf16[240,1024]{1,0:T(8,128)(2,1)S(1)}, u32[]{:S(2)}, u32[]{:S(2)}) collective-permute-start(bf16[240,1024]{1,0:T(8,128)(2,1)S(1)} %collective-permute-done.6.refs_3_), channel_id=1, source_target_pairs={{0,15},{1,0},{2,1},{3,2},{4,3},{5,4},{6,5},{7,6},{8,7},{9,8},{10,9... | collective-permute-start | bytes 1474568 | tf_op jit(solution)/shard_map/ppermute | solution.py:155
  76.4 10.9 %collective-permute-start.8 = (bf16[240,1024]{1,0:T(8,128)(2,1)S(1)}, bf16[240,1024]{1,0:T(8,128)(2,1)S(1)}, u32[]{:S(2)}, u32[]{:S(2)}) collective-permute-start(bf16[240,1024]{1,0:T(8,128)(2,1)S(1)} %collective-permute-done.5.refs_0_), channel_id=1, source_target_pairs={{0,1},{1,2},{2,3},{3,4},{4,5},{5,6},{6,7},{7,8},{8,9},{9,10},{10,1... | collective-permute-start | bytes 1474568 | tf_op jit(solution)/shard_map/ppermute | solution.py:155
  79.4 10.1 %collective-permute-start.9 = (bf16[240,1024]{1,0:T(8,128)(2,1)S(1)}, bf16[240,1024]{1,0:T(8,128)(2,1)S(1)}, u32[]{:S(2)}, u32[]{:S(2)}) collective-permute-start(bf16[240,1024]{1,0:T(8,128)(2,1)S(1)} %collective-permute-done.7.refs_1_), channel_id=1, source_target_pairs={{0,15},{1,0},{2,1},{3,2},{4,3},{5,4},{6,5},{7,6},{8,7},{9,8},{10,9... | collective-permute-start | bytes 1474568 | tf_op jit(solution)/shard_map/ppermute | solution.py:155
  82.9 24.4 %all-to-all-start.3 = ((bf16[4,8,240,128]{3,2,1,0:T(8,128)(2,1)}), bf16[4,8,240,128]{3,2,1,0:T(8,128)(2,1)}, u32[]{:S(2)}, u32[]{:S(2)}) async-start(bf16[4,8,240,128]{3,2,1,0:T(8,128)(2,1)} %pick_part.5), calls=%async_computation.3 | async-start | bytes 3932160 | tf_op jit(solution)/shard_map/all_to_all | solution.py:159
  87.4 11.2 %collective-permute-start.10 = (bf16[240,1024]{1,0:T(8,128)(2,1)S(1)}, bf16[240,1024]{1,0:T(8,128)(2,1)S(1)}, u32[]{:S(2)}, u32[]{:S(2)}) collective-permute-start(bf16[240,1024]{1,0:T(8,128)(2,1)S(1)} %collective-permute-done.8.refs_2_), channel_id=1, source_target_pairs={{0,1},{1,2},{2,3},{3,4},{4,5},{5,6},{6,7},{7,8},{8,9},{9,10},{10,1... | collective-permute-start | bytes 1474568 | tf_op jit(solution)/shard_map/ppermute | solution.py:155
  89.5 10.9 %collective-permute-start.11 = (bf16[240,1024]{1,0:T(8,128)(2,1)S(1)}, bf16[240,1024]{1,0:T(8,128)(2,1)S(1)}, u32[]{:S(2)}, u32[]{:S(2)}) collective-permute-start(bf16[240,1024]{1,0:T(8,128)(2,1)S(1)} %collective-permute-done.9.refs_3_), channel_id=1, source_target_pairs={{0,15},{1,0},{2,1},{3,2},{4,3},{5,4},{6,5},{7,6},{8,7},{9,8},{10,9... | collective-permute-start | bytes 1474568 | tf_op jit(solution)/shard_map/ppermute | solution.py:155
  100.4 11.5 %collective-permute-start.12 = (bf16[240,1024]{1,0:T(8,128)(2,1)S(1)}, bf16[240,1024]{1,0:T(8,128)(2,1)S(1)}, u32[]{:S(2)}, u32[]{:S(2)}) collective-permute-start(bf16[240,1024]{1,0:T(8,128)(2,1)S(1)} %collective-permute-done.10.refs_0_), channel_id=1, source_target_pairs={{0,1},{1,2},{2,3},{3,4},{4,5},{5,6},{6,7},{7,8},{8,9},{9,10},{10,1... | collective-permute-start | bytes 1474568 | tf_op jit(solution)/shard_map/ppermute | solution.py:155
  104.7 10.1 %collective-permute-start.13 = (bf16[240,1024]{1,0:T(8,128)(2,1)S(1)}, bf16[240,1024]{1,0:T(8,128)(2,1)S(1)}, u32[]{:S(2)}, u32[]{:S(2)}) collective-permute-start(bf16[240,1024]{1,0:T(8,128)(2,1)S(1)} %collective-permute-done.11.refs_1_), channel_id=1, source_target_pairs={{0,15},{1,0},{2,1},{3,2},{4,3},{5,4},{6,5},{7,6},{8,7},{9,8},{10,9... | collective-permute-start | bytes 1474568 | tf_op jit(solution)/shard_map/ppermute | solution.py:155
  107.3 22.2 %all-to-all-start.4 = ((bf16[4,8,240,128]{3,2,1,0:T(8,128)(2,1)}), bf16[4,8,240,128]{3,2,1,0:T(8,128)(2,1)}, u32[]{:S(2)}, u32[]{:S(2)}) async-start(bf16[4,8,240,128]{3,2,1,0:T(8,128)(2,1)} %pick_part.6), calls=%async_computation.4 | async-start | bytes 3932160 | tf_op jit(solution)/shard_map/all_to_all | solution.py:159
  114.9 11.6 %collective-permute-start.15 = (bf16[128,1024]{1,0:T(8,128)(2,1)S(1)}, bf16[128,1024]{1,0:T(8,128)(2,1)S(1)}, u32[]{:S(2)}, u32[]{:S(2)}) collective-permute-start(bf16[128,1024]{1,0:T(8,128)(2,1)S(1)} %slice.7), channel_id=1, source_target_pairs={{0,15},{1,0},{2,1},{3,2},{4,3},{5,4},{6,5},{7,6},{8,7},{9,8},{10,9... | collective-permute-start | bytes 786440 | tf_op jit(solution)/shard_map/ppermute | solution.py:155
  118.1 8.4 %collective-permute-start.14 = (bf16[112,1024]{1,0:T(8,128)(2,1)S(1)}, bf16[112,1024]{1,0:T(8,128)(2,1)S(1)}, u32[]{:S(2)}, u32[]{:S(2)}) collective-permute-start(bf16[112,1024]{1,0:T(8,128)(2,1)S(1)} %slice.6), channel_id=1, source_target_pairs={{0,1},{1,2},{2,3},{3,4},{4,5},{5,6},{6,7},{7,8},{8,9},{9,10},{10,1... | collective-permute-start | bytes 688136 | tf_op jit(solution)/shard_map/ppermute | solution.py:155
  129.4 4.0 %copy-start.2 = (s32[1,8,16]{2,1,0:T(8,128)S(1)}, s32[1,8,16]{2,1,0:T(8,128)}, u32[]{:S(2)}) copy-start(s32[1,8,16]{2,1,0:T(8,128)} %param.8) | copy-start | bytes 1540
  129.5 21.4 %all-to-all-start.5 = ((bf16[4,10,240,128]{3,2,1,0:T(8,128)(2,1)}), bf16[4,10,240,128]{3,2,1,0:T(8,128)(2,1)S(1)}, u32[]{:S(2)}, u32[]{:S(2)}) async-start(bf16[4,10,240,128]{3,2,1,0:T(8,128)(2,1)} %pick_part.7), calls=%async_computation.5 | async-start | bytes 4915200 | tf_op jit(solution)/shard_map/all_to_all | solution.py:159
  150.9 1.4 copy-start.1
  162.6 20.9 %collective-permute-start.16 = (bf16[240,1024]{1,0:T(8,128)(2,1)}, bf16[240,1024]{1,0:T(8,128)(2,1)S(1)}, u32[]{:S(2)}, u32[]{:S(2)}) collective-permute-start(bf16[240,1024]{1,0:T(8,128)(2,1)} %mix.1), channel_id=1, source_target_pairs={{0,64},{64,128},{128,192},{192,256},{256,320},{320,384},{384,448},... | collective-permute-start | bytes 1474568 | tf_op jit(solution)/shard_map/ppermute | solution.py:155

commit v7 on v6

--- a/solution.py
+++ b/solution.py
@@ -13,15 +13,15 @@
 CAP = 2
 BLOCK = 128
 PICK_VMEM = 24 * 2**20
-MIX_VMEM = 58 * 2**20
+MIX_VMEM = 50 * 2**20
 PICK_WEIGHT = 12 * 10**9
 AFTER = (2,)
-HAVE = (5, 8, 9, 9)
+HAVE = (6, 9, 9, 9)
 PARTS = (
-    (0, -1, 1),
-    (-2, 2, -3, 3),
-    (-4, 4, -5, 5),
-    (-6, 6, -7, 7, 8),
+    (0, -1, 1, -2, 2),
+    (-3, 3, -4, 4),
+    (-5, 5, -6, 6),
+    (-7, 7, 8),
 )
 
 
@@ -82,44 +82,32 @@
     return pick_call(kernel, (ids, here), flat, len(part) * CAP, rows, "pick_part")
 
 
-def mix(codes, arrays, weights, bias):
+def mix(codes, arrays, weights, bias, first, rows):
     per_device, taps = weights.shape[:2]
-    rows = arrays[0].shape[1]
+    total = sum(array.shape[0] for array in arrays)
 
     def kernel(codes_ref, *refs):
         blocks_refs = refs[: len(arrays)]
-        weight_ref, bias_ref, out_ref, held, sems = refs[len(arrays) :]
+        weight_ref, bias_ref, out_ref, held, sem = refs[len(arrays) :]
         j = pl.program_id(0)
-
-        def fetch(which, into):
-            def choose(code, k, first, last):
-                if last - first == 1:
-                    pltpu.make_async_copy(
-                        blocks_refs[first].at[code & 255],
-                        held.at[into, :, k * BLOCK : (k + 1) * BLOCK],
-                        sems.at[into],
-                    ).start()
-                    return
-                middle = (first + last) // 2
-                low = (code >> 8) < middle
-                pl.when(low)(lambda: choose(code, k, first, middle))
-                pl.when(jnp.logical_not(low))(lambda: choose(code, k, middle, last))
-
-            for k in range(taps):
-                choose(codes_ref[which * taps + k], k, 0, len(blocks_refs))
 
         @pl.when(j == 0)
         def _():
-            fetch(0, 0)
-
-        @pl.when(j + 1 < per_device)
-        def _():
-            fetch(j + 1, (j + 1) % 2)
-
-        now = j % 2
-        pltpu.make_async_copy(held.at[now], held.at[now], sems.at[now]).wait()
+            at = 0
+            for ref in blocks_refs:
+                pltpu.make_async_copy(
+                    ref.at[:, first : first + rows],
+                    held.at[at : at + ref.shape[0]],
+                    sem,
+                ).start()
+                at += ref.shape[0]
+            pltpu.make_async_copy(held, held, sem).wait()
+
+        blocks = [held[codes_ref[j * taps + k]] for k in range(taps)]
         stacked = weight_ref[0].reshape(taps * BLOCK, BLOCK)
-        mixed = jnp.dot(held[now], stacked, preferred_element_type=jnp.float32)
+        mixed = jnp.dot(
+            jnp.concatenate(blocks, axis=1), stacked, preferred_element_type=jnp.float32
+        )
         result = mixed + bias_ref[0]
         out_ref[...] = jnp.clip(result, 0.0, CLAMP_TOP).astype(jnp.bfloat16)
 
@@ -128,22 +116,22 @@
         grid_spec=pltpu.PrefetchScalarGridSpec(
             num_scalar_prefetch=1,
             grid=(per_device,),
-            in_specs=[pl.BlockSpec(memory_space=pltpu.HBM)] * len(arrays)
+            in_specs=[pl.BlockSpec(memory_space=pl.ANY)] * len(arrays)
             + [
                 pl.BlockSpec((1, taps, BLOCK, BLOCK), lambda j, s: (j, 0, 0, 0)),
                 pl.BlockSpec((1, 1, BLOCK), lambda j, s: (j, 0, 0)),
             ],
             out_specs=pl.BlockSpec((rows, BLOCK), lambda j, s: (0, j)),
             scratch_shapes=[
-                pltpu.VMEM((2, rows, taps * BLOCK), jnp.bfloat16),
-                pltpu.SemaphoreType.DMA((2,)),
+                pltpu.VMEM((total, rows, BLOCK), jnp.bfloat16),
+                pltpu.SemaphoreType.DMA,
             ],
         ),
         out_shape=jax.ShapeDtypeStruct((rows, per_device * BLOCK), jnp.bfloat16),
         compiler_params=pltpu.CompilerParams(vmem_limit_bytes=MIX_VMEM),
         cost_estimate=pl.CostEstimate(
             flops=2 * rows * per_device * taps * BLOCK * BLOCK,
-            bytes_accessed=per_device * taps * (rows + BLOCK) * BLOCK * 2,
+            bytes_accessed=(total * rows + per_device * taps * BLOCK) * BLOCK * 2,
             transcendentals=0,
         ),
         name="mix",
@@ -164,10 +152,12 @@
     line, z, c = slots >> 5, (slots >> 1) & (STEPS - 1), slots & 1
     offset = (z - here) & (STEPS - 1)
     codes = jnp.zeros_like(slots)
-    for p, part in enumerate(PARTS):
+    base = 0
+    for part in PARTS:
         for i, o in enumerate(part):
-            code = p * 256 + line * (len(part) * CAP) + i * CAP + c
+            code = base + line * (len(part) * CAP) + i * CAP + c
             codes = jnp.where(offset == o % STEPS, code, codes)
+        base += LINES * len(part) * CAP
     return codes
 
 
@@ -222,10 +212,17 @@
         if all(o in held for o in PARTS[len(ready)]):
             ready.append(step)
     pick_next()
+    picked[-1], arrived[-1] = lax.optimization_barrier((picked[-1], arrived[-1]))
     send_next()
 
-    out = mix(part_codes(slots, here), arrived, weights, bias)
-    return shifted(out, "segment", 1)[None]
+    codes = part_codes(slots, here)
+    rows = samples.shape[0]
+    upper = (rows + 31) // 32 * 16
+    outs = [
+        shifted(mix(codes, arrived, weights, bias, first, count), "segment", 1)
+        for first, count in ((0, upper), (upper, rows - upper))
+    ]
+    return jnp.concatenate(outs, axis=0)[None]
 
 
 def solution(mesh):

time: 185 us -> 193 us (1.043)
  Pallas kernels: 20.7 us -> 26.2 us
  local copies, waits for them, and re-layouts: 7.92 us -> 11.8 us
  starting transfers between devices: 97.9 us -> 94.3 us
    all_to_all x1, waiting for transfers between devices: 3.6 us -> 11.4 us  [body(): ids = lax.all_to_all(far, 'far', 0, 0, tiled=True).reshape(-1)]
    ppermute x17 -> x18, waiting for transfers between devices: 29.4 us -> 22.5 us  [shifted(): lax.ppermute(value, axis, [(i, (i + by) % count) for i in range(count)])]
    pallas_call x1 -> x2, Pallas kernels: 10.2 us -> 15.9 us  [mix(): pl.pallas_call(kernel, grid_spec=pltpu.PrefetchScalarGridSpec(num_scalar_...]
    unnamed x7 -> x16, local copies, waits for them, and re-layouts: 3.25 us -> 5.78 us
    ppermute x17 -> x18, starting transfers between devices: 74.9 us -> 72.4 us  [shifted(): lax.ppermute(value, axis, [(i, (i + by) % count) for i in range(count)])]
  transfers between devices with their start and end apart: 22 -> 23, of which waited for: 17 -> 15; matrix products, arithmetic and copies ran while one was open for 2% -> 4% of each run, Pallas kernels for 6% -> 9%
where the time goes in v7:
time: 193 us; the launch traced here: 192 us
  starting transfers between devices  94.3 us (49%)
  waiting for transfers between devices  48.1 us (25%)
  Pallas kernels  26.2 us (14%)
  local copies, waits for them, and re-layouts  11.8 us (6%)
  blocking collectives  9.43 us (5%)
    ppermute x18, starting transfers between devices, shifted(): lax.ppermute(value, axis, [(i, (i + by) % count) for i in range(count)])  72.4 us
    ppermute x18, waiting for transfers between devices, shifted(): lax.ppermute(value, axis, [(i, (i + by) % count) for i in range(count)])  22.5 us
    all_to_all x4, starting transfers between devices, over_lines(): incoming = lax.all_to_all(outgoing, 'y', 0, 0, tiled=True)  16.1 us
    pallas_call x2, Pallas kernels, mix(): pl.pallas_call(kernel, grid_spec=pltpu.PrefetchScalarGridSpec(num_scalar_...  15.9 us
    all_to_all x4, waiting for transfers between devices, over_lines(): incoming = lax.all_to_all(outgoing, 'y', 0, 0, tiled=True)  14.1 us
    all_to_all x1, waiting for transfers between devices, body(): ids = lax.all_to_all(far, 'far', 0, 0, tiled=True).reshape(-1)  11.4 us
    pallas_call x4, Pallas kernels, pick_call(): pl.pallas_call(kernel, grid_spec=pltpu.PrefetchScalarGridSpec(num_scalar_...  10.3 us
    all_to_all x1, blocking collectives, body(): near = lax.all_to_all(lists, 'near', 0, 0, tiled=True)  9.43 us
  transfers between devices with their start and end apart: 23, of which 15 were waited for; matrix products, arithmetic and copies ran while one was open for 4% of the time, Pallas kernels for 9%

profile of v7, /device:TPU:1, one launch (start us, length us, event | category | flops | bytes accessed | tf_op | source)
XLA Modules:
  0.0 191.8 jit_solution(1788712171636193518)
XLA Ops:
  0.0 11.9 %collective-permute-start.1 = (bf16[240,1024]{1,0:T(8,128)(2,1)}, bf16[240,1024]{1,0:T(8,128)(2,1)S(1)}, u32[]{:S(2)}, u32[]{:S(2)}) collective-permute-start(bf16[240,1024]{1,0:T(8,128)(2,1)} %bitcast.20), channel_id=1, source_target_pairs={{0,15},{1,0},{2,1},{3,2},{4,3},{5,4},{6,5},{7,6},{8,7},{9,8},{10,9... | collective-permute-start | bytes 1474568 | tf_op jit(solution)/shard_map/ppermute | solution.py:143
  12.0 1.9 %collective-permute-start = (bf16[240,1024]{1,0:T(8,128)(2,1)}, bf16[240,1024]{1,0:T(8,128)(2,1)S(1)}, u32[]{:S(2)}, u32[]{:S(2)}) collective-permute-start(bf16[240,1024]{1,0:T(8,128)(2,1)} %bitcast.21), channel_id=1, source_target_pairs={{0,1},{1,2},{2,3},{3,4},{4,5},{5,6},{6,7},{7,8},{8,9},{9,10},{10,1... | collective-permute-start | bytes 1474568 | tf_op jit(solution)/shard_map/ppermute | solution.py:143
  14.8 9.4 %all_to_all.30 = s32[4,4,4,2]{1,2,3,0:T(4,128)S(1)} all-to-all(s32[4,4,4,2]{1,2,3,0:T(4,128)S(1)} %copy.8), channel_id=1, replica_groups=mesh['segment'=8,'y'=4,'far'=4,'near'=4] {'near'}, dimensions={0} | all-to-all | bytes 1024 | tf_op jit(solution)/shard_map/all_to_all | solution.py:182
  24.2 2.8 %collective-permute-done.refs_1_ = bf16[240,1024]{1,0:T(8,128)(2,1)S(1)} collective-permute-done((bf16[240,1024]{1,0:T(8,128)(2,1)}, bf16[240,1024]{1,0:T(8,128)(2,1)S(1)}, u32[]{:S(2)}, u32[]{:S(2)}) %collective-permute-start) | collective-permute-done | bytes 491552 | tf_op jit(solution)/shard_map/ppermute | solution.py:143
  29.0 4.6 %collective-permute-start.3 = (bf16[240,1024]{1,0:T(8,128)(2,1)S(1)}, bf16[240,1024]{1,0:T(8,128)(2,1)S(1)}, u32[]{:S(2)}, u32[]{:S(2)}) collective-permute-start(bf16[240,1024]{1,0:T(8,128)(2,1)S(1)} %collective-permute-done.1.refs_2_), channel_id=1, source_target_pairs={{0,15},{1,0},{2,1},{3,2},{4,3},{5,4},{6,5},{7,6},{8,7},{9,8},{10,9... | collective-permute-start | bytes 1474568 | tf_op jit(solution)/shard_map/ppermute | solution.py:143
  34.3 5.8 %all-to-all-start.1 = ((s32[4,4,4,2]{1,2,3,0:T(4,128)}), s32[4,4,4,2]{1,2,3,0:T(4,128)S(1)}, u32[]{:S(2)}, u32[]{:S(2)}) async-start(s32[4,4,4,2]{1,2,3,0:T(4,128)} %copy.9), calls=%async_computation.1 | async-start | bytes 32768 | tf_op jit(solution)/shard_map/all_to_all | solution.py:190
  40.1 11.4 %all-to-all-done.1 = s32[4,4,4,2]{1,2,3,0:T(4,128)S(1)} async-done(((s32[4,4,4,2]{1,2,3,0:T(4,128)}), s32[4,4,4,2]{1,2,3,0:T(4,128)S(1)}, u32[]{:S(2)}, u32[]{:S(2)}) %all-to-all-start.1) | async-done | bytes 544 | tf_op jit(solution)/shard_map/all_to_all | solution.py:190
  51.9 1.9 %collective-permute-start.4 = (bf16[240,1024]{1,0:T(8,128)(2,1)S(1)}, bf16[240,1024]{1,0:T(8,128)(2,1)S(1)}, u32[]{:S(2)}, u32[]{:S(2)}) collective-permute-start(bf16[240,1024]{1,0:T(8,128)(2,1)S(1)} %collective-permute-done.2.refs_3_), channel_id=1, source_target_pairs={{0,1},{1,2},{2,3},{3,4},{4,5},{5,6},{6,7},{7,8},{8,9},{9,10},{10,1... | collective-permute-start | bytes 1474568 | tf_op jit(solution)/shard_map/ppermute | solution.py:143
  53.8 4.6 %collective-permute-start.5 = (bf16[240,1024]{1,0:T(8,128)(2,1)S(1)}, bf16[240,1024]{1,0:T(8,128)(2,1)}, u32[]{:S(2)}, u32[]{:S(2)}) collective-permute-start(bf16[240,1024]{1,0:T(8,128)(2,1)S(1)} %collective-permute-done.3.refs_4_), channel_id=1, source_target_pairs={{0,15},{1,0},{2,1},{3,2},{4,3},{5,4},{6,5},{7,6},{8,7},{9,8},{10,9... | collective-permute-start | bytes 1474568 | tf_op jit(solution)/shard_map/ppermute | solution.py:143
  59.4 2.9 %pick_part.4 = bf16[4,10,240,128]{3,2,1,0:T(8,128)(2,1)} custom-call(s32[128]{0:T(128)S(1)} %reshape.66.ids_ref, s32[1]{0:T(128)} %bitcast.3.here_ref, bf16[240,1024]{1,0:T(8,128)(2,1)S(1)} %bitcast.22, bf16[240,1024]{1,0:T(8,128)(2,1)S(1)} %collective-permute-done.refs_1_, bf16[240,1024]{1,0:T(8,128)(2,1)S(1)} %collective-permute-done.1.refs_2_, ...), custom_call_target="tpu_custom_call" | custom-call | flops 12000000000 | bytes 4915200 | tf_op jit(solution)/shard_map/pick_part/pallas_call | solution.py:48
  64.7 4.5 %all-to-all-start.2 = ((bf16[4,10,240,128]{3,2,1,0:T(8,128)(2,1)}), bf16[4,10,240,128]{3,2,1,0:T(8,128)(2,1)}, u32[]{:S(2)}, u32[]{:S(2)}) async-start(bf16[4,10,240,128]{3,2,1,0:T(8,128)(2,1)} %pick_part.4), calls=%async_computation.2 | async-start | bytes 4915200 | tf_op jit(solution)/shard_map/all_to_all | solution.py:147
  69.2 2.4 %collective-permute-start.6 = (bf16[240,1024]{1,0:T(8,128)(2,1)S(1)}, bf16[240,1024]{1,0:T(8,128)(2,1)S(1)}, u32[]{:S(2)}, u32[]{:S(2)}) collective-permute-start(bf16[240,1024]{1,0:T(8,128)(2,1)S(1)} %collective-permute-done.4.refs_0_), channel_id=1, source_target_pairs={{0,1},{1,2},{2,3},{3,4},{4,5},{5,6},{6,7},{7,8},{8,9},{9,10},{10,1... | collective-permute-start | bytes 1474568 | tf_op jit(solution)/shard_map/ppermute | solution.py:143
  71.6 4.9 %collective-permute-start.8 = (bf16[240,1024]{1,0:T(8,128)(2,1)}, bf16[240,1024]{1,0:T(8,128)(2,1)S(1)}, u32[]{:S(2)}, u32[]{:S(2)}) collective-permute-start(bf16[240,1024]{1,0:T(8,128)(2,1)} %collective-permute-done.5.refs_1_), channel_id=1, source_target_pairs={{0,15},{1,0},{2,1},{3,2},{4,3},{5,4},{6,5},{7,6},{8,7},{9,8},{10,9... | collective-permute-start | bytes 1474568 | tf_op jit(solution)/shard_map/ppermute | solution.py:143
  76.5 4.7 %collective-permute-done.6.refs_2_ = bf16[240,1024]{1,0:T(8,128)(2,1)S(1)} collective-permute-done((bf16[240,1024]{1,0:T(8,128)(2,1)S(1)}, bf16[240,1024]{1,0:T(8,128)(2,1)S(1)}, u32[]{:S(2)}, u32[]{:S(2)}) %collective-permute-start.6) | collective-permute-done | bytes 491552 | tf_op jit(solution)/shard_map/ppermute | solution.py:143
  83.2 4.8 %collective-permute-start.9 = (bf16[240,1024]{1,0:T(8,128)(2,1)S(1)}, bf16[240,1024]{1,0:T(8,128)(2,1)S(1)}, u32[]{:S(2)}, u32[]{:S(2)}) collective-permute-start(bf16[240,1024]{1,0:T(8,128)(2,1)S(1)} %collective-permute-done.8.refs_3_), channel_id=1, source_target_pairs={{0,15},{1,0},{2,1},{3,2},{4,3},{5,4},{6,5},{7,6},{8,7},{9,8},{10,9... | collective-permute-start | bytes 1474568 | tf_op jit(solution)/shard_map/ppermute | solution.py:143
  87.9 2.7 %pick_part.5 = bf16[4,8,240,128]{3,2,1,0:T(8,128)(2,1)S(1)} custom-call(s32[128]{0:T(128)S(1)} %reshape.66.ids_ref, s32[1]{0:T(128)} %bitcast.3.here_ref, bf16[240,1024]{1,0:T(8,128)(2,1)S(1)} %collective-permute-done.4.refs_0_, bf16[240,1024]{1,0:T(8,128)(2,1)} %collective-permute-done.5.refs_1_, bf16[240,1024]{1,0:T(8,128)(2,1)S(1)} %collective-permute-done.6.refs_2_, ...), custom_call_target="tpu_custom_call" | custom-call | flops 12000000000 | bytes 3932160 | tf_op jit(solution)/shard_map/pick_part/pallas_call | solution.py:48
  94.3 2.8 %collective-permute-start.10 = (bf16[240,1024]{1,0:T(8,128)(2,1)S(1)}, bf16[240,1024]{1,0:T(8,128)(2,1)}, u32[]{:S(2)}, u32[]{:S(2)}) collective-permute-start(bf16[240,1024]{1,0:T(8,128)(2,1)S(1)} %collective-permute-done.7.refs_0_), channel_id=1, source_target_pairs={{0,1},{1,2},{2,3},{3,4},{4,5},{5,6},{6,7},{7,8},{8,9},{9,10},{10,1... | collective-permute-start | bytes 1474568 | tf_op jit(solution)/shard_map/ppermute | solution.py:143
  97.1 4.6 %collective-permute-start.11 = (bf16[240,1024]{1,0:T(8,128)(2,1)S(1)}, bf16[240,1024]{1,0:T(8,128)(2,1)}, u32[]{:S(2)}, u32[]{:S(2)}) collective-permute-start(bf16[240,1024]{1,0:T(8,128)(2,1)S(1)} %collective-permute-done.9.refs_1_), channel_id=1, source_target_pairs={{0,15},{1,0},{2,1},{3,2},{4,3},{5,4},{6,5},{7,6},{8,7},{9,8},{10,9... | collective-permute-start | bytes 1474568 | tf_op jit(solution)/shard_map/ppermute | solution.py:143
  101.7 3.6 %all-to-all-start.3 = ((bf16[4,8,240,128]{3,2,1,0:T(8,128)(2,1)}), bf16[4,8,240,128]{3,2,1,0:T(8,128)(2,1)S(1)}, u32[]{:S(2)}, u32[]{:S(2)}) async-start(bf16[4,8,240,128]{3,2,1,0:T(8,128)(2,1)} %copy-done), calls=%async_computation.3 | async-start | bytes 3932160 | tf_op jit(solution)/shard_map/all_to_all | solution.py:147
  108.0 4.6 %collective-permute-start.13 = (bf16[240,1024]{1,0:T(8,128)(2,1)}, bf16[240,1024]{1,0:T(8,128)(2,1)S(1)}, u32[]{:S(2)}, u32[]{:S(2)}) collective-permute-start(bf16[240,1024]{1,0:T(8,128)(2,1)} %collective-permute-done.11.refs_3_), channel_id=1, source_target_pairs={{0,15},{1,0},{2,1},{3,2},{4,3},{5,4},{6,5},{7,6},{8,7},{9,8},{10,9... | collective-permute-start | bytes 1474568 | tf_op jit(solution)/shard_map/ppermute | solution.py:143
  113.6 2.9 %pick_part.6 = bf16[4,8,240,128]{3,2,1,0:T(8,128)(2,1)S(1)} custom-call(s32[128]{0:T(128)S(1)} %reshape.66.ids_ref, s32[1]{0:T(128)} %bitcast.3.here_ref, bf16[240,1024]{1,0:T(8,128)(2,1)S(1)} %collective-permute-done.7.refs_0_, bf16[240,1024]{1,0:T(8,128)(2,1)S(1)} %copy-done.6, bf16[240,1024]{1,0:T(8,128)(2,1)} %collective-permute-done.10.refs_2_, ...), custom_call_target="tpu_custom_call" | custom-call | flops 12000000000 | bytes 3932160 | tf_op jit(solution)/shard_map/pick_part/pallas_call | solution.py:48
  119.3 2.8 %all-to-all-done.3 = bf16[4,8,240,128]{3,2,1,0:T(8,128)(2,1)S(1)} async-done(((bf16[4,8,240,128]{3,2,1,0:T(8,128)(2,1)}), bf16[4,8,240,128]{3,2,1,0:T(8,128)(2,1)S(1)}, u32[]{:S(2)}, u32[]{:S(2)}) %all-to-all-start.3) | async-done | bytes 1966112 | tf_op jit(solution)/shard_map/all_to_all | solution.py:147
  122.2 4.4 %all-to-all-start.4 = ((bf16[4,8,240,128]{3,2,1,0:T(8,128)(2,1)}), bf16[4,8,240,128]{3,2,1,0:T(8,128)(2,1)}, u32[]{:S(2)}, u32[]{:S(2)}) async-start(bf16[4,8,240,128]{3,2,1,0:T(8,128)(2,1)} %copy-done.1), calls=%async_computation.4 | async-start | bytes 3932160 | tf_op jit(solution)/shard_map/all_to_all | solution.py:147
  126.6 3.1 %collective-permute-start.15 = (bf16[128,1024]{1,0:T(8,128)(2,1)S(1)}, bf16[128,1024]{1,0:T(8,128)(2,1)S(1)}, u32[]{:S(2)}, u32[]{:S(2)}) collective-permute-start(bf16[128,1024]{1,0:T(8,128)(2,1)S(1)} %slice.7), channel_id=1, source_target_pairs={{0,15},{1,0},{2,1},{3,2},{4,3},{5,4},{6,5},{7,6},{8,7},{9,8},{10,9... | collective-permute-start | bytes 786440 | tf_op jit(solution)/shard_map/ppermute | solution.py:143
  129.7 2.2 %collective-permute-start.14 = (bf16[112,1024]{1,0:T(8,128)(2,1)S(1)}, bf16[112,1024]{1,0:T(8,128)(2,1)S(1)}, u32[]{:S(2)}, u32[]{:S(2)}) collective-permute-start(bf16[112,1024]{1,0:T(8,128)(2,1)S(1)} %slice.6), channel_id=1, source_target_pairs={{0,1},{1,2},{2,3},{3,4},{4,5},{5,6},{6,7},{7,8},{8,9},{9,10},{10,1... | collective-permute-start | bytes 688136 | tf_op jit(solution)/shard_map/ppermute | solution.py:143
  131.9 5.8 %collective-permute-done.14.refs_2_ = bf16[112,1024]{1,0:T(8,128)(2,1)S(1)} collective-permute-done((bf16[112,1024]{1,0:T(8,128)(2,1)S(1)}, bf16[112,1024]{1,0:T(8,128)(2,1)S(1)}, u32[]{:S(2)}, u32[]{:S(2)}) %collective-permute-start.14) | collective-permute-done | bytes 229408 | tf_op jit(solution)/shard_map/ppermute | solution.py:143
  142.3 3.6 %all-to-all-start.5 = ((bf16[4,6,240,128]{3,2,1,0:T(8,128)(2,1)}), bf16[4,6,240,128]{3,2,1,0:T(8,128)(2,1)S(1)}, u32[]{:S(2)}, u32[]{:S(2)}) async-start(bf16[4,6,240,128]{3,2,1,0:T(8,128)(2,1)} %copy-done.2), calls=%async_computation.5 | async-start | bytes 2949120 | tf_op jit(solution)/shard_map/all_to_all | solution.py:147
  150.6 9.0 %all-to-all-done.5 = bf16[4,6,240,128]{3,2,1,0:T(8,128)(2,1)S(1)} async-done(((bf16[4,6,240,128]{3,2,1,0:T(8,128)(2,1)}), bf16[4,6,240,128]{3,2,1,0:T(8,128)(2,1)S(1)}, u32[]{:S(2)}, u32[]{:S(2)}) %all-to-all-start.5) | async-done | bytes 1474592 | tf_op jit(solution)/shard_map/all_to_all | solution.py:147
  159.6 8.0 %mix.2 = bf16[128,1024]{1,0:T(8,128)(2,1)S(1)} custom-call(s32[128]{0:T(128)S(1)} %select_select_fusion.codes_ref, bf16[40,240,128]{2,1,0:T(8,128)(2,1)} %bitcast.4.refs_0_, bf16[32,240,128]{2,1,0:T(8,128)(2,1)S(1)} %bitcast.14, bf16[32,240,128]{2,1,0:T(8,128)(2,1)} %bitcast.6.refs_2_, bf16[24,240,128]{2,1,0:T(8,128)(2,1)S(1)} %bitcast.16, ...), custom_call_target="tpu_custom_call" | custom-call | flops 536870912 | bytes 8388608 | tf_op jit(solution)/shard_map/mix/pallas_call | solution.py:114
  167.6 12.4 %collective-permute-start.16 = (bf16[128,1024]{1,0:T(8,128)(2,1)S(1)}, bf16[128,1024]{1,0:T(8,128)(2,1)S(1)}, u32[]{:S(2)}, u32[]{:S(2)}) collective-permute-start(bf16[128,1024]{1,0:T(8,128)(2,1)S(1)} %mix.2), channel_id=1, source_target_pairs={{0,64},{64,128},{128,192},{192,256},{256,320},{320,384},{384,448},... | collective-permute-start | bytes 786440 | tf_op jit(solution)/shard_map/ppermute | solution.py:143
  180.1 7.9 %mix.3 = bf16[112,1024]{1,0:T(8,128)(2,1)S(1)} custom-call(s32[128]{0:T(128)S(1)} %select_select_fusion.codes_ref, bf16[40,240,128]{2,1,0:T(8,128)(2,1)} %bitcast.4.refs_0_, bf16[32,240,128]{2,1,0:T(8,128)(2,1)S(1)} %bitcast.15, bf16[32,240,128]{2,1,0:T(8,128)(2,1)} %bitcast.6.refs_2_, bf16[24,240,128]{2,1,0:T(8,128)(2,1)S(1)} %bitcast.17, ...), custom_call_target="tpu_custom_call" | custom-call | flops 469762048 | bytes 7864320 | tf_op jit(solution)/shard_map/mix/pallas_call | solution.py:114
  188.0 3.0 %collective-permute-done.17 = bf16[112,1024]{1,0:T(8,128)(2,1)S(1)} collective-permute-done((bf16[112,1024]{1,0:T(8,128)(2,1)S(1)}, bf16[112,1024]{1,0:T(8,128)(2,1)S(1)}, u32[]{:S(2)}, u32[]{:S(2)}) %collective-permute-start.17) | collective-permute-done | bytes 229408 | tf_op jit(solution)/shard_map/ppermute | solution.py:143
  (77 shorter events, 29.5 us)
Async XLA Ops:
  0.0 24.2 %collective-permute-start.1 = (bf16[240,1024]{1,0:T(8,128)(2,1)}, bf16[240,1024]{1,0:T(8,128)(2,1)S(1)}, u32[]{:S(2)}, u32[]{:S(2)}) collective-permute-start(bf16[240,1024]{1,0:T(8,128)(2,1)} %bitcast.20), channel_id=1, source_target_pairs={{0,15},{1,0},{2,1},{3,2},{4,3},{5,4},{6,5},{7,6},{8,7},{9,8},{10,9... | collective-permute-start | bytes 1474568 | tf_op jit(solution)/shard_map/ppermute | solution.py:143
  12.0 15.1 %collective-permute-start = (bf16[240,1024]{1,0:T(8,128)(2,1)}, bf16[240,1024]{1,0:T(8,128)(2,1)S(1)}, u32[]{:S(2)}, u32[]{:S(2)}) collective-permute-start(bf16[240,1024]{1,0:T(8,128)(2,1)} %bitcast.21), channel_id=1, source_target_pairs={{0,1},{1,2},{2,3},{3,4},{4,5},{5,6},{6,7},{7,8},{8,9},{9,10},{10,1... | collective-permute-start | bytes 1474568 | tf_op jit(solution)/shard_map/ppermute | solution.py:143
  27.0 24.8 %collective-permute-start.2 = (bf16[240,1024]{1,0:T(8,128)(2,1)S(1)}, bf16[240,1024]{1,0:T(8,128)(2,1)S(1)}, u32[]{:S(2)}, u32[]{:S(2)}) collective-permute-start(bf16[240,1024]{1,0:T(8,128)(2,1)S(1)} %collective-permute-done.refs_1_), channel_id=1, source_target_pairs={{0,1},{1,2},{2,3},{3,4},{4,5},{5,6},{6,7},{7,8},{8,9},{9,10},{10,1... | collective-permute-start | bytes 1474568 | tf_op jit(solution)/shard_map/ppermute | solution.py:143
  29.0 24.9 %collective-permute-start.3 = (bf16[240,1024]{1,0:T(8,128)(2,1)S(1)}, bf16[240,1024]{1,0:T(8,128)(2,1)S(1)}, u32[]{:S(2)}, u32[]{:S(2)}) collective-permute-start(bf16[240,1024]{1,0:T(8,128)(2,1)S(1)} %collective-permute-done.1.refs_2_), channel_id=1, source_target_pairs={{0,15},{1,0},{2,1},{3,2},{4,3},{5,4},{6,5},{7,6},{8,7},{9,8},{10,9... | collective-permute-start | bytes 1474568 | tf_op jit(solution)/shard_map/ppermute | solution.py:143
  34.3 17.2 %all-to-all-start.1 = ((s32[4,4,4,2]{1,2,3,0:T(4,128)}), s32[4,4,4,2]{1,2,3,0:T(4,128)S(1)}, u32[]{:S(2)}, u32[]{:S(2)}) async-start(s32[4,4,4,2]{1,2,3,0:T(4,128)} %copy.9), calls=%async_computation.1 | async-start | bytes 32768 | tf_op jit(solution)/shard_map/all_to_all | solution.py:190
  51.9 11.9 %collective-permute-start.4 = (bf16[240,1024]{1,0:T(8,128)(2,1)S(1)}, bf16[240,1024]{1,0:T(8,128)(2,1)S(1)}, u32[]{:S(2)}, u32[]{:S(2)}) collective-permute-start(bf16[240,1024]{1,0:T(8,128)(2,1)S(1)} %collective-permute-done.2.refs_3_), channel_id=1, source_target_pairs={{0,1},{1,2},{2,3},{3,4},{4,5},{5,6},{6,7},{7,8},{8,9},{9,10},{10,1... | collective-permute-start | bytes 1474568 | tf_op jit(solution)/shard_map/ppermute | solution.py:143
  53.8 10.8 %collective-permute-start.5 = (bf16[240,1024]{1,0:T(8,128)(2,1)S(1)}, bf16[240,1024]{1,0:T(8,128)(2,1)}, u32[]{:S(2)}, u32[]{:S(2)}) collective-permute-start(bf16[240,1024]{1,0:T(8,128)(2,1)S(1)} %collective-permute-done.3.refs_4_), channel_id=1, source_target_pairs={{0,15},{1,0},{2,1},{3,2},{4,3},{5,4},{6,5},{7,6},{8,7},{9,8},{10,9... | collective-permute-start | bytes 1474568 | tf_op jit(solution)/shard_map/ppermute | solution.py:143
  58.4 1.0 copy-start.4
  64.7 29.7 %all-to-all-start.2 = ((bf16[4,10,240,128]{3,2,1,0:T(8,128)(2,1)}), bf16[4,10,240,128]{3,2,1,0:T(8,128)(2,1)}, u32[]{:S(2)}, u32[]{:S(2)}) async-start(bf16[4,10,240,128]{3,2,1,0:T(8,128)(2,1)} %pick_part.4), calls=%async_computation.2 | async-start | bytes 4915200 | tf_op jit(solution)/shard_map/all_to_all | solution.py:147
  69.2 12.0 %collective-permute-start.6 = (bf16[240,1024]{1,0:T(8,128)(2,1)S(1)}, bf16[240,1024]{1,0:T(8,128)(2,1)S(1)}, u32[]{:S(2)}, u32[]{:S(2)}) collective-permute-start(bf16[240,1024]{1,0:T(8,128)(2,1)S(1)} %collective-permute-done.4.refs_0_), channel_id=1, source_target_pairs={{0,1},{1,2},{2,3},{3,4},{4,5},{5,6},{6,7},{7,8},{8,9},{9,10},{10,1... | collective-permute-start | bytes 1474568 | tf_op jit(solution)/shard_map/ppermute | solution.py:143
  71.6 11.5 %collective-permute-start.8 = (bf16[240,1024]{1,0:T(8,128)(2,1)}, bf16[240,1024]{1,0:T(8,128)(2,1)S(1)}, u32[]{:S(2)}, u32[]{:S(2)}) collective-permute-start(bf16[240,1024]{1,0:T(8,128)(2,1)} %collective-permute-done.5.refs_1_), channel_id=1, source_target_pairs={{0,15},{1,0},{2,1},{3,2},{4,3},{5,4},{6,5},{7,6},{8,7},{9,8},{10,9... | collective-permute-start | bytes 1474568 | tf_op jit(solution)/shard_map/ppermute | solution.py:143
  81.2 10.8 %collective-permute-start.7 = (bf16[240,1024]{1,0:T(8,128)(2,1)S(1)}, bf16[240,1024]{1,0:T(8,128)(2,1)S(1)}, u32[]{:S(2)}, u32[]{:S(2)}) collective-permute-start(bf16[240,1024]{1,0:T(8,128)(2,1)S(1)} %collective-permute-done.6.refs_2_), channel_id=1, source_target_pairs={{0,1},{1,2},{2,3},{3,4},{4,5},{5,6},{6,7},{7,8},{8,9},{9,10},{10,1... | collective-permute-start | bytes 1474568 | tf_op jit(solution)/shard_map/ppermute | solution.py:143
  83.2 10.5 %collective-permute-start.9 = (bf16[240,1024]{1,0:T(8,128)(2,1)S(1)}, bf16[240,1024]{1,0:T(8,128)(2,1)S(1)}, u32[]{:S(2)}, u32[]{:S(2)}) collective-permute-start(bf16[240,1024]{1,0:T(8,128)(2,1)S(1)} %collective-permute-done.8.refs_3_), channel_id=1, source_target_pairs={{0,15},{1,0},{2,1},{3,2},{4,3},{5,4},{6,5},{7,6},{8,7},{9,8},{10,9... | collective-permute-start | bytes 1474568 | tf_op jit(solution)/shard_map/ppermute | solution.py:143
  90.7 1.3 copy-start
  93.7 8.0 %copy-start.5 = (bf16[240,1024]{1,0:T(8,128)(2,1)}, bf16[240,1024]{1,0:T(8,128)(2,1)S(1)}, u32[]{:S(2)}) copy-start(bf16[240,1024]{1,0:T(8,128)(2,1)S(1)} %collective-permute-done.9.refs_1_) | copy-start | bytes 1474564
  94.3 11.7 %collective-permute-start.10 = (bf16[240,1024]{1,0:T(8,128)(2,1)S(1)}, bf16[240,1024]{1,0:T(8,128)(2,1)}, u32[]{:S(2)}, u32[]{:S(2)}) collective-permute-start(bf16[240,1024]{1,0:T(8,128)(2,1)S(1)} %collective-permute-done.7.refs_0_), channel_id=1, source_target_pairs={{0,1},{1,2},{2,3},{3,4},{4,5},{5,6},{6,7},{7,8},{8,9},{9,10},{10,1... | collective-permute-start | bytes 1474568 | tf_op jit(solution)/shard_map/ppermute | solution.py:143
  97.1 10.9 %collective-permute-start.11 = (bf16[240,1024]{1,0:T(8,128)(2,1)S(1)}, bf16[240,1024]{1,0:T(8,128)(2,1)}, u32[]{:S(2)}, u32[]{:S(2)}) collective-permute-start(bf16[240,1024]{1,0:T(8,128)(2,1)S(1)} %collective-permute-done.9.refs_1_), channel_id=1, source_target_pairs={{0,15},{1,0},{2,1},{3,2},{4,3},{5,4},{6,5},{7,6},{8,7},{9,8},{10,9... | collective-permute-start | bytes 1474568 | tf_op jit(solution)/shard_map/ppermute | solution.py:143
  101.7 20.5 %all-to-all-start.3 = ((bf16[4,8,240,128]{3,2,1,0:T(8,128)(2,1)}), bf16[4,8,240,128]{3,2,1,0:T(8,128)(2,1)S(1)}, u32[]{:S(2)}, u32[]{:S(2)}) async-start(bf16[4,8,240,128]{3,2,1,0:T(8,128)(2,1)} %copy-done), calls=%async_computation.3 | async-start | bytes 3932160 | tf_op jit(solution)/shard_map/all_to_all | solution.py:147
  106.1 11.7 %collective-permute-start.12 = (bf16[240,1024]{1,0:T(8,128)(2,1)}, bf16[240,1024]{1,0:T(8,128)(2,1)S(1)}, u32[]{:S(2)}, u32[]{:S(2)}) collective-permute-start(bf16[240,1024]{1,0:T(8,128)(2,1)} %collective-permute-done.10.refs_2_), channel_id=1, source_target_pairs={{0,1},{1,2},{2,3},{3,4},{4,5},{5,6},{6,7},{7,8},{8,9},{9,10},{10,1... | collective-permute-start | bytes 1474568 | tf_op jit(solution)/shard_map/ppermute | solution.py:143
  108.0 11.3 %collective-permute-start.13 = (bf16[240,1024]{1,0:T(8,128)(2,1)}, bf16[240,1024]{1,0:T(8,128)(2,1)S(1)}, u32[]{:S(2)}, u32[]{:S(2)}) collective-permute-start(bf16[240,1024]{1,0:T(8,128)(2,1)} %collective-permute-done.11.refs_3_), channel_id=1, source_target_pairs={{0,15},{1,0},{2,1},{3,2},{4,3},{5,4},{6,5},{7,6},{8,7},{9,8},{10,9... | collective-permute-start | bytes 1474568 | tf_op jit(solution)/shard_map/ppermute | solution.py:143
  112.6 1.0 copy-start.6
  116.5 1.3 copy-start.1
  122.2 20.2 %all-to-all-start.4 = ((bf16[4,8,240,128]{3,2,1,0:T(8,128)(2,1)}), bf16[4,8,240,128]{3,2,1,0:T(8,128)(2,1)}, u32[]{:S(2)}, u32[]{:S(2)}) async-start(bf16[4,8,240,128]{3,2,1,0:T(8,128)(2,1)} %copy-done.1), calls=%async_computation.4 | async-start | bytes 3932160 | tf_op jit(solution)/shard_map/all_to_all | solution.py:147
  126.6 11.1 %collective-permute-start.15 = (bf16[128,1024]{1,0:T(8,128)(2,1)S(1)}, bf16[128,1024]{1,0:T(8,128)(2,1)S(1)}, u32[]{:S(2)}, u32[]{:S(2)}) collective-permute-start(bf16[128,1024]{1,0:T(8,128)(2,1)S(1)} %slice.7), channel_id=1, source_target_pairs={{0,15},{1,0},{2,1},{3,2},{4,3},{5,4},{6,5},{7,6},{8,7},{9,8},{10,9... | collective-permute-start | bytes 786440 | tf_op jit(solution)/shard_map/ppermute | solution.py:143
  129.7 8.0 %collective-permute-start.14 = (bf16[112,1024]{1,0:T(8,128)(2,1)S(1)}, bf16[112,1024]{1,0:T(8,128)(2,1)S(1)}, u32[]{:S(2)}, u32[]{:S(2)}) collective-permute-start(bf16[112,1024]{1,0:T(8,128)(2,1)S(1)} %slice.6), channel_id=1, source_target_pairs={{0,1},{1,2},{2,3},{3,4},{4,5},{5,6},{6,7},{7,8},{8,9},{9,10},{10,1... | collective-permute-start | bytes 688136 | tf_op jit(solution)/shard_map/ppermute | solution.py:143
  139.5 1.1 copy-start.2
  140.6 5.2 %copy-start.7 = (s32[1,8,16]{2,1,0:T(8,128)S(1)}, s32[1,8,16]{2,1,0:T(8,128)}, u32[]{:S(2)}) copy-start(s32[1,8,16]{2,1,0:T(8,128)} %param.8) | copy-start | bytes 1540
  140.6 19.0 %copy-start.3 = (f32[1,1024]{1,0:T(1,128)S(1)}, f32[1,1024]{1,0:T(1,128)}, u32[]{:S(2)}) copy-start(f32[1,1024]{1,0:T(1,128)} %param.7) | copy-start | bytes 12292
  142.3 17.3 %all-to-all-start.5 = ((bf16[4,6,240,128]{3,2,1,0:T(8,128)(2,1)}), bf16[4,6,240,128]{3,2,1,0:T(8,128)(2,1)S(1)}, u32[]{:S(2)}, u32[]{:S(2)}) async-start(bf16[4,6,240,128]{3,2,1,0:T(8,128)(2,1)} %copy-done.2), calls=%async_computation.5 | async-start | bytes 2949120 | tf_op jit(solution)/shard_map/all_to_all | solution.py:147
  167.6 23.3 %collective-permute-start.16 = (bf16[128,1024]{1,0:T(8,128)(2,1)S(1)}, bf16[128,1024]{1,0:T(8,128)(2,1)S(1)}, u32[]{:S(2)}, u32[]{:S(2)}) collective-permute-start(bf16[128,1024]{1,0:T(8,128)(2,1)S(1)} %mix.2), channel_id=1, source_target_pairs={{0,64},{64,128},{128,192},{192,256},{256,320},{320,384},{384,448},... | collective-permute-start | bytes 786440 | tf_op jit(solution)/shard_map/ppermute | solution.py:143
  188.0 3.0 %collective-permute-start.17 = (bf16[112,1024]{1,0:T(8,128)(2,1)S(1)}, bf16[112,1024]{1,0:T(8,128)(2,1)S(1)}, u32[]{:S(2)}, u32[]{:S(2)}) collective-permute-start(bf16[112,1024]{1,0:T(8,128)(2,1)S(1)} %mix.3), channel_id=1, source_target_pairs={{0,64},{64,128},{128,192},{192,256},{256,320},{320,384},{384,448},... | collective-permute-start | bytes 688136 | tf_op jit(solution)/shard_map/ppermute | solution.py:143

commit v8 on v7

--- a/solution.py
+++ b/solution.py
@@ -14,14 +14,16 @@
 BLOCK = 128
 PICK_VMEM = 24 * 2**20
 MIX_VMEM = 50 * 2**20
+LATE_VMEM = 50 * 2**20
+MIX_WEIGHT = 10**10
 PICK_WEIGHT = 12 * 10**9
 AFTER = (2,)
-HAVE = (6, 9, 9, 9)
+HAVE = (5, 8, 9, 9)
 PARTS = (
-    (0, -1, 1, -2, 2),
-    (-3, 3, -4, 4),
-    (-5, 5, -6, 6),
-    (-7, 7, 8),
+    (0, -1, 1),
+    (-2, 2, -3, 3),
+    (-4, 4, -5, 5),
+    (-6, 6, -7, 7, 8),
 )
 
 
@@ -82,34 +84,34 @@
     return pick_call(kernel, (ids, here), flat, len(part) * CAP, rows, "pick_part")
 
 
-def mix(codes, arrays, weights, bias, first, rows):
+def mix_early(codes, arrays, weights):
     per_device, taps = weights.shape[:2]
+    rows = arrays[0].shape[1]
     total = sum(array.shape[0] for array in arrays)
 
     def kernel(codes_ref, *refs):
         blocks_refs = refs[: len(arrays)]
-        weight_ref, bias_ref, out_ref, held, sem = refs[len(arrays) :]
+        weight_ref, out_ref, held, sem = refs[len(arrays) :]
         j = pl.program_id(0)
+        here = held.at[pl.ds(0, total)]
 
         @pl.when(j == 0)
         def _():
             at = 0
             for ref in blocks_refs:
-                pltpu.make_async_copy(
-                    ref.at[:, first : first + rows],
-                    held.at[at : at + ref.shape[0]],
-                    sem,
-                ).start()
+                pltpu.make_async_copy(ref, held.at[pl.ds(at, ref.shape[0])], sem).start()
                 at += ref.shape[0]
-            pltpu.make_async_copy(held, held, sem).wait()
-
-        blocks = [held[codes_ref[j * taps + k]] for k in range(taps)]
-        stacked = weight_ref[0].reshape(taps * BLOCK, BLOCK)
-        mixed = jnp.dot(
-            jnp.concatenate(blocks, axis=1), stacked, preferred_element_type=jnp.float32
+            held[total] = jnp.zeros((rows, BLOCK), jnp.bfloat16)
+            pltpu.make_async_copy(here, here, sem).wait()
+
+        blocks = [
+            held[jnp.minimum(codes_ref[j * taps + k], total)] for k in range(taps)
+        ]
+        out_ref[...] = jnp.dot(
+            jnp.concatenate(blocks, axis=1),
+            weight_ref[0].reshape(taps * BLOCK, BLOCK),
+            preferred_element_type=jnp.float32,
         )
-        result = mixed + bias_ref[0]
-        out_ref[...] = jnp.clip(result, 0.0, CLAMP_TOP).astype(jnp.bfloat16)
 
     return pl.pallas_call(
         kernel,
@@ -117,25 +119,69 @@
             num_scalar_prefetch=1,
             grid=(per_device,),
             in_specs=[pl.BlockSpec(memory_space=pl.ANY)] * len(arrays)
-            + [
-                pl.BlockSpec((1, taps, BLOCK, BLOCK), lambda j, s: (j, 0, 0, 0)),
-                pl.BlockSpec((1, 1, BLOCK), lambda j, s: (j, 0, 0)),
+            + [pl.BlockSpec((1, taps, BLOCK, BLOCK), lambda j, s: (j, 0, 0, 0))],
+            out_specs=pl.BlockSpec((rows, BLOCK), lambda j, s: (0, j)),
+            scratch_shapes=[
+                pltpu.VMEM((total + 1, rows, BLOCK), jnp.bfloat16),
+                pltpu.SemaphoreType.DMA,
+            ],
+        ),
+        out_shape=jax.ShapeDtypeStruct((rows, per_device * BLOCK), jnp.float32),
+        compiler_params=pltpu.CompilerParams(vmem_limit_bytes=MIX_VMEM),
+        cost_estimate=pl.CostEstimate(
+            flops=MIX_WEIGHT,
+            bytes_accessed=(total * rows + per_device * taps * BLOCK) * BLOCK * 2,
+            transcendentals=0,
+        ),
+        name="mix_early",
+    )(codes, *arrays, weights)
+
+
+def mix_late(codes, early, array, base, weights, bias, first, count):
+    taps = weights.shape[1]
+    size, rows = array.shape[:2]
+
+    def kernel(codes_ref, early_ref, blocks_ref, weight_ref, bias_ref, out_ref, total):
+        j = pl.program_id(0) + first
+        total[...] = early_ref[...] + bias_ref[0]
+        for k in range(taps):
+            place = codes_ref[j * taps + k] - base
+
+            @pl.when(place >= 0)
+            def _(k=k, place=place):
+                total[...] += jnp.dot(
+                    blocks_ref[place],
+                    weight_ref[0, k],
+                    preferred_element_type=jnp.float32,
+                )
+
+        out_ref[...] = jnp.clip(total[...], 0.0, CLAMP_TOP).astype(jnp.bfloat16)
+
+    return pl.pallas_call(
+        kernel,
+        grid_spec=pltpu.PrefetchScalarGridSpec(
+            num_scalar_prefetch=1,
+            grid=(count,),
+            in_specs=[
+                pl.BlockSpec((rows, BLOCK), lambda j, s: (0, j + first)),
+                pl.BlockSpec((size, rows, BLOCK), lambda j, s: (0, 0, 0)),
+                pl.BlockSpec(
+                    (1, taps, BLOCK, BLOCK), lambda j, s: (j + first, 0, 0, 0)
+                ),
+                pl.BlockSpec((1, 1, BLOCK), lambda j, s: (j + first, 0, 0)),
             ],
             out_specs=pl.BlockSpec((rows, BLOCK), lambda j, s: (0, j)),
-            scratch_shapes=[
-                pltpu.VMEM((total, rows, BLOCK), jnp.bfloat16),
-                pltpu.SemaphoreType.DMA,
-            ],
-        ),
-        out_shape=jax.ShapeDtypeStruct((rows, per_device * BLOCK), jnp.bfloat16),
-        compiler_params=pltpu.CompilerParams(vmem_limit_bytes=MIX_VMEM),
+            scratch_shapes=[pltpu.VMEM((rows, BLOCK), jnp.float32)],
+        ),
+        out_shape=jax.ShapeDtypeStruct((rows, count * BLOCK), jnp.bfloat16),
+        compiler_params=pltpu.CompilerParams(vmem_limit_bytes=LATE_VMEM),
         cost_estimate=pl.CostEstimate(
-            flops=2 * rows * per_device * taps * BLOCK * BLOCK,
-            bytes_accessed=(total * rows + per_device * taps * BLOCK) * BLOCK * 2,
+            flops=2 * rows * count * taps * BLOCK * BLOCK,
+            bytes_accessed=(size * rows + count * taps * BLOCK) * BLOCK * 2,
             transcendentals=0,
         ),
-        name="mix",
-    )(codes, *arrays, weights, bias.reshape(per_device, 1, BLOCK))
+        name="mix_late",
+    )(codes, early, array, weights, bias.reshape(-1, 1, BLOCK))
 
 
 def shifted(value, axis, by):
@@ -212,17 +258,18 @@
         if all(o in held for o in PARTS[len(ready)]):
             ready.append(step)
     pick_next()
-    picked[-1], arrived[-1] = lax.optimization_barrier((picked[-1], arrived[-1]))
     send_next()
 
     codes = part_codes(slots, here)
-    rows = samples.shape[0]
-    upper = (rows + 31) // 32 * 16
+    early = mix_early(codes, arrived[:-1], weights)
+    base = sum(array.shape[0] for array in arrived[:-1])
+    cut = weights.shape[0] * 5 // 8
     outs = [
-        shifted(mix(codes, arrived, weights, bias, first, count), "segment", 1)
-        for first, count in ((0, upper), (upper, rows - upper))
+        mix_late(codes, early, arrived[-1], base, weights, bias, first, last - first)
+        for first, last in ((0, cut), (cut, weights.shape[0]))
     ]
-    return jnp.concatenate(outs, axis=0)[None]
+    outs = [shifted(out, "segment", 1) for out in outs]
+    return jnp.concatenate(outs, axis=1)[None]
 
 
 def solution(mesh):

time: 193 us -> 184 us (0.953)
  waiting for transfers between devices: 48.1 us -> 33.3 us
  Pallas kernels: 26.2 us -> 32.2 us
  starting transfers between devices: 94.3 us -> 97.8 us
  local copies, waits for them, and re-layouts: 11.8 us -> 8.52 us
    all_to_all x4, waiting for transfers between devices: 14.1 us -> 3.8 us  [over_lines(): incoming = lax.all_to_all(outgoing, 'y', 0, 0, tiled=True)]
    all_to_all x1, waiting for transfers between devices: 11.4 us -> 3.6 us  [body(): ids = lax.all_to_all(far, 'far', 0, 0, tiled=True).reshape(-1)]
    pallas_call x2 -> x3, Pallas kernels: 15.9 us -> 21.9 us  [the longest x2 12.5 us: mix_late(): pl.pallas_call(kernel, grid_spec=pltpu.PrefetchScalarGridSpec(num_scalar_...]
    ppermute x18, waiting for transfers between devices: 22.5 us -> 25.9 us  [shifted(): lax.ppermute(value, axis, [(i, (i + by) % count) for i in range(count)])]
    ppermute x18, starting transfers between devices: 72.4 us -> 74.8 us  [shifted(): lax.ppermute(value, axis, [(i, (i + by) % count) for i in range(count)])]
    unnamed x16 -> x12, local copies, waits for them, and re-layouts: 5.78 us -> 3.85 us
  transfers between devices with their start and end apart: 23 -> 23, of which waited for: 15 -> 16; matrix products, arithmetic and copies ran while one was open for 4% -> 2% of each run, Pallas kernels for 9% -> 14%
where the time goes in v8:
time: 184 us; the launch traced here: 182 us
  starting transfers between devices  97.8 us (53%)
  waiting for transfers between devices  33.3 us (18%)
  Pallas kernels  32.2 us (18%)
  blocking collectives  9.43 us (5%)
  local copies, waits for them, and re-layouts  8.52 us (5%)
    ppermute x18, starting transfers between devices, shifted(): lax.ppermute(value, axis, [(i, (i + by) % count) for i in range(count)])  74.8 us
    ppermute x18, waiting for transfers between devices, shifted(): lax.ppermute(value, axis, [(i, (i + by) % count) for i in range(count)])  25.9 us
    all_to_all x4, starting transfers between devices, over_lines(): incoming = lax.all_to_all(outgoing, 'y', 0, 0, tiled=True)  17.2 us
    pallas_call x2, Pallas kernels, mix_late(): pl.pallas_call(kernel, grid_spec=pltpu.PrefetchScalarGridSpec(num_scalar_...  12.5 us
    pallas_call x4, Pallas kernels, pick_call(): pl.pallas_call(kernel, grid_spec=pltpu.PrefetchScalarGridSpec(num_scalar_...  10.3 us
    all_to_all x1, blocking collectives, body(): near = lax.all_to_all(lists, 'near', 0, 0, tiled=True)  9.43 us
    pallas_call x1, Pallas kernels, mix_early(): pl.pallas_call(kernel, grid_spec=pltpu.PrefetchScalarGridSpec(num_scalar_...  9.39 us
    all_to_all x1, starting transfers between devices, body(): ids = lax.all_to_all(far, 'far', 0, 0, tiled=True).reshape(-1)  5.81 us
  transfers between devices with their start and end apart: 23, of which 16 were waited for; matrix products, arithmetic and copies ran while one was open for 2% of the time, Pallas kernels for 14%

profile of v8, /device:TPU:1, one launch (start us, length us, event | category | flops | bytes accessed | tf_op | source)
XLA Modules:
  0.0 182.5 jit_solution(13405698846694317710)
XLA Ops:
  0.0 11.9 %collective-permute-start.1 = (bf16[240,1024]{1,0:T(8,128)(2,1)}, bf16[240,1024]{1,0:T(8,128)(2,1)S(1)}, u32[]{:S(2)}, u32[]{:S(2)}) collective-permute-start(bf16[240,1024]{1,0:T(8,128)(2,1)} %bitcast.19), channel_id=1, source_target_pairs={{0,15},{1,0},{2,1},{3,2},{4,3},{5,4},{6,5},{7,6},{8,7},{9,8},{10,9... | collective-permute-start | bytes 1474568 | tf_op jit(solution)/shard_map/ppermute | solution.py:189
  14.8 9.4 %all_to_all.30 = s32[4,4,4,2]{1,2,3,0:T(4,128)S(1)} all-to-all(s32[4,4,4,2]{1,2,3,0:T(4,128)S(1)} %copy.8), channel_id=1, replica_groups=mesh['segment'=8,'y'=4,'far'=4,'near'=4] {'near'}, dimensions={0} | all-to-all | bytes 1024 | tf_op jit(solution)/shard_map/all_to_all | solution.py:228
  24.2 2.8 %collective-permute-done.refs_1_ = bf16[240,1024]{1,0:T(8,128)(2,1)S(1)} collective-permute-done((bf16[240,1024]{1,0:T(8,128)(2,1)}, bf16[240,1024]{1,0:T(8,128)(2,1)S(1)}, u32[]{:S(2)}, u32[]{:S(2)}) %collective-permute-start) | collective-permute-done | bytes 491552 | tf_op jit(solution)/shard_map/ppermute | solution.py:189
  27.8 5.8 %all-to-all-start.1 = ((s32[4,4,4,2]{1,2,3,0:T(4,128)}), s32[4,4,4,2]{1,2,3,0:T(4,128)S(1)}, u32[]{:S(2)}, u32[]{:S(2)}) async-start(s32[4,4,4,2]{1,2,3,0:T(4,128)} %copy.9), calls=%async_computation.1 | async-start | bytes 32768 | tf_op jit(solution)/shard_map/all_to_all | solution.py:236
  35.6 5.9 %collective-permute-start.3 = (bf16[240,1024]{1,0:T(8,128)(2,1)S(1)}, bf16[240,1024]{1,0:T(8,128)(2,1)S(1)}, u32[]{:S(2)}, u32[]{:S(2)}) collective-permute-start(bf16[240,1024]{1,0:T(8,128)(2,1)S(1)} %collective-permute-done.1.refs_2_), channel_id=1, source_target_pairs={{0,15},{1,0},{2,1},{3,2},{4,3},{5,4},{6,5},{7,6},{8,7},{9,8},{10,9... | collective-permute-start | bytes 1474568 | tf_op jit(solution)/shard_map/ppermute | solution.py:189
  41.5 3.6 %all-to-all-done.1 = s32[4,4,4,2]{1,2,3,0:T(4,128)S(1)} async-done(((s32[4,4,4,2]{1,2,3,0:T(4,128)}), s32[4,4,4,2]{1,2,3,0:T(4,128)S(1)}, u32[]{:S(2)}, u32[]{:S(2)}) %all-to-all-start.1) | async-done | bytes 544 | tf_op jit(solution)/shard_map/all_to_all | solution.py:236
  46.5 2.2 %pick_part.4 = bf16[4,6,240,128]{3,2,1,0:T(8,128)(2,1)} custom-call(s32[128]{0:T(128)S(1)} %reshape.70.ids_ref, s32[1]{0:T(128)} %bitcast.3.here_ref, bf16[240,1024]{1,0:T(8,128)(2,1)S(1)} %bitcast.21, bf16[240,1024]{1,0:T(8,128)(2,1)S(1)} %collective-permute-done.refs_1_, bf16[240,1024]{1,0:T(8,128)(2,1)S(1)} %collective-permute-done.1.refs_2_), custom_call_target="tpu_custom_call" | custom-call | flops 12000000000 | bytes 2949120 | tf_op jit(solution)/shard_map/pick_part/pallas_call | solution.py:50
  51.3 5.3 %collective-permute-start.6 = (bf16[240,1024]{1,0:T(8,128)(2,1)S(1)}, bf16[240,1024]{1,0:T(8,128)(2,1)}, u32[]{:S(2)}, u32[]{:S(2)}) collective-permute-start(bf16[240,1024]{1,0:T(8,128)(2,1)S(1)} %collective-permute-done.3.refs_1_), channel_id=1, source_target_pairs={{0,15},{1,0},{2,1},{3,2},{4,3},{5,4},{6,5},{7,6},{8,7},{9,8},{10,9... | collective-permute-start | bytes 1474568 | tf_op jit(solution)/shard_map/ppermute | solution.py:189
  56.6 4.2 %all-to-all-start.2 = ((bf16[4,6,240,128]{3,2,1,0:T(8,128)(2,1)}), bf16[4,6,240,128]{3,2,1,0:T(8,128)(2,1)S(1)}, u32[]{:S(2)}, u32[]{:S(2)}) async-start(bf16[4,6,240,128]{3,2,1,0:T(8,128)(2,1)} %pick_part.4), calls=%async_computation.2 | async-start | bytes 2949120 | tf_op jit(solution)/shard_map/all_to_all | solution.py:193
  65.0 4.2 %collective-permute-start.7 = (bf16[240,1024]{1,0:T(8,128)(2,1)}, bf16[240,1024]{1,0:T(8,128)(2,1)S(1)}, u32[]{:S(2)}, u32[]{:S(2)}) collective-permute-start(bf16[240,1024]{1,0:T(8,128)(2,1)} %collective-permute-done.6.refs_3_), channel_id=1, source_target_pairs={{0,15},{1,0},{2,1},{3,2},{4,3},{5,4},{6,5},{7,6},{8,7},{9,8},{10,9... | collective-permute-start | bytes 1474568 | tf_op jit(solution)/shard_map/ppermute | solution.py:189
  69.2 2.9 %pick_part.5 = bf16[4,8,240,128]{3,2,1,0:T(8,128)(2,1)} custom-call(s32[128]{0:T(128)S(1)} %reshape.70.ids_ref, s32[1]{0:T(128)} %bitcast.3.here_ref, bf16[240,1024]{1,0:T(8,128)(2,1)S(1)} %collective-permute-done.2.refs_0_, bf16[240,1024]{1,0:T(8,128)(2,1)S(1)} %collective-permute-done.3.refs_1_, bf16[240,1024]{1,0:T(8,128)(2,1)} %collective-permute-done.4.refs_2_, ...), custom_call_target="tpu_custom_call" | custom-call | flops 12000000000 | bytes 3932160 | tf_op jit(solution)/shard_map/pick_part/pallas_call | solution.py:50
  72.1 2.3 %collective-permute-done.5.refs_0_ = bf16[240,1024]{1,0:T(8,128)(2,1)S(1)} collective-permute-done((bf16[240,1024]{1,0:T(8,128)(2,1)}, bf16[240,1024]{1,0:T(8,128)(2,1)S(1)}, u32[]{:S(2)}, u32[]{:S(2)}) %collective-permute-start.5) | collective-permute-done | bytes 491552 | tf_op jit(solution)/shard_map/ppermute | solution.py:189
  76.5 3.1 %collective-permute-start.8 = (bf16[240,1024]{1,0:T(8,128)(2,1)S(1)}, bf16[240,1024]{1,0:T(8,128)(2,1)S(1)}, u32[]{:S(2)}, u32[]{:S(2)}) collective-permute-start(bf16[240,1024]{1,0:T(8,128)(2,1)S(1)} %collective-permute-done.5.refs_0_), channel_id=1, source_target_pairs={{0,1},{1,2},{2,3},{3,4},{4,5},{5,6},{6,7},{7,8},{8,9},{9,10},{10,1... | collective-permute-start | bytes 1474568 | tf_op jit(solution)/shard_map/ppermute | solution.py:189
  79.6 3.4 %collective-permute-start.9 = (bf16[240,1024]{1,0:T(8,128)(2,1)S(1)}, bf16[240,1024]{1,0:T(8,128)(2,1)}, u32[]{:S(2)}, u32[]{:S(2)}) collective-permute-start(bf16[240,1024]{1,0:T(8,128)(2,1)S(1)} %collective-permute-done.7.refs_1_), channel_id=1, source_target_pairs={{0,15},{1,0},{2,1},{3,2},{4,3},{5,4},{6,5},{7,6},{8,7},{9,8},{10,9... | collective-permute-start | bytes 1474568 | tf_op jit(solution)/shard_map/ppermute | solution.py:189
  83.0 4.4 %all-to-all-start.3 = ((bf16[4,8,240,128]{3,2,1,0:T(8,128)(2,1)}), bf16[4,8,240,128]{3,2,1,0:T(8,128)(2,1)}, u32[]{:S(2)}, u32[]{:S(2)}) async-start(bf16[4,8,240,128]{3,2,1,0:T(8,128)(2,1)} %pick_part.5), calls=%async_computation.3 | async-start | bytes 3932160 | tf_op jit(solution)/shard_map/all_to_all | solution.py:193
  89.4 4.5 %collective-permute-start.11 = (bf16[240,1024]{1,0:T(8,128)(2,1)}, bf16[240,1024]{1,0:T(8,128)(2,1)S(1)}, u32[]{:S(2)}, u32[]{:S(2)}) collective-permute-start(bf16[240,1024]{1,0:T(8,128)(2,1)} %collective-permute-done.9.refs_3_), channel_id=1, source_target_pairs={{0,15},{1,0},{2,1},{3,2},{4,3},{5,4},{6,5},{7,6},{8,7},{9,8},{10,9... | collective-permute-start | bytes 1474568 | tf_op jit(solution)/shard_map/ppermute | solution.py:189
  93.9 3.0 %pick_part.6 = bf16[4,8,240,128]{3,2,1,0:T(8,128)(2,1)} custom-call(s32[128]{0:T(128)S(1)} %reshape.70.ids_ref, s32[1]{0:T(128)} %bitcast.3.here_ref, bf16[240,1024]{1,0:T(8,128)(2,1)S(1)} %collective-permute-done.5.refs_0_, bf16[240,1024]{1,0:T(8,128)(2,1)S(1)} %collective-permute-done.7.refs_1_, bf16[240,1024]{1,0:T(8,128)(2,1)S(1)} %collective-permute-done.8.refs_2_, ...), custom_call_target="tpu_custom_call" | custom-call | flops 12000000000 | bytes 3932160 | tf_op jit(solution)/shard_map/pick_part/pallas_call | solution.py:50
  98.6 2.3 %collective-permute-done.11.refs_1_ = bf16[240,1024]{1,0:T(8,128)(2,1)S(1)} collective-permute-done((bf16[240,1024]{1,0:T(8,128)(2,1)}, bf16[240,1024]{1,0:T(8,128)(2,1)S(1)}, u32[]{:S(2)}, u32[]{:S(2)}) %collective-permute-start.11) | collective-permute-done | bytes 491552 | tf_op jit(solution)/shard_map/ppermute | solution.py:189
  100.9 4.2 %collective-permute-start.12 = (bf16[240,1024]{1,0:T(8,128)(2,1)S(1)}, bf16[240,1024]{1,0:T(8,128)(2,1)S(1)}, u32[]{:S(2)}, u32[]{:S(2)}) collective-permute-start(bf16[240,1024]{1,0:T(8,128)(2,1)S(1)} %collective-permute-done.10.refs_0_), channel_id=1, source_target_pairs={{0,1},{1,2},{2,3},{3,4},{4,5},{5,6},{6,7},{7,8},{8,9},{9,10},{10,1... | collective-permute-start | bytes 1474568 | tf_op jit(solution)/shard_map/ppermute | solution.py:189
  105.1 2.3 %collective-permute-start.13 = (bf16[240,1024]{1,0:T(8,128)(2,1)S(1)}, bf16[240,1024]{1,0:T(8,128)(2,1)S(1)}, u32[]{:S(2)}, u32[]{:S(2)}) collective-permute-start(bf16[240,1024]{1,0:T(8,128)(2,1)S(1)} %collective-permute-done.11.refs_1_), channel_id=1, source_target_pairs={{0,15},{1,0},{2,1},{3,2},{4,3},{5,4},{6,5},{7,6},{8,7},{9,8},{10,9... | collective-permute-start | bytes 1474568 | tf_op jit(solution)/shard_map/ppermute | solution.py:189
  107.4 4.4 %all-to-all-start.4 = ((bf16[4,8,240,128]{3,2,1,0:T(8,128)(2,1)}), bf16[4,8,240,128]{3,2,1,0:T(8,128)(2,1)}, u32[]{:S(2)}, u32[]{:S(2)}) async-start(bf16[4,8,240,128]{3,2,1,0:T(8,128)(2,1)} %pick_part.6), calls=%async_computation.4 | async-start | bytes 3932160 | tf_op jit(solution)/shard_map/all_to_all | solution.py:193
  112.0 3.2 %collective-permute-done.13.refs_3_ = bf16[240,1024]{1,0:T(8,128)(2,1)S(1)} collective-permute-done((bf16[240,1024]{1,0:T(8,128)(2,1)S(1)}, bf16[240,1024]{1,0:T(8,128)(2,1)S(1)}, u32[]{:S(2)}, u32[]{:S(2)}) %collective-permute-start.13) | collective-permute-done | bytes 491552 | tf_op jit(solution)/shard_map/ppermute | solution.py:189
  115.2 2.9 %collective-permute-start.15 = (bf16[128,1024]{1,0:T(8,128)(2,1)S(1)}, bf16[128,1024]{1,0:T(8,128)(2,1)S(1)}, u32[]{:S(2)}, u32[]{:S(2)}) collective-permute-start(bf16[128,1024]{1,0:T(8,128)(2,1)S(1)} %slice.7), channel_id=1, source_target_pairs={{0,15},{1,0},{2,1},{3,2},{4,3},{5,4},{6,5},{7,6},{8,7},{9,8},{10,9... | collective-permute-start | bytes 786440 | tf_op jit(solution)/shard_map/ppermute | solution.py:189
  118.2 2.3 %collective-permute-start.14 = (bf16[112,1024]{1,0:T(8,128)(2,1)S(1)}, bf16[112,1024]{1,0:T(8,128)(2,1)S(1)}, u32[]{:S(2)}, u32[]{:S(2)}) collective-permute-start(bf16[112,1024]{1,0:T(8,128)(2,1)S(1)} %slice.6), channel_id=1, source_target_pairs={{0,1},{1,2},{2,3},{3,4},{4,5},{5,6},{6,7},{7,8},{8,9},{9,10},{10,1... | collective-permute-start | bytes 688136 | tf_op jit(solution)/shard_map/ppermute | solution.py:189
  120.6 6.0 %collective-permute-done.14.refs_4_ = bf16[112,1024]{1,0:T(8,128)(2,1)S(1)} collective-permute-done((bf16[112,1024]{1,0:T(8,128)(2,1)S(1)}, bf16[112,1024]{1,0:T(8,128)(2,1)S(1)}, u32[]{:S(2)}, u32[]{:S(2)}) %collective-permute-start.14) | collective-permute-done | bytes 229408 | tf_op jit(solution)/shard_map/ppermute | solution.py:189
  130.2 4.1 %all-to-all-start.5 = ((bf16[4,10,240,128]{3,2,1,0:T(8,128)(2,1)}), bf16[4,10,240,128]{3,2,1,0:T(8,128)(2,1)S(1)}, u32[]{:S(2)}, u32[]{:S(2)}) async-start(bf16[4,10,240,128]{3,2,1,0:T(8,128)(2,1)} %copy-done), calls=%async_computation.5 | async-start | bytes 4915200 | tf_op jit(solution)/shard_map/all_to_all | solution.py:193
  138.4 9.4 %mix_early.1.early_ref = f32[240,1024]{1,0:T(8,128)S(1)} custom-call(s32[128]{0:T(128)S(1)} %select_select_fusion.codes_ref, bf16[24,240,128]{2,1,0:T(8,128)(2,1)S(1)} %bitcast.16, bf16[32,240,128]{2,1,0:T(8,128)(2,1)} %bitcast.5.refs_1_, bf16[32,240,128]{2,1,0:T(8,128)(2,1)} %bitcast.6.refs_2_, bf16[8,16,128,128]{3,2,1,0:T(8,128)(2,1)} %bitcast.22), custom_call_target="tpu_custom_call" | custom-call | flops 10000000000 | bytes 9601024 | tf_op jit(solution)/shard_map/mix_early/pallas_call | solution.py:116
  147.8 3.8 %all-to-all-done.5 = bf16[4,10,240,128]{3,2,1,0:T(8,128)(2,1)S(1)} async-done(((bf16[4,10,240,128]{3,2,1,0:T(8,128)(2,1)}), bf16[4,10,240,128]{3,2,1,0:T(8,128)(2,1)S(1)}, u32[]{:S(2)}, u32[]{:S(2)}) %all-to-all-start.5) | async-done | bytes 2457632 | tf_op jit(solution)/shard_map/all_to_all | solution.py:193
  151.6 7.5 %mix_late.2 = bf16[240,640]{1,0:T(8,128)(2,1)S(1)} custom-call(s32[128]{0:T(128)S(1)} %select_select_fusion.codes_ref, f32[240,1024]{1,0:T(8,128)S(1)} %mix_early.1.early_ref, bf16[40,240,128]{2,1,0:T(8,128)(2,1)S(1)} %bitcast.14, bf16[8,16,128,128]{3,2,1,0:T(8,128)(2,1)} %bitcast.23, f32[8,1,128]{2,1,0:T(1,128)S(1)} %bitcast.17), custom_call_target="tpu_custom_call" | custom-call | flops 629145600 | bytes 5079040 | tf_op jit(solution)/shard_map/mix_late/pallas_call | solution.py:160
  159.1 14.5 %collective-permute-start.16 = (bf16[240,640]{1,0:T(8,128)(2,1)S(1)}, bf16[240,640]{1,0:T(8,128)(2,1)S(1)}, u32[]{:S(2)}, u32[]{:S(2)}) collective-permute-start(bf16[240,640]{1,0:T(8,128)(2,1)S(1)} %mix_late.2), channel_id=1, source_target_pairs={{0,64},{64,128},{128,192},{192,256},{256,320},{320,384},{384,448},... | collective-permute-start | bytes 921608 | tf_op jit(solution)/shard_map/ppermute | solution.py:189
  173.6 5.1 %mix_late.3 = bf16[240,384]{1,0:T(8,128)(2,1)S(1)} custom-call(s32[128]{0:T(128)S(1)} %select_select_fusion.codes_ref, f32[240,1024]{1,0:T(8,128)S(1)} %mix_early.1.early_ref, bf16[40,240,128]{2,1,0:T(8,128)(2,1)S(1)} %bitcast.15, bf16[8,16,128,128]{3,2,1,0:T(8,128)(2,1)} %bitcast.24, f32[8,1,128]{2,1,0:T(1,128)S(1)} %bitcast.18), custom_call_target="tpu_custom_call" | custom-call | flops 377487360 | bytes 4030464 | tf_op jit(solution)/shard_map/mix_late/pallas_call | solution.py:160
  179.2 2.5 %collective-permute-done.17 = bf16[240,384]{1,0:T(8,128)(2,1)S(1)} collective-permute-done((bf16[240,384]{1,0:T(8,128)(2,1)S(1)}, bf16[240,384]{1,0:T(8,128)(2,1)S(1)}, u32[]{:S(2)}, u32[]{:S(2)}) %collective-permute-start.17) | collective-permute-done | bytes 184352 | tf_op jit(solution)/shard_map/ppermute | solution.py:189
  (76 shorter events, 28.6 us)
Async XLA Ops:
  0.0 24.2 %collective-permute-start.1 = (bf16[240,1024]{1,0:T(8,128)(2,1)}, bf16[240,1024]{1,0:T(8,128)(2,1)S(1)}, u32[]{:S(2)}, u32[]{:S(2)}) collective-permute-start(bf16[240,1024]{1,0:T(8,128)(2,1)} %bitcast.19), channel_id=1, source_target_pairs={{0,15},{1,0},{2,1},{3,2},{4,3},{5,4},{6,5},{7,6},{8,7},{9,8},{10,9... | collective-permute-start | bytes 1474568 | tf_op jit(solution)/shard_map/ppermute | solution.py:189
  12.0 15.1 %collective-permute-start = (bf16[240,1024]{1,0:T(8,128)(2,1)}, bf16[240,1024]{1,0:T(8,128)(2,1)S(1)}, u32[]{:S(2)}, u32[]{:S(2)}) collective-permute-start(bf16[240,1024]{1,0:T(8,128)(2,1)} %bitcast.20), channel_id=1, source_target_pairs={{0,1},{1,2},{2,3},{3,4},{4,5},{5,6},{6,7},{7,8},{8,9},{9,10},{10,1... | collective-permute-start | bytes 1474568 | tf_op jit(solution)/shard_map/ppermute | solution.py:189
  27.8 17.4 %all-to-all-start.1 = ((s32[4,4,4,2]{1,2,3,0:T(4,128)}), s32[4,4,4,2]{1,2,3,0:T(4,128)S(1)}, u32[]{:S(2)}, u32[]{:S(2)}) async-start(s32[4,4,4,2]{1,2,3,0:T(4,128)} %copy.9), calls=%async_computation.1 | async-start | bytes 32768 | tf_op jit(solution)/shard_map/all_to_all | solution.py:236
  33.6 15.5 %collective-permute-start.2 = (bf16[240,1024]{1,0:T(8,128)(2,1)S(1)}, bf16[240,1024]{1,0:T(8,128)(2,1)S(1)}, u32[]{:S(2)}, u32[]{:S(2)}) collective-permute-start(bf16[240,1024]{1,0:T(8,128)(2,1)S(1)} %collective-permute-done.refs_1_), channel_id=1, source_target_pairs={{0,1},{1,2},{2,3},{3,4},{4,5},{5,6},{6,7},{7,8},{8,9},{9,10},{10,1... | collective-permute-start | bytes 1474568 | tf_op jit(solution)/shard_map/ppermute | solution.py:189
  35.6 13.8 %collective-permute-start.3 = (bf16[240,1024]{1,0:T(8,128)(2,1)S(1)}, bf16[240,1024]{1,0:T(8,128)(2,1)S(1)}, u32[]{:S(2)}, u32[]{:S(2)}) collective-permute-start(bf16[240,1024]{1,0:T(8,128)(2,1)S(1)} %collective-permute-done.1.refs_2_), channel_id=1, source_target_pairs={{0,15},{1,0},{2,1},{3,2},{4,3},{5,4},{6,5},{7,6},{8,7},{9,8},{10,9... | collective-permute-start | bytes 1474568 | tf_op jit(solution)/shard_map/ppermute | solution.py:189
  45.5 1.0 copy-start.4
  49.4 13.3 %collective-permute-start.4 = (bf16[240,1024]{1,0:T(8,128)(2,1)S(1)}, bf16[240,1024]{1,0:T(8,128)(2,1)}, u32[]{:S(2)}, u32[]{:S(2)}) collective-permute-start(bf16[240,1024]{1,0:T(8,128)(2,1)S(1)} %collective-permute-done.2.refs_0_), channel_id=1, source_target_pairs={{0,1},{1,2},{2,3},{3,4},{4,5},{5,6},{6,7},{7,8},{8,9},{9,10},{10,1... | collective-permute-start | bytes 1474568 | tf_op jit(solution)/shard_map/ppermute | solution.py:189
  51.3 13.7 %collective-permute-start.6 = (bf16[240,1024]{1,0:T(8,128)(2,1)S(1)}, bf16[240,1024]{1,0:T(8,128)(2,1)}, u32[]{:S(2)}, u32[]{:S(2)}) collective-permute-start(bf16[240,1024]{1,0:T(8,128)(2,1)S(1)} %collective-permute-done.3.refs_1_), channel_id=1, source_target_pairs={{0,15},{1,0},{2,1},{3,2},{4,3},{5,4},{6,5},{7,6},{8,7},{9,8},{10,9... | collective-permute-start | bytes 1474568 | tf_op jit(solution)/shard_map/ppermute | solution.py:189
  56.6 19.8 %all-to-all-start.2 = ((bf16[4,6,240,128]{3,2,1,0:T(8,128)(2,1)}), bf16[4,6,240,128]{3,2,1,0:T(8,128)(2,1)S(1)}, u32[]{:S(2)}, u32[]{:S(2)}) async-start(bf16[4,6,240,128]{3,2,1,0:T(8,128)(2,1)} %pick_part.4), calls=%async_computation.2 | async-start | bytes 2949120 | tf_op jit(solution)/shard_map/all_to_all | solution.py:193
  62.7 11.7 %collective-permute-start.5 = (bf16[240,1024]{1,0:T(8,128)(2,1)}, bf16[240,1024]{1,0:T(8,128)(2,1)S(1)}, u32[]{:S(2)}, u32[]{:S(2)}) collective-permute-start(bf16[240,1024]{1,0:T(8,128)(2,1)} %collective-permute-done.4.refs_2_), channel_id=1, source_target_pairs={{0,1},{1,2},{2,3},{3,4},{4,5},{5,6},{6,7},{7,8},{8,9},{9,10},{10,1... | collective-permute-start | bytes 1474568 | tf_op jit(solution)/shard_map/ppermute | solution.py:189
  65.0 11.5 %collective-permute-start.7 = (bf16[240,1024]{1,0:T(8,128)(2,1)}, bf16[240,1024]{1,0:T(8,128)(2,1)S(1)}, u32[]{:S(2)}, u32[]{:S(2)}) collective-permute-start(bf16[240,1024]{1,0:T(8,128)(2,1)} %collective-permute-done.6.refs_3_), channel_id=1, source_target_pairs={{0,15},{1,0},{2,1},{3,2},{4,3},{5,4},{6,5},{7,6},{8,7},{9,8},{10,9... | collective-permute-start | bytes 1474568 | tf_op jit(solution)/shard_map/ppermute | solution.py:189
  76.5 6.5 %copy-start.1 = (bf16[4,6,240,128]{3,2,1,0:T(8,128)(2,1)}, bf16[4,6,240,128]{3,2,1,0:T(8,128)(2,1)S(1)}, u32[]{:S(2)}) copy-start(bf16[4,6,240,128]{3,2,1,0:T(8,128)(2,1)S(1)} %all-to-all-done.2) | copy-start | bytes 4423684
  76.5 10.9 %collective-permute-start.8 = (bf16[240,1024]{1,0:T(8,128)(2,1)S(1)}, bf16[240,1024]{1,0:T(8,128)(2,1)S(1)}, u32[]{:S(2)}, u32[]{:S(2)}) collective-permute-start(bf16[240,1024]{1,0:T(8,128)(2,1)S(1)} %collective-permute-done.5.refs_0_), channel_id=1, source_target_pairs={{0,1},{1,2},{2,3},{3,4},{4,5},{5,6},{6,7},{7,8},{8,9},{9,10},{10,1... | collective-permute-start | bytes 1474568 | tf_op jit(solution)/shard_map/ppermute | solution.py:189
  79.6 9.9 %collective-permute-start.9 = (bf16[240,1024]{1,0:T(8,128)(2,1)S(1)}, bf16[240,1024]{1,0:T(8,128)(2,1)}, u32[]{:S(2)}, u32[]{:S(2)}) collective-permute-start(bf16[240,1024]{1,0:T(8,128)(2,1)S(1)} %collective-permute-done.7.refs_1_), channel_id=1, source_target_pairs={{0,15},{1,0},{2,1},{3,2},{4,3},{5,4},{6,5},{7,6},{8,7},{9,8},{10,9... | collective-permute-start | bytes 1474568 | tf_op jit(solution)/shard_map/ppermute | solution.py:189
  83.0 24.4 %all-to-all-start.3 = ((bf16[4,8,240,128]{3,2,1,0:T(8,128)(2,1)}), bf16[4,8,240,128]{3,2,1,0:T(8,128)(2,1)}, u32[]{:S(2)}, u32[]{:S(2)}) async-start(bf16[4,8,240,128]{3,2,1,0:T(8,128)(2,1)} %pick_part.5), calls=%async_computation.3 | async-start | bytes 3932160 | tf_op jit(solution)/shard_map/all_to_all | solution.py:193
  87.4 11.2 %collective-permute-start.10 = (bf16[240,1024]{1,0:T(8,128)(2,1)S(1)}, bf16[240,1024]{1,0:T(8,128)(2,1)S(1)}, u32[]{:S(2)}, u32[]{:S(2)}) collective-permute-start(bf16[240,1024]{1,0:T(8,128)(2,1)S(1)} %collective-permute-done.8.refs_2_), channel_id=1, source_target_pairs={{0,1},{1,2},{2,3},{3,4},{4,5},{5,6},{6,7},{7,8},{8,9},{9,10},{10,1... | collective-permute-start | bytes 1474568 | tf_op jit(solution)/shard_map/ppermute | solution.py:189
  89.4 11.4 %collective-permute-start.11 = (bf16[240,1024]{1,0:T(8,128)(2,1)}, bf16[240,1024]{1,0:T(8,128)(2,1)S(1)}, u32[]{:S(2)}, u32[]{:S(2)}) collective-permute-start(bf16[240,1024]{1,0:T(8,128)(2,1)} %collective-permute-done.9.refs_3_), channel_id=1, source_target_pairs={{0,15},{1,0},{2,1},{3,2},{4,3},{5,4},{6,5},{7,6},{8,7},{9,8},{10,9... | collective-permute-start | bytes 1474568 | tf_op jit(solution)/shard_map/ppermute | solution.py:189
  100.9 11.2 %collective-permute-start.12 = (bf16[240,1024]{1,0:T(8,128)(2,1)S(1)}, bf16[240,1024]{1,0:T(8,128)(2,1)S(1)}, u32[]{:S(2)}, u32[]{:S(2)}) collective-permute-start(bf16[240,1024]{1,0:T(8,128)(2,1)S(1)} %collective-permute-done.10.refs_0_), channel_id=1, source_target_pairs={{0,1},{1,2},{2,3},{3,4},{4,5},{5,6},{6,7},{7,8},{8,9},{9,10},{10,1... | collective-permute-start | bytes 1474568 | tf_op jit(solution)/shard_map/ppermute | solution.py:189
  105.1 10.1 %collective-permute-start.13 = (bf16[240,1024]{1,0:T(8,128)(2,1)S(1)}, bf16[240,1024]{1,0:T(8,128)(2,1)S(1)}, u32[]{:S(2)}, u32[]{:S(2)}) collective-permute-start(bf16[240,1024]{1,0:T(8,128)(2,1)S(1)} %collective-permute-done.11.refs_1_), channel_id=1, source_target_pairs={{0,15},{1,0},{2,1},{3,2},{4,3},{5,4},{6,5},{7,6},{8,7},{9,8},{10,9... | collective-permute-start | bytes 1474568 | tf_op jit(solution)/shard_map/ppermute | solution.py:189
  107.4 22.8 %all-to-all-start.4 = ((bf16[4,8,240,128]{3,2,1,0:T(8,128)(2,1)}), bf16[4,8,240,128]{3,2,1,0:T(8,128)(2,1)}, u32[]{:S(2)}, u32[]{:S(2)}) async-start(bf16[4,8,240,128]{3,2,1,0:T(8,128)(2,1)} %pick_part.6), calls=%async_computation.4 | async-start | bytes 3932160 | tf_op jit(solution)/shard_map/all_to_all | solution.py:193
  115.2 11.3 %collective-permute-start.15 = (bf16[128,1024]{1,0:T(8,128)(2,1)S(1)}, bf16[128,1024]{1,0:T(8,128)(2,1)S(1)}, u32[]{:S(2)}, u32[]{:S(2)}) collective-permute-start(bf16[128,1024]{1,0:T(8,128)(2,1)S(1)} %slice.7), channel_id=1, source_target_pairs={{0,15},{1,0},{2,1},{3,2},{4,3},{5,4},{6,5},{7,6},{8,7},{9,8},{10,9... | collective-permute-start | bytes 786440 | tf_op jit(solution)/shard_map/ppermute | solution.py:189
  118.2 8.4 %collective-permute-start.14 = (bf16[112,1024]{1,0:T(8,128)(2,1)S(1)}, bf16[112,1024]{1,0:T(8,128)(2,1)S(1)}, u32[]{:S(2)}, u32[]{:S(2)}) collective-permute-start(bf16[112,1024]{1,0:T(8,128)(2,1)S(1)} %slice.6), channel_id=1, source_target_pairs={{0,1},{1,2},{2,3},{3,4},{4,5},{5,6},{6,7},{7,8},{8,9},{9,10},{10,1... | collective-permute-start | bytes 688136 | tf_op jit(solution)/shard_map/ppermute | solution.py:189
  128.7 1.5 copy-start
  130.2 4.1 %copy-start.5 = (s32[1,8,16]{2,1,0:T(8,128)S(1)}, s32[1,8,16]{2,1,0:T(8,128)}, u32[]{:S(2)}) copy-start(s32[1,8,16]{2,1,0:T(8,128)} %param.8) | copy-start | bytes 1540
  130.2 21.4 %all-to-all-start.5 = ((bf16[4,10,240,128]{3,2,1,0:T(8,128)(2,1)}), bf16[4,10,240,128]{3,2,1,0:T(8,128)(2,1)S(1)}, u32[]{:S(2)}, u32[]{:S(2)}) async-start(bf16[4,10,240,128]{3,2,1,0:T(8,128)(2,1)} %copy-done), calls=%async_computation.5 | async-start | bytes 4915200 | tf_op jit(solution)/shard_map/all_to_all | solution.py:193
  137.0 1.4 copy-start.2
  138.4 13.2 %copy-start.3 = (f32[1,1024]{1,0:T(1,128)S(1)}, f32[1,1024]{1,0:T(1,128)}, u32[]{:S(2)}) copy-start(f32[1,1024]{1,0:T(1,128)} %param.7) | copy-start | bytes 12292
  159.1 22.6 %collective-permute-start.16 = (bf16[240,640]{1,0:T(8,128)(2,1)S(1)}, bf16[240,640]{1,0:T(8,128)(2,1)S(1)}, u32[]{:S(2)}, u32[]{:S(2)}) collective-permute-start(bf16[240,640]{1,0:T(8,128)(2,1)S(1)} %mix_late.2), channel_id=1, source_target_pairs={{0,64},{64,128},{128,192},{192,256},{256,320},{320,384},{384,448},... | collective-permute-start | bytes 921608 | tf_op jit(solution)/shard_map/ppermute | solution.py:189
  178.6 3.0 %collective-permute-start.17 = (bf16[240,384]{1,0:T(8,128)(2,1)S(1)}, bf16[240,384]{1,0:T(8,128)(2,1)S(1)}, u32[]{:S(2)}, u32[]{:S(2)}) collective-permute-start(bf16[240,384]{1,0:T(8,128)(2,1)S(1)} %mix_late.3), channel_id=1, source_target_pairs={{0,64},{64,128},{128,192},{192,256},{256,320},{320,384},{384,448},... | collective-permute-start | bytes 552968 | tf_op jit(solution)/shard_map/ppermute | solution.py:189

commit v9 on v8

--- a/solution.py
+++ b/solution.py
@@ -137,21 +137,43 @@
     )(codes, *arrays, weights)
 
 
-def mix_late(codes, early, array, base, weights, bias, first, count):
+def late_first(codes, base, per_device):
+    places = codes.reshape(per_device, -1) - base
+    taps = places.shape[1]
+    late = places >= 0
+    tap = jnp.arange(taps, dtype=jnp.int32)
+    before = (tap[None, :, None] > tap[None, None, :]) & late[:, None, :]
+    rank = jnp.sum(before.astype(jnp.int32), axis=2)
+    chosen = late[:, None, :] & (rank[:, None, :] == tap[None, :, None])
+    place = jnp.sum(jnp.where(chosen, places[:, None, :], 0), axis=2)
+    which = jnp.sum(jnp.where(chosen, tap[None, None, :], 0), axis=2)
+    count = jnp.sum(late.astype(jnp.int32), axis=1)
+    return place.reshape(-1), which.reshape(-1), count
+
+
+def mix_late(late, early, array, weights, bias, first, count):
     taps = weights.shape[1]
     size, rows = array.shape[:2]
-
-    def kernel(codes_ref, early_ref, blocks_ref, weight_ref, bias_ref, out_ref, total):
+    step = 4
+
+    def kernel(
+        place_ref, which_ref, count_ref, early_ref, blocks_ref, weight_ref, bias_ref, out_ref, total
+    ):
         j = pl.program_id(0) + first
         total[...] = early_ref[...] + bias_ref[0]
-        for k in range(taps):
-            place = codes_ref[j * taps + k] - base
-
-            @pl.when(place >= 0)
-            def _(k=k, place=place):
+        here = count_ref[j]
+        for k in range(0, taps, step):
+
+            @pl.when(k < here)
+            def _(k=k):
+                inputs, stack = [], []
+                for i in range(k, k + step):
+                    kept = jnp.where(i < here, 1.0, 0.0).astype(jnp.bfloat16)
+                    inputs.append(blocks_ref[place_ref[j * taps + i]] * kept)
+                    stack.append(weight_ref[0, which_ref[j * taps + i]])
                 total[...] += jnp.dot(
-                    blocks_ref[place],
-                    weight_ref[0, k],
+                    jnp.concatenate(inputs, axis=1),
+                    jnp.concatenate(stack, axis=0),
                     preferred_element_type=jnp.float32,
                 )
 
@@ -160,17 +182,17 @@
     return pl.pallas_call(
         kernel,
         grid_spec=pltpu.PrefetchScalarGridSpec(
-            num_scalar_prefetch=1,
+            num_scalar_prefetch=3,
             grid=(count,),
             in_specs=[
-                pl.BlockSpec((rows, BLOCK), lambda j, s: (0, j + first)),
-                pl.BlockSpec((size, rows, BLOCK), lambda j, s: (0, 0, 0)),
+                pl.BlockSpec((rows, BLOCK), lambda j, *s: (0, j + first)),
+                pl.BlockSpec((size, rows, BLOCK), lambda j, *s: (0, 0, 0)),
                 pl.BlockSpec(
-                    (1, taps, BLOCK, BLOCK), lambda j, s: (j + first, 0, 0, 0)
+                    (1, taps, BLOCK, BLOCK), lambda j, *s: (j + first, 0, 0, 0)
                 ),
-                pl.BlockSpec((1, 1, BLOCK), lambda j, s: (j + first, 0, 0)),
+                pl.BlockSpec((1, 1, BLOCK), lambda j, *s: (j + first, 0, 0)),
             ],
-            out_specs=pl.BlockSpec((rows, BLOCK), lambda j, s: (0, j)),
+            out_specs=pl.BlockSpec((rows, BLOCK), lambda j, *s: (0, j)),
             scratch_shapes=[pltpu.VMEM((rows, BLOCK), jnp.float32)],
         ),
         out_shape=jax.ShapeDtypeStruct((rows, count * BLOCK), jnp.bfloat16),
@@ -181,7 +203,7 @@
             transcendentals=0,
         ),
         name="mix_late",
-    )(codes, early, array, weights, bias.reshape(-1, 1, BLOCK))
+    )(*late, early, array, weights, bias.reshape(-1, 1, BLOCK))
 
 
 def shifted(value, axis, by):
@@ -263,9 +285,10 @@
     codes = part_codes(slots, here)
     early = mix_early(codes, arrived[:-1], weights)
     base = sum(array.shape[0] for array in arrived[:-1])
+    late = late_first(codes, base, weights.shape[0])
     cut = weights.shape[0] * 5 // 8
     outs = [
-        mix_late(codes, early, arrived[-1], base, weights, bias, first, last - first)
+        mix_late(late, early, arrived[-1], weights, bias, first, last - first)
         for first, last in ((0, cut), (cut, weights.shape[0]))
     ]
     outs = [shifted(out, "segment", 1) for out in outs]

time: 184 us -> 181 us (0.984)
  Pallas kernels: 32.2 us -> 27.9 us
    pallas_call x2, Pallas kernels: 12.5 us -> 8.29 us  [mix_late(): pl.pallas_call(kernel, grid_spec=pltpu.PrefetchScalarGridSpec(num_scalar_...]
    all_to_all x4, waiting for transfers between devices: 3.8 us -> 5.96 us  [over_lines(): incoming = lax.all_to_all(outgoing, 'y', 0, 0, tiled=True)]
  transfers between devices with their start and end apart: 23 -> 23, of which waited for: 16 -> 17; matrix products, arithmetic and copies ran while one was open for 2% -> 3% of each run, Pallas kernels for 14% -> 13%
where the time goes in v9:
time: 181 us; the launch traced here: 178 us
  starting transfers between devices  96.6 us (53%)
  waiting for transfers between devices  33.7 us (19%)
  Pallas kernels  27.9 us (15%)
  blocking collectives  9.43 us (5%)
  local copies, waits for them, and re-layouts  8.67 us (5%)
    ppermute x18, starting transfers between devices, shifted(): lax.ppermute(value, axis, [(i, (i + by) % count) for i in range(count)])  73.5 us
    ppermute x18, waiting for transfers between devices, shifted(): lax.ppermute(value, axis, [(i, (i + by) % count) for i in range(count)])  24.1 us
    all_to_all x4, starting transfers between devices, over_lines(): incoming = lax.all_to_all(outgoing, 'y', 0, 0, tiled=True)  17.3 us
    pallas_call x4, Pallas kernels, pick_call(): pl.pallas_call(kernel, grid_spec=pltpu.PrefetchScalarGridSpec(num_scalar_...  10.2 us
    all_to_all x1, blocking collectives, body(): near = lax.all_to_all(lists, 'near', 0, 0, tiled=True)  9.43 us
    pallas_call x1, Pallas kernels, mix_early(): pl.pallas_call(kernel, grid_spec=pltpu.PrefetchScalarGridSpec(num_scalar_...  9.39 us
    pallas_call x2, Pallas kernels, mix_late(): pl.pallas_call(kernel, grid_spec=pltpu.PrefetchScalarGridSpec(num_scalar_...  8.29 us
    all_to_all x4, waiting for transfers between devices, over_lines(): incoming = lax.all_to_all(outgoing, 'y', 0, 0, tiled=True)  5.96 us
  transfers between devices with their start and end apart: 23, of which 17 were waited for; matrix products, arithmetic and copies ran while one was open for 3% of the time, Pallas kernels for 13%

profile of v9, /device:TPU:1, one launch (start us, length us, event | category | flops | bytes accessed | tf_op | source)
XLA Modules:
  0.0 178.2 jit_solution(2912213409927439606)
XLA Ops:
  0.0 11.9 %collective-permute-start.1 = (bf16[240,1024]{1,0:T(8,128)(2,1)}, bf16[240,1024]{1,0:T(8,128)(2,1)S(1)}, u32[]{:S(2)}, u32[]{:S(2)}) collective-permute-start(bf16[240,1024]{1,0:T(8,128)(2,1)} %bitcast.183), channel_id=1, source_target_pairs={{0,15},{1,0},{2,1},{3,2},{4,3},{5,4},{6,5},{7,6},{8,7},{9,8},{10,9... | collective-permute-start | bytes 1474568 | tf_op jit(solution)/shard_map/ppermute | solution.py:211
  14.8 9.4 %all_to_all.30 = s32[4,4,4,2]{1,2,3,0:T(4,128)S(1)} all-to-all(s32[4,4,4,2]{1,2,3,0:T(4,128)S(1)} %copy.11), channel_id=1, replica_groups=mesh['segment'=8,'y'=4,'far'=4,'near'=4] {'near'}, dimensions={0} | all-to-all | bytes 1024 | tf_op jit(solution)/shard_map/all_to_all | solution.py:250
  24.2 2.8 %collective-permute-done.refs_1_ = bf16[240,1024]{1,0:T(8,128)(2,1)S(1)} collective-permute-done((bf16[240,1024]{1,0:T(8,128)(2,1)}, bf16[240,1024]{1,0:T(8,128)(2,1)S(1)}, u32[]{:S(2)}, u32[]{:S(2)}) %collective-permute-start) | collective-permute-done | bytes 491552 | tf_op jit(solution)/shard_map/ppermute | solution.py:211
  27.8 5.8 %all-to-all-start.1 = ((s32[4,4,4,2]{1,2,3,0:T(4,128)}), s32[4,4,4,2]{1,2,3,0:T(4,128)S(1)}, u32[]{:S(2)}, u32[]{:S(2)}) async-start(s32[4,4,4,2]{1,2,3,0:T(4,128)} %copy.12), calls=%async_computation.1 | async-start | bytes 32768 | tf_op jit(solution)/shard_map/all_to_all | solution.py:258
  35.6 5.9 %collective-permute-start.3 = (bf16[240,1024]{1,0:T(8,128)(2,1)S(1)}, bf16[240,1024]{1,0:T(8,128)(2,1)S(1)}, u32[]{:S(2)}, u32[]{:S(2)}) collective-permute-start(bf16[240,1024]{1,0:T(8,128)(2,1)S(1)} %collective-permute-done.1.refs_2_), channel_id=1, source_target_pairs={{0,15},{1,0},{2,1},{3,2},{4,3},{5,4},{6,5},{7,6},{8,7},{9,8},{10,9... | collective-permute-start | bytes 1474568 | tf_op jit(solution)/shard_map/ppermute | solution.py:211
  41.5 3.6 %all-to-all-done.1 = s32[4,4,4,2]{1,2,3,0:T(4,128)S(1)} async-done(((s32[4,4,4,2]{1,2,3,0:T(4,128)}), s32[4,4,4,2]{1,2,3,0:T(4,128)S(1)}, u32[]{:S(2)}, u32[]{:S(2)}) %all-to-all-start.1) | async-done | bytes 544 | tf_op jit(solution)/shard_map/all_to_all | solution.py:258
  46.5 2.3 %pick_part.4 = bf16[4,6,240,128]{3,2,1,0:T(8,128)(2,1)} custom-call(s32[128]{0:T(128)S(1)} %reshape.231.ids_ref, s32[1]{0:T(128)} %bitcast.34.here_ref, bf16[240,1024]{1,0:T(8,128)(2,1)S(1)} %bitcast.185, bf16[240,1024]{1,0:T(8,128)(2,1)S(1)} %collective-permute-done.refs_1_, bf16[240,1024]{1,0:T(8,128)(2,1)S(1)} %collective-permute-done.1.refs_2_), custom_call_target="tpu_custom_call" | custom-call | flops 12000000000 | bytes 2949120 | tf_op jit(solution)/shard_map/pick_part/pallas_call | solution.py:50
  51.3 5.3 %collective-permute-start.6 = (bf16[240,1024]{1,0:T(8,128)(2,1)S(1)}, bf16[240,1024]{1,0:T(8,128)(2,1)}, u32[]{:S(2)}, u32[]{:S(2)}) collective-permute-start(bf16[240,1024]{1,0:T(8,128)(2,1)S(1)} %collective-permute-done.3.refs_1_), channel_id=1, source_target_pairs={{0,15},{1,0},{2,1},{3,2},{4,3},{5,4},{6,5},{7,6},{8,7},{9,8},{10,9... | collective-permute-start | bytes 1474568 | tf_op jit(solution)/shard_map/ppermute | solution.py:211
  56.6 4.2 %all-to-all-start.2 = ((bf16[4,6,240,128]{3,2,1,0:T(8,128)(2,1)}), bf16[4,6,240,128]{3,2,1,0:T(8,128)(2,1)S(1)}, u32[]{:S(2)}, u32[]{:S(2)}) async-start(bf16[4,6,240,128]{3,2,1,0:T(8,128)(2,1)} %pick_part.4), calls=%async_computation.2 | async-start | bytes 2949120 | tf_op jit(solution)/shard_map/all_to_all | solution.py:215
  65.0 4.2 %collective-permute-start.7 = (bf16[240,1024]{1,0:T(8,128)(2,1)}, bf16[240,1024]{1,0:T(8,128)(2,1)S(1)}, u32[]{:S(2)}, u32[]{:S(2)}) collective-permute-start(bf16[240,1024]{1,0:T(8,128)(2,1)} %collective-permute-done.6.refs_3_), channel_id=1, source_target_pairs={{0,15},{1,0},{2,1},{3,2},{4,3},{5,4},{6,5},{7,6},{8,7},{9,8},{10,9... | collective-permute-start | bytes 1474568 | tf_op jit(solution)/shard_map/ppermute | solution.py:211
  69.2 2.9 %pick_part.5 = bf16[4,8,240,128]{3,2,1,0:T(8,128)(2,1)} custom-call(s32[128]{0:T(128)S(1)} %reshape.231.ids_ref, s32[1]{0:T(128)} %bitcast.34.here_ref, bf16[240,1024]{1,0:T(8,128)(2,1)S(1)} %collective-permute-done.2.refs_0_, bf16[240,1024]{1,0:T(8,128)(2,1)S(1)} %collective-permute-done.3.refs_1_, bf16[240,1024]{1,0:T(8,128)(2,1)} %collective-permute-done.4.refs_2_, ...), custom_call_target="tpu_custom_call" | custom-call | flops 12000000000 | bytes 3932160 | tf_op jit(solution)/shard_map/pick_part/pallas_call | solution.py:50
  72.1 2.3 %collective-permute-done.5.refs_0_ = bf16[240,1024]{1,0:T(8,128)(2,1)S(1)} collective-permute-done((bf16[240,1024]{1,0:T(8,128)(2,1)}, bf16[240,1024]{1,0:T(8,128)(2,1)S(1)}, u32[]{:S(2)}, u32[]{:S(2)}) %collective-permute-start.5) | collective-permute-done | bytes 491552 | tf_op jit(solution)/shard_map/ppermute | solution.py:211
  76.5 3.1 %collective-permute-start.8 = (bf16[240,1024]{1,0:T(8,128)(2,1)S(1)}, bf16[240,1024]{1,0:T(8,128)(2,1)S(1)}, u32[]{:S(2)}, u32[]{:S(2)}) collective-permute-start(bf16[240,1024]{1,0:T(8,128)(2,1)S(1)} %collective-permute-done.5.refs_0_), channel_id=1, source_target_pairs={{0,1},{1,2},{2,3},{3,4},{4,5},{5,6},{6,7},{7,8},{8,9},{9,10},{10,1... | collective-permute-start | bytes 1474568 | tf_op jit(solution)/shard_map/ppermute | solution.py:211
  79.6 3.4 %collective-permute-start.9 = (bf16[240,1024]{1,0:T(8,128)(2,1)S(1)}, bf16[240,1024]{1,0:T(8,128)(2,1)}, u32[]{:S(2)}, u32[]{:S(2)}) collective-permute-start(bf16[240,1024]{1,0:T(8,128)(2,1)S(1)} %collective-permute-done.7.refs_1_), channel_id=1, source_target_pairs={{0,15},{1,0},{2,1},{3,2},{4,3},{5,4},{6,5},{7,6},{8,7},{9,8},{10,9... | collective-permute-start | bytes 1474568 | tf_op jit(solution)/shard_map/ppermute | solution.py:211
  83.0 4.4 %all-to-all-start.3 = ((bf16[4,8,240,128]{3,2,1,0:T(8,128)(2,1)}), bf16[4,8,240,128]{3,2,1,0:T(8,128)(2,1)}, u32[]{:S(2)}, u32[]{:S(2)}) async-start(bf16[4,8,240,128]{3,2,1,0:T(8,128)(2,1)} %pick_part.5), calls=%async_computation.3 | async-start | bytes 3932160 | tf_op jit(solution)/shard_map/all_to_all | solution.py:215
  89.4 4.5 %collective-permute-start.11 = (bf16[240,1024]{1,0:T(8,128)(2,1)}, bf16[240,1024]{1,0:T(8,128)(2,1)S(1)}, u32[]{:S(2)}, u32[]{:S(2)}) collective-permute-start(bf16[240,1024]{1,0:T(8,128)(2,1)} %collective-permute-done.9.refs_3_), channel_id=1, source_target_pairs={{0,15},{1,0},{2,1},{3,2},{4,3},{5,4},{6,5},{7,6},{8,7},{9,8},{10,9... | collective-permute-start | bytes 1474568 | tf_op jit(solution)/shard_map/ppermute | solution.py:211
  94.0 2.9 %pick_part.6 = bf16[4,8,240,128]{3,2,1,0:T(8,128)(2,1)} custom-call(s32[128]{0:T(128)S(1)} %reshape.231.ids_ref, s32[1]{0:T(128)} %bitcast.34.here_ref, bf16[240,1024]{1,0:T(8,128)(2,1)S(1)} %collective-permute-done.5.refs_0_, bf16[240,1024]{1,0:T(8,128)(2,1)S(1)} %collective-permute-done.7.refs_1_, bf16[240,1024]{1,0:T(8,128)(2,1)S(1)} %collective-permute-done.8.refs_2_, ...), custom_call_target="tpu_custom_call" | custom-call | flops 12000000000 | bytes 3932160 | tf_op jit(solution)/shard_map/pick_part/pallas_call | solution.py:50
  98.6 2.2 %collective-permute-done.11.refs_1_ = bf16[240,1024]{1,0:T(8,128)(2,1)S(1)} collective-permute-done((bf16[240,1024]{1,0:T(8,128)(2,1)}, bf16[240,1024]{1,0:T(8,128)(2,1)S(1)}, u32[]{:S(2)}, u32[]{:S(2)}) %collective-permute-start.11) | collective-permute-done | bytes 491552 | tf_op jit(solution)/shard_map/ppermute | solution.py:211
  100.9 4.2 %collective-permute-start.12 = (bf16[240,1024]{1,0:T(8,128)(2,1)S(1)}, bf16[240,1024]{1,0:T(8,128)(2,1)S(1)}, u32[]{:S(2)}, u32[]{:S(2)}) collective-permute-start(bf16[240,1024]{1,0:T(8,128)(2,1)S(1)} %collective-permute-done.10.refs_0_), channel_id=1, source_target_pairs={{0,1},{1,2},{2,3},{3,4},{4,5},{5,6},{6,7},{7,8},{8,9},{9,10},{10,1... | collective-permute-start | bytes 1474568 | tf_op jit(solution)/shard_map/ppermute | solution.py:211
  105.1 2.3 %collective-permute-start.13 = (bf16[240,1024]{1,0:T(8,128)(2,1)S(1)}, bf16[240,1024]{1,0:T(8,128)(2,1)S(1)}, u32[]{:S(2)}, u32[]{:S(2)}) collective-permute-start(bf16[240,1024]{1,0:T(8,128)(2,1)S(1)} %collective-permute-done.11.refs_1_), channel_id=1, source_target_pairs={{0,15},{1,0},{2,1},{3,2},{4,3},{5,4},{6,5},{7,6},{8,7},{9,8},{10,9... | collective-permute-start | bytes 1474568 | tf_op jit(solution)/shard_map/ppermute | solution.py:211
  107.4 4.4 %all-to-all-start.4 = ((bf16[4,8,240,128]{3,2,1,0:T(8,128)(2,1)}), bf16[4,8,240,128]{3,2,1,0:T(8,128)(2,1)}, u32[]{:S(2)}, u32[]{:S(2)}) async-start(bf16[4,8,240,128]{3,2,1,0:T(8,128)(2,1)} %pick_part.6), calls=%async_computation.4 | async-start | bytes 3932160 | tf_op jit(solution)/shard_map/all_to_all | solution.py:215
  112.0 3.2 %collective-permute-done.13.refs_3_ = bf16[240,1024]{1,0:T(8,128)(2,1)S(1)} collective-permute-done((bf16[240,1024]{1,0:T(8,128)(2,1)S(1)}, bf16[240,1024]{1,0:T(8,128)(2,1)S(1)}, u32[]{:S(2)}, u32[]{:S(2)}) %collective-permute-start.13) | collective-permute-done | bytes 491552 | tf_op jit(solution)/shard_map/ppermute | solution.py:211
  115.2 3.4 %collective-permute-start.14 = (bf16[112,1024]{1,0:T(8,128)(2,1)S(1)}, bf16[112,1024]{1,0:T(8,128)(2,1)S(1)}, u32[]{:S(2)}, u32[]{:S(2)}) collective-permute-start(bf16[112,1024]{1,0:T(8,128)(2,1)S(1)} %slice.6), channel_id=1, source_target_pairs={{0,1},{1,2},{2,3},{3,4},{4,5},{5,6},{6,7},{7,8},{8,9},{9,10},{10,1... | collective-permute-start | bytes 688136 | tf_op jit(solution)/shard_map/ppermute | solution.py:211
  118.6 3.1 %collective-permute-start.15 = (bf16[128,1024]{1,0:T(8,128)(2,1)S(1)}, bf16[128,1024]{1,0:T(8,128)(2,1)S(1)}, u32[]{:S(2)}, u32[]{:S(2)}) collective-permute-start(bf16[128,1024]{1,0:T(8,128)(2,1)S(1)} %slice.7), channel_id=1, source_target_pairs={{0,15},{1,0},{2,1},{3,2},{4,3},{5,4},{6,5},{7,6},{8,7},{9,8},{10,9... | collective-permute-start | bytes 786440 | tf_op jit(solution)/shard_map/ppermute | solution.py:211
  123.2 2.9 %collective-permute-done.15.refs_5_ = bf16[128,1024]{1,0:T(8,128)(2,1)S(1)} collective-permute-done((bf16[128,1024]{1,0:T(8,128)(2,1)S(1)}, bf16[128,1024]{1,0:T(8,128)(2,1)S(1)}, u32[]{:S(2)}, u32[]{:S(2)}) %collective-permute-start.15) | collective-permute-done | bytes 262176 | tf_op jit(solution)/shard_map/ppermute | solution.py:211
  129.7 4.2 %all-to-all-start.5 = ((bf16[4,10,240,128]{3,2,1,0:T(8,128)(2,1)}), bf16[4,10,240,128]{3,2,1,0:T(8,128)(2,1)S(1)}, u32[]{:S(2)}, u32[]{:S(2)}) async-start(bf16[4,10,240,128]{3,2,1,0:T(8,128)(2,1)} %copy-done), calls=%async_computation.5 | async-start | bytes 4915200 | tf_op jit(solution)/shard_map/all_to_all | solution.py:215
  138.8 9.4 %mix_early.1.early_ref = f32[240,1024]{1,0:T(8,128)S(1)} custom-call(s32[128]{0:T(128)S(1)} %select_select_fusion.codes_ref, bf16[24,240,128]{2,1,0:T(8,128)(2,1)S(1)} %bitcast.180, bf16[32,240,128]{2,1,0:T(8,128)(2,1)} %bitcast.36.refs_1_, bf16[32,240,128]{2,1,0:T(8,128)(2,1)} %bitcast.37.refs_2_, bf16[8,16,128,128]{3,2,1,0:T(8,128)(2,1)} %bitcast.186), custom_call_target="tpu_custom_call" | custom-call | flops 10000000000 | bytes 9601024 | tf_op jit(solution)/shard_map/mix_early/pallas_call | solution.py:116
  148.2 6.0 %all-to-all-done.5 = bf16[4,10,240,128]{3,2,1,0:T(8,128)(2,1)S(1)} async-done(((bf16[4,10,240,128]{3,2,1,0:T(8,128)(2,1)}), bf16[4,10,240,128]{3,2,1,0:T(8,128)(2,1)S(1)}, u32[]{:S(2)}, u32[]{:S(2)}) %all-to-all-start.5) | async-done | bytes 2457632 | tf_op jit(solution)/shard_map/all_to_all | solution.py:215
  154.1 4.6 %mix_late.2 = bf16[240,640]{1,0:T(8,128)(2,1)S(1)} custom-call(s32[128]{0:T(128)S(1)} %reshape.228.place_ref, s32[128]{0:T(128)S(1)} %reshape.229.which_ref, s32[8]{0:T(128)S(1)} %get-tuple-element.47.count_ref, f32[240,1024]{1,0:T(8,128)S(1)} %mix_early.1.early_ref, bf16[40,240,128]{2,1,0:T(8,128)(2,1)S(1)} %bitcast.178, ...), custom_call_target="tpu_custom_call" | custom-call | flops 629145600 | bytes 5079040 | tf_op jit(solution)/shard_map/mix_late/pallas_call | solution.py:182
  158.7 12.4 %collective-permute-start.16 = (bf16[240,640]{1,0:T(8,128)(2,1)S(1)}, bf16[240,640]{1,0:T(8,128)(2,1)S(1)}, u32[]{:S(2)}, u32[]{:S(2)}) collective-permute-start(bf16[240,640]{1,0:T(8,128)(2,1)S(1)} %mix_late.2), channel_id=1, source_target_pairs={{0,64},{64,128},{128,192},{192,256},{256,320},{320,384},{384,448},... | collective-permute-start | bytes 921608 | tf_op jit(solution)/shard_map/ppermute | solution.py:211
  171.2 3.7 %mix_late.3 = bf16[240,384]{1,0:T(8,128)(2,1)S(1)} custom-call(s32[128]{0:T(128)S(1)} %reshape.228.place_ref, s32[128]{0:T(128)S(1)} %reshape.229.which_ref, s32[8]{0:T(128)S(1)} %get-tuple-element.47.count_ref, f32[240,1024]{1,0:T(8,128)S(1)} %mix_early.1.early_ref, bf16[40,240,128]{2,1,0:T(8,128)(2,1)S(1)} %bitcast.179, ...), custom_call_target="tpu_custom_call" | custom-call | flops 377487360 | bytes 4030464 | tf_op jit(solution)/shard_map/mix_late/pallas_call | solution.py:182
  174.9 2.5 %collective-permute-done.17 = bf16[240,384]{1,0:T(8,128)(2,1)S(1)} collective-permute-done((bf16[240,384]{1,0:T(8,128)(2,1)S(1)}, bf16[240,384]{1,0:T(8,128)(2,1)S(1)}, u32[]{:S(2)}, u32[]{:S(2)}) %collective-permute-start.17) | collective-permute-done | bytes 184352 | tf_op jit(solution)/shard_map/ppermute | solution.py:211
  (82 shorter events, 30.3 us)
Async XLA Ops:
  0.0 24.2 %collective-permute-start.1 = (bf16[240,1024]{1,0:T(8,128)(2,1)}, bf16[240,1024]{1,0:T(8,128)(2,1)S(1)}, u32[]{:S(2)}, u32[]{:S(2)}) collective-permute-start(bf16[240,1024]{1,0:T(8,128)(2,1)} %bitcast.183), channel_id=1, source_target_pairs={{0,15},{1,0},{2,1},{3,2},{4,3},{5,4},{6,5},{7,6},{8,7},{9,8},{10,9... | collective-permute-start | bytes 1474568 | tf_op jit(solution)/shard_map/ppermute | solution.py:211
  12.0 15.1 %collective-permute-start = (bf16[240,1024]{1,0:T(8,128)(2,1)}, bf16[240,1024]{1,0:T(8,128)(2,1)S(1)}, u32[]{:S(2)}, u32[]{:S(2)}) collective-permute-start(bf16[240,1024]{1,0:T(8,128)(2,1)} %bitcast.184), channel_id=1, source_target_pairs={{0,1},{1,2},{2,3},{3,4},{4,5},{5,6},{6,7},{7,8},{8,9},{9,10},{10,1... | collective-permute-start | bytes 1474568 | tf_op jit(solution)/shard_map/ppermute | solution.py:211
  27.8 17.4 %all-to-all-start.1 = ((s32[4,4,4,2]{1,2,3,0:T(4,128)}), s32[4,4,4,2]{1,2,3,0:T(4,128)S(1)}, u32[]{:S(2)}, u32[]{:S(2)}) async-start(s32[4,4,4,2]{1,2,3,0:T(4,128)} %copy.12), calls=%async_computation.1 | async-start | bytes 32768 | tf_op jit(solution)/shard_map/all_to_all | solution.py:258
  33.6 15.5 %collective-permute-start.2 = (bf16[240,1024]{1,0:T(8,128)(2,1)S(1)}, bf16[240,1024]{1,0:T(8,128)(2,1)S(1)}, u32[]{:S(2)}, u32[]{:S(2)}) collective-permute-start(bf16[240,1024]{1,0:T(8,128)(2,1)S(1)} %collective-permute-done.refs_1_), channel_id=1, source_target_pairs={{0,1},{1,2},{2,3},{3,4},{4,5},{5,6},{6,7},{7,8},{8,9},{9,10},{10,1... | collective-permute-start | bytes 1474568 | tf_op jit(solution)/shard_map/ppermute | solution.py:211
  35.6 13.8 %collective-permute-start.3 = (bf16[240,1024]{1,0:T(8,128)(2,1)S(1)}, bf16[240,1024]{1,0:T(8,128)(2,1)S(1)}, u32[]{:S(2)}, u32[]{:S(2)}) collective-permute-start(bf16[240,1024]{1,0:T(8,128)(2,1)S(1)} %collective-permute-done.1.refs_2_), channel_id=1, source_target_pairs={{0,15},{1,0},{2,1},{3,2},{4,3},{5,4},{6,5},{7,6},{8,7},{9,8},{10,9... | collective-permute-start | bytes 1474568 | tf_op jit(solution)/shard_map/ppermute | solution.py:211
  45.5 1.0 copy-start.4
  49.4 13.3 %collective-permute-start.4 = (bf16[240,1024]{1,0:T(8,128)(2,1)S(1)}, bf16[240,1024]{1,0:T(8,128)(2,1)}, u32[]{:S(2)}, u32[]{:S(2)}) collective-permute-start(bf16[240,1024]{1,0:T(8,128)(2,1)S(1)} %collective-permute-done.2.refs_0_), channel_id=1, source_target_pairs={{0,1},{1,2},{2,3},{3,4},{4,5},{5,6},{6,7},{7,8},{8,9},{9,10},{10,1... | collective-permute-start | bytes 1474568 | tf_op jit(solution)/shard_map/ppermute | solution.py:211
  51.3 13.7 %collective-permute-start.6 = (bf16[240,1024]{1,0:T(8,128)(2,1)S(1)}, bf16[240,1024]{1,0:T(8,128)(2,1)}, u32[]{:S(2)}, u32[]{:S(2)}) collective-permute-start(bf16[240,1024]{1,0:T(8,128)(2,1)S(1)} %collective-permute-done.3.refs_1_), channel_id=1, source_target_pairs={{0,15},{1,0},{2,1},{3,2},{4,3},{5,4},{6,5},{7,6},{8,7},{9,8},{10,9... | collective-permute-start | bytes 1474568 | tf_op jit(solution)/shard_map/ppermute | solution.py:211
  56.6 19.8 %all-to-all-start.2 = ((bf16[4,6,240,128]{3,2,1,0:T(8,128)(2,1)}), bf16[4,6,240,128]{3,2,1,0:T(8,128)(2,1)S(1)}, u32[]{:S(2)}, u32[]{:S(2)}) async-start(bf16[4,6,240,128]{3,2,1,0:T(8,128)(2,1)} %pick_part.4), calls=%async_computation.2 | async-start | bytes 2949120 | tf_op jit(solution)/shard_map/all_to_all | solution.py:215
  62.7 11.7 %collective-permute-start.5 = (bf16[240,1024]{1,0:T(8,128)(2,1)}, bf16[240,1024]{1,0:T(8,128)(2,1)S(1)}, u32[]{:S(2)}, u32[]{:S(2)}) collective-permute-start(bf16[240,1024]{1,0:T(8,128)(2,1)} %collective-permute-done.4.refs_2_), channel_id=1, source_target_pairs={{0,1},{1,2},{2,3},{3,4},{4,5},{5,6},{6,7},{7,8},{8,9},{9,10},{10,1... | collective-permute-start | bytes 1474568 | tf_op jit(solution)/shard_map/ppermute | solution.py:211
  65.0 11.5 %collective-permute-start.7 = (bf16[240,1024]{1,0:T(8,128)(2,1)}, bf16[240,1024]{1,0:T(8,128)(2,1)S(1)}, u32[]{:S(2)}, u32[]{:S(2)}) collective-permute-start(bf16[240,1024]{1,0:T(8,128)(2,1)} %collective-permute-done.6.refs_3_), channel_id=1, source_target_pairs={{0,15},{1,0},{2,1},{3,2},{4,3},{5,4},{6,5},{7,6},{8,7},{9,8},{10,9... | collective-permute-start | bytes 1474568 | tf_op jit(solution)/shard_map/ppermute | solution.py:211
  76.5 6.5 %copy-start.1 = (bf16[4,6,240,128]{3,2,1,0:T(8,128)(2,1)}, bf16[4,6,240,128]{3,2,1,0:T(8,128)(2,1)S(1)}, u32[]{:S(2)}) copy-start(bf16[4,6,240,128]{3,2,1,0:T(8,128)(2,1)S(1)} %all-to-all-done.2) | copy-start | bytes 4423684
  76.5 11.0 %collective-permute-start.8 = (bf16[240,1024]{1,0:T(8,128)(2,1)S(1)}, bf16[240,1024]{1,0:T(8,128)(2,1)S(1)}, u32[]{:S(2)}, u32[]{:S(2)}) collective-permute-start(bf16[240,1024]{1,0:T(8,128)(2,1)S(1)} %collective-permute-done.5.refs_0_), channel_id=1, source_target_pairs={{0,1},{1,2},{2,3},{3,4},{4,5},{5,6},{6,7},{7,8},{8,9},{9,10},{10,1... | collective-permute-start | bytes 1474568 | tf_op jit(solution)/shard_map/ppermute | solution.py:211
  79.6 9.9 %collective-permute-start.9 = (bf16[240,1024]{1,0:T(8,128)(2,1)S(1)}, bf16[240,1024]{1,0:T(8,128)(2,1)}, u32[]{:S(2)}, u32[]{:S(2)}) collective-permute-start(bf16[240,1024]{1,0:T(8,128)(2,1)S(1)} %collective-permute-done.7.refs_1_), channel_id=1, source_target_pairs={{0,15},{1,0},{2,1},{3,2},{4,3},{5,4},{6,5},{7,6},{8,7},{9,8},{10,9... | collective-permute-start | bytes 1474568 | tf_op jit(solution)/shard_map/ppermute | solution.py:211
  83.0 24.4 %all-to-all-start.3 = ((bf16[4,8,240,128]{3,2,1,0:T(8,128)(2,1)}), bf16[4,8,240,128]{3,2,1,0:T(8,128)(2,1)}, u32[]{:S(2)}, u32[]{:S(2)}) async-start(bf16[4,8,240,128]{3,2,1,0:T(8,128)(2,1)} %pick_part.5), calls=%async_computation.3 | async-start | bytes 3932160 | tf_op jit(solution)/shard_map/all_to_all | solution.py:215
  87.4 11.2 %collective-permute-start.10 = (bf16[240,1024]{1,0:T(8,128)(2,1)S(1)}, bf16[240,1024]{1,0:T(8,128)(2,1)S(1)}, u32[]{:S(2)}, u32[]{:S(2)}) collective-permute-start(bf16[240,1024]{1,0:T(8,128)(2,1)S(1)} %collective-permute-done.8.refs_2_), channel_id=1, source_target_pairs={{0,1},{1,2},{2,3},{3,4},{4,5},{5,6},{6,7},{7,8},{8,9},{9,10},{10,1... | collective-permute-start | bytes 1474568 | tf_op jit(solution)/shard_map/ppermute | solution.py:211
  89.4 11.4 %collective-permute-start.11 = (bf16[240,1024]{1,0:T(8,128)(2,1)}, bf16[240,1024]{1,0:T(8,128)(2,1)S(1)}, u32[]{:S(2)}, u32[]{:S(2)}) collective-permute-start(bf16[240,1024]{1,0:T(8,128)(2,1)} %collective-permute-done.9.refs_3_), channel_id=1, source_target_pairs={{0,15},{1,0},{2,1},{3,2},{4,3},{5,4},{6,5},{7,6},{8,7},{9,8},{10,9... | collective-permute-start | bytes 1474568 | tf_op jit(solution)/shard_map/ppermute | solution.py:211
  100.9 11.2 %collective-permute-start.12 = (bf16[240,1024]{1,0:T(8,128)(2,1)S(1)}, bf16[240,1024]{1,0:T(8,128)(2,1)S(1)}, u32[]{:S(2)}, u32[]{:S(2)}) collective-permute-start(bf16[240,1024]{1,0:T(8,128)(2,1)S(1)} %collective-permute-done.10.refs_0_), channel_id=1, source_target_pairs={{0,1},{1,2},{2,3},{3,4},{4,5},{5,6},{6,7},{7,8},{8,9},{9,10},{10,1... | collective-permute-start | bytes 1474568 | tf_op jit(solution)/shard_map/ppermute | solution.py:211
  105.1 10.1 %collective-permute-start.13 = (bf16[240,1024]{1,0:T(8,128)(2,1)S(1)}, bf16[240,1024]{1,0:T(8,128)(2,1)S(1)}, u32[]{:S(2)}, u32[]{:S(2)}) collective-permute-start(bf16[240,1024]{1,0:T(8,128)(2,1)S(1)} %collective-permute-done.11.refs_1_), channel_id=1, source_target_pairs={{0,15},{1,0},{2,1},{3,2},{4,3},{5,4},{6,5},{7,6},{8,7},{9,8},{10,9... | collective-permute-start | bytes 1474568 | tf_op jit(solution)/shard_map/ppermute | solution.py:211
  107.4 14.4 %copy-start.5 = (s32[1,8,16]{2,1,0:T(8,128)S(1)}, s32[1,8,16]{2,1,0:T(8,128)}, u32[]{:S(2)}) copy-start(s32[1,8,16]{2,1,0:T(8,128)} %param.8) | copy-start | bytes 1540
  107.4 22.3 %all-to-all-start.4 = ((bf16[4,8,240,128]{3,2,1,0:T(8,128)(2,1)}), bf16[4,8,240,128]{3,2,1,0:T(8,128)(2,1)}, u32[]{:S(2)}, u32[]{:S(2)}) async-start(bf16[4,8,240,128]{3,2,1,0:T(8,128)(2,1)} %pick_part.6), calls=%async_computation.4 | async-start | bytes 3932160 | tf_op jit(solution)/shard_map/all_to_all | solution.py:215
  115.2 8.0 %collective-permute-start.14 = (bf16[112,1024]{1,0:T(8,128)(2,1)S(1)}, bf16[112,1024]{1,0:T(8,128)(2,1)S(1)}, u32[]{:S(2)}, u32[]{:S(2)}) collective-permute-start(bf16[112,1024]{1,0:T(8,128)(2,1)S(1)} %slice.6), channel_id=1, source_target_pairs={{0,1},{1,2},{2,3},{3,4},{4,5},{5,6},{6,7},{7,8},{8,9},{9,10},{10,1... | collective-permute-start | bytes 688136 | tf_op jit(solution)/shard_map/ppermute | solution.py:211
  118.6 7.5 %collective-permute-start.15 = (bf16[128,1024]{1,0:T(8,128)(2,1)S(1)}, bf16[128,1024]{1,0:T(8,128)(2,1)S(1)}, u32[]{:S(2)}, u32[]{:S(2)}) collective-permute-start(bf16[128,1024]{1,0:T(8,128)(2,1)S(1)} %slice.7), channel_id=1, source_target_pairs={{0,15},{1,0},{2,1},{3,2},{4,3},{5,4},{6,5},{7,6},{8,7},{9,8},{10,9... | collective-permute-start | bytes 786440 | tf_op jit(solution)/shard_map/ppermute | solution.py:211
  128.3 1.4 copy-start
  129.7 24.4 %all-to-all-start.5 = ((bf16[4,10,240,128]{3,2,1,0:T(8,128)(2,1)}), bf16[4,10,240,128]{3,2,1,0:T(8,128)(2,1)S(1)}, u32[]{:S(2)}, u32[]{:S(2)}) async-start(bf16[4,10,240,128]{3,2,1,0:T(8,128)(2,1)} %copy-done), calls=%async_computation.5 | async-start | bytes 4915200 | tf_op jit(solution)/shard_map/all_to_all | solution.py:215
  137.4 1.4 copy-start.2
  138.8 15.4 %copy-start.3 = (f32[1,1024]{1,0:T(1,128)S(1)}, f32[1,1024]{1,0:T(1,128)}, u32[]{:S(2)}) copy-start(f32[1,1024]{1,0:T(1,128)} %param.7) | copy-start | bytes 12292
  158.7 18.6 %collective-permute-start.16 = (bf16[240,640]{1,0:T(8,128)(2,1)S(1)}, bf16[240,640]{1,0:T(8,128)(2,1)S(1)}, u32[]{:S(2)}, u32[]{:S(2)}) collective-permute-start(bf16[240,640]{1,0:T(8,128)(2,1)S(1)} %mix_late.2), channel_id=1, source_target_pairs={{0,64},{64,128},{128,192},{192,256},{256,320},{320,384},{384,448},... | collective-permute-start | bytes 921608 | tf_op jit(solution)/shard_map/ppermute | solution.py:211
  174.8 2.5 %collective-permute-start.17 = (bf16[240,384]{1,0:T(8,128)(2,1)S(1)}, bf16[240,384]{1,0:T(8,128)(2,1)S(1)}, u32[]{:S(2)}, u32[]{:S(2)}) collective-permute-start(bf16[240,384]{1,0:T(8,128)(2,1)S(1)} %mix_late.3), channel_id=1, source_target_pairs={{0,64},{64,128},{128,192},{192,256},{256,320},{320,384},{384,448},... | collective-permute-start | bytes 552968 | tf_op jit(solution)/shard_map/ppermute | solution.py:211

commit v10 on v9

--- a/solution.py
+++ b/solution.py
@@ -186,7 +186,7 @@
             grid=(count,),
             in_specs=[
                 pl.BlockSpec((rows, BLOCK), lambda j, *s: (0, j + first)),
-                pl.BlockSpec((size, rows, BLOCK), lambda j, *s: (0, 0, 0)),
+                pl.BlockSpec(memory_space=pltpu.VMEM),
                 pl.BlockSpec(
                     (1, taps, BLOCK, BLOCK), lambda j, *s: (j + first, 0, 0, 0)
                 ),

time: 181 us -> 181 us (level)
  no operation moved by 1% of the time
where the time goes in v10:
time: 181 us; the launch traced here: 178 us
  starting transfers between devices  96.1 us (53%)
  waiting for transfers between devices  33.6 us (19%)
  Pallas kernels  28.3 us (16%)
  blocking collectives  9.43 us (5%)
  local copies, waits for them, and re-layouts  8.67 us (5%)
    ppermute x18, starting transfers between devices, shifted(): lax.ppermute(value, axis, [(i, (i + by) % count) for i in range(count)])  73.1 us
    ppermute x18, waiting for transfers between devices, shifted(): lax.ppermute(value, axis, [(i, (i + by) % count) for i in range(count)])  24.1 us
    all_to_all x4, starting transfers between devices, over_lines(): incoming = lax.all_to_all(outgoing, 'y', 0, 0, tiled=True)  17.3 us
    pallas_call x4, Pallas kernels, pick_call(): pl.pallas_call(kernel, grid_spec=pltpu.PrefetchScalarGridSpec(num_scalar_...  10.2 us
    all_to_all x1, blocking collectives, body(): near = lax.all_to_all(lists, 'near', 0, 0, tiled=True)  9.43 us
    pallas_call x1, Pallas kernels, mix_early(): pl.pallas_call(kernel, grid_spec=pltpu.PrefetchScalarGridSpec(num_scalar_...  9.4 us
    pallas_call x2, Pallas kernels, mix_late(): pl.pallas_call(kernel, grid_spec=pltpu.PrefetchScalarGridSpec(num_scalar_...  8.7 us
    all_to_all x4, waiting for transfers between devices, over_lines(): incoming = lax.all_to_all(outgoing, 'y', 0, 0, tiled=True)  5.95 us
  transfers between devices with their start and end apart: 23, of which 17 were waited for; matrix products, arithmetic and copies ran while one was open for 3% of the time, Pallas kernels for 13%

profile of v10, /device:TPU:1, one launch (start us, length us, event | category | flops | bytes accessed | tf_op | source)
XLA Modules:
  0.0 178.2 jit_solution(2912213409927439606)
XLA Ops:
  0.0 11.9 %collective-permute-start.1 = (bf16[240,1024]{1,0:T(8,128)(2,1)}, bf16[240,1024]{1,0:T(8,128)(2,1)S(1)}, u32[]{:S(2)}, u32[]{:S(2)}) collective-permute-start(bf16[240,1024]{1,0:T(8,128)(2,1)} %bitcast.183), channel_id=1, source_target_pairs={{0,15},{1,0},{2,1},{3,2},{4,3},{5,4},{6,5},{7,6},{8,7},{9,8},{10,9... | collective-permute-start | bytes 1474568 | tf_op jit(solution)/shard_map/ppermute | solution.py:211
  14.8 9.4 %all_to_all.30 = s32[4,4,4,2]{1,2,3,0:T(4,128)S(1)} all-to-all(s32[4,4,4,2]{1,2,3,0:T(4,128)S(1)} %copy.11), channel_id=1, replica_groups=mesh['segment'=8,'y'=4,'far'=4,'near'=4] {'near'}, dimensions={0} | all-to-all | bytes 1024 | tf_op jit(solution)/shard_map/all_to_all | solution.py:250
  24.2 2.8 %collective-permute-done.refs_1_ = bf16[240,1024]{1,0:T(8,128)(2,1)S(1)} collective-permute-done((bf16[240,1024]{1,0:T(8,128)(2,1)}, bf16[240,1024]{1,0:T(8,128)(2,1)S(1)}, u32[]{:S(2)}, u32[]{:S(2)}) %collective-permute-start) | collective-permute-done | bytes 491552 | tf_op jit(solution)/shard_map/ppermute | solution.py:211
  27.8 5.8 %all-to-all-start.1 = ((s32[4,4,4,2]{1,2,3,0:T(4,128)}), s32[4,4,4,2]{1,2,3,0:T(4,128)S(1)}, u32[]{:S(2)}, u32[]{:S(2)}) async-start(s32[4,4,4,2]{1,2,3,0:T(4,128)} %copy.12), calls=%async_computation.1 | async-start | bytes 32768 | tf_op jit(solution)/shard_map/all_to_all | solution.py:258
  35.6 5.9 %collective-permute-start.3 = (bf16[240,1024]{1,0:T(8,128)(2,1)S(1)}, bf16[240,1024]{1,0:T(8,128)(2,1)S(1)}, u32[]{:S(2)}, u32[]{:S(2)}) collective-permute-start(bf16[240,1024]{1,0:T(8,128)(2,1)S(1)} %collective-permute-done.1.refs_2_), channel_id=1, source_target_pairs={{0,15},{1,0},{2,1},{3,2},{4,3},{5,4},{6,5},{7,6},{8,7},{9,8},{10,9... | collective-permute-start | bytes 1474568 | tf_op jit(solution)/shard_map/ppermute | solution.py:211
  41.5 3.6 %all-to-all-done.1 = s32[4,4,4,2]{1,2,3,0:T(4,128)S(1)} async-done(((s32[4,4,4,2]{1,2,3,0:T(4,128)}), s32[4,4,4,2]{1,2,3,0:T(4,128)S(1)}, u32[]{:S(2)}, u32[]{:S(2)}) %all-to-all-start.1) | async-done | bytes 544 | tf_op jit(solution)/shard_map/all_to_all | solution.py:258
  46.5 2.3 %pick_part.4 = bf16[4,6,240,128]{3,2,1,0:T(8,128)(2,1)} custom-call(s32[128]{0:T(128)S(1)} %reshape.231.ids_ref, s32[1]{0:T(128)} %bitcast.34.here_ref, bf16[240,1024]{1,0:T(8,128)(2,1)S(1)} %bitcast.185, bf16[240,1024]{1,0:T(8,128)(2,1)S(1)} %collective-permute-done.refs_1_, bf16[240,1024]{1,0:T(8,128)(2,1)S(1)} %collective-permute-done.1.refs_2_), custom_call_target="tpu_custom_call" | custom-call | flops 12000000000 | bytes 2949120 | tf_op jit(solution)/shard_map/pick_part/pallas_call | solution.py:50
  51.3 5.3 %collective-permute-start.6 = (bf16[240,1024]{1,0:T(8,128)(2,1)S(1)}, bf16[240,1024]{1,0:T(8,128)(2,1)}, u32[]{:S(2)}, u32[]{:S(2)}) collective-permute-start(bf16[240,1024]{1,0:T(8,128)(2,1)S(1)} %collective-permute-done.3.refs_1_), channel_id=1, source_target_pairs={{0,15},{1,0},{2,1},{3,2},{4,3},{5,4},{6,5},{7,6},{8,7},{9,8},{10,9... | collective-permute-start | bytes 1474568 | tf_op jit(solution)/shard_map/ppermute | solution.py:211
  56.6 4.2 %all-to-all-start.2 = ((bf16[4,6,240,128]{3,2,1,0:T(8,128)(2,1)}), bf16[4,6,240,128]{3,2,1,0:T(8,128)(2,1)S(1)}, u32[]{:S(2)}, u32[]{:S(2)}) async-start(bf16[4,6,240,128]{3,2,1,0:T(8,128)(2,1)} %pick_part.4), calls=%async_computation.2 | async-start | bytes 2949120 | tf_op jit(solution)/shard_map/all_to_all | solution.py:215
  65.0 4.2 %collective-permute-start.7 = (bf16[240,1024]{1,0:T(8,128)(2,1)}, bf16[240,1024]{1,0:T(8,128)(2,1)S(1)}, u32[]{:S(2)}, u32[]{:S(2)}) collective-permute-start(bf16[240,1024]{1,0:T(8,128)(2,1)} %collective-permute-done.6.refs_3_), channel_id=1, source_target_pairs={{0,15},{1,0},{2,1},{3,2},{4,3},{5,4},{6,5},{7,6},{8,7},{9,8},{10,9... | collective-permute-start | bytes 1474568 | tf_op jit(solution)/shard_map/ppermute | solution.py:211
  69.2 2.9 %pick_part.5 = bf16[4,8,240,128]{3,2,1,0:T(8,128)(2,1)} custom-call(s32[128]{0:T(128)S(1)} %reshape.231.ids_ref, s32[1]{0:T(128)} %bitcast.34.here_ref, bf16[240,1024]{1,0:T(8,128)(2,1)S(1)} %collective-permute-done.2.refs_0_, bf16[240,1024]{1,0:T(8,128)(2,1)S(1)} %collective-permute-done.3.refs_1_, bf16[240,1024]{1,0:T(8,128)(2,1)} %collective-permute-done.4.refs_2_, ...), custom_call_target="tpu_custom_call" | custom-call | flops 12000000000 | bytes 3932160 | tf_op jit(solution)/shard_map/pick_part/pallas_call | solution.py:50
  72.1 2.3 %collective-permute-done.5.refs_0_ = bf16[240,1024]{1,0:T(8,128)(2,1)S(1)} collective-permute-done((bf16[240,1024]{1,0:T(8,128)(2,1)}, bf16[240,1024]{1,0:T(8,128)(2,1)S(1)}, u32[]{:S(2)}, u32[]{:S(2)}) %collective-permute-start.5) | collective-permute-done | bytes 491552 | tf_op jit(solution)/shard_map/ppermute | solution.py:211
  76.5 3.1 %collective-permute-start.8 = (bf16[240,1024]{1,0:T(8,128)(2,1)S(1)}, bf16[240,1024]{1,0:T(8,128)(2,1)S(1)}, u32[]{:S(2)}, u32[]{:S(2)}) collective-permute-start(bf16[240,1024]{1,0:T(8,128)(2,1)S(1)} %collective-permute-done.5.refs_0_), channel_id=1, source_target_pairs={{0,1},{1,2},{2,3},{3,4},{4,5},{5,6},{6,7},{7,8},{8,9},{9,10},{10,1... | collective-permute-start | bytes 1474568 | tf_op jit(solution)/shard_map/ppermute | solution.py:211
  79.6 3.4 %collective-permute-start.9 = (bf16[240,1024]{1,0:T(8,128)(2,1)S(1)}, bf16[240,1024]{1,0:T(8,128)(2,1)}, u32[]{:S(2)}, u32[]{:S(2)}) collective-permute-start(bf16[240,1024]{1,0:T(8,128)(2,1)S(1)} %collective-permute-done.7.refs_1_), channel_id=1, source_target_pairs={{0,15},{1,0},{2,1},{3,2},{4,3},{5,4},{6,5},{7,6},{8,7},{9,8},{10,9... | collective-permute-start | bytes 1474568 | tf_op jit(solution)/shard_map/ppermute | solution.py:211
  83.0 4.4 %all-to-all-start.3 = ((bf16[4,8,240,128]{3,2,1,0:T(8,128)(2,1)}), bf16[4,8,240,128]{3,2,1,0:T(8,128)(2,1)}, u32[]{:S(2)}, u32[]{:S(2)}) async-start(bf16[4,8,240,128]{3,2,1,0:T(8,128)(2,1)} %pick_part.5), calls=%async_computation.3 | async-start | bytes 3932160 | tf_op jit(solution)/shard_map/all_to_all | solution.py:215
  89.4 4.5 %collective-permute-start.11 = (bf16[240,1024]{1,0:T(8,128)(2,1)}, bf16[240,1024]{1,0:T(8,128)(2,1)S(1)}, u32[]{:S(2)}, u32[]{:S(2)}) collective-permute-start(bf16[240,1024]{1,0:T(8,128)(2,1)} %collective-permute-done.9.refs_3_), channel_id=1, source_target_pairs={{0,15},{1,0},{2,1},{3,2},{4,3},{5,4},{6,5},{7,6},{8,7},{9,8},{10,9... | collective-permute-start | bytes 1474568 | tf_op jit(solution)/shard_map/ppermute | solution.py:211
  94.0 3.0 %pick_part.6 = bf16[4,8,240,128]{3,2,1,0:T(8,128)(2,1)} custom-call(s32[128]{0:T(128)S(1)} %reshape.231.ids_ref, s32[1]{0:T(128)} %bitcast.34.here_ref, bf16[240,1024]{1,0:T(8,128)(2,1)S(1)} %collective-permute-done.5.refs_0_, bf16[240,1024]{1,0:T(8,128)(2,1)S(1)} %collective-permute-done.7.refs_1_, bf16[240,1024]{1,0:T(8,128)(2,1)S(1)} %collective-permute-done.8.refs_2_, ...), custom_call_target="tpu_custom_call" | custom-call | flops 12000000000 | bytes 3932160 | tf_op jit(solution)/shard_map/pick_part/pallas_call | solution.py:50
  98.6 2.2 %collective-permute-done.11.refs_1_ = bf16[240,1024]{1,0:T(8,128)(2,1)S(1)} collective-permute-done((bf16[240,1024]{1,0:T(8,128)(2,1)}, bf16[240,1024]{1,0:T(8,128)(2,1)S(1)}, u32[]{:S(2)}, u32[]{:S(2)}) %collective-permute-start.11) | collective-permute-done | bytes 491552 | tf_op jit(solution)/shard_map/ppermute | solution.py:211
  100.9 4.2 %collective-permute-start.12 = (bf16[240,1024]{1,0:T(8,128)(2,1)S(1)}, bf16[240,1024]{1,0:T(8,128)(2,1)S(1)}, u32[]{:S(2)}, u32[]{:S(2)}) collective-permute-start(bf16[240,1024]{1,0:T(8,128)(2,1)S(1)} %collective-permute-done.10.refs_0_), channel_id=1, source_target_pairs={{0,1},{1,2},{2,3},{3,4},{4,5},{5,6},{6,7},{7,8},{8,9},{9,10},{10,1... | collective-permute-start | bytes 1474568 | tf_op jit(solution)/shard_map/ppermute | solution.py:211
  105.1 2.3 %collective-permute-start.13 = (bf16[240,1024]{1,0:T(8,128)(2,1)S(1)}, bf16[240,1024]{1,0:T(8,128)(2,1)S(1)}, u32[]{:S(2)}, u32[]{:S(2)}) collective-permute-start(bf16[240,1024]{1,0:T(8,128)(2,1)S(1)} %collective-permute-done.11.refs_1_), channel_id=1, source_target_pairs={{0,15},{1,0},{2,1},{3,2},{4,3},{5,4},{6,5},{7,6},{8,7},{9,8},{10,9... | collective-permute-start | bytes 1474568 | tf_op jit(solution)/shard_map/ppermute | solution.py:211
  107.4 4.4 %all-to-all-start.4 = ((bf16[4,8,240,128]{3,2,1,0:T(8,128)(2,1)}), bf16[4,8,240,128]{3,2,1,0:T(8,128)(2,1)}, u32[]{:S(2)}, u32[]{:S(2)}) async-start(bf16[4,8,240,128]{3,2,1,0:T(8,128)(2,1)} %pick_part.6), calls=%async_computation.4 | async-start | bytes 3932160 | tf_op jit(solution)/shard_map/all_to_all | solution.py:215
  112.0 3.2 %collective-permute-done.13.refs_3_ = bf16[240,1024]{1,0:T(8,128)(2,1)S(1)} collective-permute-done((bf16[240,1024]{1,0:T(8,128)(2,1)S(1)}, bf16[240,1024]{1,0:T(8,128)(2,1)S(1)}, u32[]{:S(2)}, u32[]{:S(2)}) %collective-permute-start.13) | collective-permute-done | bytes 491552 | tf_op jit(solution)/shard_map/ppermute | solution.py:211
  115.2 3.4 %collective-permute-start.14 = (bf16[112,1024]{1,0:T(8,128)(2,1)S(1)}, bf16[112,1024]{1,0:T(8,128)(2,1)S(1)}, u32[]{:S(2)}, u32[]{:S(2)}) collective-permute-start(bf16[112,1024]{1,0:T(8,128)(2,1)S(1)} %slice.6), channel_id=1, source_target_pairs={{0,1},{1,2},{2,3},{3,4},{4,5},{5,6},{6,7},{7,8},{8,9},{9,10},{10,1... | collective-permute-start | bytes 688136 | tf_op jit(solution)/shard_map/ppermute | solution.py:211
  118.6 3.1 %collective-permute-start.15 = (bf16[128,1024]{1,0:T(8,128)(2,1)S(1)}, bf16[128,1024]{1,0:T(8,128)(2,1)S(1)}, u32[]{:S(2)}, u32[]{:S(2)}) collective-permute-start(bf16[128,1024]{1,0:T(8,128)(2,1)S(1)} %slice.7), channel_id=1, source_target_pairs={{0,15},{1,0},{2,1},{3,2},{4,3},{5,4},{6,5},{7,6},{8,7},{9,8},{10,9... | collective-permute-start | bytes 786440 | tf_op jit(solution)/shard_map/ppermute | solution.py:211
  123.2 2.9 %collective-permute-done.15.refs_5_ = bf16[128,1024]{1,0:T(8,128)(2,1)S(1)} collective-permute-done((bf16[128,1024]{1,0:T(8,128)(2,1)S(1)}, bf16[128,1024]{1,0:T(8,128)(2,1)S(1)}, u32[]{:S(2)}, u32[]{:S(2)}) %collective-permute-start.15) | collective-permute-done | bytes 262176 | tf_op jit(solution)/shard_map/ppermute | solution.py:211
  129.7 4.2 %all-to-all-start.5 = ((bf16[4,10,240,128]{3,2,1,0:T(8,128)(2,1)}), bf16[4,10,240,128]{3,2,1,0:T(8,128)(2,1)S(1)}, u32[]{:S(2)}, u32[]{:S(2)}) async-start(bf16[4,10,240,128]{3,2,1,0:T(8,128)(2,1)} %copy-done), calls=%async_computation.5 | async-start | bytes 4915200 | tf_op jit(solution)/shard_map/all_to_all | solution.py:215
  138.8 9.4 %mix_early.1.early_ref = f32[240,1024]{1,0:T(8,128)S(1)} custom-call(s32[128]{0:T(128)S(1)} %select_select_fusion.codes_ref, bf16[24,240,128]{2,1,0:T(8,128)(2,1)S(1)} %bitcast.180, bf16[32,240,128]{2,1,0:T(8,128)(2,1)} %bitcast.36.refs_1_, bf16[32,240,128]{2,1,0:T(8,128)(2,1)} %bitcast.37.refs_2_, bf16[8,16,128,128]{3,2,1,0:T(8,128)(2,1)} %bitcast.186), custom_call_target="tpu_custom_call" | custom-call | flops 10000000000 | bytes 9601024 | tf_op jit(solution)/shard_map/mix_early/pallas_call | solution.py:116
  148.2 5.9 %all-to-all-done.5 = bf16[4,10,240,128]{3,2,1,0:T(8,128)(2,1)S(1)} async-done(((bf16[4,10,240,128]{3,2,1,0:T(8,128)(2,1)}), bf16[4,10,240,128]{3,2,1,0:T(8,128)(2,1)S(1)}, u32[]{:S(2)}, u32[]{:S(2)}) %all-to-all-start.5) | async-done | bytes 2457632 | tf_op jit(solution)/shard_map/all_to_all | solution.py:215
  154.1 5.0 %mix_late.2 = bf16[240,640]{1,0:T(8,128)(2,1)S(1)} custom-call(s32[128]{0:T(128)S(1)} %reshape.228.place_ref, s32[128]{0:T(128)S(1)} %reshape.229.which_ref, s32[8]{0:T(128)S(1)} %get-tuple-element.47.count_ref, f32[240,1024]{1,0:T(8,128)S(1)} %mix_early.1.early_ref, bf16[40,240,128]{2,1,0:T(8,128)(2,1)S(1)} %bitcast.178, ...), custom_call_target="tpu_custom_call" | custom-call | flops 629145600 | bytes 5079040 | tf_op jit(solution)/shard_map/mix_late/pallas_call | solution.py:182
  159.1 12.0 %collective-permute-start.16 = (bf16[240,640]{1,0:T(8,128)(2,1)S(1)}, bf16[240,640]{1,0:T(8,128)(2,1)S(1)}, u32[]{:S(2)}, u32[]{:S(2)}) collective-permute-start(bf16[240,640]{1,0:T(8,128)(2,1)S(1)} %mix_late.2), channel_id=1, source_target_pairs={{0,64},{64,128},{128,192},{192,256},{256,320},{320,384},{384,448},... | collective-permute-start | bytes 921608 | tf_op jit(solution)/shard_map/ppermute | solution.py:211
  171.2 3.7 %mix_late.3 = bf16[240,384]{1,0:T(8,128)(2,1)S(1)} custom-call(s32[128]{0:T(128)S(1)} %reshape.228.place_ref, s32[128]{0:T(128)S(1)} %reshape.229.which_ref, s32[8]{0:T(128)S(1)} %get-tuple-element.47.count_ref, f32[240,1024]{1,0:T(8,128)S(1)} %mix_early.1.early_ref, bf16[40,240,128]{2,1,0:T(8,128)(2,1)S(1)} %bitcast.179, ...), custom_call_target="tpu_custom_call" | custom-call | flops 377487360 | bytes 4030464 | tf_op jit(solution)/shard_map/mix_late/pallas_call | solution.py:182
  174.9 2.5 %collective-permute-done.17 = bf16[240,384]{1,0:T(8,128)(2,1)S(1)} collective-permute-done((bf16[240,384]{1,0:T(8,128)(2,1)S(1)}, bf16[240,384]{1,0:T(8,128)(2,1)S(1)}, u32[]{:S(2)}, u32[]{:S(2)}) %collective-permute-start.17) | collective-permute-done | bytes 184352 | tf_op jit(solution)/shard_map/ppermute | solution.py:211
  (82 shorter events, 30.2 us)
Async XLA Ops:
  0.0 24.2 %collective-permute-start.1 = (bf16[240,1024]{1,0:T(8,128)(2,1)}, bf16[240,1024]{1,0:T(8,128)(2,1)S(1)}, u32[]{:S(2)}, u32[]{:S(2)}) collective-permute-start(bf16[240,1024]{1,0:T(8,128)(2,1)} %bitcast.183), channel_id=1, source_target_pairs={{0,15},{1,0},{2,1},{3,2},{4,3},{5,4},{6,5},{7,6},{8,7},{9,8},{10,9... | collective-permute-start | bytes 1474568 | tf_op jit(solution)/shard_map/ppermute | solution.py:211
  12.0 15.1 %collective-permute-start = (bf16[240,1024]{1,0:T(8,128)(2,1)}, bf16[240,1024]{1,0:T(8,128)(2,1)S(1)}, u32[]{:S(2)}, u32[]{:S(2)}) collective-permute-start(bf16[240,1024]{1,0:T(8,128)(2,1)} %bitcast.184), channel_id=1, source_target_pairs={{0,1},{1,2},{2,3},{3,4},{4,5},{5,6},{6,7},{7,8},{8,9},{9,10},{10,1... | collective-permute-start | bytes 1474568 | tf_op jit(solution)/shard_map/ppermute | solution.py:211
  27.8 17.4 %all-to-all-start.1 = ((s32[4,4,4,2]{1,2,3,0:T(4,128)}), s32[4,4,4,2]{1,2,3,0:T(4,128)S(1)}, u32[]{:S(2)}, u32[]{:S(2)}) async-start(s32[4,4,4,2]{1,2,3,0:T(4,128)} %copy.12), calls=%async_computation.1 | async-start | bytes 32768 | tf_op jit(solution)/shard_map/all_to_all | solution.py:258
  33.6 15.5 %collective-permute-start.2 = (bf16[240,1024]{1,0:T(8,128)(2,1)S(1)}, bf16[240,1024]{1,0:T(8,128)(2,1)S(1)}, u32[]{:S(2)}, u32[]{:S(2)}) collective-permute-start(bf16[240,1024]{1,0:T(8,128)(2,1)S(1)} %collective-permute-done.refs_1_), channel_id=1, source_target_pairs={{0,1},{1,2},{2,3},{3,4},{4,5},{5,6},{6,7},{7,8},{8,9},{9,10},{10,1... | collective-permute-start | bytes 1474568 | tf_op jit(solution)/shard_map/ppermute | solution.py:211
  35.6 13.8 %collective-permute-start.3 = (bf16[240,1024]{1,0:T(8,128)(2,1)S(1)}, bf16[240,1024]{1,0:T(8,128)(2,1)S(1)}, u32[]{:S(2)}, u32[]{:S(2)}) collective-permute-start(bf16[240,1024]{1,0:T(8,128)(2,1)S(1)} %collective-permute-done.1.refs_2_), channel_id=1, source_target_pairs={{0,15},{1,0},{2,1},{3,2},{4,3},{5,4},{6,5},{7,6},{8,7},{9,8},{10,9... | collective-permute-start | bytes 1474568 | tf_op jit(solution)/shard_map/ppermute | solution.py:211
  45.5 1.0 copy-start.4
  49.4 13.3 %collective-permute-start.4 = (bf16[240,1024]{1,0:T(8,128)(2,1)S(1)}, bf16[240,1024]{1,0:T(8,128)(2,1)}, u32[]{:S(2)}, u32[]{:S(2)}) collective-permute-start(bf16[240,1024]{1,0:T(8,128)(2,1)S(1)} %collective-permute-done.2.refs_0_), channel_id=1, source_target_pairs={{0,1},{1,2},{2,3},{3,4},{4,5},{5,6},{6,7},{7,8},{8,9},{9,10},{10,1... | collective-permute-start | bytes 1474568 | tf_op jit(solution)/shard_map/ppermute | solution.py:211
  51.3 13.7 %collective-permute-start.6 = (bf16[240,1024]{1,0:T(8,128)(2,1)S(1)}, bf16[240,1024]{1,0:T(8,128)(2,1)}, u32[]{:S(2)}, u32[]{:S(2)}) collective-permute-start(bf16[240,1024]{1,0:T(8,128)(2,1)S(1)} %collective-permute-done.3.refs_1_), channel_id=1, source_target_pairs={{0,15},{1,0},{2,1},{3,2},{4,3},{5,4},{6,5},{7,6},{8,7},{9,8},{10,9... | collective-permute-start | bytes 1474568 | tf_op jit(solution)/shard_map/ppermute | solution.py:211
  56.6 19.8 %all-to-all-start.2 = ((bf16[4,6,240,128]{3,2,1,0:T(8,128)(2,1)}), bf16[4,6,240,128]{3,2,1,0:T(8,128)(2,1)S(1)}, u32[]{:S(2)}, u32[]{:S(2)}) async-start(bf16[4,6,240,128]{3,2,1,0:T(8,128)(2,1)} %pick_part.4), calls=%async_computation.2 | async-start | bytes 2949120 | tf_op jit(solution)/shard_map/all_to_all | solution.py:215
  62.7 11.7 %collective-permute-start.5 = (bf16[240,1024]{1,0:T(8,128)(2,1)}, bf16[240,1024]{1,0:T(8,128)(2,1)S(1)}, u32[]{:S(2)}, u32[]{:S(2)}) collective-permute-start(bf16[240,1024]{1,0:T(8,128)(2,1)} %collective-permute-done.4.refs_2_), channel_id=1, source_target_pairs={{0,1},{1,2},{2,3},{3,4},{4,5},{5,6},{6,7},{7,8},{8,9},{9,10},{10,1... | collective-permute-start | bytes 1474568 | tf_op jit(solution)/shard_map/ppermute | solution.py:211
  65.0 11.5 %collective-permute-start.7 = (bf16[240,1024]{1,0:T(8,128)(2,1)}, bf16[240,1024]{1,0:T(8,128)(2,1)S(1)}, u32[]{:S(2)}, u32[]{:S(2)}) collective-permute-start(bf16[240,1024]{1,0:T(8,128)(2,1)} %collective-permute-done.6.refs_3_), channel_id=1, source_target_pairs={{0,15},{1,0},{2,1},{3,2},{4,3},{5,4},{6,5},{7,6},{8,7},{9,8},{10,9... | collective-permute-start | bytes 1474568 | tf_op jit(solution)/shard_map/ppermute | solution.py:211
  76.5 6.5 %copy-start.1 = (bf16[4,6,240,128]{3,2,1,0:T(8,128)(2,1)}, bf16[4,6,240,128]{3,2,1,0:T(8,128)(2,1)S(1)}, u32[]{:S(2)}) copy-start(bf16[4,6,240,128]{3,2,1,0:T(8,128)(2,1)S(1)} %all-to-all-done.2) | copy-start | bytes 4423684
  76.5 11.0 %collective-permute-start.8 = (bf16[240,1024]{1,0:T(8,128)(2,1)S(1)}, bf16[240,1024]{1,0:T(8,128)(2,1)S(1)}, u32[]{:S(2)}, u32[]{:S(2)}) collective-permute-start(bf16[240,1024]{1,0:T(8,128)(2,1)S(1)} %collective-permute-done.5.refs_0_), channel_id=1, source_target_pairs={{0,1},{1,2},{2,3},{3,4},{4,5},{5,6},{6,7},{7,8},{8,9},{9,10},{10,1... | collective-permute-start | bytes 1474568 | tf_op jit(solution)/shard_map/ppermute | solution.py:211
  79.6 9.9 %collective-permute-start.9 = (bf16[240,1024]{1,0:T(8,128)(2,1)S(1)}, bf16[240,1024]{1,0:T(8,128)(2,1)}, u32[]{:S(2)}, u32[]{:S(2)}) collective-permute-start(bf16[240,1024]{1,0:T(8,128)(2,1)S(1)} %collective-permute-done.7.refs_1_), channel_id=1, source_target_pairs={{0,15},{1,0},{2,1},{3,2},{4,3},{5,4},{6,5},{7,6},{8,7},{9,8},{10,9... | collective-permute-start | bytes 1474568 | tf_op jit(solution)/shard_map/ppermute | solution.py:211
  83.0 24.4 %all-to-all-start.3 = ((bf16[4,8,240,128]{3,2,1,0:T(8,128)(2,1)}), bf16[4,8,240,128]{3,2,1,0:T(8,128)(2,1)}, u32[]{:S(2)}, u32[]{:S(2)}) async-start(bf16[4,8,240,128]{3,2,1,0:T(8,128)(2,1)} %pick_part.5), calls=%async_computation.3 | async-start | bytes 3932160 | tf_op jit(solution)/shard_map/all_to_all | solution.py:215
  87.4 11.2 %collective-permute-start.10 = (bf16[240,1024]{1,0:T(8,128)(2,1)S(1)}, bf16[240,1024]{1,0:T(8,128)(2,1)S(1)}, u32[]{:S(2)}, u32[]{:S(2)}) collective-permute-start(bf16[240,1024]{1,0:T(8,128)(2,1)S(1)} %collective-permute-done.8.refs_2_), channel_id=1, source_target_pairs={{0,1},{1,2},{2,3},{3,4},{4,5},{5,6},{6,7},{7,8},{8,9},{9,10},{10,1... | collective-permute-start | bytes 1474568 | tf_op jit(solution)/shard_map/ppermute | solution.py:211
  89.4 11.4 %collective-permute-start.11 = (bf16[240,1024]{1,0:T(8,128)(2,1)}, bf16[240,1024]{1,0:T(8,128)(2,1)S(1)}, u32[]{:S(2)}, u32[]{:S(2)}) collective-permute-start(bf16[240,1024]{1,0:T(8,128)(2,1)} %collective-permute-done.9.refs_3_), channel_id=1, source_target_pairs={{0,15},{1,0},{2,1},{3,2},{4,3},{5,4},{6,5},{7,6},{8,7},{9,8},{10,9... | collective-permute-start | bytes 1474568 | tf_op jit(solution)/shard_map/ppermute | solution.py:211
  100.9 11.2 %collective-permute-start.12 = (bf16[240,1024]{1,0:T(8,128)(2,1)S(1)}, bf16[240,1024]{1,0:T(8,128)(2,1)S(1)}, u32[]{:S(2)}, u32[]{:S(2)}) collective-permute-start(bf16[240,1024]{1,0:T(8,128)(2,1)S(1)} %collective-permute-done.10.refs_0_), channel_id=1, source_target_pairs={{0,1},{1,2},{2,3},{3,4},{4,5},{5,6},{6,7},{7,8},{8,9},{9,10},{10,1... | collective-permute-start | bytes 1474568 | tf_op jit(solution)/shard_map/ppermute | solution.py:211
  105.1 10.1 %collective-permute-start.13 = (bf16[240,1024]{1,0:T(8,128)(2,1)S(1)}, bf16[240,1024]{1,0:T(8,128)(2,1)S(1)}, u32[]{:S(2)}, u32[]{:S(2)}) collective-permute-start(bf16[240,1024]{1,0:T(8,128)(2,1)S(1)} %collective-permute-done.11.refs_1_), channel_id=1, source_target_pairs={{0,15},{1,0},{2,1},{3,2},{4,3},{5,4},{6,5},{7,6},{8,7},{9,8},{10,9... | collective-permute-start | bytes 1474568 | tf_op jit(solution)/shard_map/ppermute | solution.py:211
  107.4 14.4 %copy-start.5 = (s32[1,8,16]{2,1,0:T(8,128)S(1)}, s32[1,8,16]{2,1,0:T(8,128)}, u32[]{:S(2)}) copy-start(s32[1,8,16]{2,1,0:T(8,128)} %param.8) | copy-start | bytes 1540
  107.4 22.3 %all-to-all-start.4 = ((bf16[4,8,240,128]{3,2,1,0:T(8,128)(2,1)}), bf16[4,8,240,128]{3,2,1,0:T(8,128)(2,1)}, u32[]{:S(2)}, u32[]{:S(2)}) async-start(bf16[4,8,240,128]{3,2,1,0:T(8,128)(2,1)} %pick_part.6), calls=%async_computation.4 | async-start | bytes 3932160 | tf_op jit(solution)/shard_map/all_to_all | solution.py:215
  115.2 8.0 %collective-permute-start.14 = (bf16[112,1024]{1,0:T(8,128)(2,1)S(1)}, bf16[112,1024]{1,0:T(8,128)(2,1)S(1)}, u32[]{:S(2)}, u32[]{:S(2)}) collective-permute-start(bf16[112,1024]{1,0:T(8,128)(2,1)S(1)} %slice.6), channel_id=1, source_target_pairs={{0,1},{1,2},{2,3},{3,4},{4,5},{5,6},{6,7},{7,8},{8,9},{9,10},{10,1... | collective-permute-start | bytes 688136 | tf_op jit(solution)/shard_map/ppermute | solution.py:211
  118.6 7.5 %collective-permute-start.15 = (bf16[128,1024]{1,0:T(8,128)(2,1)S(1)}, bf16[128,1024]{1,0:T(8,128)(2,1)S(1)}, u32[]{:S(2)}, u32[]{:S(2)}) collective-permute-start(bf16[128,1024]{1,0:T(8,128)(2,1)S(1)} %slice.7), channel_id=1, source_target_pairs={{0,15},{1,0},{2,1},{3,2},{4,3},{5,4},{6,5},{7,6},{8,7},{9,8},{10,9... | collective-permute-start | bytes 786440 | tf_op jit(solution)/shard_map/ppermute | solution.py:211
  128.3 1.4 copy-start
  129.7 24.4 %all-to-all-start.5 = ((bf16[4,10,240,128]{3,2,1,0:T(8,128)(2,1)}), bf16[4,10,240,128]{3,2,1,0:T(8,128)(2,1)S(1)}, u32[]{:S(2)}, u32[]{:S(2)}) async-start(bf16[4,10,240,128]{3,2,1,0:T(8,128)(2,1)} %copy-done), calls=%async_computation.5 | async-start | bytes 4915200 | tf_op jit(solution)/shard_map/all_to_all | solution.py:215
  137.4 1.4 copy-start.2
  138.8 15.4 %copy-start.3 = (f32[1,1024]{1,0:T(1,128)S(1)}, f32[1,1024]{1,0:T(1,128)}, u32[]{:S(2)}) copy-start(f32[1,1024]{1,0:T(1,128)} %param.7) | copy-start | bytes 12292
  159.1 18.2 %collective-permute-start.16 = (bf16[240,640]{1,0:T(8,128)(2,1)S(1)}, bf16[240,640]{1,0:T(8,128)(2,1)S(1)}, u32[]{:S(2)}, u32[]{:S(2)}) collective-permute-start(bf16[240,640]{1,0:T(8,128)(2,1)S(1)} %mix_late.2), channel_id=1, source_target_pairs={{0,64},{64,128},{128,192},{192,256},{256,320},{320,384},{384,448},... | collective-permute-start | bytes 921608 | tf_op jit(solution)/shard_map/ppermute | solution.py:211
  174.8 2.5 %collective-permute-start.17 = (bf16[240,384]{1,0:T(8,128)(2,1)S(1)}, bf16[240,384]{1,0:T(8,128)(2,1)S(1)}, u32[]{:S(2)}, u32[]{:S(2)}) collective-permute-start(bf16[240,384]{1,0:T(8,128)(2,1)S(1)} %mix_late.3), channel_id=1, source_target_pairs={{0,64},{64,128},{128,192},{192,256},{256,320},{320,384},{384,448},... | collective-permute-start | bytes 552968 | tf_op jit(solution)/shard_map/ppermute | solution.py:211

commit v11 on v10

--- a/solution.py
+++ b/solution.py
@@ -44,7 +44,7 @@
     pltpu.make_async_copy(held, held, out_sem).wait()
 
 
-def pick_call(kernel, scalars, operands, count, rows, name):
+def pick_call(kernel, scalars, operands, count, rows, name, vmem):
     shape = (LINES, count, rows, BLOCK)
     size = LINES * count * rows * BLOCK * 2
     return pl.pallas_call(
@@ -61,7 +61,7 @@
             ],
         ),
         out_shape=jax.ShapeDtypeStruct(shape, jnp.bfloat16),
-        compiler_params=pltpu.CompilerParams(vmem_limit_bytes=PICK_VMEM),
+        compiler_params=pltpu.CompilerParams(vmem_limit_bytes=vmem),
         cost_estimate=pl.CostEstimate(
             flops=PICK_WEIGHT, bytes_accessed=2 * size, transcendentals=0
         ),
@@ -81,7 +81,8 @@
             at += len(ps)
         copy_blocks(ids_ref, senders, out_ref, held, in_sems, out_sem)
 
-    return pick_call(kernel, (ids, here), flat, len(part) * CAP, rows, "pick_part")
+    vmem = MIX_VMEM if part == PARTS[-1] else PICK_VMEM
+    return pick_call(kernel, (ids, here), flat, len(part) * CAP, rows, "pick_part", vmem)
 
 
 def mix_early(codes, arrays, weights):

time: 181 us -> 180 us (level)
    unnamed x12 -> x10, local copies, waits for them, and re-layouts: 3.84 us -> 2.41 us
  transfers between devices with their start and end apart: 23 -> 23, of which waited for: 17 -> 17; matrix products, arithmetic and copies ran while one was open for 3% -> 3% of each run, Pallas kernels for 13% -> 14%
where the time goes in v11:
time: 180 us; the launch traced here: 177 us
  starting transfers between devices  96.2 us (53%)
  waiting for transfers between devices  33.6 us (19%)
  Pallas kernels  28.9 us (16%)
  blocking collectives  9.43 us (5%)
  local copies, waits for them, and re-layouts  7.23 us (4%)
    ppermute x18, starting transfers between devices, shifted(): lax.ppermute(value, axis, [(i, (i + by) % count) for i in range(count)])  73.1 us
    ppermute x18, waiting for transfers between devices, shifted(): lax.ppermute(value, axis, [(i, (i + by) % count) for i in range(count)])  24.1 us
    all_to_all x4, starting transfers between devices, over_lines(): incoming = lax.all_to_all(outgoing, 'y', 0, 0, tiled=True)  17.3 us
    pallas_call x4, Pallas kernels, pick_call(): pl.pallas_call(kernel, grid_spec=pltpu.PrefetchScalarGridSpec(num_scalar_...  11.1 us
    all_to_all x1, blocking collectives, body(): near = lax.all_to_all(lists, 'near', 0, 0, tiled=True)  9.43 us
    pallas_call x1, Pallas kernels, mix_early(): pl.pallas_call(kernel, grid_spec=pltpu.PrefetchScalarGridSpec(num_scalar_...  9.4 us
    pallas_call x2, Pallas kernels, mix_late(): pl.pallas_call(kernel, grid_spec=pltpu.PrefetchScalarGridSpec(num_scalar_...  8.46 us
    all_to_all x4, waiting for transfers between devices, over_lines(): incoming = lax.all_to_all(outgoing, 'y', 0, 0, tiled=True)  5.95 us
  transfers between devices with their start and end apart: 23, of which 17 were waited for; matrix products, arithmetic and copies ran while one was open for 3% of the time, Pallas kernels for 14%

profile of v11, /device:TPU:1, one launch (start us, length us, event | category | flops | bytes accessed | tf_op | source)
XLA Modules:
  0.0 177.4 jit_solution(15126178216639646121)
XLA Ops:
  0.0 11.9 %collective-permute-start.1 = (bf16[240,1024]{1,0:T(8,128)(2,1)}, bf16[240,1024]{1,0:T(8,128)(2,1)S(1)}, u32[]{:S(2)}, u32[]{:S(2)}) collective-permute-start(bf16[240,1024]{1,0:T(8,128)(2,1)} %bitcast.183), channel_id=1, source_target_pairs={{0,15},{1,0},{2,1},{3,2},{4,3},{5,4},{6,5},{7,6},{8,7},{9,8},{10,9... | collective-permute-start | bytes 1474568 | tf_op jit(solution)/shard_map/ppermute | solution.py:212
  14.8 9.4 %all_to_all.30 = s32[4,4,4,2]{1,2,3,0:T(4,128)S(1)} all-to-all(s32[4,4,4,2]{1,2,3,0:T(4,128)S(1)} %copy.11), channel_id=1, replica_groups=mesh['segment'=8,'y'=4,'far'=4,'near'=4] {'near'}, dimensions={0} | all-to-all | bytes 1024 | tf_op jit(solution)/shard_map/all_to_all | solution.py:251
  24.2 2.8 %collective-permute-done.refs_1_ = bf16[240,1024]{1,0:T(8,128)(2,1)S(1)} collective-permute-done((bf16[240,1024]{1,0:T(8,128)(2,1)}, bf16[240,1024]{1,0:T(8,128)(2,1)S(1)}, u32[]{:S(2)}, u32[]{:S(2)}) %collective-permute-start) | collective-permute-done | bytes 491552 | tf_op jit(solution)/shard_map/ppermute | solution.py:212
  27.8 5.8 %all-to-all-start.1 = ((s32[4,4,4,2]{1,2,3,0:T(4,128)}), s32[4,4,4,2]{1,2,3,0:T(4,128)S(1)}, u32[]{:S(2)}, u32[]{:S(2)}) async-start(s32[4,4,4,2]{1,2,3,0:T(4,128)} %copy.12), calls=%async_computation.1 | async-start | bytes 32768 | tf_op jit(solution)/shard_map/all_to_all | solution.py:259
  35.6 5.9 %collective-permute-start.3 = (bf16[240,1024]{1,0:T(8,128)(2,1)S(1)}, bf16[240,1024]{1,0:T(8,128)(2,1)S(1)}, u32[]{:S(2)}, u32[]{:S(2)}) collective-permute-start(bf16[240,1024]{1,0:T(8,128)(2,1)S(1)} %collective-permute-done.1.refs_2_), channel_id=1, source_target_pairs={{0,15},{1,0},{2,1},{3,2},{4,3},{5,4},{6,5},{7,6},{8,7},{9,8},{10,9... | collective-permute-start | bytes 1474568 | tf_op jit(solution)/shard_map/ppermute | solution.py:212
  41.5 3.6 %all-to-all-done.1 = s32[4,4,4,2]{1,2,3,0:T(4,128)S(1)} async-done(((s32[4,4,4,2]{1,2,3,0:T(4,128)}), s32[4,4,4,2]{1,2,3,0:T(4,128)S(1)}, u32[]{:S(2)}, u32[]{:S(2)}) %all-to-all-start.1) | async-done | bytes 544 | tf_op jit(solution)/shard_map/all_to_all | solution.py:259
  46.5 2.3 %pick_part.4 = bf16[4,6,240,128]{3,2,1,0:T(8,128)(2,1)} custom-call(s32[128]{0:T(128)S(1)} %reshape.231.ids_ref, s32[1]{0:T(128)} %bitcast.34.here_ref, bf16[240,1024]{1,0:T(8,128)(2,1)S(1)} %bitcast.185, bf16[240,1024]{1,0:T(8,128)(2,1)S(1)} %collective-permute-done.refs_1_, bf16[240,1024]{1,0:T(8,128)(2,1)S(1)} %collective-permute-done.1.refs_2_), custom_call_target="tpu_custom_call" | custom-call | flops 12000000000 | bytes 2949120 | tf_op jit(solution)/shard_map/pick_part/pallas_call | solution.py:50
  51.3 5.3 %collective-permute-start.6 = (bf16[240,1024]{1,0:T(8,128)(2,1)S(1)}, bf16[240,1024]{1,0:T(8,128)(2,1)}, u32[]{:S(2)}, u32[]{:S(2)}) collective-permute-start(bf16[240,1024]{1,0:T(8,128)(2,1)S(1)} %collective-permute-done.3.refs_1_), channel_id=1, source_target_pairs={{0,15},{1,0},{2,1},{3,2},{4,3},{5,4},{6,5},{7,6},{8,7},{9,8},{10,9... | collective-permute-start | bytes 1474568 | tf_op jit(solution)/shard_map/ppermute | solution.py:212
  56.6 4.2 %all-to-all-start.2 = ((bf16[4,6,240,128]{3,2,1,0:T(8,128)(2,1)}), bf16[4,6,240,128]{3,2,1,0:T(8,128)(2,1)S(1)}, u32[]{:S(2)}, u32[]{:S(2)}) async-start(bf16[4,6,240,128]{3,2,1,0:T(8,128)(2,1)} %pick_part.4), calls=%async_computation.2 | async-start | bytes 2949120 | tf_op jit(solution)/shard_map/all_to_all | solution.py:216
  65.0 4.2 %collective-permute-start.7 = (bf16[240,1024]{1,0:T(8,128)(2,1)}, bf16[240,1024]{1,0:T(8,128)(2,1)S(1)}, u32[]{:S(2)}, u32[]{:S(2)}) collective-permute-start(bf16[240,1024]{1,0:T(8,128)(2,1)} %collective-permute-done.6.refs_3_), channel_id=1, source_target_pairs={{0,15},{1,0},{2,1},{3,2},{4,3},{5,4},{6,5},{7,6},{8,7},{9,8},{10,9... | collective-permute-start | bytes 1474568 | tf_op jit(solution)/shard_map/ppermute | solution.py:212
  69.2 2.9 %pick_part.5 = bf16[4,8,240,128]{3,2,1,0:T(8,128)(2,1)} custom-call(s32[128]{0:T(128)S(1)} %reshape.231.ids_ref, s32[1]{0:T(128)} %bitcast.34.here_ref, bf16[240,1024]{1,0:T(8,128)(2,1)S(1)} %collective-permute-done.2.refs_0_, bf16[240,1024]{1,0:T(8,128)(2,1)S(1)} %collective-permute-done.3.refs_1_, bf16[240,1024]{1,0:T(8,128)(2,1)} %collective-permute-done.4.refs_2_, ...), custom_call_target="tpu_custom_call" | custom-call | flops 12000000000 | bytes 3932160 | tf_op jit(solution)/shard_map/pick_part/pallas_call | solution.py:50
  72.1 2.3 %collective-permute-done.5.refs_0_ = bf16[240,1024]{1,0:T(8,128)(2,1)S(1)} collective-permute-done((bf16[240,1024]{1,0:T(8,128)(2,1)}, bf16[240,1024]{1,0:T(8,128)(2,1)S(1)}, u32[]{:S(2)}, u32[]{:S(2)}) %collective-permute-start.5) | collective-permute-done | bytes 491552 | tf_op jit(solution)/shard_map/ppermute | solution.py:212
  76.5 3.1 %collective-permute-start.8 = (bf16[240,1024]{1,0:T(8,128)(2,1)S(1)}, bf16[240,1024]{1,0:T(8,128)(2,1)S(1)}, u32[]{:S(2)}, u32[]{:S(2)}) collective-permute-start(bf16[240,1024]{1,0:T(8,128)(2,1)S(1)} %collective-permute-done.5.refs_0_), channel_id=1, source_target_pairs={{0,1},{1,2},{2,3},{3,4},{4,5},{5,6},{6,7},{7,8},{8,9},{9,10},{10,1... | collective-permute-start | bytes 1474568 | tf_op jit(solution)/shard_map/ppermute | solution.py:212
  79.6 3.4 %collective-permute-start.9 = (bf16[240,1024]{1,0:T(8,128)(2,1)S(1)}, bf16[240,1024]{1,0:T(8,128)(2,1)}, u32[]{:S(2)}, u32[]{:S(2)}) collective-permute-start(bf16[240,1024]{1,0:T(8,128)(2,1)S(1)} %collective-permute-done.7.refs_1_), channel_id=1, source_target_pairs={{0,15},{1,0},{2,1},{3,2},{4,3},{5,4},{6,5},{7,6},{8,7},{9,8},{10,9... | collective-permute-start | bytes 1474568 | tf_op jit(solution)/shard_map/ppermute | solution.py:212
  83.0 4.4 %all-to-all-start.3 = ((bf16[4,8,240,128]{3,2,1,0:T(8,128)(2,1)}), bf16[4,8,240,128]{3,2,1,0:T(8,128)(2,1)}, u32[]{:S(2)}, u32[]{:S(2)}) async-start(bf16[4,8,240,128]{3,2,1,0:T(8,128)(2,1)} %pick_part.5), calls=%async_computation.3 | async-start | bytes 3932160 | tf_op jit(solution)/shard_map/all_to_all | solution.py:216
  89.4 4.5 %collective-permute-start.11 = (bf16[240,1024]{1,0:T(8,128)(2,1)}, bf16[240,1024]{1,0:T(8,128)(2,1)S(1)}, u32[]{:S(2)}, u32[]{:S(2)}) collective-permute-start(bf16[240,1024]{1,0:T(8,128)(2,1)} %collective-permute-done.9.refs_3_), channel_id=1, source_target_pairs={{0,15},{1,0},{2,1},{3,2},{4,3},{5,4},{6,5},{7,6},{8,7},{9,8},{10,9... | collective-permute-start | bytes 1474568 | tf_op jit(solution)/shard_map/ppermute | solution.py:212
  94.0 2.9 %pick_part.6 = bf16[4,8,240,128]{3,2,1,0:T(8,128)(2,1)} custom-call(s32[128]{0:T(128)S(1)} %reshape.231.ids_ref, s32[1]{0:T(128)} %bitcast.34.here_ref, bf16[240,1024]{1,0:T(8,128)(2,1)S(1)} %collective-permute-done.5.refs_0_, bf16[240,1024]{1,0:T(8,128)(2,1)S(1)} %collective-permute-done.7.refs_1_, bf16[240,1024]{1,0:T(8,128)(2,1)S(1)} %collective-permute-done.8.refs_2_, ...), custom_call_target="tpu_custom_call" | custom-call | flops 12000000000 | bytes 3932160 | tf_op jit(solution)/shard_map/pick_part/pallas_call | solution.py:50
  100.9 4.2 %collective-permute-start.12 = (bf16[240,1024]{1,0:T(8,128)(2,1)S(1)}, bf16[240,1024]{1,0:T(8,128)(2,1)S(1)}, u32[]{:S(2)}, u32[]{:S(2)}) collective-permute-start(bf16[240,1024]{1,0:T(8,128)(2,1)S(1)} %collective-permute-done.10.refs_0_), channel_id=1, source_target_pairs={{0,1},{1,2},{2,3},{3,4},{4,5},{5,6},{6,7},{7,8},{8,9},{9,10},{10,1... | collective-permute-start | bytes 1474568 | tf_op jit(solution)/shard_map/ppermute | solution.py:212
  105.1 2.3 %collective-permute-start.13 = (bf16[240,1024]{1,0:T(8,128)(2,1)S(1)}, bf16[240,1024]{1,0:T(8,128)(2,1)S(1)}, u32[]{:S(2)}, u32[]{:S(2)}) collective-permute-start(bf16[240,1024]{1,0:T(8,128)(2,1)S(1)} %collective-permute-done.11.refs_1_), channel_id=1, source_target_pairs={{0,15},{1,0},{2,1},{3,2},{4,3},{5,4},{6,5},{7,6},{8,7},{9,8},{10,9... | collective-permute-start | bytes 1474568 | tf_op jit(solution)/shard_map/ppermute | solution.py:212
  107.4 4.4 %all-to-all-start.4 = ((bf16[4,8,240,128]{3,2,1,0:T(8,128)(2,1)}), bf16[4,8,240,128]{3,2,1,0:T(8,128)(2,1)}, u32[]{:S(2)}, u32[]{:S(2)}) async-start(bf16[4,8,240,128]{3,2,1,0:T(8,128)(2,1)} %pick_part.6), calls=%async_computation.4 | async-start | bytes 3932160 | tf_op jit(solution)/shard_map/all_to_all | solution.py:216
  112.0 3.2 %collective-permute-done.13.refs_3_ = bf16[240,1024]{1,0:T(8,128)(2,1)S(1)} collective-permute-done((bf16[240,1024]{1,0:T(8,128)(2,1)S(1)}, bf16[240,1024]{1,0:T(8,128)(2,1)S(1)}, u32[]{:S(2)}, u32[]{:S(2)}) %collective-permute-start.13) | collective-permute-done | bytes 491552 | tf_op jit(solution)/shard_map/ppermute | solution.py:212
  115.2 3.4 %collective-permute-start.14 = (bf16[112,1024]{1,0:T(8,128)(2,1)S(1)}, bf16[112,1024]{1,0:T(8,128)(2,1)S(1)}, u32[]{:S(2)}, u32[]{:S(2)}) collective-permute-start(bf16[112,1024]{1,0:T(8,128)(2,1)S(1)} %slice.6), channel_id=1, source_target_pairs={{0,1},{1,2},{2,3},{3,4},{4,5},{5,6},{6,7},{7,8},{8,9},{9,10},{10,1... | collective-permute-start | bytes 688136 | tf_op jit(solution)/shard_map/ppermute | solution.py:212
  118.6 3.1 %collective-permute-start.15 = (bf16[128,1024]{1,0:T(8,128)(2,1)S(1)}, bf16[128,1024]{1,0:T(8,128)(2,1)S(1)}, u32[]{:S(2)}, u32[]{:S(2)}) collective-permute-start(bf16[128,1024]{1,0:T(8,128)(2,1)S(1)} %slice.7), channel_id=1, source_target_pairs={{0,15},{1,0},{2,1},{3,2},{4,3},{5,4},{6,5},{7,6},{8,7},{9,8},{10,9... | collective-permute-start | bytes 786440 | tf_op jit(solution)/shard_map/ppermute | solution.py:212
  123.2 2.9 %collective-permute-done.15.refs_5_ = bf16[128,1024]{1,0:T(8,128)(2,1)S(1)} collective-permute-done((bf16[128,1024]{1,0:T(8,128)(2,1)S(1)}, bf16[128,1024]{1,0:T(8,128)(2,1)S(1)}, u32[]{:S(2)}, u32[]{:S(2)}) %collective-permute-start.15) | collective-permute-done | bytes 262176 | tf_op jit(solution)/shard_map/ppermute | solution.py:212
  126.1 2.9 %pick_part.7 = bf16[4,10,240,128]{3,2,1,0:T(8,128)(2,1)} custom-call(s32[128]{0:T(128)S(1)} %reshape.231.ids_ref, s32[1]{0:T(128)} %bitcast.34.here_ref, bf16[240,1024]{1,0:T(8,128)(2,1)S(1)} %collective-permute-done.10.refs_0_, bf16[240,1024]{1,0:T(8,128)(2,1)S(1)} %collective-permute-done.11.refs_1_, ...), custom_call_target="tpu_custom_call" | custom-call | flops 12000000000 | bytes 4915200 | tf_op jit(solution)/shard_map/pick_part/pallas_call | solution.py:50
  129.1 4.2 %all-to-all-start.5 = ((bf16[4,10,240,128]{3,2,1,0:T(8,128)(2,1)}), bf16[4,10,240,128]{3,2,1,0:T(8,128)(2,1)S(1)}, u32[]{:S(2)}, u32[]{:S(2)}) async-start(bf16[4,10,240,128]{3,2,1,0:T(8,128)(2,1)} %pick_part.7), calls=%async_computation.5 | async-start | bytes 4915200 | tf_op jit(solution)/shard_map/all_to_all | solution.py:216
  138.2 9.4 %mix_early.1.early_ref = f32[240,1024]{1,0:T(8,128)S(1)} custom-call(s32[128]{0:T(128)S(1)} %select_select_fusion.codes_ref, bf16[24,240,128]{2,1,0:T(8,128)(2,1)S(1)} %bitcast.180, bf16[32,240,128]{2,1,0:T(8,128)(2,1)} %bitcast.36.refs_1_, bf16[32,240,128]{2,1,0:T(8,128)(2,1)} %bitcast.37.refs_2_, bf16[8,16,128,128]{3,2,1,0:T(8,128)(2,1)} %bitcast.186), custom_call_target="tpu_custom_call" | custom-call | flops 10000000000 | bytes 9601024 | tf_op jit(solution)/shard_map/mix_early/pallas_call | solution.py:117
  147.6 5.9 %all-to-all-done.5 = bf16[4,10,240,128]{3,2,1,0:T(8,128)(2,1)S(1)} async-done(((bf16[4,10,240,128]{3,2,1,0:T(8,128)(2,1)}), bf16[4,10,240,128]{3,2,1,0:T(8,128)(2,1)S(1)}, u32[]{:S(2)}, u32[]{:S(2)}) %all-to-all-start.5) | async-done | bytes 2457632 | tf_op jit(solution)/shard_map/all_to_all | solution.py:216
  153.5 4.8 %mix_late.2 = bf16[240,640]{1,0:T(8,128)(2,1)S(1)} custom-call(s32[128]{0:T(128)S(1)} %reshape.228.place_ref, s32[128]{0:T(128)S(1)} %reshape.229.which_ref, s32[8]{0:T(128)S(1)} %get-tuple-element.47.count_ref, f32[240,1024]{1,0:T(8,128)S(1)} %mix_early.1.early_ref, bf16[40,240,128]{2,1,0:T(8,128)(2,1)S(1)} %bitcast.178, ...), custom_call_target="tpu_custom_call" | custom-call | flops 629145600 | bytes 5079040 | tf_op jit(solution)/shard_map/mix_late/pallas_call | solution.py:183
  158.3 12.0 %collective-permute-start.16 = (bf16[240,640]{1,0:T(8,128)(2,1)S(1)}, bf16[240,640]{1,0:T(8,128)(2,1)S(1)}, u32[]{:S(2)}, u32[]{:S(2)}) collective-permute-start(bf16[240,640]{1,0:T(8,128)(2,1)S(1)} %mix_late.2), channel_id=1, source_target_pairs={{0,64},{64,128},{128,192},{192,256},{256,320},{320,384},{384,448},... | collective-permute-start | bytes 921608 | tf_op jit(solution)/shard_map/ppermute | solution.py:212
  170.3 3.7 %mix_late.3 = bf16[240,384]{1,0:T(8,128)(2,1)S(1)} custom-call(s32[128]{0:T(128)S(1)} %reshape.228.place_ref, s32[128]{0:T(128)S(1)} %reshape.229.which_ref, s32[8]{0:T(128)S(1)} %get-tuple-element.47.count_ref, f32[240,1024]{1,0:T(8,128)S(1)} %mix_early.1.early_ref, bf16[40,240,128]{2,1,0:T(8,128)(2,1)S(1)} %bitcast.179, ...), custom_call_target="tpu_custom_call" | custom-call | flops 377487360 | bytes 4030464 | tf_op jit(solution)/shard_map/mix_late/pallas_call | solution.py:183
  174.0 2.5 %collective-permute-done.17 = bf16[240,384]{1,0:T(8,128)(2,1)S(1)} collective-permute-done((bf16[240,384]{1,0:T(8,128)(2,1)S(1)}, bf16[240,384]{1,0:T(8,128)(2,1)S(1)}, u32[]{:S(2)}, u32[]{:S(2)}) %collective-permute-start.17) | collective-permute-done | bytes 184352 | tf_op jit(solution)/shard_map/ppermute | solution.py:212
  (80 shorter events, 28.9 us)
Async XLA Ops:
  0.0 24.2 %collective-permute-start.1 = (bf16[240,1024]{1,0:T(8,128)(2,1)}, bf16[240,1024]{1,0:T(8,128)(2,1)S(1)}, u32[]{:S(2)}, u32[]{:S(2)}) collective-permute-start(bf16[240,1024]{1,0:T(8,128)(2,1)} %bitcast.183), channel_id=1, source_target_pairs={{0,15},{1,0},{2,1},{3,2},{4,3},{5,4},{6,5},{7,6},{8,7},{9,8},{10,9... | collective-permute-start | bytes 1474568 | tf_op jit(solution)/shard_map/ppermute | solution.py:212
  12.0 15.1 %collective-permute-start = (bf16[240,1024]{1,0:T(8,128)(2,1)}, bf16[240,1024]{1,0:T(8,128)(2,1)S(1)}, u32[]{:S(2)}, u32[]{:S(2)}) collective-permute-start(bf16[240,1024]{1,0:T(8,128)(2,1)} %bitcast.184), channel_id=1, source_target_pairs={{0,1},{1,2},{2,3},{3,4},{4,5},{5,6},{6,7},{7,8},{8,9},{9,10},{10,1... | collective-permute-start | bytes 1474568 | tf_op jit(solution)/shard_map/ppermute | solution.py:212
  27.8 17.4 %all-to-all-start.1 = ((s32[4,4,4,2]{1,2,3,0:T(4,128)}), s32[4,4,4,2]{1,2,3,0:T(4,128)S(1)}, u32[]{:S(2)}, u32[]{:S(2)}) async-start(s32[4,4,4,2]{1,2,3,0:T(4,128)} %copy.12), calls=%async_computation.1 | async-start | bytes 32768 | tf_op jit(solution)/shard_map/all_to_all | solution.py:259
  33.6 15.5 %collective-permute-start.2 = (bf16[240,1024]{1,0:T(8,128)(2,1)S(1)}, bf16[240,1024]{1,0:T(8,128)(2,1)S(1)}, u32[]{:S(2)}, u32[]{:S(2)}) collective-permute-start(bf16[240,1024]{1,0:T(8,128)(2,1)S(1)} %collective-permute-done.refs_1_), channel_id=1, source_target_pairs={{0,1},{1,2},{2,3},{3,4},{4,5},{5,6},{6,7},{7,8},{8,9},{9,10},{10,1... | collective-permute-start | bytes 1474568 | tf_op jit(solution)/shard_map/ppermute | solution.py:212
  35.6 13.8 %collective-permute-start.3 = (bf16[240,1024]{1,0:T(8,128)(2,1)S(1)}, bf16[240,1024]{1,0:T(8,128)(2,1)S(1)}, u32[]{:S(2)}, u32[]{:S(2)}) collective-permute-start(bf16[240,1024]{1,0:T(8,128)(2,1)S(1)} %collective-permute-done.1.refs_2_), channel_id=1, source_target_pairs={{0,15},{1,0},{2,1},{3,2},{4,3},{5,4},{6,5},{7,6},{8,7},{9,8},{10,9... | collective-permute-start | bytes 1474568 | tf_op jit(solution)/shard_map/ppermute | solution.py:212
  45.5 1.0 copy-start.3
  49.4 13.3 %collective-permute-start.4 = (bf16[240,1024]{1,0:T(8,128)(2,1)S(1)}, bf16[240,1024]{1,0:T(8,128)(2,1)}, u32[]{:S(2)}, u32[]{:S(2)}) collective-permute-start(bf16[240,1024]{1,0:T(8,128)(2,1)S(1)} %collective-permute-done.2.refs_0_), channel_id=1, source_target_pairs={{0,1},{1,2},{2,3},{3,4},{4,5},{5,6},{6,7},{7,8},{8,9},{9,10},{10,1... | collective-permute-start | bytes 1474568 | tf_op jit(solution)/shard_map/ppermute | solution.py:212
  51.3 13.7 %collective-permute-start.6 = (bf16[240,1024]{1,0:T(8,128)(2,1)S(1)}, bf16[240,1024]{1,0:T(8,128)(2,1)}, u32[]{:S(2)}, u32[]{:S(2)}) collective-permute-start(bf16[240,1024]{1,0:T(8,128)(2,1)S(1)} %collective-permute-done.3.refs_1_), channel_id=1, source_target_pairs={{0,15},{1,0},{2,1},{3,2},{4,3},{5,4},{6,5},{7,6},{8,7},{9,8},{10,9... | collective-permute-start | bytes 1474568 | tf_op jit(solution)/shard_map/ppermute | solution.py:212
  56.6 19.8 %all-to-all-start.2 = ((bf16[4,6,240,128]{3,2,1,0:T(8,128)(2,1)}), bf16[4,6,240,128]{3,2,1,0:T(8,128)(2,1)S(1)}, u32[]{:S(2)}, u32[]{:S(2)}) async-start(bf16[4,6,240,128]{3,2,1,0:T(8,128)(2,1)} %pick_part.4), calls=%async_computation.2 | async-start | bytes 2949120 | tf_op jit(solution)/shard_map/all_to_all | solution.py:216
  62.7 11.7 %collective-permute-start.5 = (bf16[240,1024]{1,0:T(8,128)(2,1)}, bf16[240,1024]{1,0:T(8,128)(2,1)S(1)}, u32[]{:S(2)}, u32[]{:S(2)}) collective-permute-start(bf16[240,1024]{1,0:T(8,128)(2,1)} %collective-permute-done.4.refs_2_), channel_id=1, source_target_pairs={{0,1},{1,2},{2,3},{3,4},{4,5},{5,6},{6,7},{7,8},{8,9},{9,10},{10,1... | collective-permute-start | bytes 1474568 | tf_op jit(solution)/shard_map/ppermute | solution.py:212
  65.0 11.5 %collective-permute-start.7 = (bf16[240,1024]{1,0:T(8,128)(2,1)}, bf16[240,1024]{1,0:T(8,128)(2,1)S(1)}, u32[]{:S(2)}, u32[]{:S(2)}) collective-permute-start(bf16[240,1024]{1,0:T(8,128)(2,1)} %collective-permute-done.6.refs_3_), channel_id=1, source_target_pairs={{0,15},{1,0},{2,1},{3,2},{4,3},{5,4},{6,5},{7,6},{8,7},{9,8},{10,9... | collective-permute-start | bytes 1474568 | tf_op jit(solution)/shard_map/ppermute | solution.py:212
  76.5 6.5 %copy-start = (bf16[4,6,240,128]{3,2,1,0:T(8,128)(2,1)}, bf16[4,6,240,128]{3,2,1,0:T(8,128)(2,1)S(1)}, u32[]{:S(2)}) copy-start(bf16[4,6,240,128]{3,2,1,0:T(8,128)(2,1)S(1)} %all-to-all-done.2) | copy-start | bytes 4423684
  76.5 11.0 %collective-permute-start.8 = (bf16[240,1024]{1,0:T(8,128)(2,1)S(1)}, bf16[240,1024]{1,0:T(8,128)(2,1)S(1)}, u32[]{:S(2)}, u32[]{:S(2)}) collective-permute-start(bf16[240,1024]{1,0:T(8,128)(2,1)S(1)} %collective-permute-done.5.refs_0_), channel_id=1, source_target_pairs={{0,1},{1,2},{2,3},{3,4},{4,5},{5,6},{6,7},{7,8},{8,9},{9,10},{10,1... | collective-permute-start | bytes 1474568 | tf_op jit(solution)/shard_map/ppermute | solution.py:212
  79.6 9.9 %collective-permute-start.9 = (bf16[240,1024]{1,0:T(8,128)(2,1)S(1)}, bf16[240,1024]{1,0:T(8,128)(2,1)}, u32[]{:S(2)}, u32[]{:S(2)}) collective-permute-start(bf16[240,1024]{1,0:T(8,128)(2,1)S(1)} %collective-permute-done.7.refs_1_), channel_id=1, source_target_pairs={{0,15},{1,0},{2,1},{3,2},{4,3},{5,4},{6,5},{7,6},{8,7},{9,8},{10,9... | collective-permute-start | bytes 1474568 | tf_op jit(solution)/shard_map/ppermute | solution.py:212
  83.0 24.4 %all-to-all-start.3 = ((bf16[4,8,240,128]{3,2,1,0:T(8,128)(2,1)}), bf16[4,8,240,128]{3,2,1,0:T(8,128)(2,1)}, u32[]{:S(2)}, u32[]{:S(2)}) async-start(bf16[4,8,240,128]{3,2,1,0:T(8,128)(2,1)} %pick_part.5), calls=%async_computation.3 | async-start | bytes 3932160 | tf_op jit(solution)/shard_map/all_to_all | solution.py:216
  87.5 11.2 %collective-permute-start.10 = (bf16[240,1024]{1,0:T(8,128)(2,1)S(1)}, bf16[240,1024]{1,0:T(8,128)(2,1)S(1)}, u32[]{:S(2)}, u32[]{:S(2)}) collective-permute-start(bf16[240,1024]{1,0:T(8,128)(2,1)S(1)} %collective-permute-done.8.refs_2_), channel_id=1, source_target_pairs={{0,1},{1,2},{2,3},{3,4},{4,5},{5,6},{6,7},{7,8},{8,9},{9,10},{10,1... | collective-permute-start | bytes 1474568 | tf_op jit(solution)/shard_map/ppermute | solution.py:212
  89.4 11.4 %collective-permute-start.11 = (bf16[240,1024]{1,0:T(8,128)(2,1)}, bf16[240,1024]{1,0:T(8,128)(2,1)S(1)}, u32[]{:S(2)}, u32[]{:S(2)}) collective-permute-start(bf16[240,1024]{1,0:T(8,128)(2,1)} %collective-permute-done.9.refs_3_), channel_id=1, source_target_pairs={{0,15},{1,0},{2,1},{3,2},{4,3},{5,4},{6,5},{7,6},{8,7},{9,8},{10,9... | collective-permute-start | bytes 1474568 | tf_op jit(solution)/shard_map/ppermute | solution.py:212
  100.9 11.2 %collective-permute-start.12 = (bf16[240,1024]{1,0:T(8,128)(2,1)S(1)}, bf16[240,1024]{1,0:T(8,128)(2,1)S(1)}, u32[]{:S(2)}, u32[]{:S(2)}) collective-permute-start(bf16[240,1024]{1,0:T(8,128)(2,1)S(1)} %collective-permute-done.10.refs_0_), channel_id=1, source_target_pairs={{0,1},{1,2},{2,3},{3,4},{4,5},{5,6},{6,7},{7,8},{8,9},{9,10},{10,1... | collective-permute-start | bytes 1474568 | tf_op jit(solution)/shard_map/ppermute | solution.py:212
  105.1 10.1 %collective-permute-start.13 = (bf16[240,1024]{1,0:T(8,128)(2,1)S(1)}, bf16[240,1024]{1,0:T(8,128)(2,1)S(1)}, u32[]{:S(2)}, u32[]{:S(2)}) collective-permute-start(bf16[240,1024]{1,0:T(8,128)(2,1)S(1)} %collective-permute-done.11.refs_1_), channel_id=1, source_target_pairs={{0,15},{1,0},{2,1},{3,2},{4,3},{5,4},{6,5},{7,6},{8,7},{9,8},{10,9... | collective-permute-start | bytes 1474568 | tf_op jit(solution)/shard_map/ppermute | solution.py:212
  107.4 14.4 %copy-start.4 = (s32[1,8,16]{2,1,0:T(8,128)S(1)}, s32[1,8,16]{2,1,0:T(8,128)}, u32[]{:S(2)}) copy-start(s32[1,8,16]{2,1,0:T(8,128)} %param.8) | copy-start | bytes 1540
  107.4 21.7 %all-to-all-start.4 = ((bf16[4,8,240,128]{3,2,1,0:T(8,128)(2,1)}), bf16[4,8,240,128]{3,2,1,0:T(8,128)(2,1)}, u32[]{:S(2)}, u32[]{:S(2)}) async-start(bf16[4,8,240,128]{3,2,1,0:T(8,128)(2,1)} %pick_part.6), calls=%async_computation.4 | async-start | bytes 3932160 | tf_op jit(solution)/shard_map/all_to_all | solution.py:216
  115.2 8.0 %collective-permute-start.14 = (bf16[112,1024]{1,0:T(8,128)(2,1)S(1)}, bf16[112,1024]{1,0:T(8,128)(2,1)S(1)}, u32[]{:S(2)}, u32[]{:S(2)}) collective-permute-start(bf16[112,1024]{1,0:T(8,128)(2,1)S(1)} %slice.6), channel_id=1, source_target_pairs={{0,1},{1,2},{2,3},{3,4},{4,5},{5,6},{6,7},{7,8},{8,9},{9,10},{10,1... | collective-permute-start | bytes 688136 | tf_op jit(solution)/shard_map/ppermute | solution.py:212
  118.6 7.5 %collective-permute-start.15 = (bf16[128,1024]{1,0:T(8,128)(2,1)S(1)}, bf16[128,1024]{1,0:T(8,128)(2,1)S(1)}, u32[]{:S(2)}, u32[]{:S(2)}) collective-permute-start(bf16[128,1024]{1,0:T(8,128)(2,1)S(1)} %slice.7), channel_id=1, source_target_pairs={{0,15},{1,0},{2,1},{3,2},{4,3},{5,4},{6,5},{7,6},{8,7},{9,8},{10,9... | collective-permute-start | bytes 786440 | tf_op jit(solution)/shard_map/ppermute | solution.py:212
  129.1 24.4 %all-to-all-start.5 = ((bf16[4,10,240,128]{3,2,1,0:T(8,128)(2,1)}), bf16[4,10,240,128]{3,2,1,0:T(8,128)(2,1)S(1)}, u32[]{:S(2)}, u32[]{:S(2)}) async-start(bf16[4,10,240,128]{3,2,1,0:T(8,128)(2,1)} %pick_part.7), calls=%async_computation.5 | async-start | bytes 4915200 | tf_op jit(solution)/shard_map/all_to_all | solution.py:216
  136.8 1.4 copy-start.1
  138.2 15.4 %copy-start.2 = (f32[1,1024]{1,0:T(1,128)S(1)}, f32[1,1024]{1,0:T(1,128)}, u32[]{:S(2)}) copy-start(f32[1,1024]{1,0:T(1,128)} %param.7) | copy-start | bytes 12292
  158.3 18.2 %collective-permute-start.16 = (bf16[240,640]{1,0:T(8,128)(2,1)S(1)}, bf16[240,640]{1,0:T(8,128)(2,1)S(1)}, u32[]{:S(2)}, u32[]{:S(2)}) collective-permute-start(bf16[240,640]{1,0:T(8,128)(2,1)S(1)} %mix_late.2), channel_id=1, source_target_pairs={{0,64},{64,128},{128,192},{192,256},{256,320},{320,384},{384,448},... | collective-permute-start | bytes 921608 | tf_op jit(solution)/shard_map/ppermute | solution.py:212
  174.0 2.5 %collective-permute-start.17 = (bf16[240,384]{1,0:T(8,128)(2,1)S(1)}, bf16[240,384]{1,0:T(8,128)(2,1)S(1)}, u32[]{:S(2)}, u32[]{:S(2)}) collective-permute-start(bf16[240,384]{1,0:T(8,128)(2,1)S(1)} %mix_late.3), channel_id=1, source_target_pairs={{0,64},{64,128},{128,192},{192,256},{256,320},{320,384},{384,448},... | collective-permute-start | bytes 552968 | tf_op jit(solution)/shard_map/ppermute | solution.py:212

commit v12 on v10

--- a/solution.py
+++ b/solution.py
@@ -17,13 +17,14 @@
 LATE_VMEM = 50 * 2**20
 MIX_WEIGHT = 10**10
 PICK_WEIGHT = 12 * 10**9
-AFTER = (2,)
-HAVE = (5, 8, 9, 9)
+AFTER = (2, 3)
+HAVE = (5, 8, 9, 9, 9)
 PARTS = (
     (0, -1, 1),
     (-2, 2, -3, 3),
     (-4, 4, -5, 5),
-    (-6, 6, -7, 7, 8),
+    (-6, 6),
+    (-7, 7, 8),
 )
 
 
@@ -280,6 +281,7 @@
         if all(o in held for o in PARTS[len(ready)]):
             ready.append(step)
     pick_next()
+    picked[-1], arrived[-1] = lax.optimization_barrier((picked[-1], arrived[-1]))
     send_next()
 
     codes = part_codes(slots, here)

time: 181 us -> 193 us (1.066)
  waiting for transfers between devices: 33.6 us -> 40.8 us
  starting transfers between devices: 96.1 us -> 101 us
    all_to_all x4 -> x5, waiting for transfers between devices: 5.95 us -> 10.3 us  [over_lines(): incoming = lax.all_to_all(outgoing, 'y', 0, 0, tiled=True)]
    all_to_all x4 -> x5, starting transfers between devices: 17.3 us -> 21.1 us  [over_lines(): incoming = lax.all_to_all(outgoing, 'y', 0, 0, tiled=True)]
    ppermute x18, waiting for transfers between devices: 24.1 us -> 26.8 us  [shifted(): lax.ppermute(value, axis, [(i, (i + by) % count) for i in range(count)])]
    pallas_call x4 -> x5, Pallas kernels: 10.2 us -> 12.3 us  [pick_call(): pl.pallas_call(kernel, grid_spec=pltpu.PrefetchScalarGridSpec(num_scalar_...]
  transfers between devices with their start and end apart: 23 -> 24, of which waited for: 17 -> 16; matrix products, arithmetic and copies ran while one was open for 3% -> 2% of each run, Pallas kernels for 13% -> 13%
where the time goes in v12:
time: 193 us; the launch traced here: 191 us
  starting transfers between devices  101 us (52%)
  waiting for transfers between devices  40.8 us (21%)
  Pallas kernels  29.7 us (15%)
  blocking collectives  9.43 us (5%)
  local copies, waits for them, and re-layouts  8.12 us (4%)
    ppermute x18, starting transfers between devices, shifted(): lax.ppermute(value, axis, [(i, (i + by) % count) for i in range(count)])  73.8 us
    ppermute x18, waiting for transfers between devices, shifted(): lax.ppermute(value, axis, [(i, (i + by) % count) for i in range(count)])  26.8 us
    all_to_all x5, starting transfers between devices, over_lines(): incoming = lax.all_to_all(outgoing, 'y', 0, 0, tiled=True)  21.1 us
    pallas_call x5, Pallas kernels, pick_call(): pl.pallas_call(kernel, grid_spec=pltpu.PrefetchScalarGridSpec(num_scalar_...  12.3 us
    all_to_all x5, waiting for transfers between devices, over_lines(): incoming = lax.all_to_all(outgoing, 'y', 0, 0, tiled=True)  10.3 us
    all_to_all x1, blocking collectives, body(): near = lax.all_to_all(lists, 'near', 0, 0, tiled=True)  9.43 us
    pallas_call x1, Pallas kernels, mix_early(): pl.pallas_call(kernel, grid_spec=pltpu.PrefetchScalarGridSpec(num_scalar_...  9.4 us
    pallas_call x2, Pallas kernels, mix_late(): pl.pallas_call(kernel, grid_spec=pltpu.PrefetchScalarGridSpec(num_scalar_...  8.02 us
  transfers between devices with their start and end apart: 24, of which 16 were waited for; matrix products, arithmetic and copies ran while one was open for 2% of the time, Pallas kernels for 13%

profile of v12, /device:TPU:1, one launch (start us, length us, event | category | flops | bytes accessed | tf_op | source)
XLA Modules:
  0.0 190.6 jit_solution(15183557992340114798)
XLA Ops:
  0.0 11.9 %collective-permute-start.1 = (bf16[240,1024]{1,0:T(8,128)(2,1)}, bf16[240,1024]{1,0:T(8,128)(2,1)S(1)}, u32[]{:S(2)}, u32[]{:S(2)}) collective-permute-start(bf16[240,1024]{1,0:T(8,128)(2,1)} %bitcast.190), channel_id=1, source_target_pairs={{0,15},{1,0},{2,1},{3,2},{4,3},{5,4},{6,5},{7,6},{8,7},{9,8},{10,9... | collective-permute-start | bytes 1474568 | tf_op jit(solution)/shard_map/ppermute | solution.py:212
  14.8 9.4 %all_to_all.35 = s32[4,4,4,2]{1,2,3,0:T(4,128)S(1)} all-to-all(s32[4,4,4,2]{1,2,3,0:T(4,128)S(1)} %copy.11), channel_id=1, replica_groups=mesh['segment'=8,'y'=4,'far'=4,'near'=4] {'near'}, dimensions={0} | all-to-all | bytes 1024 | tf_op jit(solution)/shard_map/all_to_all | solution.py:251
  24.2 2.8 %collective-permute-done.refs_1_ = bf16[240,1024]{1,0:T(8,128)(2,1)S(1)} collective-permute-done((bf16[240,1024]{1,0:T(8,128)(2,1)}, bf16[240,1024]{1,0:T(8,128)(2,1)S(1)}, u32[]{:S(2)}, u32[]{:S(2)}) %collective-permute-start) | collective-permute-done | bytes 491552 | tf_op jit(solution)/shard_map/ppermute | solution.py:212
  27.8 5.8 %all-to-all-start.1 = ((s32[4,4,4,2]{1,2,3,0:T(4,128)}), s32[4,4,4,2]{1,2,3,0:T(4,128)S(1)}, u32[]{:S(2)}, u32[]{:S(2)}) async-start(s32[4,4,4,2]{1,2,3,0:T(4,128)} %copy.12), calls=%async_computation.1 | async-start | bytes 32768 | tf_op jit(solution)/shard_map/all_to_all | solution.py:259
  35.6 5.9 %collective-permute-start.3 = (bf16[240,1024]{1,0:T(8,128)(2,1)S(1)}, bf16[240,1024]{1,0:T(8,128)(2,1)S(1)}, u32[]{:S(2)}, u32[]{:S(2)}) collective-permute-start(bf16[240,1024]{1,0:T(8,128)(2,1)S(1)} %collective-permute-done.1.refs_2_), channel_id=1, source_target_pairs={{0,15},{1,0},{2,1},{3,2},{4,3},{5,4},{6,5},{7,6},{8,7},{9,8},{10,9... | collective-permute-start | bytes 1474568 | tf_op jit(solution)/shard_map/ppermute | solution.py:212
  41.5 3.6 %all-to-all-done.1 = s32[4,4,4,2]{1,2,3,0:T(4,128)S(1)} async-done(((s32[4,4,4,2]{1,2,3,0:T(4,128)}), s32[4,4,4,2]{1,2,3,0:T(4,128)S(1)}, u32[]{:S(2)}, u32[]{:S(2)}) %all-to-all-start.1) | async-done | bytes 544 | tf_op jit(solution)/shard_map/all_to_all | solution.py:259
  51.3 5.3 %collective-permute-start.6 = (bf16[240,1024]{1,0:T(8,128)(2,1)S(1)}, bf16[240,1024]{1,0:T(8,128)(2,1)}, u32[]{:S(2)}, u32[]{:S(2)}) collective-permute-start(bf16[240,1024]{1,0:T(8,128)(2,1)S(1)} %collective-permute-done.3.refs_1_), channel_id=1, source_target_pairs={{0,15},{1,0},{2,1},{3,2},{4,3},{5,4},{6,5},{7,6},{8,7},{9,8},{10,9... | collective-permute-start | bytes 1474568 | tf_op jit(solution)/shard_map/ppermute | solution.py:212
  56.6 4.2 %all-to-all-start.2 = ((bf16[4,6,240,128]{3,2,1,0:T(8,128)(2,1)}), bf16[4,6,240,128]{3,2,1,0:T(8,128)(2,1)S(1)}, u32[]{:S(2)}, u32[]{:S(2)}) async-start(bf16[4,6,240,128]{3,2,1,0:T(8,128)(2,1)} %pick_part.5), calls=%async_computation.2 | async-start | bytes 2949120 | tf_op jit(solution)/shard_map/all_to_all | solution.py:216
  65.0 4.2 %collective-permute-start.7 = (bf16[240,1024]{1,0:T(8,128)(2,1)}, bf16[240,1024]{1,0:T(8,128)(2,1)S(1)}, u32[]{:S(2)}, u32[]{:S(2)}) collective-permute-start(bf16[240,1024]{1,0:T(8,128)(2,1)} %collective-permute-done.6.refs_3_), channel_id=1, source_target_pairs={{0,15},{1,0},{2,1},{3,2},{4,3},{5,4},{6,5},{7,6},{8,7},{9,8},{10,9... | collective-permute-start | bytes 1474568 | tf_op jit(solution)/shard_map/ppermute | solution.py:212
  69.2 3.1 %pick_part.6 = bf16[4,8,240,128]{3,2,1,0:T(8,128)(2,1)} custom-call(s32[128]{0:T(128)S(1)} %reshape.223.ids_ref, s32[1]{0:T(128)} %bitcast.31.here_ref, bf16[240,1024]{1,0:T(8,128)(2,1)S(1)} %collective-permute-done.2.refs_0_, bf16[240,1024]{1,0:T(8,128)(2,1)S(1)} %collective-permute-done.3.refs_1_, bf16[240,1024]{1,0:T(8,128)(2,1)} %collective-permute-done.4.refs_2_, ...), custom_call_target="tpu_custom_call" | custom-call | flops 12000000000 | bytes 3932160 | tf_op jit(solution)/shard_map/pick_part/pallas_call | solution.py:51
  77.6 4.4 %all-to-all-start.3 = ((bf16[4,8,240,128]{3,2,1,0:T(8,128)(2,1)}), bf16[4,8,240,128]{3,2,1,0:T(8,128)(2,1)}, u32[]{:S(2)}, u32[]{:S(2)}) async-start(bf16[4,8,240,128]{3,2,1,0:T(8,128)(2,1)} %pick_part.6), calls=%async_computation.3 | async-start | bytes 3932160 | tf_op jit(solution)/shard_map/all_to_all | solution.py:216
  82.0 3.1 %collective-permute-start.8 = (bf16[240,1024]{1,0:T(8,128)(2,1)S(1)}, bf16[240,1024]{1,0:T(8,128)(2,1)S(1)}, u32[]{:S(2)}, u32[]{:S(2)}) collective-permute-start(bf16[240,1024]{1,0:T(8,128)(2,1)S(1)} %collective-permute-done.5.refs_0_), channel_id=1, source_target_pairs={{0,1},{1,2},{2,3},{3,4},{4,5},{5,6},{6,7},{7,8},{8,9},{9,10},{10,1... | collective-permute-start | bytes 1474568 | tf_op jit(solution)/shard_map/ppermute | solution.py:212
  85.1 3.4 %collective-permute-start.9 = (bf16[240,1024]{1,0:T(8,128)(2,1)S(1)}, bf16[240,1024]{1,0:T(8,128)(2,1)S(1)}, u32[]{:S(2)}, u32[]{:S(2)}) collective-permute-start(bf16[240,1024]{1,0:T(8,128)(2,1)S(1)} %collective-permute-done.7.refs_1_), channel_id=1, source_target_pairs={{0,15},{1,0},{2,1},{3,2},{4,3},{5,4},{6,5},{7,6},{8,7},{9,8},{10,9... | collective-permute-start | bytes 1474568 | tf_op jit(solution)/shard_map/ppermute | solution.py:212
  88.7 4.5 %collective-permute-done.8.refs_2_ = bf16[240,1024]{1,0:T(8,128)(2,1)S(1)} collective-permute-done((bf16[240,1024]{1,0:T(8,128)(2,1)S(1)}, bf16[240,1024]{1,0:T(8,128)(2,1)S(1)}, u32[]{:S(2)}, u32[]{:S(2)}) %collective-permute-start.8) | collective-permute-done | bytes 491552 | tf_op jit(solution)/shard_map/ppermute | solution.py:212
  95.2 4.6 %collective-permute-start.11 = (bf16[240,1024]{1,0:T(8,128)(2,1)S(1)}, bf16[240,1024]{1,0:T(8,128)(2,1)S(1)}, u32[]{:S(2)}, u32[]{:S(2)}) collective-permute-start(bf16[240,1024]{1,0:T(8,128)(2,1)S(1)} %collective-permute-done.9.refs_3_), channel_id=1, source_target_pairs={{0,15},{1,0},{2,1},{3,2},{4,3},{5,4},{6,5},{7,6},{8,7},{9,8},{10,9... | collective-permute-start | bytes 1474568 | tf_op jit(solution)/shard_map/ppermute | solution.py:212
  99.7 2.6 %pick_part.7 = bf16[4,8,240,128]{3,2,1,0:T(8,128)(2,1)} custom-call(s32[128]{0:T(128)S(1)} %reshape.223.ids_ref, s32[1]{0:T(128)} %bitcast.31.here_ref, bf16[240,1024]{1,0:T(8,128)(2,1)S(1)} %collective-permute-done.5.refs_0_, bf16[240,1024]{1,0:T(8,128)(2,1)S(1)} %collective-permute-done.7.refs_1_, bf16[240,1024]{1,0:T(8,128)(2,1)S(1)} %collective-permute-done.8.refs_2_, ...), custom_call_target="tpu_custom_call" | custom-call | flops 12000000000 | bytes 3932160 | tf_op jit(solution)/shard_map/pick_part/pallas_call | solution.py:51
  106.3 4.4 %all-to-all-start.4 = ((bf16[4,8,240,128]{3,2,1,0:T(8,128)(2,1)}), bf16[4,8,240,128]{3,2,1,0:T(8,128)(2,1)}, u32[]{:S(2)}, u32[]{:S(2)}) async-start(bf16[4,8,240,128]{3,2,1,0:T(8,128)(2,1)} %pick_part.7), calls=%async_computation.4 | async-start | bytes 3932160 | tf_op jit(solution)/shard_map/all_to_all | solution.py:216
  111.0 4.3 %collective-permute-start.12 = (bf16[240,1024]{1,0:T(8,128)(2,1)S(1)}, bf16[240,1024]{1,0:T(8,128)(2,1)S(1)}, u32[]{:S(2)}, u32[]{:S(2)}) collective-permute-start(bf16[240,1024]{1,0:T(8,128)(2,1)S(1)} %collective-permute-done.10.refs_0_), channel_id=1, source_target_pairs={{0,1},{1,2},{2,3},{3,4},{4,5},{5,6},{6,7},{7,8},{8,9},{9,10},{10,1... | collective-permute-start | bytes 1474568 | tf_op jit(solution)/shard_map/ppermute | solution.py:212
  119.5 2.3 %collective-permute-done.12.refs_0_ = bf16[240,1024]{1,0:T(8,128)(2,1)S(1)} collective-permute-done((bf16[240,1024]{1,0:T(8,128)(2,1)S(1)}, bf16[240,1024]{1,0:T(8,128)(2,1)S(1)}, u32[]{:S(2)}, u32[]{:S(2)}) %collective-permute-start.12) | collective-permute-done | bytes 491552 | tf_op jit(solution)/shard_map/ppermute | solution.py:212
  121.8 3.8 %collective-permute-done.13.refs_1_ = bf16[240,1024]{1,0:T(8,128)(2,1)S(1)} collective-permute-done((bf16[240,1024]{1,0:T(8,128)(2,1)S(1)}, bf16[240,1024]{1,0:T(8,128)(2,1)S(1)}, u32[]{:S(2)}, u32[]{:S(2)}) %collective-permute-start.13) | collective-permute-done | bytes 491552 | tf_op jit(solution)/shard_map/ppermute | solution.py:212
  125.6 3.4 %collective-permute-start.14 = (bf16[112,1024]{1,0:T(8,128)(2,1)S(1)}, bf16[112,1024]{1,0:T(8,128)(2,1)S(1)}, u32[]{:S(2)}, u32[]{:S(2)}) collective-permute-start(bf16[112,1024]{1,0:T(8,128)(2,1)S(1)} %slice.6), channel_id=1, source_target_pairs={{0,1},{1,2},{2,3},{3,4},{4,5},{5,6},{6,7},{7,8},{8,9},{9,10},{10,1... | collective-permute-start | bytes 688136 | tf_op jit(solution)/shard_map/ppermute | solution.py:212
  129.0 3.1 %collective-permute-start.15 = (bf16[128,1024]{1,0:T(8,128)(2,1)S(1)}, bf16[128,1024]{1,0:T(8,128)(2,1)S(1)}, u32[]{:S(2)}, u32[]{:S(2)}) collective-permute-start(bf16[128,1024]{1,0:T(8,128)(2,1)S(1)} %slice.7), channel_id=1, source_target_pairs={{0,15},{1,0},{2,1},{3,2},{4,3},{5,4},{6,5},{7,6},{8,7},{9,8},{10,9... | collective-permute-start | bytes 786440 | tf_op jit(solution)/shard_map/ppermute | solution.py:212
  135.1 4.4 %all-to-all-start.5 = ((bf16[4,4,240,128]{3,2,1,0:T(8,128)(2,1)}), bf16[4,4,240,128]{3,2,1,0:T(8,128)(2,1)S(1)}, u32[]{:S(2)}, u32[]{:S(2)}) async-start(bf16[4,4,240,128]{3,2,1,0:T(8,128)(2,1)} %pick_part.8), calls=%async_computation.5 | async-start | bytes 1966080 | tf_op jit(solution)/shard_map/all_to_all | solution.py:216
  139.5 2.3 %pick_part.9 = bf16[4,6,240,128]{3,2,1,0:T(8,128)(2,1)} custom-call(s32[128]{0:T(128)S(1)} %reshape.223.ids_ref, s32[1]{0:T(128)} %bitcast.31.here_ref, bf16[240,1024]{1,0:T(8,128)(2,1)S(1)} %collective-permute-done.12.refs_0_, bf16[240,1024]{1,0:T(8,128)(2,1)S(1)} %collective-permute-done.13.refs_1_, bf16[112,1024]{1,0:T(8,128)(2,1)S(1)} %collective-permute-done.14.refs_2_, ...), custom_call_target="tpu_custom_call" | custom-call | flops 12000000000 | bytes 2949120 | tf_op jit(solution)/shard_map/pick_part/pallas_call | solution.py:51
  141.8 7.1 %all-to-all-done.5 = bf16[4,4,240,128]{3,2,1,0:T(8,128)(2,1)S(1)} async-done(((bf16[4,4,240,128]{3,2,1,0:T(8,128)(2,1)}), bf16[4,4,240,128]{3,2,1,0:T(8,128)(2,1)S(1)}, u32[]{:S(2)}, u32[]{:S(2)}) %all-to-all-start.5) | async-done | bytes 983072 | tf_op jit(solution)/shard_map/all_to_all | solution.py:216
  148.9 3.6 %all-to-all-start.6 = ((bf16[4,6,240,128]{3,2,1,0:T(8,128)(2,1)}), bf16[4,6,240,128]{3,2,1,0:T(8,128)(2,1)S(1)}, u32[]{:S(2)}, u32[]{:S(2)}) async-start(bf16[4,6,240,128]{3,2,1,0:T(8,128)(2,1)} %pick_part.9), calls=%async_computation.6 | async-start | bytes 2949120 | tf_op jit(solution)/shard_map/all_to_all | solution.py:216
  153.9 9.4 %mix_early.1.early_ref = f32[240,1024]{1,0:T(8,128)S(1)} custom-call(s32[128]{0:T(128)S(1)} %select_select_fusion.codes_ref, bf16[24,240,128]{2,1,0:T(8,128)(2,1)S(1)} %bitcast.186, bf16[32,240,128]{2,1,0:T(8,128)(2,1)} %bitcast.33.refs_1_, bf16[32,240,128]{2,1,0:T(8,128)(2,1)} %bitcast.34.refs_2_, bf16[16,240,128]{2,1,0:T(8,128)(2,1)S(1)} %bitcast.187, ...), custom_call_target="tpu_custom_call" | custom-call | flops 10000000000 | bytes 10584064 | tf_op jit(solution)/shard_map/mix_early/pallas_call | solution.py:117
  163.3 3.3 %all-to-all-done.6 = bf16[4,6,240,128]{3,2,1,0:T(8,128)(2,1)S(1)} async-done(((bf16[4,6,240,128]{3,2,1,0:T(8,128)(2,1)}), bf16[4,6,240,128]{3,2,1,0:T(8,128)(2,1)S(1)}, u32[]{:S(2)}, u32[]{:S(2)}) %all-to-all-start.6) | async-done | bytes 1474592 | tf_op jit(solution)/shard_map/all_to_all | solution.py:216
  166.6 4.6 %mix_late.2 = bf16[240,640]{1,0:T(8,128)(2,1)S(1)} custom-call(s32[128]{0:T(128)S(1)} %reshape.220.place_ref, s32[128]{0:T(128)S(1)} %reshape.221.which_ref, s32[8]{0:T(128)S(1)} %get-tuple-element.61.count_ref, f32[240,1024]{1,0:T(8,128)S(1)} %mix_early.1.early_ref, bf16[24,240,128]{2,1,0:T(8,128)(2,1)S(1)} %bitcast.184, ...), custom_call_target="tpu_custom_call" | custom-call | flops 629145600 | bytes 4096000 | tf_op jit(solution)/shard_map/mix_late/pallas_call | solution.py:183
  171.1 12.6 %collective-permute-start.16 = (bf16[240,640]{1,0:T(8,128)(2,1)S(1)}, bf16[240,640]{1,0:T(8,128)(2,1)S(1)}, u32[]{:S(2)}, u32[]{:S(2)}) collective-permute-start(bf16[240,640]{1,0:T(8,128)(2,1)S(1)} %mix_late.2), channel_id=1, source_target_pairs={{0,64},{64,128},{128,192},{192,256},{256,320},{320,384},{384,448},... | collective-permute-start | bytes 921608 | tf_op jit(solution)/shard_map/ppermute | solution.py:212
  183.8 3.4 %mix_late.3 = bf16[240,384]{1,0:T(8,128)(2,1)S(1)} custom-call(s32[128]{0:T(128)S(1)} %reshape.220.place_ref, s32[128]{0:T(128)S(1)} %reshape.221.which_ref, s32[8]{0:T(128)S(1)} %get-tuple-element.61.count_ref, f32[240,1024]{1,0:T(8,128)S(1)} %mix_early.1.early_ref, bf16[24,240,128]{2,1,0:T(8,128)(2,1)S(1)} %bitcast.185, ...), custom_call_target="tpu_custom_call" | custom-call | flops 377487360 | bytes 3047424 | tf_op jit(solution)/shard_map/mix_late/pallas_call | solution.py:183
  187.2 2.5 %collective-permute-done.17 = bf16[240,384]{1,0:T(8,128)(2,1)S(1)} collective-permute-done((bf16[240,384]{1,0:T(8,128)(2,1)S(1)}, bf16[240,384]{1,0:T(8,128)(2,1)S(1)}, u32[]{:S(2)}, u32[]{:S(2)}) %collective-permute-start.17) | collective-permute-done | bytes 184352 | tf_op jit(solution)/shard_map/ppermute | solution.py:212
  (80 shorter events, 36.9 us)
Async XLA Ops:
  0.0 24.2 %collective-permute-start.1 = (bf16[240,1024]{1,0:T(8,128)(2,1)}, bf16[240,1024]{1,0:T(8,128)(2,1)S(1)}, u32[]{:S(2)}, u32[]{:S(2)}) collective-permute-start(bf16[240,1024]{1,0:T(8,128)(2,1)} %bitcast.190), channel_id=1, source_target_pairs={{0,15},{1,0},{2,1},{3,2},{4,3},{5,4},{6,5},{7,6},{8,7},{9,8},{10,9... | collective-permute-start | bytes 1474568 | tf_op jit(solution)/shard_map/ppermute | solution.py:212
  12.0 15.1 %collective-permute-start = (bf16[240,1024]{1,0:T(8,128)(2,1)}, bf16[240,1024]{1,0:T(8,128)(2,1)S(1)}, u32[]{:S(2)}, u32[]{:S(2)}) collective-permute-start(bf16[240,1024]{1,0:T(8,128)(2,1)} %bitcast.191), channel_id=1, source_target_pairs={{0,1},{1,2},{2,3},{3,4},{4,5},{5,6},{6,7},{7,8},{8,9},{9,10},{10,1... | collective-permute-start | bytes 1474568 | tf_op jit(solution)/shard_map/ppermute | solution.py:212
  27.8 17.4 %all-to-all-start.1 = ((s32[4,4,4,2]{1,2,3,0:T(4,128)}), s32[4,4,4,2]{1,2,3,0:T(4,128)S(1)}, u32[]{:S(2)}, u32[]{:S(2)}) async-start(s32[4,4,4,2]{1,2,3,0:T(4,128)} %copy.12), calls=%async_computation.1 | async-start | bytes 32768 | tf_op jit(solution)/shard_map/all_to_all | solution.py:259
  33.6 15.5 %collective-permute-start.2 = (bf16[240,1024]{1,0:T(8,128)(2,1)S(1)}, bf16[240,1024]{1,0:T(8,128)(2,1)S(1)}, u32[]{:S(2)}, u32[]{:S(2)}) collective-permute-start(bf16[240,1024]{1,0:T(8,128)(2,1)S(1)} %collective-permute-done.refs_1_), channel_id=1, source_target_pairs={{0,1},{1,2},{2,3},{3,4},{4,5},{5,6},{6,7},{7,8},{8,9},{9,10},{10,1... | collective-permute-start | bytes 1474568 | tf_op jit(solution)/shard_map/ppermute | solution.py:212
  35.6 13.8 %collective-permute-start.3 = (bf16[240,1024]{1,0:T(8,128)(2,1)S(1)}, bf16[240,1024]{1,0:T(8,128)(2,1)S(1)}, u32[]{:S(2)}, u32[]{:S(2)}) collective-permute-start(bf16[240,1024]{1,0:T(8,128)(2,1)S(1)} %collective-permute-done.1.refs_2_), channel_id=1, source_target_pairs={{0,15},{1,0},{2,1},{3,2},{4,3},{5,4},{6,5},{7,6},{8,7},{9,8},{10,9... | collective-permute-start | bytes 1474568 | tf_op jit(solution)/shard_map/ppermute | solution.py:212
  45.5 1.0 copy-start.3
  49.4 13.3 %collective-permute-start.4 = (bf16[240,1024]{1,0:T(8,128)(2,1)S(1)}, bf16[240,1024]{1,0:T(8,128)(2,1)}, u32[]{:S(2)}, u32[]{:S(2)}) collective-permute-start(bf16[240,1024]{1,0:T(8,128)(2,1)S(1)} %collective-permute-done.2.refs_0_), channel_id=1, source_target_pairs={{0,1},{1,2},{2,3},{3,4},{4,5},{5,6},{6,7},{7,8},{8,9},{9,10},{10,1... | collective-permute-start | bytes 1474568 | tf_op jit(solution)/shard_map/ppermute | solution.py:212
  51.3 13.7 %collective-permute-start.6 = (bf16[240,1024]{1,0:T(8,128)(2,1)S(1)}, bf16[240,1024]{1,0:T(8,128)(2,1)}, u32[]{:S(2)}, u32[]{:S(2)}) collective-permute-start(bf16[240,1024]{1,0:T(8,128)(2,1)S(1)} %collective-permute-done.3.refs_1_), channel_id=1, source_target_pairs={{0,15},{1,0},{2,1},{3,2},{4,3},{5,4},{6,5},{7,6},{8,7},{9,8},{10,9... | collective-permute-start | bytes 1474568 | tf_op jit(solution)/shard_map/ppermute | solution.py:212
  56.6 19.8 %all-to-all-start.2 = ((bf16[4,6,240,128]{3,2,1,0:T(8,128)(2,1)}), bf16[4,6,240,128]{3,2,1,0:T(8,128)(2,1)S(1)}, u32[]{:S(2)}, u32[]{:S(2)}) async-start(bf16[4,6,240,128]{3,2,1,0:T(8,128)(2,1)} %pick_part.5), calls=%async_computation.2 | async-start | bytes 2949120 | tf_op jit(solution)/shard_map/all_to_all | solution.py:216
  62.7 11.7 %collective-permute-start.5 = (bf16[240,1024]{1,0:T(8,128)(2,1)}, bf16[240,1024]{1,0:T(8,128)(2,1)S(1)}, u32[]{:S(2)}, u32[]{:S(2)}) collective-permute-start(bf16[240,1024]{1,0:T(8,128)(2,1)} %collective-permute-done.4.refs_2_), channel_id=1, source_target_pairs={{0,1},{1,2},{2,3},{3,4},{4,5},{5,6},{6,7},{7,8},{8,9},{9,10},{10,1... | collective-permute-start | bytes 1474568 | tf_op jit(solution)/shard_map/ppermute | solution.py:212
  65.0 11.5 %collective-permute-start.7 = (bf16[240,1024]{1,0:T(8,128)(2,1)}, bf16[240,1024]{1,0:T(8,128)(2,1)S(1)}, u32[]{:S(2)}, u32[]{:S(2)}) collective-permute-start(bf16[240,1024]{1,0:T(8,128)(2,1)} %collective-permute-done.6.refs_3_), channel_id=1, source_target_pairs={{0,15},{1,0},{2,1},{3,2},{4,3},{5,4},{6,5},{7,6},{8,7},{9,8},{10,9... | collective-permute-start | bytes 1474568 | tf_op jit(solution)/shard_map/ppermute | solution.py:212
  76.5 1.1 copy-start
  76.5 12.1 %copy-start.4 = (s32[1,8,16]{2,1,0:T(8,128)S(1)}, s32[1,8,16]{2,1,0:T(8,128)}, u32[]{:S(2)}) copy-start(s32[1,8,16]{2,1,0:T(8,128)} %param.8) | copy-start | bytes 1540
  77.6 28.7 %all-to-all-start.3 = ((bf16[4,8,240,128]{3,2,1,0:T(8,128)(2,1)}), bf16[4,8,240,128]{3,2,1,0:T(8,128)(2,1)}, u32[]{:S(2)}, u32[]{:S(2)}) async-start(bf16[4,8,240,128]{3,2,1,0:T(8,128)(2,1)} %pick_part.6), calls=%async_computation.3 | async-start | bytes 3932160 | tf_op jit(solution)/shard_map/all_to_all | solution.py:216
  82.0 11.2 %collective-permute-start.8 = (bf16[240,1024]{1,0:T(8,128)(2,1)S(1)}, bf16[240,1024]{1,0:T(8,128)(2,1)S(1)}, u32[]{:S(2)}, u32[]{:S(2)}) collective-permute-start(bf16[240,1024]{1,0:T(8,128)(2,1)S(1)} %collective-permute-done.5.refs_0_), channel_id=1, source_target_pairs={{0,1},{1,2},{2,3},{3,4},{4,5},{5,6},{6,7},{7,8},{8,9},{9,10},{10,1... | collective-permute-start | bytes 1474568 | tf_op jit(solution)/shard_map/ppermute | solution.py:212
  85.1 10.0 %collective-permute-start.9 = (bf16[240,1024]{1,0:T(8,128)(2,1)S(1)}, bf16[240,1024]{1,0:T(8,128)(2,1)S(1)}, u32[]{:S(2)}, u32[]{:S(2)}) collective-permute-start(bf16[240,1024]{1,0:T(8,128)(2,1)S(1)} %collective-permute-done.7.refs_1_), channel_id=1, source_target_pairs={{0,15},{1,0},{2,1},{3,2},{4,3},{5,4},{6,5},{7,6},{8,7},{9,8},{10,9... | collective-permute-start | bytes 1474568 | tf_op jit(solution)/shard_map/ppermute | solution.py:212
  93.2 11.2 %collective-permute-start.10 = (bf16[240,1024]{1,0:T(8,128)(2,1)S(1)}, bf16[240,1024]{1,0:T(8,128)(2,1)S(1)}, u32[]{:S(2)}, u32[]{:S(2)}) collective-permute-start(bf16[240,1024]{1,0:T(8,128)(2,1)S(1)} %collective-permute-done.8.refs_2_), channel_id=1, source_target_pairs={{0,1},{1,2},{2,3},{3,4},{4,5},{5,6},{6,7},{7,8},{8,9},{9,10},{10,1... | collective-permute-start | bytes 1474568 | tf_op jit(solution)/shard_map/ppermute | solution.py:212
  95.2 11.2 %collective-permute-start.11 = (bf16[240,1024]{1,0:T(8,128)(2,1)S(1)}, bf16[240,1024]{1,0:T(8,128)(2,1)S(1)}, u32[]{:S(2)}, u32[]{:S(2)}) collective-permute-start(bf16[240,1024]{1,0:T(8,128)(2,1)S(1)} %collective-permute-done.9.refs_3_), channel_id=1, source_target_pairs={{0,15},{1,0},{2,1},{3,2},{4,3},{5,4},{6,5},{7,6},{8,7},{9,8},{10,9... | collective-permute-start | bytes 1474568 | tf_op jit(solution)/shard_map/ppermute | solution.py:212
  106.3 28.7 %all-to-all-start.4 = ((bf16[4,8,240,128]{3,2,1,0:T(8,128)(2,1)}), bf16[4,8,240,128]{3,2,1,0:T(8,128)(2,1)}, u32[]{:S(2)}, u32[]{:S(2)}) async-start(bf16[4,8,240,128]{3,2,1,0:T(8,128)(2,1)} %pick_part.7), calls=%async_computation.4 | async-start | bytes 3932160 | tf_op jit(solution)/shard_map/all_to_all | solution.py:216
  111.0 10.8 %collective-permute-start.12 = (bf16[240,1024]{1,0:T(8,128)(2,1)S(1)}, bf16[240,1024]{1,0:T(8,128)(2,1)S(1)}, u32[]{:S(2)}, u32[]{:S(2)}) collective-permute-start(bf16[240,1024]{1,0:T(8,128)(2,1)S(1)} %collective-permute-done.10.refs_0_), channel_id=1, source_target_pairs={{0,1},{1,2},{2,3},{3,4},{4,5},{5,6},{6,7},{7,8},{8,9},{9,10},{10,1... | collective-permute-start | bytes 1474568 | tf_op jit(solution)/shard_map/ppermute | solution.py:212
  115.3 10.2 %collective-permute-start.13 = (bf16[240,1024]{1,0:T(8,128)(2,1)S(1)}, bf16[240,1024]{1,0:T(8,128)(2,1)S(1)}, u32[]{:S(2)}, u32[]{:S(2)}) collective-permute-start(bf16[240,1024]{1,0:T(8,128)(2,1)S(1)} %collective-permute-done.11.refs_1_), channel_id=1, source_target_pairs={{0,15},{1,0},{2,1},{3,2},{4,3},{5,4},{6,5},{7,6},{8,7},{9,8},{10,9... | collective-permute-start | bytes 1474568 | tf_op jit(solution)/shard_map/ppermute | solution.py:212
  125.6 14.0 %collective-permute-start.14 = (bf16[112,1024]{1,0:T(8,128)(2,1)S(1)}, bf16[112,1024]{1,0:T(8,128)(2,1)S(1)}, u32[]{:S(2)}, u32[]{:S(2)}) collective-permute-start(bf16[112,1024]{1,0:T(8,128)(2,1)S(1)} %slice.6), channel_id=1, source_target_pairs={{0,1},{1,2},{2,3},{3,4},{4,5},{5,6},{6,7},{7,8},{8,9},{9,10},{10,1... | collective-permute-start | bytes 688136 | tf_op jit(solution)/shard_map/ppermute | solution.py:212
  129.0 10.6 %collective-permute-start.15 = (bf16[128,1024]{1,0:T(8,128)(2,1)S(1)}, bf16[128,1024]{1,0:T(8,128)(2,1)S(1)}, u32[]{:S(2)}, u32[]{:S(2)}) collective-permute-start(bf16[128,1024]{1,0:T(8,128)(2,1)S(1)} %slice.7), channel_id=1, source_target_pairs={{0,15},{1,0},{2,1},{3,2},{4,3},{5,4},{6,5},{7,6},{8,7},{9,8},{10,9... | collective-permute-start | bytes 786440 | tf_op jit(solution)/shard_map/ppermute | solution.py:212
  135.1 13.8 %all-to-all-start.5 = ((bf16[4,4,240,128]{3,2,1,0:T(8,128)(2,1)}), bf16[4,4,240,128]{3,2,1,0:T(8,128)(2,1)S(1)}, u32[]{:S(2)}, u32[]{:S(2)}) async-start(bf16[4,4,240,128]{3,2,1,0:T(8,128)(2,1)} %pick_part.8), calls=%async_computation.5 | async-start | bytes 1966080 | tf_op jit(solution)/shard_map/all_to_all | solution.py:216
  148.9 17.6 %all-to-all-start.6 = ((bf16[4,6,240,128]{3,2,1,0:T(8,128)(2,1)}), bf16[4,6,240,128]{3,2,1,0:T(8,128)(2,1)S(1)}, u32[]{:S(2)}, u32[]{:S(2)}) async-start(bf16[4,6,240,128]{3,2,1,0:T(8,128)(2,1)} %pick_part.9), calls=%async_computation.6 | async-start | bytes 2949120 | tf_op jit(solution)/shard_map/all_to_all | solution.py:216
  152.5 1.4 copy-start.1
  153.9 12.7 %copy-start.2 = (f32[1,1024]{1,0:T(1,128)S(1)}, f32[1,1024]{1,0:T(1,128)}, u32[]{:S(2)}) copy-start(f32[1,1024]{1,0:T(1,128)} %param.7) | copy-start | bytes 12292
  171.1 18.6 %collective-permute-start.16 = (bf16[240,640]{1,0:T(8,128)(2,1)S(1)}, bf16[240,640]{1,0:T(8,128)(2,1)S(1)}, u32[]{:S(2)}, u32[]{:S(2)}) collective-permute-start(bf16[240,640]{1,0:T(8,128)(2,1)S(1)} %mix_late.2), channel_id=1, source_target_pairs={{0,64},{64,128},{128,192},{192,256},{256,320},{320,384},{384,448},... | collective-permute-start | bytes 921608 | tf_op jit(solution)/shard_map/ppermute | solution.py:212
  187.2 2.5 %collective-permute-start.17 = (bf16[240,384]{1,0:T(8,128)(2,1)S(1)}, bf16[240,384]{1,0:T(8,128)(2,1)S(1)}, u32[]{:S(2)}, u32[]{:S(2)}) collective-permute-start(bf16[240,384]{1,0:T(8,128)(2,1)S(1)} %mix_late.3), channel_id=1, source_target_pairs={{0,64},{64,128},{128,192},{192,256},{256,320},{320,384},{384,448},... | collective-permute-start | bytes 552968 | tf_op jit(solution)/shard_map/ppermute | solution.py:212
